TPU v7x, 512 devices: a whole 4x8x8 slice. The times are simulated.
512 devices in a mesh: dp: 2 (over core), row: 16 (over y, z_hi), col: 16 (over x, z_lo).
Axes of the slice: x: 4, y: 8, z: 8 (z_hi: 2, z_lo: 4; z = z_hi * 4 + z_lo), core: 2. Of those that a mesh axis runs over, the one named last changes fastest.
Arguments:
- patches: bfloat16 [1536, 6144], P(('dp', 'col'), 'row'), may hold values from -250 to 250
- norm_gain: float32 [6144], P('row'), may hold values from 0.1 to 1.9
- w_in: bfloat16 [6144, 12288], P('row', 'col'), may hold values from -0.078125 to 0.078125
- w_out: bfloat16 [12288, 6144], P('col', 'row'), may hold values from -0.0546875 to 0.0546875
- out_grad: bfloat16 [1536, 6144], P(('dp', 'col'), 'row'), may hold values from -3 to 3
Outputs:
- branch: bfloat16 [1536, 6144], P(('dp', 'col'), 'row')
- grad_patches: bfloat16 [1536, 6144], P(('dp', 'col'), 'row')
- grad_w_in: float32 [6144, 12288], P('row', 'col')
- grad_w_out: float32 [12288, 6144], P('col', 'row')
- grad_gain: float32 [6144], P('row')
All inputs are finite; a program needn't handle non-finite values.
Results may differ from a plain program's by a relative error of at most 0.034.
Values may be sent and summed in bfloat16 or wider, within the bound.
No kernel may reach another device: no remote copies, remote signals or barrier semaphores. Data moves between devices by JAX's collectives and lax.ppermute only.
A program may use at most 64 MiB of HBM per device.

v0:
```python
import jax
import jax.numpy as jnp
from jax import lax
from jax.sharding import PartitionSpec as P

D = 6144


def contract_tokens(left, right):
    return lax.dot_general(
        left, right, (((0,), (0,)), ((), ())), preferred_element_type=jnp.float32
    )


def contract_last(left, right):
    return lax.dot_general(
        left, right, (((1,), (1,)), ((), ())), preferred_element_type=jnp.float32
    )


def statistics(values):
    return (jnp.sum(values, axis=1), jnp.sum(values * values, axis=1))


def finish_norm(values, sums, squares):
    average = (sums / D)[:, None]
    inverse = lax.rsqrt((squares / D)[:, None] - average * average + 1e-06)
    return ((values - average) * inverse, inverse)


def shards(patches, norm_gain, w_in, w_out, out_grad):
    values = patches.astype(jnp.float32)
    sums, squares = lax.psum(statistics(values), "row")
    centred, inverse = finish_norm(values, sums, squares)
    normed_panel = lax.all_gather(
        (centred * norm_gain).astype(jnp.bfloat16), "col", axis=0, tiled=True
    )
    picked = normed_panel
    pre = lax.psum_scatter(
        jnp.dot(picked, w_in, preferred_element_type=jnp.float32).astype(jnp.bfloat16),
        "row",
        scatter_dimension=0,
        tiled=True,
    ).astype(jnp.float32)
    activation, slope = jax.vjp(jax.nn.gelu, pre)
    hidden_panel = lax.all_gather(activation.astype(jnp.bfloat16), "row", axis=0, tiled=True)
    picked = hidden_panel
    branch = lax.psum_scatter(
        jnp.dot(picked, w_out, preferred_element_type=jnp.float32).astype(jnp.bfloat16),
        "col",
        scatter_dimension=0,
        tiled=True,
    )
    cotangent = lax.all_gather(out_grad, "col", axis=0, tiled=True)
    picked = cotangent
    hid_grad = lax.psum_scatter(
        contract_last(picked, w_out).astype(jnp.bfloat16), "row", scatter_dimension=0, tiled=True
    ).astype(jnp.float32)
    pre_grad = lax.all_gather(slope(hid_grad)[0].astype(jnp.bfloat16), "row", axis=0, tiled=True)
    picked = pre_grad
    normed_grad = lax.psum_scatter(
        contract_last(picked, w_in).astype(jnp.bfloat16), "col", scatter_dimension=0, tiled=True
    ).astype(jnp.float32)
    local_in = contract_tokens(normed_panel, pre_grad).astype(jnp.bfloat16)
    local_out = contract_tokens(hidden_panel, cotangent).astype(jnp.bfloat16)
    grad_w_in, grad_w_out = (
        lax.psum(local_in, "dp").astype(jnp.float32),
        lax.psum(local_out, "dp").astype(jnp.float32),
    )
    grad_gain = lax.psum(jnp.sum(normed_grad * centred, axis=0), ("dp", "col"))
    scaled = normed_grad * norm_gain
    first, second = lax.psum((jnp.sum(scaled, axis=1), jnp.sum(scaled * centred, axis=1)), "row")
    grad_patches = inverse * (scaled - (first / D)[:, None] - centred * (second / D)[:, None])
    return (branch, grad_patches.astype(jnp.bfloat16), grad_w_in, grad_w_out, grad_gain)


def solution(mesh):
    return jax.shard_map(
        shards,
        mesh=mesh,
        in_specs=(
            P(("dp", "col"), "row"),
            P("row"),
            P("row", "col"),
            P("col", "row"),
            P(("dp", "col"), "row"),
        ),
        out_specs=(
            P(("dp", "col"), "row"),
            P(("dp", "col"), "row"),
            P("row", "col"),
            P("col", "row"),
            P("row"),
        ),
        check_vma=False,
    )
```

profile of v0, /device:TPU:1, one launch (start us, length us, event | category | flops | bytes accessed | tf_op | source)
XLA Modules:
  0.0 960.2 jit_solution(9653182310607125442)
XLA Ops:
  7.2 0.0 copy-start
  7.2 0.0 reduce-scatter.9.cloned.1.call-start
  7.2 44.4 %all_gather.14 = bf16[768,384]{1,0:T(8,128)(2,1)S(1)} all-gather(bf16[48,384]{1,0:T(8,128)(2,1)} %param.9), channel_id=1, replica_groups=mesh['dp'=2,'row'=16,'col'=16] {'col'}, dimensions={0}, use_global_device_ids=true | all-gather | bytes 626688 | tf_op jit(solution)/shard_map/all_gather | solution.py:54
  51.6 2.9 convolution_convert_fusion
  54.5 0.0 copy-start.2
  54.5 0.0 reduce-scatter.9.cloned.1.call-update
  54.5 0.0 reduce-scatter.5.cloned.1.call-start
  54.6 0.7 copy-done.2
  55.3 0.1 convert_reduce_fusion
  55.4 48.4 %all-reduce.1 = (f32[48]{0:T(128)S(1)}, f32[48]{0:T(128)S(1)}) all-reduce(f32[48]{0:T(128)S(1)} %get-tuple-element.9, f32[48]{0:T(128)S(1)} %get-tuple-element.8), channel_id=1, replica_groups=mesh['dp'=2,'row'=16,'col'=16] {'row'}, use_global_device_ids=true, to_apply=%region_3.0 | all-reduce | flops 96 | bytes 768 | tf_op jit(solution)/shard_map/psum | solution.py:33
  103.8 0.0 copy-done.4
  103.8 0.1 fusion.22
  103.9 36.7 %all_gather.12 = bf16[768,384]{1,0:T(8,128)(2,1)S(1)} all-gather(bf16[48,384]{1,0:T(8,128)(2,1)S(1)} %fusion.22), channel_id=1, replica_groups=mesh['dp'=2,'row'=16,'col'=16] {'col'}, dimensions={0}, use_global_device_ids=true | all-gather | bytes 626688 | tf_op jit(solution)/shard_map/all_gather | solution.py:35
  140.5 0.0 copy-done
  140.5 1.8 convolution_convert_fusion.1
  142.3 0.0 reduce-scatter.5.cloned.1.call-update
  142.3 0.0 all-gather.5.cloned.1.call-start
  142.4 141.0 %reduce-scatter.9.cloned.1.call-done = bf16[48,768]{1,0:T(8,128)(2,1)} async-done(((bf16[768,768]{1,0:T(8,128)(2,1)}), bf16[48,768]{1,0:T(8,128)(2,1)}) %reduce-scatter.9.cloned.1.call-update) | async-done | bytes 73744 | tf_op jit(solution)/shard_map/reduce_scatter | solution.py:56
  283.4 227.1 %reduce-scatter.5.cloned.1.call-done = bf16[48,768]{1,0:T(8,128)(2,1)} async-done(((bf16[768,768]{1,0:T(8,128)(2,1)}), bf16[48,768]{1,0:T(8,128)(2,1)}) %reduce-scatter.5.cloned.1.call-update) | async-done | bytes 73744 | tf_op jit(solution)/shard_map/reduce_scatter | solution.py:39
  510.5 1.7 fusion.3
  512.2 0.0 all-gather.5.cloned.1.call-update
  512.2 0.0 all-gather.3.cloned.1.call-start
  512.3 0.5 all-gather.3.cloned.1.call-update
  512.8 0.0 all-reduce.5.cloned.1.call-start
  512.8 93.0 %all-gather.5.cloned.1.call-done = bf16[768,768]{1,0:T(8,128)(2,1)} async-done(((bf16[48,768]{1,0:T(8,128)(2,1)}), bf16[768,768]{1,0:T(8,128)(2,1)}) %all-gather.5.cloned.1.call-update) | async-done | bytes 1179664 | tf_op jit(solution)/shard_map/all_gather | solution.py:59
  605.9 2.7 convolution_convert_fusion.3
  608.6 89.5 %all-gather.3.cloned.1.call-done = bf16[768,768]{1,0:T(8,128)(2,1)} async-done(((bf16[48,768]{1,0:T(8,128)(2,1)}), bf16[768,768]{1,0:T(8,128)(2,1)}) %all-gather.3.cloned.1.call-update) | async-done | bytes 1179664 | tf_op jit(solution)/shard_map/all_gather | solution.py:46
  698.1 2.9 convolution_convert_fusion.2
  701.0 0.0 all-reduce.5.cloned.1.call-update
  701.0 0.0 copy-start.3
  701.0 0.0 copy-start.5
  701.0 0.0 reduce-scatter.11.cloned.1.call-start
  701.1 3.0 convolution_convert_fusion.4
  704.1 0.0 reduce-scatter.11.cloned.1.call-update
  704.1 0.0 reduce-scatter.7.cloned.1.call-start
  704.1 0.0 copy-done.3
  704.1 0.0 copy-done.5
  704.2 1.6 convolution_convert_fusion.5
  705.7 0.0 reduce-scatter.7.cloned.1.call-update
  705.8 30.6 %all-reduce.5.cloned.1.call-done = (bf16[384,768]{1,0:T(8,128)(2,1)}, bf16[768,384]{1,0:T(8,128)(2,1)}) async-done(((bf16[384,768]{1,0:T(8,128)(2,1)}, bf16[768,384]{1,0:T(8,128)(2,1)}), (bf16[384,768]{1,0:T(8,128)(2,1)}, bf16[768,384]{1,0:T(8,128)(2,1)})) %all-reduce.5.cloned.1.call-update) | async-done | bytes 1179664 | tf_op jit(solution)/shard_map/psum | solution.py:67
  736.4 2.2 convert_element_type.61
  738.6 0.0 copy-done.1
  738.6 1.1 convert_element_type.63
  739.7 76.1 %reduce-scatter.11.cloned.1.call-done = bf16[48,384]{1,0:T(8,128)(2,1)} async-done(((bf16[768,384]{1,0:T(8,128)(2,1)}), bf16[48,384]{1,0:T(8,128)(2,1)}) %reduce-scatter.11.cloned.1.call-update) | async-done | bytes 36880 | tf_op jit(solution)/shard_map/reduce_scatter | solution.py:61
  815.8 1.0 fusion.18
  816.8 44.9 %all-reduce = (f32[48]{0:T(128)S(1)}, f32[48]{0:T(128)S(1)}) all-reduce(f32[48]{0:T(128)S(1)} %get-tuple-element.6, f32[48]{0:T(128)S(1)} %get-tuple-element.7), channel_id=1, replica_groups=mesh['dp'=2,'row'=16,'col'=16] {'row'}, use_global_device_ids=true, to_apply=%region_11.0 | all-reduce | flops 96 | bytes 768 | tf_op jit(solution)/shard_map/psum | solution.py:72
  861.7 90.1 %psum.55 = f32[384]{0:T(512)} all-reduce(f32[384]{0:T(512)S(1)} %get-tuple-element.5), channel_id=1, replica_groups=mesh['dp'=2,'row'=16,'col'=16] {'dp','col'}, use_global_device_ids=true, to_apply=%region_15.0 | all-reduce | flops 384 | bytes 3072 | tf_op jit(solution)/shard_map/psum | solution.py:70
  951.9 1.5 fusion.16
  (5 shorter events, 0.0 us)
Async XLA Ops:
  7.2 133.4 %copy-start = (bf16[384,768]{1,0:T(8,128)(2,1)S(1)}, bf16[384,768]{1,0:T(8,128)(2,1)}, u32[]{:S(2)}) copy-start(bf16[384,768]{1,0:T(8,128)(2,1)} %param.7) | copy-start | bytes 1769476
  7.2 276.2 %reduce-scatter.9.cloned.1.call-start = ((), (), s32[]{:S(2)}) async-start(), calls=%async_computation.7 | async-start | bytes 1253376 | tf_op jit(solution)/shard_map/reduce_scatter | solution.py:56
  54.5 0.8 copy-start.2
  54.5 49.3 %copy-start.4 = (f32[384]{0:T(512)S(1)}, f32[384]{0:T(512)}, u32[]{:S(2)}) copy-start(f32[384]{0:T(512)} %param.6) | copy-start | bytes 4612
  54.5 456.0 %reduce-scatter.5.cloned.1.call-start = ((), (), s32[]{:S(2)}) async-start(), calls=%async_computation.4 | async-start | bytes 1253376 | tf_op jit(solution)/shard_map/reduce_scatter | solution.py:39
  142.3 463.5 %all-gather.5.cloned.1.call-start = ((), (), s32[]{:S(2)}) async-start(), calls=%async_computation.8 | async-start | bytes 1253376 | tf_op jit(solution)/shard_map/all_gather | solution.py:59
  512.2 185.9 %all-gather.3.cloned.1.call-start = ((), (), s32[]{:S(2)}) async-start(), calls=%async_computation.5 | async-start | bytes 1253376 | tf_op jit(solution)/shard_map/all_gather | solution.py:46
  512.8 223.6 %all-reduce.5.cloned.1.call-start = ((), (), s32[]{:S(2)}) async-start(), calls=%async_computation.10 | async-start | bytes 2359296 | tf_op jit(solution)/shard_map/psum | solution.py:67
  701.0 3.1 copy-start.3
  701.0 3.1 copy-start.5
  701.0 114.8 %reduce-scatter.11.cloned.1.call-start = ((), (), s32[]{:S(2)}) async-start(), calls=%async_computation.9 | async-start | bytes 626688 | tf_op jit(solution)/shard_map/reduce_scatter | solution.py:61
  704.1 249.3 %reduce-scatter.7.cloned.1.call-start = ((), (), s32[]{:S(2)}) async-start(), calls=%async_computation.6 | async-start | bytes 626688 | tf_op jit(solution)/shard_map/reduce_scatter | solution.py:48
  736.4 2.2 copy-start.1
Sparse Core Ops, SparseCore 0:
  54.6 228.7 reduce-scatter.8
  288.5 221.9 reduce-scatter.4
  514.3 91.5 all-gather.4
  609.5 88.5 all-gather.2
  701.4 34.9 all-reduce.4
  739.3 76.5 reduce-scatter.10
  819.2 84.6 reduce-scatter.6
where the time goes:
time: 961 us; the launch traced here: 960 us
  waiting for transfers between devices  658 us (68%)
  blocking collectives  265 us (28%)
  matrix products  14.9 us (2%)
  between operations  14.2 us (1%)
    reduce_scatter x1, waiting for transfers between devices, shards(): lax.psum_scatter(jnp.dot(picked, w_in, preferred_element_type=jnp.float32...  227 us
    reduce_scatter x1, waiting for transfers between devices, shards(): lax.psum_scatter(contract_last(picked, w_out).astype(jnp.bfloat16), 'row'...  141 us
    all_gather x1, waiting for transfers between devices, shards(): lax.all_gather(slope(hid_grad)[0].astype(jnp.bfloat16), 'row', axis=0, ti...  93 us
    psum x1, blocking collectives, shards(): grad_gain = lax.psum(jnp.sum(normed_grad * centred, axis=0), ('dp', 'col'))  90.1 us
    all_gather x1, waiting for transfers between devices, shards(): lax.all_gather(activation.astype(jnp.bfloat16), 'row', axis=0, tiled=True)  89.5 us
    reduce_scatter x1, waiting for transfers between devices, shards(): lax.psum_scatter(contract_last(picked, w_in).astype(jnp.bfloat16), 'col',...  76.1 us
    psum x1, blocking collectives, shards(): sums, squares = lax.psum(statistics(values), 'row')  48.4 us
    psum x1, blocking collectives, shards(): lax.psum((jnp.sum(scaled, axis=1), jnp.sum(scaled * centred, axis=1)), 'r...  44.9 us
  transfers between devices with their start and end apart: 7, of which 6 were waited for; matrix products, arithmetic and copies ran while one was open for 2% of the time, Pallas kernels for 0%

commit v1 on v0

v1 whole, which is shorter than its diff:
```python
import jax
import jax.numpy as jnp
from jax import lax
from jax.sharding import Mesh, PartitionSpec as P

Y, ZH, X, ZL = 8, 2, 4, 4
ROW = ("y", "zh")
COL = ("x", "zl")
F32, BF16 = jnp.float32, jnp.bfloat16
LANES = 128


def contract_tokens(left, right):
    return lax.dot_general(
        left, right, (((0,), (0,)), ((), ())), preferred_element_type=F32
    )


def contract_last(left, right):
    return lax.dot_general(
        left, right, (((1,), (1,)), ((), ())), preferred_element_type=F32
    )


def shift(values, axis, size, by):
    return lax.ppermute(values, axis, [(i, (i + by) % size) for i in range(size)])


def add(*terms):
    total = terms[0].astype(F32)
    for term in terms[1:]:
        total = total + term.astype(F32)
    return total


def split_high_low(values):
    high = lax.reduce_precision(values, 8, 7)
    return high.astype(BF16), (values - high).astype(BF16)


def as_rows(values, width):
    row = jnp.concatenate(split_high_low(values))
    row = jnp.pad(row, (0, width - row.shape[0]))
    return jnp.broadcast_to(row[None], (8, width))


def whole(rows):
    size = rows.shape[1] // LANES // 2 * LANES
    return rows[0, :size].astype(F32) + rows[0, size : 2 * size].astype(F32)


def gather_x(block):
    half = block.shape[0] // 2
    below, above = shift(block, "x", X, 1), shift(block, "x", X, -1)
    far = (shift(below[:half], "x", X, 1), shift(above[half:], "x", X, -1))
    return block, below, above, jnp.concatenate(far, axis=0)


def scatter_x(own, below, above, far, gain):
    half = own.shape[0] // 2
    up = shift(jnp.concatenate([far[:half], gain], axis=0), "x", X, 1)
    down = shift(jnp.concatenate([far[half:], gain], axis=0), "x", X, -1)
    up_gain, down_gain = up[half:], down[half:]
    up = jnp.concatenate(
        [add(up[:half], above[:half]).astype(BF16), above[half:], up_gain], axis=0
    )
    down = jnp.concatenate(
        [below[:half], add(down[:half], below[half:]).astype(BF16)], axis=0
    )
    up, down = shift(up, "x", X, 1), shift(down, "x", X, -1)
    gains = [whole(g) for g in (gain, up[2 * half :], up_gain, down_gain)]
    gain = (gains[0] + gains[1]) + (gains[2] + gains[3])
    return add(own, up[: 2 * half], down).astype(BF16), gain


def scatter_y(part):
    me = lax.axis_index("y")

    def at(by):
        return part((me + (by + Y)) & (Y - 1))

    far = at(Y // 2)
    half = far.shape[0] // 2
    up, down = shift(far[:half], "y", Y, 1), shift(far[half:], "y", Y, -1)
    above, below = at(Y // 2 - 1), at(1 - Y // 2)
    up = jnp.concatenate([add(up, above[:half]).astype(BF16), above[half:]], axis=0)
    down = jnp.concatenate([below[:half], add(down, below[half:]).astype(BF16)], axis=0)
    for by in range(Y // 2 - 2, -1, -1):
        up, down = shift(up, "y", Y, 1), shift(down, "y", Y, -1)
        if by:
            up, down = add(up, at(by)).astype(BF16), add(down, at(-by)).astype(BF16)
    return add(at(0), up, down)


def gather_y(blocks):
    me, rows = lax.axis_index("y"), blocks[0].shape[0]
    half = rows // 2
    panels = [jnp.zeros((Y * rows, b.shape[1]), b.dtype) for b in blocks]
    edges = [0]
    for b in blocks:
        edges.append(edges[-1] + b.shape[1])

    def put(panels, values, by, offset=0):
        start = ((me + (by + Y)) & (Y - 1)) * rows + offset
        return [
            lax.dynamic_update_slice(
                panel, values[:, low:high], (start, 0), allow_negative_indices=False
            )
            for panel, low, high in zip(panels, edges[:-1], edges[1:])
        ]

    block = jnp.concatenate(blocks, axis=1)
    panels = put(panels, block, 0)
    below = above = block
    for by in range(1, Y // 2):
        below, above = shift(below, "y", Y, 1), shift(above, "y", Y, -1)
        panels = put(put(panels, below, -by), above, by)
    panels = put(panels, shift(below[:half], "y", Y, 1), Y // 2)
    return put(panels, shift(above[half:], "y", Y, -1), Y // 2, half)


def shards(patches, norm_gain, w_in, w_out, out_grad):
    tokens, width = patches.shape
    hidden_width = w_in.shape[1]
    model_width = width * Y * ZH
    values = patches.astype(F32)
    image = jnp.sum(norm_gain[:, None] * w_in.astype(F32), axis=0)
    mine = jnp.concatenate([jnp.sum(values, axis=1), jnp.sum(values * values, axis=1), image])
    theirs = lax.all_to_all(
        jnp.broadcast_to(mine, (Y * ZH,) + mine.shape), ROW, 0, 0, tiled=True
    )
    sums = jnp.sum(theirs, axis=0)
    average = (sums[:tokens] / model_width)[:, None]
    squares = (sums[tokens : 2 * tokens] / model_width)[:, None]
    image = sums[2 * tokens :]
    inverse = lax.rsqrt(squares - average * average + 1e-06)
    centred = (values - average) * inverse
    normed = (centred * norm_gain).astype(BF16)
    both = lax.all_gather(
        jnp.concatenate([normed, out_grad], axis=1), "zl", axis=0, tiled=True
    )
    both = jnp.concatenate(gather_x(both), axis=0)
    normed_panel, cotangent = both[:, :width], both[:, width:]
    pre_part = jnp.dot(normed_panel, w_in, preferred_element_type=F32).astype(BF16)
    hid_part = contract_last(cotangent, w_out).astype(BF16)
    rows = both.shape[0] // Y

    def part(place):
        return jnp.concatenate(
            [
                lax.dynamic_slice(
                    a, (place * rows, 0), (rows, hidden_width), allow_negative_indices=False
                )
                for a in (pre_part, hid_part)
            ],
            axis=1,
        )

    half_sum = scatter_y(part).astype(BF16)
    total = add(half_sum, shift(half_sum, "zh", ZH, 1))
    pre, hid_grad = total[:, :hidden_width], total[:, hidden_width:]
    activation, slope = jax.vjp(jax.nn.gelu, pre)
    pre_grad = slope(hid_grad)[0].astype(BF16)
    first = jnp.sum(pre_grad.astype(F32) * image, axis=1, keepdims=True)
    second = jnp.sum(pre_grad.astype(F32) * pre, axis=1, keepdims=True)
    lane = lax.broadcasted_iota(jnp.int32, (rows, LANES), 1)
    shares = jnp.zeros((rows, LANES), BF16)
    for place, term in enumerate(split_high_low(first) + split_high_low(second)):
        shares = jnp.where(lane == place, term, shares)
    hidden_panel, pre_grad_panel, shares = gather_y(
        [activation.astype(BF16), pre_grad, shares]
    )
    branch_part = jnp.dot(hidden_panel, w_out, preferred_element_type=F32).astype(BF16)
    normed_grad_part = contract_last(pre_grad_panel, w_in)
    gain_part = jnp.sum(normed_grad_part * normed_panel.astype(F32), axis=0)
    sent = jnp.concatenate([branch_part, normed_grad_part.astype(BF16), shares], axis=1)
    block = both.shape[0] // X
    parts = [sent[i * block : (i + 1) * block] for i in range(X)]
    back, gain_part = scatter_x(*parts, as_rows(gain_part, sent.shape[1]))
    back = back.reshape(ZL, tokens, -1)
    gain_part = jnp.broadcast_to(as_rows(gain_part, sent.shape[1])[None], (ZL, 8, sent.shape[1]))
    back = lax.all_to_all(
        jnp.concatenate([back, gain_part], axis=1), "zl", 0, 0, tiled=True
    )
    gain_sum = whole(jnp.sum(back[:, tokens : tokens + 1].astype(F32), axis=0))
    back = jnp.sum(back[:, :tokens].astype(F32), axis=0)
    branch = back[:, :width].astype(BF16)
    normed_grad = back[:, width : 2 * width]
    rest = back[:, 2 * width :]
    lane = lax.broadcasted_iota(jnp.int32, rest.shape, 1)
    first = jnp.sum(jnp.where(lane < 2, rest, 0), axis=1, keepdims=True) / model_width
    second = jnp.sum(jnp.where(lane >= 2, rest, 0), axis=1, keepdims=True) / model_width
    grad_gain = (gain_sum + shift(gain_sum, "dp", 2, 1)) / norm_gain
    grad_patches = inverse * (normed_grad * norm_gain - first - centred * second)
    local_in = contract_tokens(normed_panel, pre_grad_panel).astype(BF16)
    local_out = contract_tokens(hidden_panel, cotangent).astype(BF16)
    grad_w_in = add(local_in, shift(local_in, "dp", 2, 1))
    grad_w_out = add(local_out, shift(local_out, "dp", 2, 1))
    return (branch, grad_patches.astype(BF16), grad_w_in, grad_w_out, grad_gain)


def solution(mesh):
    fine = Mesh(mesh.devices.reshape(-1, Y, ZH, X, ZL), ("dp",) + ROW + COL)
    return jax.shard_map(
        shards,
        mesh=fine,
        in_specs=(
            P(("dp",) + COL, ROW),
            P(ROW),
            P(ROW, COL),
            P(COL, ROW),
            P(("dp",) + COL, ROW),
        ),
        out_specs=(
            P(("dp",) + COL, ROW),
            P(("dp",) + COL, ROW),
            P(ROW, COL),
            P(COL, ROW),
            P(ROW),
        ),
        check_vma=False,
    )
```

time: 961 us -> 225 us (0.23)
  waiting for transfers between devices: 658 us -> 49.9 us
  blocking collectives: 265 us -> 39 us
  starting transfers between devices: 0.29 us -> 113 us
  between operations: 14.2 us -> 1.47 us
  matrix products: 14.9 us -> 4.63 us
    reduce_scatter x4 -> x0, waiting for transfers between devices: 444 us -> none  [the longest x1 227 us: shards(): lax.psum_scatter(jnp.dot(picked, w_in, preferred_element_type=jnp.float32...]
    psum x3 -> x0, blocking collectives: 183 us -> none  [the longest x1 90.1 us: shards(): grad_gain = lax.psum(jnp.sum(normed_grad * centred, axis=0), ('dp', 'col'))]
    all_gather x2 -> x0, waiting for transfers between devices: 182 us -> none  [the longest x1 93 us: shards(): lax.all_gather(slope(hid_grad)[0].astype(jnp.bfloat16), 'row', axis=0, ti...]
    ppermute x0 -> x28, starting transfers between devices: none -> 108 us  [shift(): lax.ppermute(values, axis, [(i, (i + by) % size) for i in range(size)])]
    all_gather x2 -> x1, blocking collectives: 81 us -> 11.2 us  [shards(): lax.all_gather(jnp.concatenate([normed, out_grad], axis=1), 'zl', axis=0,...]
    ppermute x0 -> x28, waiting for transfers between devices: none -> 43.7 us  [shift(): lax.ppermute(values, axis, [(i, (i + by) % size) for i in range(size)])]
    psum x1 -> x0, waiting for transfers between devices: 30.6 us -> none  [shards(): lax.psum(local_in, 'dp').astype(jnp.float32)]
    all_to_all x0 -> x1, blocking collectives: none -> 27.8 us  [shards(): lax.all_to_all(jnp.broadcast_to(mine, (Y * ZH,) + mine.shape), ROW, 0, 0,...]
  transfers between devices with their start and end apart: 7 -> 29, of which waited for: 6 -> 17; matrix products, arithmetic and copies ran while one was open for 2% -> 4% of each run, Pallas kernels for 0% -> 0%
where the time goes in v1:
time: 225 us; the launch traced here: 223 us
  starting transfers between devices  113 us (50%)
  waiting for transfers between devices  49.9 us (22%)
  blocking collectives  39 us (17%)
  other arithmetic  11.6 us (5%)
  matrix products  4.63 us (2%)
  local copies, waits for them, and re-layouts  4.2 us (2%)
    ppermute x28, starting transfers between devices, shift(): lax.ppermute(values, axis, [(i, (i + by) % size) for i in range(size)])  108 us
    ppermute x28, waiting for transfers between devices, shift(): lax.ppermute(values, axis, [(i, (i + by) % size) for i in range(size)])  43.7 us
    all_to_all x1, blocking collectives, shards(): lax.all_to_all(jnp.broadcast_to(mine, (Y * ZH,) + mine.shape), ROW, 0, 0,...  27.8 us
    all_gather x1, blocking collectives, shards(): lax.all_gather(jnp.concatenate([normed, out_grad], axis=1), 'zl', axis=0,...  11.2 us
    all_to_all x1, waiting for transfers between devices, shards(): lax.all_to_all(jnp.concatenate([back, gain_part], axis=1), 'zl', 0, 0, ti...  6.25 us
  transfers between devices with their start and end apart: 29, of which 17 were waited for; matrix products, arithmetic and copies ran while one was open for 4% of the time, Pallas kernels for 0%

profile of v1, /device:TPU:1, one launch (start us, length us, event | category | flops | bytes accessed | tf_op | source)
XLA Modules:
  0.0 223.5 jit_solution(15975596603052269667)
XLA Ops:
  0.6 0.9 convert_reduce_fusion.1
  1.6 1.3 multiply_reduce_fusion.1
  3.0 27.8 %all_to_all.11 = f32[16,1,864]{2,1,0:T(1,128)S(1)} all-to-all(f32[16,1,864]{2,1,0:T(1,128)S(1)} %broadcast_in_dim.54), channel_id=1, replica_groups=mesh['dp'=2,'y'=8,'zh'=2,'x'=4,'zl'=4] {'y','zh'}, dimensions={0} | all-to-all | bytes 110592 | tf_op jit(solution)/shard_map/all_to_all | solution.py:129
  32.5 11.2 %all_gather.3 = bf16[192,768]{1,0:T(8,128)(2,1)S(1)} all-gather(bf16[48,768]{1,0:T(8,128)(2,1)S(1)} %pad_maximum_fusion.10), channel_id=1, replica_groups=mesh['dp'=2,'y'=8,'zh'=2,'x'=4,'zl'=4] {'zl'}, dimensions={0}, use_global_device_ids=true | all-gather | bytes 368640 | tf_op jit(solution)/shard_map/all_gather | solution.py:139
  43.7 3.1 %collective-permute-start = (bf16[192,768]{1,0:T(8,128)(2,1)S(1)}, bf16[192,768]{1,0:T(8,128)(2,1)S(1)}, u32[]{:S(2)}, u32[]{:S(2)}) collective-permute-start(bf16[192,768]{1,0:T(8,128)(2,1)S(1)} %all_gather.3), channel_id=1, source_target_pairs={{0,4},{4,8},{8,12},{12,0},{1,5},{5,9},{9,13},{13,1},{2,6},{6,10},{... | collective-permute-start | bytes 884744 | tf_op jit(solution)/shard_map/ppermute | solution.py:26
  46.8 3.4 %collective-permute-start.1 = (bf16[192,768]{1,0:T(8,128)(2,1)S(1)}, bf16[192,768]{1,0:T(8,128)(2,1)S(1)}, u32[]{:S(2)}, u32[]{:S(2)}) collective-permute-start(bf16[192,768]{1,0:T(8,128)(2,1)S(1)} %all_gather.3), channel_id=1, source_target_pairs={{0,12},{4,0},{8,4},{12,8},{1,13},{5,1},{9,5},{13,9},{2,14},{6,2},{... | collective-permute-start | bytes 884744 | tf_op jit(solution)/shard_map/ppermute | solution.py:26
  50.3 2.1 collective-permute-done
  52.4 1.9 collective-permute-start.2
  54.4 4.6 %collective-permute-start.3 = (bf16[96,768]{1,0:T(8,128)(2,1)S(1)}, bf16[96,768]{1,0:T(8,128)(2,1)S(1)}, u32[]{:S(2)}, u32[]{:S(2)}) collective-permute-start(bf16[96,768]{1,0:T(8,128)(2,1)S(1)} %slice.285), channel_id=1, source_target_pairs={{0,12},{4,0},{8,4},{12,8},{1,13},{5,1},{9,5},{13,9},{2,14},{6,2},{... | collective-permute-start | bytes 442376 | tf_op jit(solution)/shard_map/ppermute | solution.py:26
  59.6 2.4 %collective-permute-done.3 = bf16[96,768]{1,0:T(8,128)(2,1)S(1)} collective-permute-done((bf16[96,768]{1,0:T(8,128)(2,1)S(1)}, bf16[96,768]{1,0:T(8,128)(2,1)S(1)}, u32[]{:S(2)}, u32[]{:S(2)}) %collective-permute-start.3) | collective-permute-done | bytes 147488 | tf_op jit(solution)/shard_map/ppermute | solution.py:26
  64.3 2.0 collective-permute-start.4
  66.3 4.5 %collective-permute-start.8 = (bf16[48,1536]{1,0:T(8,128)(2,1)S(1)}, bf16[48,1536]{1,0:T(8,128)(2,1)S(1)}, u32[]{:S(2)}, u32[]{:S(2)}) collective-permute-start(bf16[48,1536]{1,0:T(8,128)(2,1)S(1)} %get-tuple-element.49), channel_id=1, source_target_pairs={{0,224},{32,0},{64,32},{96,64},{128,96},{160,128},{192,160},{224,1... | collective-permute-start | bytes 442376 | tf_op jit(solution)/shard_map/ppermute | solution.py:26
  71.4 1.9 collective-permute-start.5
  73.5 4.6 %collective-permute-start.9 = (bf16[96,1536]{1,0:T(8,128)(2,1)S(1)}, bf16[96,1536]{1,0:T(8,128)(2,1)S(1)}, u32[]{:S(2)}, u32[]{:S(2)}) collective-permute-start(bf16[96,1536]{1,0:T(8,128)(2,1)S(1)} %pad_maximum_fusion.3), channel_id=1, source_target_pairs={{0,224},{32,0},{64,32},{96,64},{128,96},{160,128},{192,160},{224,1... | collective-permute-start | bytes 884744 | tf_op jit(solution)/shard_map/ppermute | solution.py:26
  78.0 3.7 %collective-permute-done.5 = bf16[96,1536]{1,0:T(8,128)(2,1)S(1)} collective-permute-done((bf16[96,1536]{1,0:T(8,128)(2,1)S(1)}, bf16[96,1536]{1,0:T(8,128)(2,1)S(1)}, u32[]{:S(2)}, u32[]{:S(2)}) %collective-permute-start.5) | collective-permute-done | bytes 294944 | tf_op jit(solution)/shard_map/ppermute | solution.py:26
  81.8 1.9 collective-permute-start.6
  83.8 4.6 %collective-permute-start.10 = (bf16[96,1536]{1,0:T(8,128)(2,1)S(1)}, bf16[96,1536]{1,0:T(8,128)(2,1)S(1)}, u32[]{:S(2)}, u32[]{:S(2)}) collective-permute-start(bf16[96,1536]{1,0:T(8,128)(2,1)S(1)} %add_convert_fusion.3), channel_id=1, source_target_pairs={{0,224},{32,0},{64,32},{96,64},{128,96},{160,128},{192,160},{224,1... | collective-permute-start | bytes 884744 | tf_op jit(solution)/shard_map/ppermute | solution.py:26
  88.4 5.3 %collective-permute-done.6 = bf16[96,1536]{1,0:T(8,128)(2,1)S(1)} collective-permute-done((bf16[96,1536]{1,0:T(8,128)(2,1)S(1)}, bf16[96,1536]{1,0:T(8,128)(2,1)S(1)}, u32[]{:S(2)}, u32[]{:S(2)}) %collective-permute-start.6) | collective-permute-done | bytes 294944 | tf_op jit(solution)/shard_map/ppermute | solution.py:26
  93.7 1.9 collective-permute-start.7
  95.8 4.6 %collective-permute-start.11 = (bf16[96,1536]{1,0:T(8,128)(2,1)S(1)}, bf16[96,1536]{1,0:T(8,128)(2,1)S(1)}, u32[]{:S(2)}, u32[]{:S(2)}) collective-permute-start(bf16[96,1536]{1,0:T(8,128)(2,1)S(1)} %add_convert_fusion.2), channel_id=1, source_target_pairs={{0,224},{32,0},{64,32},{96,64},{128,96},{160,128},{192,160},{224,1... | collective-permute-start | bytes 884744 | tf_op jit(solution)/shard_map/ppermute | solution.py:26
  100.3 4.4 %collective-permute-done.7 = bf16[96,1536]{1,0:T(8,128)(2,1)S(1)} collective-permute-done((bf16[96,1536]{1,0:T(8,128)(2,1)S(1)}, bf16[96,1536]{1,0:T(8,128)(2,1)S(1)}, u32[]{:S(2)}, u32[]{:S(2)}) %collective-permute-start.7) | collective-permute-done | bytes 294944 | tf_op jit(solution)/shard_map/ppermute | solution.py:26
  104.7 0.9 collective-permute-done.11
  105.8 2.2 %collective-permute-start.12 = (bf16[96,1536]{1,0:T(8,128)(2,1)S(1)}, bf16[96,1536]{1,0:T(8,128)(2,1)S(1)}, u32[]{:S(2)}, u32[]{:S(2)}) collective-permute-start(bf16[96,1536]{1,0:T(8,128)(2,1)S(1)} %add_convert_fusion.1), channel_id=1, source_target_pairs={{0,16},{16,0},{1,17},{17,1},{2,18},{18,2},{3,19},{19,3},{4,20},{20... | collective-permute-start | bytes 884744 | tf_op jit(solution)/shard_map/ppermute | solution.py:26
  108.2 9.2 %collective-permute-done.12 = bf16[96,1536]{1,0:T(8,128)(2,1)S(1)} collective-permute-done((bf16[96,1536]{1,0:T(8,128)(2,1)S(1)}, bf16[96,1536]{1,0:T(8,128)(2,1)S(1)}, u32[]{:S(2)}, u32[]{:S(2)}) %collective-permute-start.12) | collective-permute-done | bytes 294944 | tf_op jit(solution)/shard_map/ppermute | solution.py:26
  118.2 1.9 collective-permute-start.13
  120.1 5.3 %collective-permute-start.14 = (bf16[96,1664]{1,0:T(8,128)(2,1)S(1)}, bf16[96,1664]{1,0:T(8,128)(2,1)S(1)}, u32[]{:S(2)}, u32[]{:S(2)}) collective-permute-start(bf16[96,1664]{1,0:T(8,128)(2,1)S(1)} %pad_maximum_fusion.2), channel_id=1, source_target_pairs={{0,224},{32,0},{64,32},{96,64},{128,96},{160,128},{192,160},{224,1... | collective-permute-start | bytes 958472 | tf_op jit(solution)/shard_map/ppermute | solution.py:26
  125.5 2.6 %collective-permute-done.13 = bf16[96,1664]{1,0:T(8,128)(2,1)} collective-permute-done((bf16[96,1664]{1,0:T(8,128)(2,1)S(1)}, bf16[96,1664]{1,0:T(8,128)(2,1)}, u32[]{:S(2)}, u32[]{:S(2)}) %collective-permute-start.13) | collective-permute-done | bytes 319520 | tf_op jit(solution)/shard_map/ppermute | solution.py:26
  128.2 1.9 collective-permute-start.15
  130.1 4.6 %collective-permute-start.16 = (bf16[96,1664]{1,0:T(8,128)(2,1)S(1)}, bf16[96,1664]{1,0:T(8,128)(2,1)S(1)}, u32[]{:S(2)}, u32[]{:S(2)}) collective-permute-start(bf16[96,1664]{1,0:T(8,128)(2,1)S(1)} %collective-permute-done.14), channel_id=1, source_target_pairs={{0,224},{32,0},{64,32},{96,64},{128,96},{160,128},{192,160},{224,1... | collective-permute-start | bytes 958472 | tf_op jit(solution)/shard_map/ppermute | solution.py:26
  134.7 1.0 slice_dynamic-update-slice_fusion.11
  137.3 1.9 collective-permute-start.17
  139.2 4.6 %collective-permute-start.18 = (bf16[96,1664]{1,0:T(8,128)(2,1)S(1)}, bf16[96,1664]{1,0:T(8,128)(2,1)S(1)}, u32[]{:S(2)}, u32[]{:S(2)}) collective-permute-start(bf16[96,1664]{1,0:T(8,128)(2,1)S(1)} %collective-permute-done.16), channel_id=1, source_target_pairs={{0,224},{32,0},{64,32},{96,64},{128,96},{160,128},{192,160},{224,1... | collective-permute-start | bytes 958472 | tf_op jit(solution)/shard_map/ppermute | solution.py:26
  143.9 2.3 %collective-permute-done.17 = bf16[96,1664]{1,0:T(8,128)(2,1)S(1)} collective-permute-done((bf16[96,1664]{1,0:T(8,128)(2,1)S(1)}, bf16[96,1664]{1,0:T(8,128)(2,1)S(1)}, u32[]{:S(2)}, u32[]{:S(2)}) %collective-permute-start.17) | collective-permute-done | bytes 319520 | tf_op jit(solution)/shard_map/ppermute | solution.py:26
  146.2 1.9 collective-permute-start.19
  148.2 4.6 %collective-permute-start.20 = (bf16[48,1664]{1,0:T(8,128)(2,1)S(1)}, bf16[48,1664]{1,0:T(8,128)(2,1)S(1)}, u32[]{:S(2)}, u32[]{:S(2)}) collective-permute-start(bf16[48,1664]{1,0:T(8,128)(2,1)S(1)} %slice.304), channel_id=1, source_target_pairs={{0,224},{32,0},{64,32},{96,64},{128,96},{160,128},{192,160},{224,1... | collective-permute-start | bytes 479240 | tf_op jit(solution)/shard_map/ppermute | solution.py:26
  153.6 1.5 collective-permute-done.20
  158.2 2.7 %collective-permute-start.21 = (bf16[104,896]{1,0:T(8,128)(2,1)S(1)}, bf16[104,896]{1,0:T(8,128)(2,1)S(1)}, u32[]{:S(2)}, u32[]{:S(2)}) collective-permute-start(bf16[104,896]{1,0:T(8,128)(2,1)S(1)} %get-tuple-element.14), channel_id=1, source_target_pairs={{0,4},{4,8},{8,12},{12,0},{1,5},{5,9},{9,13},{13,1},{2,6},{6,10},{... | collective-permute-start | bytes 559112 | tf_op jit(solution)/shard_map/ppermute | solution.py:26
  160.9 3.8 %collective-permute-start.23 = (bf16[104,896]{1,0:T(8,128)(2,1)S(1)}, bf16[104,896]{1,0:T(8,128)(2,1)S(1)}, u32[]{:S(2)}, u32[]{:S(2)}) collective-permute-start(bf16[104,896]{1,0:T(8,128)(2,1)S(1)} %get-tuple-element.15), channel_id=1, source_target_pairs={{0,12},{4,0},{8,4},{12,8},{1,13},{5,1},{9,5},{13,9},{2,14},{6,2},{... | collective-permute-start | bytes 559112 | tf_op jit(solution)/shard_map/ppermute | solution.py:26
  164.7 20.4 %collective-permute-start.26 = (bf16[768,384]{1,0:T(8,128)(2,1)S(1)}, bf16[768,384]{1,0:T(8,128)(2,1)S(1)}, u32[]{:S(2)}, u32[]{:S(2)}) collective-permute-start(bf16[768,384]{1,0:T(8,128)(2,1)S(1)} %convolution_convert_fusion.2), channel_id=1, source_target_pairs={{0,256},{256,0},{1,257},{257,1},{2,258},{258,2},{3,259},{259,3},{4... | collective-permute-start | bytes 1769480 | tf_op jit(solution)/shard_map/ppermute | solution.py:26
  185.7 1.9 collective-permute-start.25
  187.8 1.9 collective-permute-start.22
  189.9 4.6 %collective-permute-start.24 = (bf16[192,896]{1,0:T(8,128)(2,1)S(1)}, bf16[192,896]{1,0:T(8,128)(2,1)S(1)}, u32[]{:S(2)}, u32[]{:S(2)}) collective-permute-start(bf16[192,896]{1,0:T(8,128)(2,1)S(1)} %fusion.22), channel_id=1, source_target_pairs={{0,12},{4,0},{8,4},{12,8},{1,13},{5,1},{9,5},{13,9},{2,14},{6,2},{... | collective-permute-start | bytes 1032200 | tf_op jit(solution)/shard_map/ppermute | solution.py:26
  194.5 5.8 %collective-permute-done.22 = bf16[200,896]{1,0:T(8,128)(2,1)S(1)} collective-permute-done((bf16[200,896]{1,0:T(8,128)(2,1)S(1)}, bf16[200,896]{1,0:T(8,128)(2,1)S(1)}, u32[]{:S(2)}, u32[]{:S(2)}) %collective-permute-start.22) | collective-permute-done | bytes 358432 | tf_op jit(solution)/shard_map/ppermute | solution.py:26
  202.1 4.5 %all-to-all-start.1 = ((bf16[4,56,896]{2,1,0:T(8,128)(2,1)}), bf16[4,56,896]{2,1,0:T(8,128)(2,1)S(1)}, u32[]{:S(2)}, u32[]{:S(2)}) async-start(bf16[4,56,896]{2,1,0:T(8,128)(2,1)} %pad_maximum_fusion.1), calls=%async_computation.1 | async-start | bytes 802816 | tf_op jit(solution)/shard_map/all_to_all | solution.py:182
  206.6 1.1 convert_add_fusion
  207.7 2.2 %convert_add_fusion.1 = f32[384,768]{1,0:T(8,128)} fusion(bf16[384,768]{1,0:T(8,128)(2,1)} %collective-permute-done.25, bf16[384,768]{1,0:T(8,128)(2,1)S(1)} %convolution_convert_fusion.3), kind=kLoop, calls=%fused_computation.7 | loop fusion | flops 884736 | bytes 2359296 | tf_op jit(solution)/shard_map/add | solution.py:32
  209.9 6.2 %all-to-all-done.1 = bf16[4,56,896]{2,1,0:T(8,128)(2,1)S(1)} async-done(((bf16[4,56,896]{2,1,0:T(8,128)(2,1)}), bf16[4,56,896]{2,1,0:T(8,128)(2,1)S(1)}, u32[]{:S(2)}, u32[]{:S(2)}) %all-to-all-start.1) | async-done | bytes 401440 | tf_op jit(solution)/shard_map/all_to_all | solution.py:182
  216.3 5.1 %collective-permute-start.27 = (f32[384]{0:T(512)S(1)}, f32[384]{0:T(512)S(1)}, u32[]{:S(2)}, u32[]{:S(2)}) collective-permute-start(f32[384]{0:T(512)S(1)} %fusion.57), channel_id=1, source_target_pairs={{0,256},{256,0},{1,257},{257,1},{2,258},{258,2},{3,259},{259,3},{4... | collective-permute-start | bytes 4616 | tf_op jit(solution)/shard_map/ppermute | solution.py:26
  (118 shorter events, 17.2 us)
Async XLA Ops:
  0.6 62.4 %copy-start = (bf16[768,384]{1,0:T(8,128)(2,1)S(1)}, bf16[768,384]{1,0:T(8,128)(2,1)}, u32[]{:S(2)}) copy-start(bf16[768,384]{1,0:T(8,128)(2,1)} %param.8) | copy-start | bytes 1769476
  43.7 8.7 %collective-permute-start = (bf16[192,768]{1,0:T(8,128)(2,1)S(1)}, bf16[192,768]{1,0:T(8,128)(2,1)S(1)}, u32[]{:S(2)}, u32[]{:S(2)}) collective-permute-start(bf16[192,768]{1,0:T(8,128)(2,1)S(1)} %all_gather.3), channel_id=1, source_target_pairs={{0,4},{4,8},{8,12},{12,0},{1,5},{5,9},{9,13},{13,1},{2,6},{6,10},{... | collective-permute-start | bytes 884744 | tf_op jit(solution)/shard_map/ppermute | solution.py:26
  46.8 7.5 %collective-permute-start.1 = (bf16[192,768]{1,0:T(8,128)(2,1)S(1)}, bf16[192,768]{1,0:T(8,128)(2,1)S(1)}, u32[]{:S(2)}, u32[]{:S(2)}) collective-permute-start(bf16[192,768]{1,0:T(8,128)(2,1)S(1)} %all_gather.3), channel_id=1, source_target_pairs={{0,12},{4,0},{8,4},{12,8},{1,13},{5,1},{9,5},{13,9},{2,14},{6,2},{... | collective-permute-start | bytes 884744 | tf_op jit(solution)/shard_map/ppermute | solution.py:26
  50.3 11.8 %copy-start.1 = (bf16[384,768]{1,0:T(8,128)(2,1)S(1)}, bf16[384,768]{1,0:T(8,128)(2,1)}, u32[]{:S(2)}) copy-start(bf16[384,768]{1,0:T(8,128)(2,1)} %param.7) | copy-start | bytes 1769476
  52.4 7.2 %collective-permute-start.2 = (bf16[96,768]{1,0:T(8,128)(2,1)S(1)}, bf16[96,768]{1,0:T(8,128)(2,1)S(1)}, u32[]{:S(2)}, u32[]{:S(2)}) collective-permute-start(bf16[96,768]{1,0:T(8,128)(2,1)S(1)} %slice.284), channel_id=1, source_target_pairs={{0,4},{4,8},{8,12},{12,0},{1,5},{5,9},{9,13},{13,1},{2,6},{6,10},{... | collective-permute-start | bytes 442376 | tf_op jit(solution)/shard_map/ppermute | solution.py:26
  54.4 7.7 %collective-permute-start.3 = (bf16[96,768]{1,0:T(8,128)(2,1)S(1)}, bf16[96,768]{1,0:T(8,128)(2,1)S(1)}, u32[]{:S(2)}, u32[]{:S(2)}) collective-permute-start(bf16[96,768]{1,0:T(8,128)(2,1)S(1)} %slice.285), channel_id=1, source_target_pairs={{0,12},{4,0},{8,4},{12,8},{1,13},{5,1},{9,5},{13,9},{2,14},{6,2},{... | collective-permute-start | bytes 442376 | tf_op jit(solution)/shard_map/ppermute | solution.py:26
  62.1 1.0 copy-start.3
  64.3 7.1 %collective-permute-start.4 = (bf16[48,1536]{1,0:T(8,128)(2,1)S(1)}, bf16[48,1536]{1,0:T(8,128)(2,1)S(1)}, u32[]{:S(2)}, u32[]{:S(2)}) collective-permute-start(bf16[48,1536]{1,0:T(8,128)(2,1)S(1)} %get-tuple-element.48), channel_id=1, source_target_pairs={{0,32},{32,64},{64,96},{96,128},{128,160},{160,192},{192,224},{224... | collective-permute-start | bytes 442376 | tf_op jit(solution)/shard_map/ppermute | solution.py:26
  66.3 7.1 %collective-permute-start.8 = (bf16[48,1536]{1,0:T(8,128)(2,1)S(1)}, bf16[48,1536]{1,0:T(8,128)(2,1)S(1)}, u32[]{:S(2)}, u32[]{:S(2)}) collective-permute-start(bf16[48,1536]{1,0:T(8,128)(2,1)S(1)} %get-tuple-element.49), channel_id=1, source_target_pairs={{0,224},{32,0},{64,32},{96,64},{128,96},{160,128},{192,160},{224,1... | collective-permute-start | bytes 442376 | tf_op jit(solution)/shard_map/ppermute | solution.py:26
  71.4 10.3 %collective-permute-start.5 = (bf16[96,1536]{1,0:T(8,128)(2,1)S(1)}, bf16[96,1536]{1,0:T(8,128)(2,1)S(1)}, u32[]{:S(2)}, u32[]{:S(2)}) collective-permute-start(bf16[96,1536]{1,0:T(8,128)(2,1)S(1)} %fusion.33), channel_id=1, source_target_pairs={{0,32},{32,64},{64,96},{96,128},{128,160},{160,192},{192,224},{224... | collective-permute-start | bytes 884744 | tf_op jit(solution)/shard_map/ppermute | solution.py:26
  73.5 10.3 %collective-permute-start.9 = (bf16[96,1536]{1,0:T(8,128)(2,1)S(1)}, bf16[96,1536]{1,0:T(8,128)(2,1)S(1)}, u32[]{:S(2)}, u32[]{:S(2)}) collective-permute-start(bf16[96,1536]{1,0:T(8,128)(2,1)S(1)} %pad_maximum_fusion.3), channel_id=1, source_target_pairs={{0,224},{32,0},{64,32},{96,64},{128,96},{160,128},{192,160},{224,1... | collective-permute-start | bytes 884744 | tf_op jit(solution)/shard_map/ppermute | solution.py:26
  81.8 11.9 %collective-permute-start.6 = (bf16[96,1536]{1,0:T(8,128)(2,1)S(1)}, bf16[96,1536]{1,0:T(8,128)(2,1)S(1)}, u32[]{:S(2)}, u32[]{:S(2)}) collective-permute-start(bf16[96,1536]{1,0:T(8,128)(2,1)S(1)} %add_convert_fusion.5), channel_id=1, source_target_pairs={{0,32},{32,64},{64,96},{96,128},{128,160},{160,192},{192,224},{224... | collective-permute-start | bytes 884744 | tf_op jit(solution)/shard_map/ppermute | solution.py:26
  83.8 11.9 %collective-permute-start.10 = (bf16[96,1536]{1,0:T(8,128)(2,1)S(1)}, bf16[96,1536]{1,0:T(8,128)(2,1)S(1)}, u32[]{:S(2)}, u32[]{:S(2)}) collective-permute-start(bf16[96,1536]{1,0:T(8,128)(2,1)S(1)} %add_convert_fusion.3), channel_id=1, source_target_pairs={{0,224},{32,0},{64,32},{96,64},{128,96},{160,128},{192,160},{224,1... | collective-permute-start | bytes 884744 | tf_op jit(solution)/shard_map/ppermute | solution.py:26
  93.7 11.0 %collective-permute-start.7 = (bf16[96,1536]{1,0:T(8,128)(2,1)S(1)}, bf16[96,1536]{1,0:T(8,128)(2,1)S(1)}, u32[]{:S(2)}, u32[]{:S(2)}) collective-permute-start(bf16[96,1536]{1,0:T(8,128)(2,1)S(1)} %add_convert_fusion.4), channel_id=1, source_target_pairs={{0,32},{32,64},{64,96},{96,128},{128,160},{160,192},{192,224},{224... | collective-permute-start | bytes 884744 | tf_op jit(solution)/shard_map/ppermute | solution.py:26
  95.8 9.9 %collective-permute-start.11 = (bf16[96,1536]{1,0:T(8,128)(2,1)S(1)}, bf16[96,1536]{1,0:T(8,128)(2,1)S(1)}, u32[]{:S(2)}, u32[]{:S(2)}) collective-permute-start(bf16[96,1536]{1,0:T(8,128)(2,1)S(1)} %add_convert_fusion.2), channel_id=1, source_target_pairs={{0,224},{32,0},{64,32},{96,64},{128,96},{160,128},{192,160},{224,1... | collective-permute-start | bytes 884744 | tf_op jit(solution)/shard_map/ppermute | solution.py:26
  105.8 11.5 %collective-permute-start.12 = (bf16[96,1536]{1,0:T(8,128)(2,1)S(1)}, bf16[96,1536]{1,0:T(8,128)(2,1)S(1)}, u32[]{:S(2)}, u32[]{:S(2)}) collective-permute-start(bf16[96,1536]{1,0:T(8,128)(2,1)S(1)} %add_convert_fusion.1), channel_id=1, source_target_pairs={{0,16},{16,0},{1,17},{17,1},{2,18},{18,2},{3,19},{19,3},{4,20},{20... | collective-permute-start | bytes 884744 | tf_op jit(solution)/shard_map/ppermute | solution.py:26
  118.2 10.0 %collective-permute-start.13 = (bf16[96,1664]{1,0:T(8,128)(2,1)S(1)}, bf16[96,1664]{1,0:T(8,128)(2,1)}, u32[]{:S(2)}, u32[]{:S(2)}) collective-permute-start(bf16[96,1664]{1,0:T(8,128)(2,1)S(1)} %pad_maximum_fusion.2), channel_id=1, source_target_pairs={{0,32},{32,64},{64,96},{96,128},{128,160},{160,192},{192,224},{224... | collective-permute-start | bytes 958472 | tf_op jit(solution)/shard_map/ppermute | solution.py:26
  120.1 10.0 %collective-permute-start.14 = (bf16[96,1664]{1,0:T(8,128)(2,1)S(1)}, bf16[96,1664]{1,0:T(8,128)(2,1)S(1)}, u32[]{:S(2)}, u32[]{:S(2)}) collective-permute-start(bf16[96,1664]{1,0:T(8,128)(2,1)S(1)} %pad_maximum_fusion.2), channel_id=1, source_target_pairs={{0,224},{32,0},{64,32},{96,64},{128,96},{160,128},{192,160},{224,1... | collective-permute-start | bytes 958472 | tf_op jit(solution)/shard_map/ppermute | solution.py:26
  128.2 9.1 %collective-permute-start.15 = (bf16[96,1664]{1,0:T(8,128)(2,1)}, bf16[96,1664]{1,0:T(8,128)(2,1)S(1)}, u32[]{:S(2)}, u32[]{:S(2)}) collective-permute-start(bf16[96,1664]{1,0:T(8,128)(2,1)} %collective-permute-done.13), channel_id=1, source_target_pairs={{0,32},{32,64},{64,96},{96,128},{128,160},{160,192},{192,224},{224... | collective-permute-start | bytes 958472 | tf_op jit(solution)/shard_map/ppermute | solution.py:26
  130.1 9.2 %collective-permute-start.16 = (bf16[96,1664]{1,0:T(8,128)(2,1)S(1)}, bf16[96,1664]{1,0:T(8,128)(2,1)S(1)}, u32[]{:S(2)}, u32[]{:S(2)}) collective-permute-start(bf16[96,1664]{1,0:T(8,128)(2,1)S(1)} %collective-permute-done.14), channel_id=1, source_target_pairs={{0,224},{32,0},{64,32},{96,64},{128,96},{160,128},{192,160},{224,1... | collective-permute-start | bytes 958472 | tf_op jit(solution)/shard_map/ppermute | solution.py:26
  137.3 8.9 %collective-permute-start.17 = (bf16[96,1664]{1,0:T(8,128)(2,1)S(1)}, bf16[96,1664]{1,0:T(8,128)(2,1)S(1)}, u32[]{:S(2)}, u32[]{:S(2)}) collective-permute-start(bf16[96,1664]{1,0:T(8,128)(2,1)S(1)} %collective-permute-done.15), channel_id=1, source_target_pairs={{0,32},{32,64},{64,96},{96,128},{128,160},{160,192},{192,224},{224... | collective-permute-start | bytes 958472 | tf_op jit(solution)/shard_map/ppermute | solution.py:26
  139.2 8.9 %collective-permute-start.18 = (bf16[96,1664]{1,0:T(8,128)(2,1)S(1)}, bf16[96,1664]{1,0:T(8,128)(2,1)S(1)}, u32[]{:S(2)}, u32[]{:S(2)}) collective-permute-start(bf16[96,1664]{1,0:T(8,128)(2,1)S(1)} %collective-permute-done.16), channel_id=1, source_target_pairs={{0,224},{32,0},{64,32},{96,64},{128,96},{160,128},{192,160},{224,1... | collective-permute-start | bytes 958472 | tf_op jit(solution)/shard_map/ppermute | solution.py:26
  146.2 7.3 %collective-permute-start.19 = (bf16[48,1664]{1,0:T(8,128)(2,1)S(1)}, bf16[48,1664]{1,0:T(8,128)(2,1)S(1)}, u32[]{:S(2)}, u32[]{:S(2)}) collective-permute-start(bf16[48,1664]{1,0:T(8,128)(2,1)S(1)} %slice.302), channel_id=1, source_target_pairs={{0,32},{32,64},{64,96},{96,128},{128,160},{160,192},{192,224},{224... | collective-permute-start | bytes 479240 | tf_op jit(solution)/shard_map/ppermute | solution.py:26
  148.2 6.9 %collective-permute-start.20 = (bf16[48,1664]{1,0:T(8,128)(2,1)S(1)}, bf16[48,1664]{1,0:T(8,128)(2,1)S(1)}, u32[]{:S(2)}, u32[]{:S(2)}) collective-permute-start(bf16[48,1664]{1,0:T(8,128)(2,1)S(1)} %slice.304), channel_id=1, source_target_pairs={{0,224},{32,0},{64,32},{96,64},{128,96},{160,128},{192,160},{224,1... | collective-permute-start | bytes 479240 | tf_op jit(solution)/shard_map/ppermute | solution.py:26
  155.1 1.3 copy-start.4
  158.2 29.5 %collective-permute-start.21 = (bf16[104,896]{1,0:T(8,128)(2,1)S(1)}, bf16[104,896]{1,0:T(8,128)(2,1)S(1)}, u32[]{:S(2)}, u32[]{:S(2)}) collective-permute-start(bf16[104,896]{1,0:T(8,128)(2,1)S(1)} %get-tuple-element.14), channel_id=1, source_target_pairs={{0,4},{4,8},{8,12},{12,0},{1,5},{5,9},{9,13},{13,1},{2,6},{6,10},{... | collective-permute-start | bytes 559112 | tf_op jit(solution)/shard_map/ppermute | solution.py:26
  160.9 26.8 %collective-permute-start.23 = (bf16[104,896]{1,0:T(8,128)(2,1)S(1)}, bf16[104,896]{1,0:T(8,128)(2,1)S(1)}, u32[]{:S(2)}, u32[]{:S(2)}) collective-permute-start(bf16[104,896]{1,0:T(8,128)(2,1)S(1)} %get-tuple-element.15), channel_id=1, source_target_pairs={{0,12},{4,0},{8,4},{12,8},{1,13},{5,1},{9,5},{13,9},{2,14},{6,2},{... | collective-permute-start | bytes 559112 | tf_op jit(solution)/shard_map/ppermute | solution.py:26
  164.7 41.9 %collective-permute-start.26 = (bf16[768,384]{1,0:T(8,128)(2,1)S(1)}, bf16[768,384]{1,0:T(8,128)(2,1)S(1)}, u32[]{:S(2)}, u32[]{:S(2)}) collective-permute-start(bf16[768,384]{1,0:T(8,128)(2,1)S(1)} %convolution_convert_fusion.2), channel_id=1, source_target_pairs={{0,256},{256,0},{1,257},{257,1},{2,258},{258,2},{3,259},{259,3},{4... | collective-permute-start | bytes 1769480 | tf_op jit(solution)/shard_map/ppermute | solution.py:26
  185.7 22.0 %collective-permute-start.25 = (bf16[384,768]{1,0:T(8,128)(2,1)S(1)}, bf16[384,768]{1,0:T(8,128)(2,1)}, u32[]{:S(2)}, u32[]{:S(2)}) collective-permute-start(bf16[384,768]{1,0:T(8,128)(2,1)S(1)} %convolution_convert_fusion.3), channel_id=1, source_target_pairs={{0,256},{256,0},{1,257},{257,1},{2,258},{258,2},{3,259},{259,3},{4... | collective-permute-start | bytes 1769480 | tf_op jit(solution)/shard_map/ppermute | solution.py:26
  187.8 12.5 %collective-permute-start.22 = (bf16[200,896]{1,0:T(8,128)(2,1)S(1)}, bf16[200,896]{1,0:T(8,128)(2,1)S(1)}, u32[]{:S(2)}, u32[]{:S(2)}) collective-permute-start(bf16[200,896]{1,0:T(8,128)(2,1)S(1)} %fusion.19), channel_id=1, source_target_pairs={{0,4},{4,8},{8,12},{12,0},{1,5},{5,9},{9,13},{13,1},{2,6},{6,10},{... | collective-permute-start | bytes 1075208 | tf_op jit(solution)/shard_map/ppermute | solution.py:26
  189.9 11.2 %collective-permute-start.24 = (bf16[192,896]{1,0:T(8,128)(2,1)S(1)}, bf16[192,896]{1,0:T(8,128)(2,1)S(1)}, u32[]{:S(2)}, u32[]{:S(2)}) collective-permute-start(bf16[192,896]{1,0:T(8,128)(2,1)S(1)} %fusion.22), channel_id=1, source_target_pairs={{0,12},{4,0},{8,4},{12,8},{1,13},{5,1},{9,5},{13,9},{2,14},{6,2},{... | collective-permute-start | bytes 1032200 | tf_op jit(solution)/shard_map/ppermute | solution.py:26
  202.1 14.1 %all-to-all-start.1 = ((bf16[4,56,896]{2,1,0:T(8,128)(2,1)}), bf16[4,56,896]{2,1,0:T(8,128)(2,1)S(1)}, u32[]{:S(2)}, u32[]{:S(2)}) async-start(bf16[4,56,896]{2,1,0:T(8,128)(2,1)} %pad_maximum_fusion.1), calls=%async_computation.1 | async-start | bytes 802816 | tf_op jit(solution)/shard_map/all_to_all | solution.py:182
  207.7 13.8 %copy-start.2 = (bf16[48,384]{1,0:T(8,128)(2,1)S(1)}, bf16[48,384]{1,0:T(8,128)(2,1)}, u32[]{:S(2)}) copy-start(bf16[48,384]{1,0:T(8,128)(2,1)} %param.5) | copy-start | bytes 110596
  207.7 13.8 %copy-start.5 = (f32[384]{0:T(512)S(1)}, f32[384]{0:T(512)}, u32[]{:S(2)}) copy-start(f32[384]{0:T(512)} %param.6) | copy-start | bytes 4612
  216.3 6.6 %collective-permute-start.27 = (f32[384]{0:T(512)S(1)}, f32[384]{0:T(512)S(1)}, u32[]{:S(2)}, u32[]{:S(2)}) collective-permute-start(f32[384]{0:T(512)S(1)} %fusion.57), channel_id=1, source_target_pairs={{0,256},{256,0},{1,257},{257,1},{2,258},{258,2},{3,259},{259,3},{4... | collective-permute-start | bytes 4616 | tf_op jit(solution)/shard_map/ppermute | solution.py:26

commit v2 on v1

--- a/solution.py
+++ b/solution.py
@@ -33,44 +33,15 @@
     return total
 
 
+def to_all(values, axes):
+    count = {ROW: Y * ZH, COL: X * ZL}[axes]
+    copies = jnp.broadcast_to(values, (count,) + values.shape)
+    return lax.all_to_all(copies, axes, 0, 0, tiled=True)
+
+
 def split_high_low(values):
     high = lax.reduce_precision(values, 8, 7)
     return high.astype(BF16), (values - high).astype(BF16)
-
-
-def as_rows(values, width):
-    row = jnp.concatenate(split_high_low(values))
-    row = jnp.pad(row, (0, width - row.shape[0]))
-    return jnp.broadcast_to(row[None], (8, width))
-
-
-def whole(rows):
-    size = rows.shape[1] // LANES // 2 * LANES
-    return rows[0, :size].astype(F32) + rows[0, size : 2 * size].astype(F32)
-
-
-def gather_x(block):
-    half = block.shape[0] // 2
-    below, above = shift(block, "x", X, 1), shift(block, "x", X, -1)
-    far = (shift(below[:half], "x", X, 1), shift(above[half:], "x", X, -1))
-    return block, below, above, jnp.concatenate(far, axis=0)
-
-
-def scatter_x(own, below, above, far, gain):
-    half = own.shape[0] // 2
-    up = shift(jnp.concatenate([far[:half], gain], axis=0), "x", X, 1)
-    down = shift(jnp.concatenate([far[half:], gain], axis=0), "x", X, -1)
-    up_gain, down_gain = up[half:], down[half:]
-    up = jnp.concatenate(
-        [add(up[:half], above[:half]).astype(BF16), above[half:], up_gain], axis=0
-    )
-    down = jnp.concatenate(
-        [below[:half], add(down[:half], below[half:]).astype(BF16)], axis=0
-    )
-    up, down = shift(up, "x", X, 1), shift(down, "x", X, -1)
-    gains = [whole(g) for g in (gain, up[2 * half :], up_gain, down_gain)]
-    gain = (gains[0] + gains[1]) + (gains[2] + gains[3])
-    return add(own, up[: 2 * half], down).astype(BF16), gain
 
 
 def scatter_y(part):
@@ -92,16 +63,16 @@
     return add(at(0), up, down)
 
 
-def gather_y(blocks):
-    me, rows = lax.axis_index("y"), blocks[0].shape[0]
+def gather_ring(blocks, axis, size):
+    me, rows = lax.axis_index(axis), blocks[0].shape[0]
     half = rows // 2
-    panels = [jnp.zeros((Y * rows, b.shape[1]), b.dtype) for b in blocks]
+    panels = [jnp.zeros((size * rows, b.shape[1]), b.dtype) for b in blocks]
     edges = [0]
     for b in blocks:
         edges.append(edges[-1] + b.shape[1])
 
     def put(panels, values, by, offset=0):
-        start = ((me + (by + Y)) & (Y - 1)) * rows + offset
+        start = ((me + (by + size)) & (size - 1)) * rows + offset
         return [
             lax.dynamic_update_slice(
                 panel, values[:, low:high], (start, 0), allow_negative_indices=False
@@ -112,35 +83,55 @@
     block = jnp.concatenate(blocks, axis=1)
     panels = put(panels, block, 0)
     below = above = block
-    for by in range(1, Y // 2):
-        below, above = shift(below, "y", Y, 1), shift(above, "y", Y, -1)
+    for by in range(1, size // 2):
+        below, above = shift(below, axis, size, 1), shift(above, axis, size, -1)
         panels = put(put(panels, below, -by), above, by)
-    panels = put(panels, shift(below[:half], "y", Y, 1), Y // 2)
-    return put(panels, shift(above[half:], "y", Y, -1), Y // 2, half)
+    panels = put(panels, shift(below[:half], axis, size, 1), size // 2)
+    return put(panels, shift(above[half:], axis, size, -1), size // 2, half)
+
+
+def scatter(sent, vector, axis, size):
+    width, long = sent.shape[1], vector.shape[0]
+    row = jnp.pad(jnp.concatenate(split_high_low(vector)), (0, width - 2 * long))
+    parts = jnp.concatenate(
+        [sent.reshape(size, -1, width), jnp.broadcast_to(row, (size, 8, width))], axis=1
+    )
+    back = lax.all_to_all(parts, axis, 0, 0, tiled=True)
+    rows = back.shape[1] - 8
+    row = jnp.sum(back[:, rows].astype(F32), axis=0)
+    total = jnp.sum(back[:, :rows].astype(F32), axis=0)
+    return total, row[:long] + row[long : 2 * long]
 
 
 def shards(patches, norm_gain, w_in, w_out, out_grad):
     tokens, width = patches.shape
     hidden_width = w_in.shape[1]
     model_width = width * Y * ZH
+    both = lax.all_gather(
+        jnp.concatenate([patches, out_grad], axis=1), "zl", axis=0, tiled=True
+    )
+    both = gather_ring([both], "x", X)[0]
     values = patches.astype(F32)
     image = jnp.sum(norm_gain[:, None] * w_in.astype(F32), axis=0)
-    mine = jnp.concatenate([jnp.sum(values, axis=1), jnp.sum(values * values, axis=1), image])
-    theirs = lax.all_to_all(
-        jnp.broadcast_to(mine, (Y * ZH,) + mine.shape), ROW, 0, 0, tiled=True
-    )
-    sums = jnp.sum(theirs, axis=0)
-    average = (sums[:tokens] / model_width)[:, None]
-    squares = (sums[tokens : 2 * tokens] / model_width)[:, None]
+    sums = jnp.sum(
+        to_all(
+            jnp.concatenate([jnp.sum(values, axis=1), jnp.sum(values * values, axis=1), image]),
+            ROW,
+        ),
+        axis=0,
+    )
+    average = sums[:tokens] / model_width
+    squares = sums[tokens : 2 * tokens] / model_width
     image = sums[2 * tokens :]
     inverse = lax.rsqrt(squares - average * average + 1e-06)
+    scales = to_all(jnp.concatenate([average, inverse]), COL)
+    averages = scales[:, :tokens].reshape(-1, 1)
+    inverses = scales[:, tokens:].reshape(-1, 1)
+    average, inverse = average[:, None], inverse[:, None]
     centred = (values - average) * inverse
-    normed = (centred * norm_gain).astype(BF16)
-    both = lax.all_gather(
-        jnp.concatenate([normed, out_grad], axis=1), "zl", axis=0, tiled=True
-    )
-    both = jnp.concatenate(gather_x(both), axis=0)
-    normed_panel, cotangent = both[:, :width], both[:, width:]
+    normed_panel = both[:, :width].astype(F32)
+    normed_panel = ((normed_panel - averages) * inverses * norm_gain).astype(BF16)
+    cotangent = both[:, width:]
     pre_part = jnp.dot(normed_panel, w_in, preferred_element_type=F32).astype(BF16)
     hid_part = contract_last(cotangent, w_out).astype(BF16)
     rows = both.shape[0] // Y
@@ -167,23 +158,15 @@
     shares = jnp.zeros((rows, LANES), BF16)
     for place, term in enumerate(split_high_low(first) + split_high_low(second)):
         shares = jnp.where(lane == place, term, shares)
-    hidden_panel, pre_grad_panel, shares = gather_y(
-        [activation.astype(BF16), pre_grad, shares]
+    hidden_panel, pre_grad_panel, shares = gather_ring(
+        [activation.astype(BF16), pre_grad, shares], "y", Y
     )
     branch_part = jnp.dot(hidden_panel, w_out, preferred_element_type=F32).astype(BF16)
     normed_grad_part = contract_last(pre_grad_panel, w_in)
     gain_part = jnp.sum(normed_grad_part * normed_panel.astype(F32), axis=0)
     sent = jnp.concatenate([branch_part, normed_grad_part.astype(BF16), shares], axis=1)
-    block = both.shape[0] // X
-    parts = [sent[i * block : (i + 1) * block] for i in range(X)]
-    back, gain_part = scatter_x(*parts, as_rows(gain_part, sent.shape[1]))
-    back = back.reshape(ZL, tokens, -1)
-    gain_part = jnp.broadcast_to(as_rows(gain_part, sent.shape[1])[None], (ZL, 8, sent.shape[1]))
-    back = lax.all_to_all(
-        jnp.concatenate([back, gain_part], axis=1), "zl", 0, 0, tiled=True
-    )
-    gain_sum = whole(jnp.sum(back[:, tokens : tokens + 1].astype(F32), axis=0))
-    back = jnp.sum(back[:, :tokens].astype(F32), axis=0)
+    back, gain_sum = scatter(sent, gain_part, "x", X)
+    back, gain_sum = scatter(back.astype(BF16), gain_sum, "zl", ZL)
     branch = back[:, :width].astype(BF16)
     normed_grad = back[:, width : 2 * width]
     rest = back[:, 2 * width :]

time: 225 us -> 232 us (1.031)
  blocking collectives: 39 us -> 12.7 us
  local copies, waits for them, and re-layouts: 4.2 us -> 25.9 us
  starting transfers between devices: 113 us -> 130 us
  waiting for transfers between devices: 49.9 us -> 38.3 us
  matrix products: 4.63 us -> 7.75 us
  other arithmetic: 11.6 us -> 14.1 us
    all_to_all x1 -> x0, blocking collectives: 27.8 us -> none  [shards(): lax.all_to_all(jnp.broadcast_to(mine, (Y * ZH,) + mine.shape), ROW, 0, 0,...]
    all_to_all x1 -> x4, starting transfers between devices: 4.48 us -> 29.1 us  [the longest x2 21.3 us: to_all(): return lax.all_to_all(copies, axes, 0, 0, tiled=True)]
    ppermute x28 -> x24, waiting for transfers between devices: 43.7 us -> 28.5 us  [shift(): lax.ppermute(values, axis, [(i, (i + by) % size) for i in range(size)])]
    slice x5 -> x22, local copies, waits for them, and re-layouts: 0.05 us -> 9.41 us  [the longest x16 6.1 us: put(): values[:, low:high]]
    dynamic_update_slice x17 -> x23, local copies, waits for them, and re-layouts: 2.04 us -> 10.8 us  [put(): lax.dynamic_update_slice(panel, values[:, low:high], (start, 0), allow_ne...]
    ppermute x28 -> x24, starting transfers between devices: 108 us -> 101 us  [shift(): lax.ppermute(values, axis, [(i, (i + by) % size) for i in range(size)])]
    all_to_all x1 -> x4, waiting for transfers between devices: 6.25 us -> 9.8 us  [the longest x2 6.5 us: to_all(): return lax.all_to_all(copies, axes, 0, 0, tiled=True)]
    dot_general x2, matrix products: 1.47 us -> 3.8 us  [contract_tokens(): lax.dot_general(left, right, (((0,), (0,)), ((), ())), preferred_element_...]
  transfers between devices with their start and end apart: 29 -> 28, of which waited for: 17 -> 11; matrix products, arithmetic and copies ran while one was open for 4% -> 13% of each run, Pallas kernels for 0% -> 0%
where the time goes in v2:
time: 232 us; the launch traced here: 231 us
  starting transfers between devices  130 us (56%)
  waiting for transfers between devices  38.3 us (17%)
  local copies, waits for them, and re-layouts  25.9 us (11%)
  other arithmetic  14.1 us (6%)
  blocking collectives  12.7 us (5%)
  matrix products  7.75 us (3%)
    ppermute x24, starting transfers between devices, shift(): lax.ppermute(values, axis, [(i, (i + by) % size) for i in range(size)])  101 us
    ppermute x24, waiting for transfers between devices, shift(): lax.ppermute(values, axis, [(i, (i + by) % size) for i in range(size)])  28.5 us
    all_to_all x2, starting transfers between devices, to_all(): return lax.all_to_all(copies, axes, 0, 0, tiled=True)  21.3 us
    all_gather x1, blocking collectives, shards(): lax.all_gather(jnp.concatenate([patches, out_grad], axis=1), 'zl', axis=0...  12.7 us
    dynamic_update_slice x23, local copies, waits for them, and re-layouts, put(): lax.dynamic_update_slice(panel, values[:, low:high], (start, 0), allow_ne...  10.8 us
    all_to_all x2, starting transfers between devices, scatter(): back = lax.all_to_all(parts, axis, 0, 0, tiled=True)  7.78 us
    all_to_all x2, waiting for transfers between devices, to_all(): return lax.all_to_all(copies, axes, 0, 0, tiled=True)  6.5 us
    slice x16, local copies, waits for them, and re-layouts, put(): values[:, low:high]  6.1 us
  transfers between devices with their start and end apart: 28, of which 11 were waited for; matrix products, arithmetic and copies ran while one was open for 13% of the time, Pallas kernels for 0%

profile of v2, /device:TPU:1, one launch (start us, length us, event | category | flops | bytes accessed | tf_op | source)
XLA Modules:
  0.0 230.6 jit_solution(12589408185593573172)
XLA Ops:
  1.6 1.3 multiply_reduce_fusion.1
  3.6 16.2 %all-to-all-start = ((f32[16,1,864]{2,1,0:T(1,128)}), f32[16,1,864]{2,1,0:T(1,128)S(1)}, u32[]{:S(2)}, u32[]{:S(2)}) async-start(f32[16,1,864]{2,1,0:T(1,128)} %broadcast_in_dim.56), calls=%async_computation | async-start | bytes 114688 | tf_op jit(solution)/shard_map/all_to_all | solution.py:39
  20.6 12.7 %all_gather.3 = bf16[192,768]{1,0:T(8,128)(2,1)S(1)} all-gather(bf16[48,768]{1,0:T(8,128)(2,1)S(1)} %pad_maximum_fusion.7), channel_id=1, replica_groups=mesh['dp'=2,'y'=8,'zh'=2,'x'=4,'zl'=4] {'zl'}, dimensions={0}, use_global_device_ids=true | all-gather | bytes 368640 | tf_op jit(solution)/shard_map/all_gather | solution.py:110
  33.3 3.1 %collective-permute-start = (bf16[192,768]{1,0:T(8,128)(2,1)S(1)}, bf16[192,768]{1,0:T(8,128)(2,1)S(1)}, u32[]{:S(2)}, u32[]{:S(2)}) collective-permute-start(bf16[192,768]{1,0:T(8,128)(2,1)S(1)} %all_gather.3), channel_id=1, source_target_pairs={{0,4},{4,8},{8,12},{12,0},{1,5},{5,9},{9,13},{13,1},{2,6},{6,10},{... | collective-permute-start | bytes 884744 | tf_op jit(solution)/shard_map/ppermute | solution.py:26
  36.4 3.4 %collective-permute-start.1 = (bf16[192,768]{1,0:T(8,128)(2,1)S(1)}, bf16[192,768]{1,0:T(8,128)(2,1)S(1)}, u32[]{:S(2)}, u32[]{:S(2)}) collective-permute-start(bf16[192,768]{1,0:T(8,128)(2,1)S(1)} %all_gather.3), channel_id=1, source_target_pairs={{0,12},{4,0},{8,4},{12,8},{1,13},{5,1},{9,5},{13,9},{2,14},{6,2},{... | collective-permute-start | bytes 884744 | tf_op jit(solution)/shard_map/ppermute | solution.py:26
  40.6 5.1 %all-to-all-start.1 = ((f32[16,1,96]{2,1,0:T(1,128)}), f32[16,1,96]{2,1,0:T(1,128)S(1)}, u32[]{:S(2)}, u32[]{:S(2)}) async-start(f32[16,1,96]{2,1,0:T(1,128)} %broadcast_in_dim.57), calls=%async_computation.1 | async-start | bytes 16384 | tf_op jit(solution)/shard_map/all_to_all | solution.py:39
  45.9 6.5 %all-to-all-done.1 = f32[16,1,96]{2,1,0:T(1,128)S(1)} async-done(((f32[16,1,96]{2,1,0:T(1,128)}), f32[16,1,96]{2,1,0:T(1,128)S(1)}, u32[]{:S(2)}, u32[]{:S(2)}) %all-to-all-start.1) | async-done | bytes 6176 | tf_op jit(solution)/shard_map/all_to_all | solution.py:39
  52.6 2.2 collective-permute-start.2
  54.9 4.3 %collective-permute-start.3 = (bf16[96,768]{1,0:T(8,128)(2,1)S(1)}, bf16[96,768]{1,0:T(8,128)(2,1)S(1)}, u32[]{:S(2)}, u32[]{:S(2)}) collective-permute-start(bf16[96,768]{1,0:T(8,128)(2,1)S(1)} %slice.218), channel_id=1, source_target_pairs={{0,12},{4,0},{8,4},{12,8},{1,13},{5,1},{9,5},{13,9},{2,14},{6,2},{... | collective-permute-start | bytes 442376 | tf_op jit(solution)/shard_map/ppermute | solution.py:26
  59.7 1.5 collective-permute-done.3
  64.0 4.2 %collective-permute-start.8 = (bf16[48,1536]{1,0:T(8,128)(2,1)S(1)}, bf16[48,1536]{1,0:T(8,128)(2,1)S(1)}, u32[]{:S(2)}, u32[]{:S(2)}) collective-permute-start(bf16[48,1536]{1,0:T(8,128)(2,1)S(1)} %get-tuple-element.43), channel_id=1, source_target_pairs={{0,224},{32,0},{64,32},{96,64},{128,96},{160,128},{192,160},{224,1... | collective-permute-start | bytes 442376 | tf_op jit(solution)/shard_map/ppermute | solution.py:26
  68.2 1.9 collective-permute-start.4
  70.4 5.0 %collective-permute-start.9 = (bf16[96,1536]{1,0:T(8,128)(2,1)S(1)}, bf16[96,1536]{1,0:T(8,128)(2,1)S(1)}, u32[]{:S(2)}, u32[]{:S(2)}) collective-permute-start(bf16[96,1536]{1,0:T(8,128)(2,1)S(1)} %pad_maximum_fusion.4), channel_id=1, source_target_pairs={{0,224},{32,0},{64,32},{96,64},{128,96},{160,128},{192,160},{224,1... | collective-permute-start | bytes 884744 | tf_op jit(solution)/shard_map/ppermute | solution.py:26
  75.5 1.9 collective-permute-start.5
  77.4 3.2 %collective-permute-done.9 = bf16[96,1536]{1,0:T(8,128)(2,1)S(1)} collective-permute-done((bf16[96,1536]{1,0:T(8,128)(2,1)S(1)}, bf16[96,1536]{1,0:T(8,128)(2,1)S(1)}, u32[]{:S(2)}, u32[]{:S(2)}) %collective-permute-start.9) | collective-permute-done | bytes 294944 | tf_op jit(solution)/shard_map/ppermute | solution.py:26
  80.7 5.0 %collective-permute-start.10 = (bf16[96,1536]{1,0:T(8,128)(2,1)S(1)}, bf16[96,1536]{1,0:T(8,128)(2,1)S(1)}, u32[]{:S(2)}, u32[]{:S(2)}) collective-permute-start(bf16[96,1536]{1,0:T(8,128)(2,1)S(1)} %add_convert_fusion.2), channel_id=1, source_target_pairs={{0,224},{32,0},{64,32},{96,64},{128,96},{160,128},{192,160},{224,1... | collective-permute-start | bytes 884744 | tf_op jit(solution)/shard_map/ppermute | solution.py:26
  85.8 1.9 collective-permute-start.6
  87.8 4.6 %collective-permute-done.10 = bf16[96,1536]{1,0:T(8,128)(2,1)S(1)} collective-permute-done((bf16[96,1536]{1,0:T(8,128)(2,1)S(1)}, bf16[96,1536]{1,0:T(8,128)(2,1)S(1)}, u32[]{:S(2)}, u32[]{:S(2)}) %collective-permute-start.10) | collective-permute-done | bytes 294944 | tf_op jit(solution)/shard_map/ppermute | solution.py:26
  92.4 5.3 %collective-permute-start.11 = (bf16[96,1536]{1,0:T(8,128)(2,1)S(1)}, bf16[96,1536]{1,0:T(8,128)(2,1)S(1)}, u32[]{:S(2)}, u32[]{:S(2)}) collective-permute-start(bf16[96,1536]{1,0:T(8,128)(2,1)S(1)} %add_convert_fusion.1), channel_id=1, source_target_pairs={{0,224},{32,0},{64,32},{96,64},{128,96},{160,128},{192,160},{224,1... | collective-permute-start | bytes 884744 | tf_op jit(solution)/shard_map/ppermute | solution.py:26
  97.8 1.9 collective-permute-start.7
  99.7 3.7 %collective-permute-done.11 = bf16[96,1536]{1,0:T(8,128)(2,1)S(1)} collective-permute-done((bf16[96,1536]{1,0:T(8,128)(2,1)S(1)}, bf16[96,1536]{1,0:T(8,128)(2,1)S(1)}, u32[]{:S(2)}, u32[]{:S(2)}) %collective-permute-start.11) | collective-permute-done | bytes 294944 | tf_op jit(solution)/shard_map/ppermute | solution.py:26
  103.4 5.1 %collective-permute-done.7 = bf16[96,1536]{1,0:T(8,128)(2,1)S(1)} collective-permute-done((bf16[96,1536]{1,0:T(8,128)(2,1)S(1)}, bf16[96,1536]{1,0:T(8,128)(2,1)S(1)}, u32[]{:S(2)}, u32[]{:S(2)}) %collective-permute-start.7) | collective-permute-done | bytes 294944 | tf_op jit(solution)/shard_map/ppermute | solution.py:26
  108.6 6.5 %collective-permute-start.12 = (bf16[96,1536]{1,0:T(8,128)(2,1)S(1)}, bf16[96,1536]{1,0:T(8,128)(2,1)S(1)}, u32[]{:S(2)}, u32[]{:S(2)}) collective-permute-start(bf16[96,1536]{1,0:T(8,128)(2,1)S(1)} %add_convert_fusion), channel_id=1, source_target_pairs={{0,16},{16,0},{1,17},{17,1},{2,18},{18,2},{3,19},{19,3},{4,20},{20... | collective-permute-start | bytes 884744 | tf_op jit(solution)/shard_map/ppermute | solution.py:26
  115.2 7.3 %collective-permute-done.12 = bf16[96,1536]{1,0:T(8,128)(2,1)S(1)} collective-permute-done((bf16[96,1536]{1,0:T(8,128)(2,1)S(1)}, bf16[96,1536]{1,0:T(8,128)(2,1)S(1)}, u32[]{:S(2)}, u32[]{:S(2)}) %collective-permute-start.12) | collective-permute-done | bytes 294944 | tf_op jit(solution)/shard_map/ppermute | solution.py:26
  124.0 1.9 collective-permute-start.13
  126.0 4.6 %collective-permute-start.14 = (bf16[96,1664]{1,0:T(8,128)(2,1)}, bf16[96,1664]{1,0:T(8,128)(2,1)}, u32[]{:S(2)}, u32[]{:S(2)}) collective-permute-start(bf16[96,1664]{1,0:T(8,128)(2,1)} %pad_maximum_fusion.3), channel_id=1, source_target_pairs={{0,224},{32,0},{64,32},{96,64},{128,96},{160,128},{192,160},{224,1... | collective-permute-start | bytes 958472 | tf_op jit(solution)/shard_map/ppermute | solution.py:26
  131.0 2.4 %collective-permute-done.13 = bf16[96,1664]{1,0:T(8,128)(2,1)} collective-permute-done((bf16[96,1664]{1,0:T(8,128)(2,1)}, bf16[96,1664]{1,0:T(8,128)(2,1)}, u32[]{:S(2)}, u32[]{:S(2)}) %collective-permute-start.13) | collective-permute-done | bytes 319520 | tf_op jit(solution)/shard_map/ppermute | solution.py:26
  133.5 1.9 collective-permute-start.15
  135.4 4.6 %collective-permute-start.16 = (bf16[96,1664]{1,0:T(8,128)(2,1)}, bf16[96,1664]{1,0:T(8,128)(2,1)}, u32[]{:S(2)}, u32[]{:S(2)}) collective-permute-start(bf16[96,1664]{1,0:T(8,128)(2,1)} %collective-permute-done.14), channel_id=1, source_target_pairs={{0,224},{32,0},{64,32},{96,64},{128,96},{160,128},{192,160},{224,1... | collective-permute-start | bytes 958472 | tf_op jit(solution)/shard_map/ppermute | solution.py:26
  144.6 1.9 collective-permute-start.17
  146.6 4.6 %collective-permute-start.18 = (bf16[96,1664]{1,0:T(8,128)(2,1)}, bf16[96,1664]{1,0:T(8,128)(2,1)}, u32[]{:S(2)}, u32[]{:S(2)}) collective-permute-start(bf16[96,1664]{1,0:T(8,128)(2,1)} %collective-permute-done.16), channel_id=1, source_target_pairs={{0,224},{32,0},{64,32},{96,64},{128,96},{160,128},{192,160},{224,1... | collective-permute-start | bytes 958472 | tf_op jit(solution)/shard_map/ppermute | solution.py:26
  155.8 1.6 slice.237
  157.4 1.9 collective-permute-start.19
  159.3 1.6 slice.239
  160.9 4.7 %collective-permute-start.20 = (bf16[48,1664]{1,0:T(8,128)(2,1)}, bf16[48,1664]{1,0:T(8,128)(2,1)}, u32[]{:S(2)}, u32[]{:S(2)}) collective-permute-start(bf16[48,1664]{1,0:T(8,128)(2,1)} %slice.239), channel_id=1, source_target_pairs={{0,224},{32,0},{64,32},{96,64},{128,96},{160,128},{192,160},{224,1... | collective-permute-start | bytes 479240 | tf_op jit(solution)/shard_map/ppermute | solution.py:26
  168.3 1.1 slice_dynamic-update-slice_fusion.7
  171.5 1.6 multiply_reduce_fusion
  174.7 1.3 copy.83
  178.4 1.3 pad_maximum_fusion
  179.6 4.3 %all-to-all-start.2 = ((bf16[4,200,896]{2,1,0:T(8,128)(2,1)}), bf16[4,200,896]{2,1,0:T(8,128)(2,1)S(1)}, u32[]{:S(2)}, u32[]{:S(2)}) async-start(bf16[4,200,896]{2,1,0:T(8,128)(2,1)} %pad_maximum_fusion), calls=%async_computation.2 | async-start | bytes 2867200 | tf_op jit(solution)/shard_map/all_to_all | solution.py:99
  184.0 3.0 %convolution_convert_fusion.3 = bf16[384,768]{1,0:T(8,128)(2,1)} fusion(bf16[768,768]{1,0:T(8,128)(2,1)S(1)} %copy-done.2, bf16[768,768]{1,0:T(8,128)(2,1)} %copy-done.5, f32[384]{0:T(512)S(1)} %copy-done.11, f32[768]{0:T(1024)S(1)} %mul.182, f32[768]{0:T(1024)S(1)} %sub.58), kind=kOutput, calls=%fused_computation.6 | convolution fusion | flops 454754304 | bytes 2366976 | tf_op jit(solution)/shard_map/dot_general | solution.py:14
  187.0 18.0 %collective-permute-start.21 = (bf16[384,768]{1,0:T(8,128)(2,1)}, bf16[384,768]{1,0:T(8,128)(2,1)S(1)}, u32[]{:S(2)}, u32[]{:S(2)}) collective-permute-start(bf16[384,768]{1,0:T(8,128)(2,1)} %convolution_convert_fusion.3), channel_id=1, source_target_pairs={{0,256},{256,0},{1,257},{257,1},{2,258},{258,2},{3,259},{259,3},{4... | collective-permute-start | bytes 1769480 | tf_op jit(solution)/shard_map/ppermute | solution.py:26
  205.8 1.9 collective-permute-start.22
  208.8 3.5 %all-to-all-start.3 = ((bf16[4,56,896]{2,1,0:T(8,128)(2,1)}), bf16[4,56,896]{2,1,0:T(8,128)(2,1)S(1)}, u32[]{:S(2)}, u32[]{:S(2)}) async-start(bf16[4,56,896]{2,1,0:T(8,128)(2,1)} %pad_maximum_fusion.2), calls=%async_computation.3 | async-start | bytes 802816 | tf_op jit(solution)/shard_map/all_to_all | solution.py:99
  212.3 2.2 convert_add_fusion.1
  214.5 2.2 convert_add_fusion
  216.7 3.3 %all-to-all-done.3 = bf16[4,56,896]{2,1,0:T(8,128)(2,1)S(1)} async-done(((bf16[4,56,896]{2,1,0:T(8,128)(2,1)}), bf16[4,56,896]{2,1,0:T(8,128)(2,1)S(1)}, u32[]{:S(2)}, u32[]{:S(2)}) %all-to-all-start.3) | async-done | bytes 401440 | tf_op jit(solution)/shard_map/all_to_all | solution.py:99
  220.3 8.3 %collective-permute-start.23 = (f32[384]{0:T(512)S(1)}, f32[384]{0:T(512)S(1)}, u32[]{:S(2)}, u32[]{:S(2)}) collective-permute-start(f32[384]{0:T(512)S(1)} %slice_add_fusion), channel_id=1, source_target_pairs={{0,256},{256,0},{1,257},{257,1},{2,258},{258,2},{3,259},{259,3},{4... | collective-permute-start | bytes 4616 | tf_op jit(solution)/shard_map/ppermute | solution.py:26
  (157 shorter events, 31.2 us)
Async XLA Ops:
  0.6 60.6 %copy-start = (bf16[768,384]{1,0:T(8,128)(2,1)S(1)}, bf16[768,384]{1,0:T(8,128)(2,1)}, u32[]{:S(2)}) copy-start(bf16[768,384]{1,0:T(8,128)(2,1)} %param.8) | copy-start | bytes 1769476
  3.6 36.2 %all-to-all-start = ((f32[16,1,864]{2,1,0:T(1,128)}), f32[16,1,864]{2,1,0:T(1,128)S(1)}, u32[]{:S(2)}, u32[]{:S(2)}) async-start(f32[16,1,864]{2,1,0:T(1,128)} %broadcast_in_dim.56), calls=%async_computation | async-start | bytes 114688 | tf_op jit(solution)/shard_map/all_to_all | solution.py:39
  33.3 19.3 %collective-permute-start = (bf16[192,768]{1,0:T(8,128)(2,1)S(1)}, bf16[192,768]{1,0:T(8,128)(2,1)S(1)}, u32[]{:S(2)}, u32[]{:S(2)}) collective-permute-start(bf16[192,768]{1,0:T(8,128)(2,1)S(1)} %all_gather.3), channel_id=1, source_target_pairs={{0,4},{4,8},{8,12},{12,0},{1,5},{5,9},{9,13},{13,1},{2,6},{6,10},{... | collective-permute-start | bytes 884744 | tf_op jit(solution)/shard_map/ppermute | solution.py:26
  36.4 18.4 %collective-permute-start.1 = (bf16[192,768]{1,0:T(8,128)(2,1)S(1)}, bf16[192,768]{1,0:T(8,128)(2,1)S(1)}, u32[]{:S(2)}, u32[]{:S(2)}) collective-permute-start(bf16[192,768]{1,0:T(8,128)(2,1)S(1)} %all_gather.3), channel_id=1, source_target_pairs={{0,12},{4,0},{8,4},{12,8},{1,13},{5,1},{9,5},{13,9},{2,14},{6,2},{... | collective-permute-start | bytes 884744 | tf_op jit(solution)/shard_map/ppermute | solution.py:26
  39.9 0.7 copy-start.13
  39.9 0.7 copy-start.15
  40.6 11.7 %all-to-all-start.1 = ((f32[16,1,96]{2,1,0:T(1,128)}), f32[16,1,96]{2,1,0:T(1,128)S(1)}, u32[]{:S(2)}, u32[]{:S(2)}) async-start(f32[16,1,96]{2,1,0:T(1,128)} %broadcast_in_dim.57), calls=%async_computation.1 | async-start | bytes 16384 | tf_op jit(solution)/shard_map/all_to_all | solution.py:39
  52.6 7.1 %collective-permute-start.2 = (bf16[96,768]{1,0:T(8,128)(2,1)S(1)}, bf16[96,768]{1,0:T(8,128)(2,1)S(1)}, u32[]{:S(2)}, u32[]{:S(2)}) collective-permute-start(bf16[96,768]{1,0:T(8,128)(2,1)S(1)} %slice.217), channel_id=1, source_target_pairs={{0,4},{4,8},{8,12},{12,0},{1,5},{5,9},{9,13},{13,1},{2,6},{6,10},{... | collective-permute-start | bytes 442376 | tf_op jit(solution)/shard_map/ppermute | solution.py:26
  54.9 6.4 %collective-permute-start.3 = (bf16[96,768]{1,0:T(8,128)(2,1)S(1)}, bf16[96,768]{1,0:T(8,128)(2,1)S(1)}, u32[]{:S(2)}, u32[]{:S(2)}) collective-permute-start(bf16[96,768]{1,0:T(8,128)(2,1)S(1)} %slice.218), channel_id=1, source_target_pairs={{0,12},{4,0},{8,4},{12,8},{1,13},{5,1},{9,5},{13,9},{2,14},{6,2},{... | collective-permute-start | bytes 442376 | tf_op jit(solution)/shard_map/ppermute | solution.py:26
  61.3 2.7 %copy-start.5 = (bf16[768,768]{1,0:T(8,128)(2,1)}, bf16[768,768]{1,0:T(8,128)(2,1)S(1)}, u32[]{:S(2)}) copy-start(bf16[768,768]{1,0:T(8,128)(2,1)S(1)} %constant_dynamic-update-slice_fusion.2) | copy-start | bytes 3538948
  61.3 1.5 copy-start.8
  61.3 1.5 copy-start.11
  64.0 6.3 %collective-permute-start.8 = (bf16[48,1536]{1,0:T(8,128)(2,1)S(1)}, bf16[48,1536]{1,0:T(8,128)(2,1)S(1)}, u32[]{:S(2)}, u32[]{:S(2)}) collective-permute-start(bf16[48,1536]{1,0:T(8,128)(2,1)S(1)} %get-tuple-element.43), channel_id=1, source_target_pairs={{0,224},{32,0},{64,32},{96,64},{128,96},{160,128},{192,160},{224,1... | collective-permute-start | bytes 442376 | tf_op jit(solution)/shard_map/ppermute | solution.py:26
  68.2 7.2 %collective-permute-start.4 = (bf16[48,1536]{1,0:T(8,128)(2,1)S(1)}, bf16[48,1536]{1,0:T(8,128)(2,1)S(1)}, u32[]{:S(2)}, u32[]{:S(2)}) collective-permute-start(bf16[48,1536]{1,0:T(8,128)(2,1)S(1)} %get-tuple-element.42), channel_id=1, source_target_pairs={{0,32},{32,64},{64,96},{96,128},{128,160},{160,192},{192,224},{224... | collective-permute-start | bytes 442376 | tf_op jit(solution)/shard_map/ppermute | solution.py:26
  70.4 10.2 %collective-permute-start.9 = (bf16[96,1536]{1,0:T(8,128)(2,1)S(1)}, bf16[96,1536]{1,0:T(8,128)(2,1)S(1)}, u32[]{:S(2)}, u32[]{:S(2)}) collective-permute-start(bf16[96,1536]{1,0:T(8,128)(2,1)S(1)} %pad_maximum_fusion.4), channel_id=1, source_target_pairs={{0,224},{32,0},{64,32},{96,64},{128,96},{160,128},{192,160},{224,1... | collective-permute-start | bytes 884744 | tf_op jit(solution)/shard_map/ppermute | solution.py:26
  75.5 10.3 %collective-permute-start.5 = (bf16[96,1536]{1,0:T(8,128)(2,1)S(1)}, bf16[96,1536]{1,0:T(8,128)(2,1)S(1)}, u32[]{:S(2)}, u32[]{:S(2)}) collective-permute-start(bf16[96,1536]{1,0:T(8,128)(2,1)S(1)} %fusion.14), channel_id=1, source_target_pairs={{0,32},{32,64},{64,96},{96,128},{128,160},{160,192},{192,224},{224... | collective-permute-start | bytes 884744 | tf_op jit(solution)/shard_map/ppermute | solution.py:26
  80.7 11.6 %collective-permute-start.10 = (bf16[96,1536]{1,0:T(8,128)(2,1)S(1)}, bf16[96,1536]{1,0:T(8,128)(2,1)S(1)}, u32[]{:S(2)}, u32[]{:S(2)}) collective-permute-start(bf16[96,1536]{1,0:T(8,128)(2,1)S(1)} %add_convert_fusion.2), channel_id=1, source_target_pairs={{0,224},{32,0},{64,32},{96,64},{128,96},{160,128},{192,160},{224,1... | collective-permute-start | bytes 884744 | tf_op jit(solution)/shard_map/ppermute | solution.py:26
  85.8 11.9 %collective-permute-start.6 = (bf16[96,1536]{1,0:T(8,128)(2,1)S(1)}, bf16[96,1536]{1,0:T(8,128)(2,1)S(1)}, u32[]{:S(2)}, u32[]{:S(2)}) collective-permute-start(bf16[96,1536]{1,0:T(8,128)(2,1)S(1)} %add_convert_fusion.4), channel_id=1, source_target_pairs={{0,32},{32,64},{64,96},{96,128},{128,160},{160,192},{192,224},{224... | collective-permute-start | bytes 884744 | tf_op jit(solution)/shard_map/ppermute | solution.py:26
  92.4 11.0 %collective-permute-start.11 = (bf16[96,1536]{1,0:T(8,128)(2,1)S(1)}, bf16[96,1536]{1,0:T(8,128)(2,1)S(1)}, u32[]{:S(2)}, u32[]{:S(2)}) collective-permute-start(bf16[96,1536]{1,0:T(8,128)(2,1)S(1)} %add_convert_fusion.1), channel_id=1, source_target_pairs={{0,224},{32,0},{64,32},{96,64},{128,96},{160,128},{192,160},{224,1... | collective-permute-start | bytes 884744 | tf_op jit(solution)/shard_map/ppermute | solution.py:26
  97.8 10.7 %collective-permute-start.7 = (bf16[96,1536]{1,0:T(8,128)(2,1)S(1)}, bf16[96,1536]{1,0:T(8,128)(2,1)S(1)}, u32[]{:S(2)}, u32[]{:S(2)}) collective-permute-start(bf16[96,1536]{1,0:T(8,128)(2,1)S(1)} %add_convert_fusion.3), channel_id=1, source_target_pairs={{0,32},{32,64},{64,96},{96,128},{128,160},{160,192},{192,224},{224... | collective-permute-start | bytes 884744 | tf_op jit(solution)/shard_map/ppermute | solution.py:26
  108.6 13.9 %collective-permute-start.12 = (bf16[96,1536]{1,0:T(8,128)(2,1)S(1)}, bf16[96,1536]{1,0:T(8,128)(2,1)S(1)}, u32[]{:S(2)}, u32[]{:S(2)}) collective-permute-start(bf16[96,1536]{1,0:T(8,128)(2,1)S(1)} %add_convert_fusion), channel_id=1, source_target_pairs={{0,16},{16,0},{1,17},{17,1},{2,18},{18,2},{3,19},{19,3},{4,20},{20... | collective-permute-start | bytes 884744 | tf_op jit(solution)/shard_map/ppermute | solution.py:26
  124.0 9.4 %collective-permute-start.13 = (bf16[96,1664]{1,0:T(8,128)(2,1)}, bf16[96,1664]{1,0:T(8,128)(2,1)}, u32[]{:S(2)}, u32[]{:S(2)}) collective-permute-start(bf16[96,1664]{1,0:T(8,128)(2,1)} %pad_maximum_fusion.3), channel_id=1, source_target_pairs={{0,32},{32,64},{64,96},{96,128},{128,160},{160,192},{192,224},{224... | collective-permute-start | bytes 958472 | tf_op jit(solution)/shard_map/ppermute | solution.py:26
  126.0 9.4 %collective-permute-start.14 = (bf16[96,1664]{1,0:T(8,128)(2,1)}, bf16[96,1664]{1,0:T(8,128)(2,1)}, u32[]{:S(2)}, u32[]{:S(2)}) collective-permute-start(bf16[96,1664]{1,0:T(8,128)(2,1)} %pad_maximum_fusion.3), channel_id=1, source_target_pairs={{0,224},{32,0},{64,32},{96,64},{128,96},{160,128},{192,160},{224,1... | collective-permute-start | bytes 958472 | tf_op jit(solution)/shard_map/ppermute | solution.py:26
  133.5 11.1 %collective-permute-start.15 = (bf16[96,1664]{1,0:T(8,128)(2,1)}, bf16[96,1664]{1,0:T(8,128)(2,1)}, u32[]{:S(2)}, u32[]{:S(2)}) collective-permute-start(bf16[96,1664]{1,0:T(8,128)(2,1)} %collective-permute-done.13), channel_id=1, source_target_pairs={{0,32},{32,64},{64,96},{96,128},{128,160},{160,192},{192,224},{224... | collective-permute-start | bytes 958472 | tf_op jit(solution)/shard_map/ppermute | solution.py:26
  135.4 11.1 %collective-permute-start.16 = (bf16[96,1664]{1,0:T(8,128)(2,1)}, bf16[96,1664]{1,0:T(8,128)(2,1)}, u32[]{:S(2)}, u32[]{:S(2)}) collective-permute-start(bf16[96,1664]{1,0:T(8,128)(2,1)} %collective-permute-done.14), channel_id=1, source_target_pairs={{0,224},{32,0},{64,32},{96,64},{128,96},{160,128},{192,160},{224,1... | collective-permute-start | bytes 958472 | tf_op jit(solution)/shard_map/ppermute | solution.py:26
  144.6 11.2 %collective-permute-start.17 = (bf16[96,1664]{1,0:T(8,128)(2,1)}, bf16[96,1664]{1,0:T(8,128)(2,1)}, u32[]{:S(2)}, u32[]{:S(2)}) collective-permute-start(bf16[96,1664]{1,0:T(8,128)(2,1)} %collective-permute-done.15), channel_id=1, source_target_pairs={{0,32},{32,64},{64,96},{96,128},{128,160},{160,192},{192,224},{224... | collective-permute-start | bytes 958472 | tf_op jit(solution)/shard_map/ppermute | solution.py:26
  146.6 12.7 %collective-permute-start.18 = (bf16[96,1664]{1,0:T(8,128)(2,1)}, bf16[96,1664]{1,0:T(8,128)(2,1)}, u32[]{:S(2)}, u32[]{:S(2)}) collective-permute-start(bf16[96,1664]{1,0:T(8,128)(2,1)} %collective-permute-done.16), channel_id=1, source_target_pairs={{0,224},{32,0},{64,32},{96,64},{128,96},{160,128},{192,160},{224,1... | collective-permute-start | bytes 958472 | tf_op jit(solution)/shard_map/ppermute | solution.py:26
  157.4 13.1 %collective-permute-start.19 = (bf16[48,1664]{1,0:T(8,128)(2,1)}, bf16[48,1664]{1,0:T(8,128)(2,1)S(1)}, u32[]{:S(2)}, u32[]{:S(2)}) collective-permute-start(bf16[48,1664]{1,0:T(8,128)(2,1)} %slice.237), channel_id=1, source_target_pairs={{0,32},{32,64},{64,96},{96,128},{128,160},{160,192},{192,224},{224... | collective-permute-start | bytes 479240 | tf_op jit(solution)/shard_map/ppermute | solution.py:26
  160.9 9.6 %collective-permute-start.20 = (bf16[48,1664]{1,0:T(8,128)(2,1)}, bf16[48,1664]{1,0:T(8,128)(2,1)}, u32[]{:S(2)}, u32[]{:S(2)}) collective-permute-start(bf16[48,1664]{1,0:T(8,128)(2,1)} %slice.239), channel_id=1, source_target_pairs={{0,224},{32,0},{64,32},{96,64},{128,96},{160,128},{192,160},{224,1... | collective-permute-start | bytes 479240 | tf_op jit(solution)/shard_map/ppermute | solution.py:26
  168.3 3.2 %copy-start.6 = (bf16[768,768]{1,0:T(8,128)(2,1)S(1)}, bf16[768,768]{1,0:T(8,128)(2,1)}, u32[]{:S(2)}) copy-start(bf16[768,768]{1,0:T(8,128)(2,1)} %copy-done.5) | copy-start | bytes 3538948
  168.3 3.2 %copy-start.9 = (bf16[384,768]{1,0:T(8,128)(2,1)S(1)}, bf16[384,768]{1,0:T(8,128)(2,1)}, u32[]{:S(2)}) copy-start(bf16[384,768]{1,0:T(8,128)(2,1)} %param.7) | copy-start | bytes 1769476
  171.4 1.7 copy-start.1
  171.5 4.5 %copy-start.3 = (bf16[768,768]{1,0:T(8,128)(2,1)}, bf16[768,768]{1,0:T(8,128)(2,1)S(1)}, u32[]{:S(2)}) copy-start(bf16[768,768]{1,0:T(8,128)(2,1)S(1)} %get-tuple-element.44) | copy-start | bytes 3538948
  177.4 0.9 copy-start.12
  179.6 4.3 %copy-start.2 = (bf16[768,768]{1,0:T(8,128)(2,1)S(1)}, bf16[768,768]{1,0:T(8,128)(2,1)}, u32[]{:S(2)}) copy-start(bf16[768,768]{1,0:T(8,128)(2,1)} %copy-done.1) | copy-start | bytes 3538948
  179.6 28.1 %all-to-all-start.2 = ((bf16[4,200,896]{2,1,0:T(8,128)(2,1)}), bf16[4,200,896]{2,1,0:T(8,128)(2,1)S(1)}, u32[]{:S(2)}, u32[]{:S(2)}) async-start(bf16[4,200,896]{2,1,0:T(8,128)(2,1)} %pad_maximum_fusion), calls=%async_computation.2 | async-start | bytes 2867200 | tf_op jit(solution)/shard_map/all_to_all | solution.py:99
  184.0 21.0 %copy-start.4 = (bf16[768,768]{1,0:T(8,128)(2,1)S(1)}, bf16[768,768]{1,0:T(8,128)(2,1)}, u32[]{:S(2)}) copy-start(bf16[768,768]{1,0:T(8,128)(2,1)} %copy-done.3) | copy-start | bytes 3538948
  184.0 21.0 %copy-start.7 = (bf16[768,768]{1,0:T(8,128)(2,1)S(1)}, bf16[768,768]{1,0:T(8,128)(2,1)}, u32[]{:S(2)}) copy-start(bf16[768,768]{1,0:T(8,128)(2,1)} %copy-done.5) | copy-start | bytes 3538948
  187.0 25.3 %collective-permute-start.21 = (bf16[384,768]{1,0:T(8,128)(2,1)}, bf16[384,768]{1,0:T(8,128)(2,1)S(1)}, u32[]{:S(2)}, u32[]{:S(2)}) collective-permute-start(bf16[384,768]{1,0:T(8,128)(2,1)} %convolution_convert_fusion.3), channel_id=1, source_target_pairs={{0,256},{256,0},{1,257},{257,1},{2,258},{258,2},{3,259},{259,3},{4... | collective-permute-start | bytes 1769480 | tf_op jit(solution)/shard_map/ppermute | solution.py:26
  205.8 8.7 %collective-permute-start.22 = (bf16[768,384]{1,0:T(8,128)(2,1)S(1)}, bf16[768,384]{1,0:T(8,128)(2,1)}, u32[]{:S(2)}, u32[]{:S(2)}) collective-permute-start(bf16[768,384]{1,0:T(8,128)(2,1)S(1)} %convolution_convert_fusion.2), channel_id=1, source_target_pairs={{0,256},{256,0},{1,257},{257,1},{2,258},{258,2},{3,259},{259,3},{4... | collective-permute-start | bytes 1769480 | tf_op jit(solution)/shard_map/ppermute | solution.py:26
  208.8 11.3 %all-to-all-start.3 = ((bf16[4,56,896]{2,1,0:T(8,128)(2,1)}), bf16[4,56,896]{2,1,0:T(8,128)(2,1)S(1)}, u32[]{:S(2)}, u32[]{:S(2)}) async-start(bf16[4,56,896]{2,1,0:T(8,128)(2,1)} %pad_maximum_fusion.2), calls=%async_computation.3 | async-start | bytes 802816 | tf_op jit(solution)/shard_map/all_to_all | solution.py:99
  214.5 14.1 %copy-start.10 = (bf16[48,384]{1,0:T(8,128)(2,1)S(1)}, bf16[48,384]{1,0:T(8,128)(2,1)}, u32[]{:S(2)}) copy-start(bf16[48,384]{1,0:T(8,128)(2,1)} %param.5) | copy-start | bytes 110596
  214.5 14.1 %copy-start.14 = (f32[48]{0:T(128)S(1)}, f32[48]{0:T(128)}, u32[]{:S(2)}) copy-start(f32[48]{0:T(128)} %copy-done.13) | copy-start | bytes 580
  214.5 14.1 %copy-start.16 = (f32[48]{0:T(128)S(1)}, f32[48]{0:T(128)}, u32[]{:S(2)}) copy-start(f32[48]{0:T(128)} %copy-done.15) | copy-start | bytes 580
  220.3 9.7 %collective-permute-start.23 = (f32[384]{0:T(512)S(1)}, f32[384]{0:T(512)S(1)}, u32[]{:S(2)}, u32[]{:S(2)}) collective-permute-start(f32[384]{0:T(512)S(1)} %slice_add_fusion), channel_id=1, source_target_pairs={{0,256},{256,0},{1,257},{257,1},{2,258},{258,2},{3,259},{259,3},{4... | collective-permute-start | bytes 4616 | tf_op jit(solution)/shard_map/ppermute | solution.py:26

commit v3 on v2

--- a/solution.py
+++ b/solution.py
@@ -1,6 +1,7 @@
 import jax
 import jax.numpy as jnp
 from jax import lax
+from jax.experimental.layout import Layout, with_layout_constraint
 from jax.sharding import Mesh, PartitionSpec as P
 
 Y, ZH, X, ZL = 8, 2, 4, 4
@@ -24,6 +25,10 @@
 
 def shift(values, axis, size, by):
     return lax.ppermute(values, axis, [(i, (i + by) % size) for i in range(size)])
+
+
+def row_major(values):
+    return with_layout_constraint(values, Layout((0, 1)))
 
 
 def add(*terms):
@@ -107,11 +112,12 @@
     tokens, width = patches.shape
     hidden_width = w_in.shape[1]
     model_width = width * Y * ZH
-    both = lax.all_gather(
+    near = lax.all_gather(
         jnp.concatenate([patches, out_grad], axis=1), "zl", axis=0, tiled=True
     )
-    both = gather_ring([both], "x", X)[0]
-    values = patches.astype(F32)
+    cotangent = near[:, width:]
+    below, above = shift(cotangent, "x", X, 1), shift(cotangent, "x", X, -1)
+    values = near[:, :width].astype(F32)
     image = jnp.sum(norm_gain[:, None] * w_in.astype(F32), axis=0)
     sums = jnp.sum(
         to_all(
@@ -120,21 +126,44 @@
         ),
         axis=0,
     )
-    average = sums[:tokens] / model_width
-    squares = sums[tokens : 2 * tokens] / model_width
-    image = sums[2 * tokens :]
+    count = near.shape[0]
+    average = (sums[:count] / model_width)[:, None]
+    squares = (sums[count : 2 * count] / model_width)[:, None]
+    image = sums[2 * count :]
     inverse = lax.rsqrt(squares - average * average + 1e-06)
-    scales = to_all(jnp.concatenate([average, inverse]), COL)
-    averages = scales[:, :tokens].reshape(-1, 1)
-    inverses = scales[:, tokens:].reshape(-1, 1)
-    average, inverse = average[:, None], inverse[:, None]
     centred = (values - average) * inverse
-    normed_panel = both[:, :width].astype(F32)
-    normed_panel = ((normed_panel - averages) * inverses * norm_gain).astype(BF16)
-    cotangent = both[:, width:]
+    normed, below, above = lax.optimization_barrier(
+        ((centred * norm_gain).astype(BF16), below, above)
+    )
+    half = count // 2
+    place = lax.axis_index("x")
+
+    def panel(own, below, above, far):
+        whole = jnp.zeros((X * count, width), BF16)
+        for by, block in ((0, own), (-1, below), (1, above), (2, far)):
+            start = ((place + (by + X)) & (X - 1)) * count
+            whole = lax.dynamic_update_slice(
+                whole, block, (start, 0), allow_negative_indices=False
+            )
+        return whole
+
+    up = shift(jnp.concatenate([normed, below[:half]], axis=0), "x", X, 1)
+    down = shift(jnp.concatenate([normed, above[half:]], axis=0), "x", X, -1)
+    far = jnp.concatenate([up[count:], down[count:]], axis=0)
+    cotangent = panel(cotangent, below, above, far)
+    below, above = up[:count], down[:count]
+    far = shift(below[:half], "x", X, 1), shift(above[half:], "x", X, -1)
+    normed_panel = panel(normed, below, above, jnp.concatenate(far, axis=0))
+    own = lax.axis_index("zl") * tokens
+    centred, inverse = (
+        lax.dynamic_slice(
+            a, (own, 0), (tokens, a.shape[1]), allow_negative_indices=False
+        )
+        for a in (centred, inverse)
+    )
     pre_part = jnp.dot(normed_panel, w_in, preferred_element_type=F32).astype(BF16)
     hid_part = contract_last(cotangent, w_out).astype(BF16)
-    rows = both.shape[0] // Y
+    rows = cotangent.shape[0] // Y
 
     def part(place):
         return jnp.concatenate(
@@ -164,7 +193,9 @@
     branch_part = jnp.dot(hidden_panel, w_out, preferred_element_type=F32).astype(BF16)
     normed_grad_part = contract_last(pre_grad_panel, w_in)
     gain_part = jnp.sum(normed_grad_part * normed_panel.astype(F32), axis=0)
-    sent = jnp.concatenate([branch_part, normed_grad_part.astype(BF16), shares], axis=1)
+    sent = row_major(
+        jnp.concatenate([branch_part, normed_grad_part.astype(BF16), shares], axis=1)
+    )
     back, gain_sum = scatter(sent, gain_part, "x", X)
     back, gain_sum = scatter(back.astype(BF16), gain_sum, "zl", ZL)
     branch = back[:, :width].astype(BF16)

time: 232 us -> 214 us (0.922)
  local copies, waits for them, and re-layouts: 25.9 us -> 7.85 us
  blocking collectives: 12.7 us -> 15.6 us
    all_to_all x2 -> x1, starting transfers between devices: 21.3 us -> 12.9 us  [to_all(): return lax.all_to_all(copies, axes, 0, 0, tiled=True)]
    dynamic_update_slice x23 -> x17, local copies, waits for them, and re-layouts: 10.8 us -> 3.76 us  [put(): lax.dynamic_update_slice(panel, values[:, low:high], (start, 0), allow_ne...]
    slice x18 -> x6, local copies, waits for them, and re-layouts: 6.25 us -> 0.1 us  [the longest x1 0.05 us: shards(): cotangent = near[:, width:]]
    ppermute x24 -> x26, starting transfers between devices: 101 us -> 106 us  [shift(): lax.ppermute(values, axis, [(i, (i + by) % size) for i in range(size)])]
    all_gather x1, blocking collectives: 12.7 us -> 15.6 us  [shards(): lax.all_gather(jnp.concatenate([patches, out_grad], axis=1), 'zl', axis=0...]
    ppermute x24 -> x26, waiting for transfers between devices: 28.5 us -> 30.6 us  [shift(): lax.ppermute(values, axis, [(i, (i + by) % size) for i in range(size)])]
    all_to_all x2 -> x1, waiting for transfers between devices: 6.5 us -> 5.31 us  [to_all(): return lax.all_to_all(copies, axes, 0, 0, tiled=True)]
  transfers between devices with their start and end apart: 28 -> 29, of which waited for: 11 -> 16; matrix products, arithmetic and copies ran while one was open for 13% -> 8% of each run, Pallas kernels for 0% -> 0%
where the time goes in v3:
time: 214 us; the launch traced here: 212 us
  starting transfers between devices  128 us (60%)
  waiting for transfers between devices  39.1 us (18%)
  blocking collectives  15.6 us (7%)
  other arithmetic  12.3 us (6%)
  local copies, waits for them, and re-layouts  7.85 us (4%)
  matrix products  7.63 us (4%)
    ppermute x26, starting transfers between devices, shift(): lax.ppermute(values, axis, [(i, (i + by) % size) for i in range(size)])  106 us
    ppermute x26, waiting for transfers between devices, shift(): lax.ppermute(values, axis, [(i, (i + by) % size) for i in range(size)])  30.6 us
    all_gather x1, blocking collectives, shards(): lax.all_gather(jnp.concatenate([patches, out_grad], axis=1), 'zl', axis=0...  15.6 us
    all_to_all x1, starting transfers between devices, to_all(): return lax.all_to_all(copies, axes, 0, 0, tiled=True)  12.9 us
    all_to_all x2, starting transfers between devices, scatter(): back = lax.all_to_all(parts, axis, 0, 0, tiled=True)  9.3 us
    all_to_all x1, waiting for transfers between devices, to_all(): return lax.all_to_all(copies, axes, 0, 0, tiled=True)  5.31 us
    add x3, other arithmetic, add(): total = total + term.astype(F32)  4.66 us
    dot_general x2, matrix products, contract_tokens(): lax.dot_general(left, right, (((0,), (0,)), ((), ())), preferred_element_...  4.49 us
  transfers between devices with their start and end apart: 29, of which 16 were waited for; matrix products, arithmetic and copies ran while one was open for 8% of the time, Pallas kernels for 0%

profile of v3, /device:TPU:1, one launch (start us, length us, event | category | flops | bytes accessed | tf_op | source)
XLA Modules:
  0.0 212.3 jit_solution(5576557734883303703)
XLA Ops:
  1.5 15.6 %all_gather.3 = bf16[192,768]{1,0:T(8,128)(2,1)S(1)} all-gather(bf16[48,768]{1,0:T(8,128)(2,1)S(1)} %pad_maximum_fusion.9), channel_id=1, replica_groups=mesh['dp'=2,'y'=8,'zh'=2,'x'=4,'zl'=4] {'zl'}, dimensions={0}, use_global_device_ids=true | all-gather | bytes 368640 | tf_op jit(solution)/shard_map/all_gather | solution.py:115
  17.3 1.3 multiply_reduce_fusion.1
  19.3 12.9 %all-to-all-start = ((f32[16,1,1152]{2,1,0:T(1,128)}), f32[16,1,1152]{2,1,0:T(1,128)S(1)}, u32[]{:S(2)}, u32[]{:S(2)}) async-start(f32[16,1,1152]{2,1,0:T(1,128)} %broadcast_in_dim.53), calls=%async_computation | async-start | bytes 147456 | tf_op jit(solution)/shard_map/all_to_all | solution.py:44
  32.3 3.1 %collective-permute-start = (bf16[192,384]{1,0:T(8,128)(2,1)S(1)}, bf16[192,384]{1,0:T(8,128)(2,1)S(1)}, u32[]{:S(2)}, u32[]{:S(2)}) collective-permute-start(bf16[192,384]{1,0:T(8,128)(2,1)S(1)} %get-tuple-element.54), channel_id=1, source_target_pairs={{0,4},{4,8},{8,12},{12,0},{1,5},{5,9},{9,13},{13,1},{2,6},{6,10},{... | collective-permute-start | bytes 442376 | tf_op jit(solution)/shard_map/ppermute | solution.py:27
  35.4 3.4 %collective-permute-start.1 = (bf16[192,384]{1,0:T(8,128)(2,1)S(1)}, bf16[192,384]{1,0:T(8,128)(2,1)S(1)}, u32[]{:S(2)}, u32[]{:S(2)}) collective-permute-start(bf16[192,384]{1,0:T(8,128)(2,1)S(1)} %get-tuple-element.54), channel_id=1, source_target_pairs={{0,12},{4,0},{8,4},{12,8},{1,13},{5,1},{9,5},{13,9},{2,14},{6,2},{... | collective-permute-start | bytes 442376 | tf_op jit(solution)/shard_map/ppermute | solution.py:27
  38.8 5.3 %all-to-all-done = f32[16,1,1152]{2,1,0:T(1,128)S(1)} async-done(((f32[16,1,1152]{2,1,0:T(1,128)}), f32[16,1,1152]{2,1,0:T(1,128)S(1)}, u32[]{:S(2)}, u32[]{:S(2)}) %all-to-all-start) | async-done | bytes 73760 | tf_op jit(solution)/shard_map/all_to_all | solution.py:44
  44.5 3.1 %collective-permute-start.2 = (bf16[288,384]{1,0:T(8,128)(2,1)S(1)}, bf16[288,384]{1,0:T(8,128)(2,1)S(1)}, u32[]{:S(2)}, u32[]{:S(2)}) collective-permute-start(bf16[288,384]{1,0:T(8,128)(2,1)S(1)} %get-tuple-element.64), channel_id=1, source_target_pairs={{0,4},{4,8},{8,12},{12,0},{1,5},{5,9},{9,13},{13,1},{2,6},{6,10},{... | collective-permute-start | bytes 663560 | tf_op jit(solution)/shard_map/ppermute | solution.py:27
  47.7 3.4 %collective-permute-start.3 = (bf16[288,384]{1,0:T(8,128)(2,1)S(1)}, bf16[288,384]{1,0:T(8,128)(2,1)S(1)}, u32[]{:S(2)}, u32[]{:S(2)}) collective-permute-start(bf16[288,384]{1,0:T(8,128)(2,1)S(1)} %get-tuple-element.65), channel_id=1, source_target_pairs={{0,12},{4,0},{8,4},{12,8},{1,13},{5,1},{9,5},{13,9},{2,14},{6,2},{... | collective-permute-start | bytes 663560 | tf_op jit(solution)/shard_map/ppermute | solution.py:27
  51.2 1.2 collective-permute-done.2
  52.4 1.9 collective-permute-start.4
  54.6 4.3 %collective-permute-start.5 = (bf16[96,384]{1,0:T(8,128)(2,1)S(1)}, bf16[96,384]{1,0:T(8,128)(2,1)S(1)}, u32[]{:S(2)}, u32[]{:S(2)}) collective-permute-start(bf16[96,384]{1,0:T(8,128)(2,1)S(1)} %get-tuple-element.58), channel_id=1, source_target_pairs={{0,12},{4,0},{8,4},{12,8},{1,13},{5,1},{9,5},{13,9},{2,14},{6,2},{... | collective-permute-start | bytes 221192 | tf_op jit(solution)/shard_map/ppermute | solution.py:27
  61.9 2.0 collective-permute-start.6
  63.9 4.5 %collective-permute-start.10 = (bf16[48,1536]{1,0:T(8,128)(2,1)S(1)}, bf16[48,1536]{1,0:T(8,128)(2,1)S(1)}, u32[]{:S(2)}, u32[]{:S(2)}) collective-permute-start(bf16[48,1536]{1,0:T(8,128)(2,1)S(1)} %get-tuple-element.53), channel_id=1, source_target_pairs={{0,224},{32,0},{64,32},{96,64},{128,96},{160,128},{192,160},{224,1... | collective-permute-start | bytes 442376 | tf_op jit(solution)/shard_map/ppermute | solution.py:27
  69.1 1.9 collective-permute-start.7
  71.1 4.6 %collective-permute-start.11 = (bf16[96,1536]{1,0:T(8,128)(2,1)S(1)}, bf16[96,1536]{1,0:T(8,128)(2,1)S(1)}, u32[]{:S(2)}, u32[]{:S(2)}) collective-permute-start(bf16[96,1536]{1,0:T(8,128)(2,1)S(1)} %pad_maximum_fusion.4), channel_id=1, source_target_pairs={{0,224},{32,0},{64,32},{96,64},{128,96},{160,128},{192,160},{224,1... | collective-permute-start | bytes 884744 | tf_op jit(solution)/shard_map/ppermute | solution.py:27
  75.7 2.3 %collective-permute-done.7 = bf16[96,1536]{1,0:T(8,128)(2,1)S(1)} collective-permute-done((bf16[96,1536]{1,0:T(8,128)(2,1)S(1)}, bf16[96,1536]{1,0:T(8,128)(2,1)S(1)}, u32[]{:S(2)}, u32[]{:S(2)}) %collective-permute-start.7) | collective-permute-done | bytes 294944 | tf_op jit(solution)/shard_map/ppermute | solution.py:27
  78.1 1.9 collective-permute-start.8
  80.1 4.8 %collective-permute-start.12 = (bf16[96,1536]{1,0:T(8,128)(2,1)S(1)}, bf16[96,1536]{1,0:T(8,128)(2,1)S(1)}, u32[]{:S(2)}, u32[]{:S(2)}) collective-permute-start(bf16[96,1536]{1,0:T(8,128)(2,1)S(1)} %add_convert_fusion.2), channel_id=1, source_target_pairs={{0,224},{32,0},{64,32},{96,64},{128,96},{160,128},{192,160},{224,1... | collective-permute-start | bytes 884744 | tf_op jit(solution)/shard_map/ppermute | solution.py:27
  84.9 3.2 %collective-permute-done.8 = bf16[96,1536]{1,0:T(8,128)(2,1)S(1)} collective-permute-done((bf16[96,1536]{1,0:T(8,128)(2,1)S(1)}, bf16[96,1536]{1,0:T(8,128)(2,1)S(1)}, u32[]{:S(2)}, u32[]{:S(2)}) %collective-permute-start.8) | collective-permute-done | bytes 294944 | tf_op jit(solution)/shard_map/ppermute | solution.py:27
  88.2 1.9 collective-permute-start.9
  90.2 5.0 %collective-permute-start.13 = (bf16[96,1536]{1,0:T(8,128)(2,1)S(1)}, bf16[96,1536]{1,0:T(8,128)(2,1)S(1)}, u32[]{:S(2)}, u32[]{:S(2)}) collective-permute-start(bf16[96,1536]{1,0:T(8,128)(2,1)S(1)} %add_convert_fusion.1), channel_id=1, source_target_pairs={{0,224},{32,0},{64,32},{96,64},{128,96},{160,128},{192,160},{224,1... | collective-permute-start | bytes 884744 | tf_op jit(solution)/shard_map/ppermute | solution.py:27
  95.2 4.1 %collective-permute-done.9 = bf16[96,1536]{1,0:T(8,128)(2,1)S(1)} collective-permute-done((bf16[96,1536]{1,0:T(8,128)(2,1)S(1)}, bf16[96,1536]{1,0:T(8,128)(2,1)S(1)}, u32[]{:S(2)}, u32[]{:S(2)}) %collective-permute-start.9) | collective-permute-done | bytes 294944 | tf_op jit(solution)/shard_map/ppermute | solution.py:27
  99.3 2.2 %collective-permute-done.13 = bf16[96,1536]{1,0:T(8,128)(2,1)S(1)} collective-permute-done((bf16[96,1536]{1,0:T(8,128)(2,1)S(1)}, bf16[96,1536]{1,0:T(8,128)(2,1)S(1)}, u32[]{:S(2)}, u32[]{:S(2)}) %collective-permute-start.13) | collective-permute-done | bytes 294944 | tf_op jit(solution)/shard_map/ppermute | solution.py:27
  101.6 5.6 %collective-permute-start.14 = (bf16[96,1536]{1,0:T(8,128)(2,1)S(1)}, bf16[96,1536]{1,0:T(8,128)(2,1)S(1)}, u32[]{:S(2)}, u32[]{:S(2)}) collective-permute-start(bf16[96,1536]{1,0:T(8,128)(2,1)S(1)} %add_convert_fusion), channel_id=1, source_target_pairs={{0,16},{16,0},{1,17},{17,1},{2,18},{18,2},{3,19},{19,3},{4,20},{20... | collective-permute-start | bytes 884744 | tf_op jit(solution)/shard_map/ppermute | solution.py:27
  107.2 9.0 %collective-permute-done.14 = bf16[96,1536]{1,0:T(8,128)(2,1)S(1)} collective-permute-done((bf16[96,1536]{1,0:T(8,128)(2,1)S(1)}, bf16[96,1536]{1,0:T(8,128)(2,1)S(1)}, u32[]{:S(2)}, u32[]{:S(2)}) %collective-permute-start.14) | collective-permute-done | bytes 294944 | tf_op jit(solution)/shard_map/ppermute | solution.py:27
  118.0 1.9 collective-permute-start.15
  120.0 5.0 %collective-permute-start.16 = (bf16[96,1664]{1,0:T(8,128)(2,1)S(1)}, bf16[96,1664]{1,0:T(8,128)(2,1)}, u32[]{:S(2)}, u32[]{:S(2)}) collective-permute-start(bf16[96,1664]{1,0:T(8,128)(2,1)S(1)} %pad_maximum_fusion.3), channel_id=1, source_target_pairs={{0,224},{32,0},{64,32},{96,64},{128,96},{160,128},{192,160},{224,1... | collective-permute-start | bytes 958472 | tf_op jit(solution)/shard_map/ppermute | solution.py:27
  125.1 2.4 %collective-permute-done.15 = bf16[96,1664]{1,0:T(8,128)(2,1)} collective-permute-done((bf16[96,1664]{1,0:T(8,128)(2,1)S(1)}, bf16[96,1664]{1,0:T(8,128)(2,1)}, u32[]{:S(2)}, u32[]{:S(2)}) %collective-permute-start.15) | collective-permute-done | bytes 319520 | tf_op jit(solution)/shard_map/ppermute | solution.py:27
  127.5 1.9 collective-permute-start.17
  129.4 4.6 %collective-permute-start.18 = (bf16[96,1664]{1,0:T(8,128)(2,1)}, bf16[96,1664]{1,0:T(8,128)(2,1)S(1)}, u32[]{:S(2)}, u32[]{:S(2)}) collective-permute-start(bf16[96,1664]{1,0:T(8,128)(2,1)} %collective-permute-done.16), channel_id=1, source_target_pairs={{0,224},{32,0},{64,32},{96,64},{128,96},{160,128},{192,160},{224,1... | collective-permute-start | bytes 958472 | tf_op jit(solution)/shard_map/ppermute | solution.py:27
  134.0 1.0 slice_dynamic-update-slice_fusion.11
  138.2 1.9 collective-permute-start.19
  140.1 4.6 %collective-permute-start.20 = (bf16[96,1664]{1,0:T(8,128)(2,1)S(1)}, bf16[96,1664]{1,0:T(8,128)(2,1)S(1)}, u32[]{:S(2)}, u32[]{:S(2)}) collective-permute-start(bf16[96,1664]{1,0:T(8,128)(2,1)S(1)} %collective-permute-done.18), channel_id=1, source_target_pairs={{0,224},{32,0},{64,32},{96,64},{128,96},{160,128},{192,160},{224,1... | collective-permute-start | bytes 958472 | tf_op jit(solution)/shard_map/ppermute | solution.py:27
  144.8 2.3 %collective-permute-done.19 = bf16[96,1664]{1,0:T(8,128)(2,1)S(1)} collective-permute-done((bf16[96,1664]{1,0:T(8,128)(2,1)S(1)}, bf16[96,1664]{1,0:T(8,128)(2,1)S(1)}, u32[]{:S(2)}, u32[]{:S(2)}) %collective-permute-start.19) | collective-permute-done | bytes 319520 | tf_op jit(solution)/shard_map/ppermute | solution.py:27
  147.1 1.9 collective-permute-start.21
  149.1 4.6 %collective-permute-start.22 = (bf16[48,1664]{1,0:T(8,128)(2,1)S(1)}, bf16[48,1664]{1,0:T(8,128)(2,1)S(1)}, u32[]{:S(2)}, u32[]{:S(2)}) collective-permute-start(bf16[48,1664]{1,0:T(8,128)(2,1)S(1)} %slice.262), channel_id=1, source_target_pairs={{0,224},{32,0},{64,32},{96,64},{128,96},{160,128},{192,160},{224,1... | collective-permute-start | bytes 479240 | tf_op jit(solution)/shard_map/ppermute | solution.py:27
  154.4 1.5 collective-permute-done.22
  157.9 1.2 pad_maximum_fusion
  159.1 5.2 %all-to-all-start.1 = ((bf16[4,200,896]{2,1,0:T(8,128)(2,1)}), bf16[4,200,896]{2,1,0:T(8,128)(2,1)S(1)}, u32[]{:S(2)}, u32[]{:S(2)}) async-start(bf16[4,200,896]{2,1,0:T(8,128)(2,1)} %pad_maximum_fusion), calls=%async_computation.1 | async-start | bytes 2867200 | tf_op jit(solution)/shard_map/all_to_all | solution.py:104
  164.3 3.0 %convolution_convert_fusion.2 = bf16[768,384]{1,0:T(8,128)(2,1)} fusion(bf16[768,768]{1,0:T(8,128)(2,1)} %copy-done.4, bf16[768,384]{1,0:T(8,128)(2,1)S(1)} %maximum_dynamic-update-slice_fusion.1), kind=kOutput, calls=%fused_computation.5 | convolution fusion | flops 453279744 | bytes 2359296 | tf_op jit(solution)/shard_map/dot_general | solution.py:15
  167.3 18.4 %collective-permute-start.24 = (bf16[768,384]{1,0:T(8,128)(2,1)}, bf16[768,384]{1,0:T(8,128)(2,1)}, u32[]{:S(2)}, u32[]{:S(2)}) collective-permute-start(bf16[768,384]{1,0:T(8,128)(2,1)} %convolution_convert_fusion.2), channel_id=1, source_target_pairs={{0,256},{256,0},{1,257},{257,1},{2,258},{258,2},{3,259},{259,3},{4... | collective-permute-start | bytes 1769480 | tf_op jit(solution)/shard_map/ppermute | solution.py:27
  185.7 1.5 convolution_convert_fusion.3
  187.2 1.9 collective-permute-start.23
  190.2 4.1 %all-to-all-start.2 = ((bf16[4,56,896]{2,1,0:T(8,128)(2,1)}), bf16[4,56,896]{2,1,0:T(8,128)(2,1)S(1)}, u32[]{:S(2)}, u32[]{:S(2)}) async-start(bf16[4,56,896]{2,1,0:T(8,128)(2,1)} %pad_maximum_fusion.2), calls=%async_computation.2 | async-start | bytes 802816 | tf_op jit(solution)/shard_map/all_to_all | solution.py:104
  194.4 2.4 %convert_add_fusion = f32[768,384]{1,0:T(8,128)} fusion(bf16[768,384]{1,0:T(8,128)(2,1)} %collective-permute-done.24, bf16[768,384]{1,0:T(8,128)(2,1)} %convolution_convert_fusion.2), kind=kLoop, calls=%fused_computation.8 | loop fusion | flops 884736 | bytes 2359296 | tf_op jit(solution)/shard_map/add | solution.py:37
  196.8 2.2 %convert_add_fusion.1 = f32[384,768]{1,0:T(8,128)} fusion(bf16[384,768]{1,0:T(8,128)(2,1)S(1)} %collective-permute-done.23, bf16[384,768]{1,0:T(8,128)(2,1)} %convolution_convert_fusion.3), kind=kLoop, calls=%fused_computation.9 | loop fusion | flops 884736 | bytes 2359296 | tf_op jit(solution)/shard_map/add | solution.py:37
  199.0 3.1 %all-to-all-done.2 = bf16[4,56,896]{2,1,0:T(8,128)(2,1)S(1)} async-done(((bf16[4,56,896]{2,1,0:T(8,128)(2,1)}), bf16[4,56,896]{2,1,0:T(8,128)(2,1)S(1)}, u32[]{:S(2)}, u32[]{:S(2)}) %all-to-all-start.2) | async-done | bytes 401440 | tf_op jit(solution)/shard_map/all_to_all | solution.py:104
  202.2 8.0 %collective-permute-start.25 = (f32[384]{0:T(512)S(1)}, f32[384]{0:T(512)S(1)}, u32[]{:S(2)}, u32[]{:S(2)}) collective-permute-start(f32[384]{0:T(512)S(1)} %slice_add_fusion), channel_id=1, source_target_pairs={{0,256},{256,0},{1,257},{257,1},{2,258},{258,2},{3,259},{259,3},{4... | collective-permute-start | bytes 4616 | tf_op jit(solution)/shard_map/ppermute | solution.py:27
  (125 shorter events, 17.6 us)
Async XLA Ops:
  0.6 58.4 %copy-start = (bf16[768,384]{1,0:T(8,128)(2,1)S(1)}, bf16[768,384]{1,0:T(8,128)(2,1)}, u32[]{:S(2)}) copy-start(bf16[768,384]{1,0:T(8,128)(2,1)} %param.8) | copy-start | bytes 1769476
  17.1 27.2 %copy-start.7 = (f32[384]{0:T(512)S(1)}, f32[384]{0:T(512)}, u32[]{:S(2)}) copy-start(f32[384]{0:T(512)} %param.6) | copy-start | bytes 4612
  19.3 24.8 %all-to-all-start = ((f32[16,1,1152]{2,1,0:T(1,128)}), f32[16,1,1152]{2,1,0:T(1,128)S(1)}, u32[]{:S(2)}, u32[]{:S(2)}) async-start(f32[16,1,1152]{2,1,0:T(1,128)} %broadcast_in_dim.53), calls=%async_computation | async-start | bytes 147456 | tf_op jit(solution)/shard_map/all_to_all | solution.py:44
  32.3 12.1 %collective-permute-start = (bf16[192,384]{1,0:T(8,128)(2,1)S(1)}, bf16[192,384]{1,0:T(8,128)(2,1)S(1)}, u32[]{:S(2)}, u32[]{:S(2)}) collective-permute-start(bf16[192,384]{1,0:T(8,128)(2,1)S(1)} %get-tuple-element.54), channel_id=1, source_target_pairs={{0,4},{4,8},{8,12},{12,0},{1,5},{5,9},{9,13},{13,1},{2,6},{6,10},{... | collective-permute-start | bytes 442376 | tf_op jit(solution)/shard_map/ppermute | solution.py:27
  35.4 9.0 %collective-permute-start.1 = (bf16[192,384]{1,0:T(8,128)(2,1)S(1)}, bf16[192,384]{1,0:T(8,128)(2,1)S(1)}, u32[]{:S(2)}, u32[]{:S(2)}) collective-permute-start(bf16[192,384]{1,0:T(8,128)(2,1)S(1)} %get-tuple-element.54), channel_id=1, source_target_pairs={{0,12},{4,0},{8,4},{12,8},{1,13},{5,1},{9,5},{13,9},{2,14},{6,2},{... | collective-permute-start | bytes 442376 | tf_op jit(solution)/shard_map/ppermute | solution.py:27
  44.5 7.9 %collective-permute-start.2 = (bf16[288,384]{1,0:T(8,128)(2,1)S(1)}, bf16[288,384]{1,0:T(8,128)(2,1)S(1)}, u32[]{:S(2)}, u32[]{:S(2)}) collective-permute-start(bf16[288,384]{1,0:T(8,128)(2,1)S(1)} %get-tuple-element.64), channel_id=1, source_target_pairs={{0,4},{4,8},{8,12},{12,0},{1,5},{5,9},{9,13},{13,1},{2,6},{6,10},{... | collective-permute-start | bytes 663560 | tf_op jit(solution)/shard_map/ppermute | solution.py:27
  47.7 7.0 %collective-permute-start.3 = (bf16[288,384]{1,0:T(8,128)(2,1)S(1)}, bf16[288,384]{1,0:T(8,128)(2,1)S(1)}, u32[]{:S(2)}, u32[]{:S(2)}) collective-permute-start(bf16[288,384]{1,0:T(8,128)(2,1)S(1)} %get-tuple-element.65), channel_id=1, source_target_pairs={{0,12},{4,0},{8,4},{12,8},{1,13},{5,1},{9,5},{13,9},{2,14},{6,2},{... | collective-permute-start | bytes 663560 | tf_op jit(solution)/shard_map/ppermute | solution.py:27
  52.4 7.6 %collective-permute-start.4 = (bf16[96,384]{1,0:T(8,128)(2,1)S(1)}, bf16[96,384]{1,0:T(8,128)(2,1)S(1)}, u32[]{:S(2)}, u32[]{:S(2)}) collective-permute-start(bf16[96,384]{1,0:T(8,128)(2,1)S(1)} %get-tuple-element.56), channel_id=1, source_target_pairs={{0,4},{4,8},{8,12},{12,0},{1,5},{5,9},{9,13},{13,1},{2,6},{6,10},{... | collective-permute-start | bytes 221192 | tf_op jit(solution)/shard_map/ppermute | solution.py:27
  54.6 5.7 %collective-permute-start.5 = (bf16[96,384]{1,0:T(8,128)(2,1)S(1)}, bf16[96,384]{1,0:T(8,128)(2,1)S(1)}, u32[]{:S(2)}, u32[]{:S(2)}) collective-permute-start(bf16[96,384]{1,0:T(8,128)(2,1)S(1)} %get-tuple-element.58), channel_id=1, source_target_pairs={{0,12},{4,0},{8,4},{12,8},{1,13},{5,1},{9,5},{13,9},{2,14},{6,2},{... | collective-permute-start | bytes 221192 | tf_op jit(solution)/shard_map/ppermute | solution.py:27
  59.9 1.1 copy-start.1
  61.9 7.1 %collective-permute-start.6 = (bf16[48,1536]{1,0:T(8,128)(2,1)S(1)}, bf16[48,1536]{1,0:T(8,128)(2,1)S(1)}, u32[]{:S(2)}, u32[]{:S(2)}) collective-permute-start(bf16[48,1536]{1,0:T(8,128)(2,1)S(1)} %get-tuple-element.52), channel_id=1, source_target_pairs={{0,32},{32,64},{64,96},{96,128},{128,160},{160,192},{192,224},{224... | collective-permute-start | bytes 442376 | tf_op jit(solution)/shard_map/ppermute | solution.py:27
  63.9 7.1 %collective-permute-start.10 = (bf16[48,1536]{1,0:T(8,128)(2,1)S(1)}, bf16[48,1536]{1,0:T(8,128)(2,1)S(1)}, u32[]{:S(2)}, u32[]{:S(2)}) collective-permute-start(bf16[48,1536]{1,0:T(8,128)(2,1)S(1)} %get-tuple-element.53), channel_id=1, source_target_pairs={{0,224},{32,0},{64,32},{96,64},{128,96},{160,128},{192,160},{224,1... | collective-permute-start | bytes 442376 | tf_op jit(solution)/shard_map/ppermute | solution.py:27
  69.1 8.9 %collective-permute-start.7 = (bf16[96,1536]{1,0:T(8,128)(2,1)S(1)}, bf16[96,1536]{1,0:T(8,128)(2,1)S(1)}, u32[]{:S(2)}, u32[]{:S(2)}) collective-permute-start(bf16[96,1536]{1,0:T(8,128)(2,1)S(1)} %fusion.14), channel_id=1, source_target_pairs={{0,32},{32,64},{64,96},{96,128},{128,160},{160,192},{192,224},{224... | collective-permute-start | bytes 884744 | tf_op jit(solution)/shard_map/ppermute | solution.py:27
  71.1 8.9 %collective-permute-start.11 = (bf16[96,1536]{1,0:T(8,128)(2,1)S(1)}, bf16[96,1536]{1,0:T(8,128)(2,1)S(1)}, u32[]{:S(2)}, u32[]{:S(2)}) collective-permute-start(bf16[96,1536]{1,0:T(8,128)(2,1)S(1)} %pad_maximum_fusion.4), channel_id=1, source_target_pairs={{0,224},{32,0},{64,32},{96,64},{128,96},{160,128},{192,160},{224,1... | collective-permute-start | bytes 884744 | tf_op jit(solution)/shard_map/ppermute | solution.py:27
  78.1 10.0 %collective-permute-start.8 = (bf16[96,1536]{1,0:T(8,128)(2,1)S(1)}, bf16[96,1536]{1,0:T(8,128)(2,1)S(1)}, u32[]{:S(2)}, u32[]{:S(2)}) collective-permute-start(bf16[96,1536]{1,0:T(8,128)(2,1)S(1)} %add_convert_fusion.4), channel_id=1, source_target_pairs={{0,32},{32,64},{64,96},{96,128},{128,160},{160,192},{192,224},{224... | collective-permute-start | bytes 884744 | tf_op jit(solution)/shard_map/ppermute | solution.py:27
  80.1 10.0 %collective-permute-start.12 = (bf16[96,1536]{1,0:T(8,128)(2,1)S(1)}, bf16[96,1536]{1,0:T(8,128)(2,1)S(1)}, u32[]{:S(2)}, u32[]{:S(2)}) collective-permute-start(bf16[96,1536]{1,0:T(8,128)(2,1)S(1)} %add_convert_fusion.2), channel_id=1, source_target_pairs={{0,224},{32,0},{64,32},{96,64},{128,96},{160,128},{192,160},{224,1... | collective-permute-start | bytes 884744 | tf_op jit(solution)/shard_map/ppermute | solution.py:27
  88.2 11.1 %collective-permute-start.9 = (bf16[96,1536]{1,0:T(8,128)(2,1)S(1)}, bf16[96,1536]{1,0:T(8,128)(2,1)S(1)}, u32[]{:S(2)}, u32[]{:S(2)}) collective-permute-start(bf16[96,1536]{1,0:T(8,128)(2,1)S(1)} %add_convert_fusion.3), channel_id=1, source_target_pairs={{0,32},{32,64},{64,96},{96,128},{128,160},{160,192},{192,224},{224... | collective-permute-start | bytes 884744 | tf_op jit(solution)/shard_map/ppermute | solution.py:27
  90.2 11.3 %collective-permute-start.13 = (bf16[96,1536]{1,0:T(8,128)(2,1)S(1)}, bf16[96,1536]{1,0:T(8,128)(2,1)S(1)}, u32[]{:S(2)}, u32[]{:S(2)}) collective-permute-start(bf16[96,1536]{1,0:T(8,128)(2,1)S(1)} %add_convert_fusion.1), channel_id=1, source_target_pairs={{0,224},{32,0},{64,32},{96,64},{128,96},{160,128},{192,160},{224,1... | collective-permute-start | bytes 884744 | tf_op jit(solution)/shard_map/ppermute | solution.py:27
  101.6 14.6 %collective-permute-start.14 = (bf16[96,1536]{1,0:T(8,128)(2,1)S(1)}, bf16[96,1536]{1,0:T(8,128)(2,1)S(1)}, u32[]{:S(2)}, u32[]{:S(2)}) collective-permute-start(bf16[96,1536]{1,0:T(8,128)(2,1)S(1)} %add_convert_fusion), channel_id=1, source_target_pairs={{0,16},{16,0},{1,17},{17,1},{2,18},{18,2},{3,19},{19,3},{4,20},{20... | collective-permute-start | bytes 884744 | tf_op jit(solution)/shard_map/ppermute | solution.py:27
  116.8 1.0 copy-start.2
  118.0 9.5 %collective-permute-start.15 = (bf16[96,1664]{1,0:T(8,128)(2,1)S(1)}, bf16[96,1664]{1,0:T(8,128)(2,1)}, u32[]{:S(2)}, u32[]{:S(2)}) collective-permute-start(bf16[96,1664]{1,0:T(8,128)(2,1)S(1)} %pad_maximum_fusion.3), channel_id=1, source_target_pairs={{0,32},{32,64},{64,96},{96,128},{128,160},{160,192},{192,224},{224... | collective-permute-start | bytes 958472 | tf_op jit(solution)/shard_map/ppermute | solution.py:27
  120.0 9.5 %collective-permute-start.16 = (bf16[96,1664]{1,0:T(8,128)(2,1)S(1)}, bf16[96,1664]{1,0:T(8,128)(2,1)}, u32[]{:S(2)}, u32[]{:S(2)}) collective-permute-start(bf16[96,1664]{1,0:T(8,128)(2,1)S(1)} %pad_maximum_fusion.3), channel_id=1, source_target_pairs={{0,224},{32,0},{64,32},{96,64},{128,96},{160,128},{192,160},{224,1... | collective-permute-start | bytes 958472 | tf_op jit(solution)/shard_map/ppermute | solution.py:27
  125.0 9.0 %copy-start.3 = (bf16[768,768]{1,0:T(8,128)(2,1)S(1)}, bf16[768,768]{1,0:T(8,128)(2,1)}, u32[]{:S(2)}) copy-start(bf16[768,768]{1,0:T(8,128)(2,1)} %copy-done.2) | copy-start | bytes 3538948
  127.5 10.7 %collective-permute-start.17 = (bf16[96,1664]{1,0:T(8,128)(2,1)}, bf16[96,1664]{1,0:T(8,128)(2,1)S(1)}, u32[]{:S(2)}, u32[]{:S(2)}) collective-permute-start(bf16[96,1664]{1,0:T(8,128)(2,1)} %collective-permute-done.15), channel_id=1, source_target_pairs={{0,32},{32,64},{64,96},{96,128},{128,160},{160,192},{192,224},{224... | collective-permute-start | bytes 958472 | tf_op jit(solution)/shard_map/ppermute | solution.py:27
  129.4 10.7 %collective-permute-start.18 = (bf16[96,1664]{1,0:T(8,128)(2,1)}, bf16[96,1664]{1,0:T(8,128)(2,1)S(1)}, u32[]{:S(2)}, u32[]{:S(2)}) collective-permute-start(bf16[96,1664]{1,0:T(8,128)(2,1)} %collective-permute-done.16), channel_id=1, source_target_pairs={{0,224},{32,0},{64,32},{96,64},{128,96},{160,128},{192,160},{224,1... | collective-permute-start | bytes 958472 | tf_op jit(solution)/shard_map/ppermute | solution.py:27
  138.2 8.9 %collective-permute-start.19 = (bf16[96,1664]{1,0:T(8,128)(2,1)S(1)}, bf16[96,1664]{1,0:T(8,128)(2,1)S(1)}, u32[]{:S(2)}, u32[]{:S(2)}) collective-permute-start(bf16[96,1664]{1,0:T(8,128)(2,1)S(1)} %collective-permute-done.17), channel_id=1, source_target_pairs={{0,32},{32,64},{64,96},{96,128},{128,160},{160,192},{192,224},{224... | collective-permute-start | bytes 958472 | tf_op jit(solution)/shard_map/ppermute | solution.py:27
  140.1 8.9 %collective-permute-start.20 = (bf16[96,1664]{1,0:T(8,128)(2,1)S(1)}, bf16[96,1664]{1,0:T(8,128)(2,1)S(1)}, u32[]{:S(2)}, u32[]{:S(2)}) collective-permute-start(bf16[96,1664]{1,0:T(8,128)(2,1)S(1)} %collective-permute-done.18), channel_id=1, source_target_pairs={{0,224},{32,0},{64,32},{96,64},{128,96},{160,128},{192,160},{224,1... | collective-permute-start | bytes 958472 | tf_op jit(solution)/shard_map/ppermute | solution.py:27
  147.1 7.2 %collective-permute-start.21 = (bf16[48,1664]{1,0:T(8,128)(2,1)S(1)}, bf16[48,1664]{1,0:T(8,128)(2,1)S(1)}, u32[]{:S(2)}, u32[]{:S(2)}) collective-permute-start(bf16[48,1664]{1,0:T(8,128)(2,1)S(1)} %slice.260), channel_id=1, source_target_pairs={{0,32},{32,64},{64,96},{96,128},{128,160},{160,192},{192,224},{224... | collective-permute-start | bytes 479240 | tf_op jit(solution)/shard_map/ppermute | solution.py:27
  149.1 6.8 %collective-permute-start.22 = (bf16[48,1664]{1,0:T(8,128)(2,1)S(1)}, bf16[48,1664]{1,0:T(8,128)(2,1)S(1)}, u32[]{:S(2)}, u32[]{:S(2)}) collective-permute-start(bf16[48,1664]{1,0:T(8,128)(2,1)S(1)} %slice.262), channel_id=1, source_target_pairs={{0,224},{32,0},{64,32},{96,64},{128,96},{160,128},{192,160},{224,1... | collective-permute-start | bytes 479240 | tf_op jit(solution)/shard_map/ppermute | solution.py:27
  155.9 1.0 copy-start.5
  155.9 1.9 copy-start.4
  159.1 30.0 %all-to-all-start.1 = ((bf16[4,200,896]{2,1,0:T(8,128)(2,1)}), bf16[4,200,896]{2,1,0:T(8,128)(2,1)S(1)}, u32[]{:S(2)}, u32[]{:S(2)}) async-start(bf16[4,200,896]{2,1,0:T(8,128)(2,1)} %pad_maximum_fusion), calls=%async_computation.1 | async-start | bytes 2867200 | tf_op jit(solution)/shard_map/all_to_all | solution.py:104
  164.3 21.4 %copy-start.6 = (bf16[768,768]{1,0:T(8,128)(2,1)S(1)}, bf16[768,768]{1,0:T(8,128)(2,1)}, u32[]{:S(2)}) copy-start(bf16[768,768]{1,0:T(8,128)(2,1)} %copy-done.5) | copy-start | bytes 3538948
  167.3 27.1 %collective-permute-start.24 = (bf16[768,384]{1,0:T(8,128)(2,1)}, bf16[768,384]{1,0:T(8,128)(2,1)}, u32[]{:S(2)}, u32[]{:S(2)}) collective-permute-start(bf16[768,384]{1,0:T(8,128)(2,1)} %convolution_convert_fusion.2), channel_id=1, source_target_pairs={{0,256},{256,0},{1,257},{257,1},{2,258},{258,2},{3,259},{259,3},{4... | collective-permute-start | bytes 1769480 | tf_op jit(solution)/shard_map/ppermute | solution.py:27
  187.2 9.6 %collective-permute-start.23 = (bf16[384,768]{1,0:T(8,128)(2,1)}, bf16[384,768]{1,0:T(8,128)(2,1)S(1)}, u32[]{:S(2)}, u32[]{:S(2)}) collective-permute-start(bf16[384,768]{1,0:T(8,128)(2,1)} %convolution_convert_fusion.3), channel_id=1, source_target_pairs={{0,256},{256,0},{1,257},{257,1},{2,258},{258,2},{3,259},{259,3},{4... | collective-permute-start | bytes 1769480 | tf_op jit(solution)/shard_map/ppermute | solution.py:27
  190.2 11.9 %all-to-all-start.2 = ((bf16[4,56,896]{2,1,0:T(8,128)(2,1)}), bf16[4,56,896]{2,1,0:T(8,128)(2,1)S(1)}, u32[]{:S(2)}, u32[]{:S(2)}) async-start(bf16[4,56,896]{2,1,0:T(8,128)(2,1)} %pad_maximum_fusion.2), calls=%async_computation.2 | async-start | bytes 802816 | tf_op jit(solution)/shard_map/all_to_all | solution.py:104
  202.2 9.5 %collective-permute-start.25 = (f32[384]{0:T(512)S(1)}, f32[384]{0:T(512)S(1)}, u32[]{:S(2)}, u32[]{:S(2)}) collective-permute-start(f32[384]{0:T(512)S(1)} %slice_add_fusion), channel_id=1, source_target_pairs={{0,256},{256,0},{1,257},{257,1},{2,258},{258,2},{3,259},{259,3},{4... | collective-permute-start | bytes 4616 | tf_op jit(solution)/shard_map/ppermute | solution.py:27

commit v4 on v3

--- a/solution.py
+++ b/solution.py
@@ -23,8 +23,19 @@
     )
 
 
+def swap(values, axis):
+    return lax.ppermute(values, axis, [(0, 1), (1, 0)])
+
+
 def shift(values, axis, size, by):
-    return lax.ppermute(values, axis, [(i, (i + by) % size) for i in range(size)])
+    pairs = [(i, (i + by) % size) for i in range(size)]
+    pairs += [(size + i, size + (i - by) % size) for i in range(size)]
+    return lax.ppermute(values, ("dp", axis), pairs)
+
+
+def places(axis, size):
+    me, way = lax.axis_index(axis) + size, 1 - 2 * lax.axis_index("dp")
+    return lambda by: (me + by * way) & (size - 1)
 
 
 def row_major(values):
@@ -50,10 +61,10 @@
 
 
 def scatter_y(part):
-    me = lax.axis_index("y")
+    place = places("y", Y)
 
     def at(by):
-        return part((me + (by + Y)) & (Y - 1))
+        return part(place(by))
 
     far = at(Y // 2)
     half = far.shape[0] // 2
@@ -69,7 +80,7 @@
 
 
 def gather_ring(blocks, axis, size):
-    me, rows = lax.axis_index(axis), blocks[0].shape[0]
+    place, rows = places(axis, size), blocks[0].shape[0]
     half = rows // 2
     panels = [jnp.zeros((size * rows, b.shape[1]), b.dtype) for b in blocks]
     edges = [0]
@@ -77,7 +88,7 @@
         edges.append(edges[-1] + b.shape[1])
 
     def put(panels, values, by, offset=0):
-        start = ((me + (by + size)) & (size - 1)) * rows + offset
+        start = place(by) * rows + offset
         return [
             lax.dynamic_update_slice(
                 panel, values[:, low:high], (start, 0), allow_negative_indices=False
@@ -136,14 +147,13 @@
         ((centred * norm_gain).astype(BF16), below, above)
     )
     half = count // 2
-    place = lax.axis_index("x")
+    place = places("x", X)
 
     def panel(own, below, above, far):
         whole = jnp.zeros((X * count, width), BF16)
         for by, block in ((0, own), (-1, below), (1, above), (2, far)):
-            start = ((place + (by + X)) & (X - 1)) * count
             whole = lax.dynamic_update_slice(
-                whole, block, (start, 0), allow_negative_indices=False
+                whole, block, (place(by) * count, 0), allow_negative_indices=False
             )
         return whole
 
@@ -177,7 +187,7 @@
         )
 
     half_sum = scatter_y(part).astype(BF16)
-    total = add(half_sum, shift(half_sum, "zh", ZH, 1))
+    total = add(half_sum, swap(half_sum, "zh"))
     pre, hid_grad = total[:, :hidden_width], total[:, hidden_width:]
     activation, slope = jax.vjp(jax.nn.gelu, pre)
     pre_grad = slope(hid_grad)[0].astype(BF16)
@@ -185,8 +195,8 @@
     second = jnp.sum(pre_grad.astype(F32) * pre, axis=1, keepdims=True)
     lane = lax.broadcasted_iota(jnp.int32, (rows, LANES), 1)
     shares = jnp.zeros((rows, LANES), BF16)
-    for place, term in enumerate(split_high_low(first) + split_high_low(second)):
-        shares = jnp.where(lane == place, term, shares)
+    for spot, term in enumerate(split_high_low(first) + split_high_low(second)):
+        shares = jnp.where(lane == spot, term, shares)
     hidden_panel, pre_grad_panel, shares = gather_ring(
         [activation.astype(BF16), pre_grad, shares], "y", Y
     )
@@ -204,12 +214,12 @@
     lane = lax.broadcasted_iota(jnp.int32, rest.shape, 1)
     first = jnp.sum(jnp.where(lane < 2, rest, 0), axis=1, keepdims=True) / model_width
     second = jnp.sum(jnp.where(lane >= 2, rest, 0), axis=1, keepdims=True) / model_width
-    grad_gain = (gain_sum + shift(gain_sum, "dp", 2, 1)) / norm_gain
+    grad_gain = (gain_sum + swap(gain_sum, "dp")) / norm_gain
     grad_patches = inverse * (normed_grad * norm_gain - first - centred * second)
     local_in = contract_tokens(normed_panel, pre_grad_panel).astype(BF16)
     local_out = contract_tokens(hidden_panel, cotangent).astype(BF16)
-    grad_w_in = add(local_in, shift(local_in, "dp", 2, 1))
-    grad_w_out = add(local_out, shift(local_out, "dp", 2, 1))
+    grad_w_in = add(local_in, swap(local_in, "dp"))
+    grad_w_out = add(local_out, swap(local_out, "dp"))
     return (branch, grad_patches.astype(BF16), grad_w_in, grad_w_out, grad_gain)
 
 

time: 214 us -> 217 us (1.014)
  waiting for transfers between devices: 39.1 us -> 48.4 us
  starting transfers between devices: 128 us -> 123 us
    ppermute x26, waiting for transfers between devices: 30.6 us -> 39.7 us  [the longest x22 35.5 us: shift(): return lax.ppermute(values, ('dp', axis), pairs)]
    ppermute x26, starting transfers between devices: 106 us -> 103 us  [the longest x22 69.4 us: shift(): return lax.ppermute(values, ('dp', axis), pairs)]
    all_to_all x2, starting transfers between devices: 9.3 us -> 7.01 us  [scatter(): back = lax.all_to_all(parts, axis, 0, 0, tiled=True)]
  transfers between devices with their start and end apart: 29 -> 29, of which waited for: 16 -> 15; matrix products, arithmetic and copies ran while one was open for 8% -> 8% of each run, Pallas kernels for 0% -> 0%
where the time goes in v4:
time: 217 us; the launch traced here: 216 us
  starting transfers between devices  123 us (57%)
  waiting for transfers between devices  48.4 us (22%)
  blocking collectives  15.6 us (7%)
  other arithmetic  12.3 us (6%)
  matrix products  7.63 us (4%)
  local copies, waits for them, and re-layouts  7.28 us (3%)
    ppermute x22, starting transfers between devices, shift(): return lax.ppermute(values, ('dp', axis), pairs)  69.4 us
    ppermute x22, waiting for transfers between devices, shift(): return lax.ppermute(values, ('dp', axis), pairs)  35.5 us
    ppermute x4, starting transfers between devices, swap(): return lax.ppermute(values, axis, [(0, 1), (1, 0)])  33.8 us
    all_gather x1, blocking collectives, shards(): lax.all_gather(jnp.concatenate([patches, out_grad], axis=1), 'zl', axis=0...  15.6 us
    all_to_all x1, starting transfers between devices, to_all(): return lax.all_to_all(copies, axes, 0, 0, tiled=True)  12.9 us
    all_to_all x2, starting transfers between devices, scatter(): back = lax.all_to_all(parts, axis, 0, 0, tiled=True)  7.01 us
    all_to_all x1, waiting for transfers between devices, to_all(): return lax.all_to_all(copies, axes, 0, 0, tiled=True)  5.48 us
    add x3, other arithmetic, add(): total = total + term.astype(F32)  4.66 us
  transfers between devices with their start and end apart: 29, of which 15 were waited for; matrix products, arithmetic and copies ran while one was open for 8% of the time, Pallas kernels for 0%

profile of v4, /device:TPU:1, one launch (start us, length us, event | category | flops | bytes accessed | tf_op | source)
XLA Modules:
  0.0 215.8 jit_solution(616629810116329142)
XLA Ops:
  1.5 15.6 %all_gather.3 = bf16[192,768]{1,0:T(8,128)(2,1)S(1)} all-gather(bf16[48,768]{1,0:T(8,128)(2,1)S(1)} %pad_maximum_fusion.9), channel_id=1, replica_groups=mesh['dp'=2,'y'=8,'zh'=2,'x'=4,'zl'=4] {'zl'}, dimensions={0}, use_global_device_ids=true | all-gather | bytes 368640 | tf_op jit(solution)/shard_map/all_gather | solution.py:126
  17.3 1.3 multiply_reduce_fusion.1
  19.3 12.9 %all-to-all-start = ((f32[16,1,1152]{2,1,0:T(1,128)}), f32[16,1,1152]{2,1,0:T(1,128)S(1)}, u32[]{:S(2)}, u32[]{:S(2)}) async-start(f32[16,1,1152]{2,1,0:T(1,128)} %broadcast_in_dim.53), calls=%async_computation | async-start | bytes 147456 | tf_op jit(solution)/shard_map/all_to_all | solution.py:55
  32.3 4.4 %collective-permute-start = (bf16[192,384]{1,0:T(8,128)(2,1)S(1)}, bf16[192,384]{1,0:T(8,128)(2,1)S(1)}, u32[]{:S(2)}, u32[]{:S(2)}) collective-permute-start(bf16[192,384]{1,0:T(8,128)(2,1)S(1)} %get-tuple-element.54), channel_id=1, source_target_pairs={{0,4},{4,8},{8,12},{12,0},{256,268},{260,256},{264,260},{268,264},... | collective-permute-start | bytes 442376 | tf_op jit(solution)/shard_map/ppermute | solution.py:33
  36.7 1.9 collective-permute-start.1
  38.7 5.5 %all-to-all-done = f32[16,1,1152]{2,1,0:T(1,128)S(1)} async-done(((f32[16,1,1152]{2,1,0:T(1,128)}), f32[16,1,1152]{2,1,0:T(1,128)S(1)}, u32[]{:S(2)}, u32[]{:S(2)}) %all-to-all-start) | async-done | bytes 73760 | tf_op jit(solution)/shard_map/all_to_all | solution.py:55
  44.5 4.4 %collective-permute-start.2 = (bf16[288,384]{1,0:T(8,128)(2,1)S(1)}, bf16[288,384]{1,0:T(8,128)(2,1)S(1)}, u32[]{:S(2)}, u32[]{:S(2)}) collective-permute-start(bf16[288,384]{1,0:T(8,128)(2,1)S(1)} %get-tuple-element.64), channel_id=1, source_target_pairs={{0,4},{4,8},{8,12},{12,0},{256,268},{260,256},{264,260},{268,264},... | collective-permute-start | bytes 663560 | tf_op jit(solution)/shard_map/ppermute | solution.py:33
  48.9 1.9 collective-permute-start.3
  51.8 5.0 %collective-permute-start.4 = (bf16[96,384]{1,0:T(8,128)(2,1)S(1)}, bf16[96,384]{1,0:T(8,128)(2,1)S(1)}, u32[]{:S(2)}, u32[]{:S(2)}) collective-permute-start(bf16[96,384]{1,0:T(8,128)(2,1)S(1)} %get-tuple-element.56), channel_id=1, source_target_pairs={{0,4},{4,8},{8,12},{12,0},{256,268},{260,256},{264,260},{268,264},... | collective-permute-start | bytes 221192 | tf_op jit(solution)/shard_map/ppermute | solution.py:33
  56.8 2.1 collective-permute-done.3
  59.0 1.9 collective-permute-start.5
  62.0 3.3 %collective-permute-done.5 = bf16[96,384]{1,0:T(8,128)(2,1)S(1)} collective-permute-done((bf16[96,384]{1,0:T(8,128)(2,1)S(1)}, bf16[96,384]{1,0:T(8,128)(2,1)S(1)}, u32[]{:S(2)}, u32[]{:S(2)}) %collective-permute-start.5) | collective-permute-done | bytes 73760 | tf_op jit(solution)/shard_map/ppermute | solution.py:33
  66.2 2.1 collective-permute-start.6
  68.3 3.2 %collective-permute-start.10 = (bf16[48,1536]{1,0:T(8,128)(2,1)S(1)}, bf16[48,1536]{1,0:T(8,128)(2,1)S(1)}, u32[]{:S(2)}, u32[]{:S(2)}) collective-permute-start(bf16[48,1536]{1,0:T(8,128)(2,1)S(1)} %get-tuple-element.53), channel_id=1, source_target_pairs={{0,224},{32,0},{64,32},{96,64},{128,96},{160,128},{192,160},{224,1... | collective-permute-start | bytes 442376 | tf_op jit(solution)/shard_map/ppermute | solution.py:33
  72.2 3.3 %collective-permute-start.7 = (bf16[96,1536]{1,0:T(8,128)(2,1)S(1)}, bf16[96,1536]{1,0:T(8,128)(2,1)S(1)}, u32[]{:S(2)}, u32[]{:S(2)}) collective-permute-start(bf16[96,1536]{1,0:T(8,128)(2,1)S(1)} %fusion.14), channel_id=1, source_target_pairs={{0,32},{32,64},{64,96},{96,128},{128,160},{160,192},{192,224},{224... | collective-permute-start | bytes 884744 | tf_op jit(solution)/shard_map/ppermute | solution.py:33
  75.6 3.3 %collective-permute-start.11 = (bf16[96,1536]{1,0:T(8,128)(2,1)S(1)}, bf16[96,1536]{1,0:T(8,128)(2,1)S(1)}, u32[]{:S(2)}, u32[]{:S(2)}) collective-permute-start(bf16[96,1536]{1,0:T(8,128)(2,1)S(1)} %pad_maximum_fusion.4), channel_id=1, source_target_pairs={{0,224},{32,0},{64,32},{96,64},{128,96},{160,128},{192,160},{224,1... | collective-permute-start | bytes 884744 | tf_op jit(solution)/shard_map/ppermute | solution.py:33
  78.9 2.3 %collective-permute-done.7 = bf16[96,1536]{1,0:T(8,128)(2,1)S(1)} collective-permute-done((bf16[96,1536]{1,0:T(8,128)(2,1)S(1)}, bf16[96,1536]{1,0:T(8,128)(2,1)S(1)}, u32[]{:S(2)}, u32[]{:S(2)}) %collective-permute-start.7) | collective-permute-done | bytes 294944 | tf_op jit(solution)/shard_map/ppermute | solution.py:33
  81.3 4.5 %collective-permute-start.8 = (bf16[96,1536]{1,0:T(8,128)(2,1)S(1)}, bf16[96,1536]{1,0:T(8,128)(2,1)S(1)}, u32[]{:S(2)}, u32[]{:S(2)}) collective-permute-start(bf16[96,1536]{1,0:T(8,128)(2,1)S(1)} %add_convert_fusion.4), channel_id=1, source_target_pairs={{0,32},{32,64},{64,96},{96,128},{128,160},{160,192},{192,224},{224... | collective-permute-start | bytes 884744 | tf_op jit(solution)/shard_map/ppermute | solution.py:33
  85.9 2.6 %collective-permute-start.12 = (bf16[96,1536]{1,0:T(8,128)(2,1)S(1)}, bf16[96,1536]{1,0:T(8,128)(2,1)S(1)}, u32[]{:S(2)}, u32[]{:S(2)}) collective-permute-start(bf16[96,1536]{1,0:T(8,128)(2,1)S(1)} %add_convert_fusion.2), channel_id=1, source_target_pairs={{0,224},{32,0},{64,32},{96,64},{128,96},{160,128},{192,160},{224,1... | collective-permute-start | bytes 884744 | tf_op jit(solution)/shard_map/ppermute | solution.py:33
  88.6 3.5 %collective-permute-done.8 = bf16[96,1536]{1,0:T(8,128)(2,1)S(1)} collective-permute-done((bf16[96,1536]{1,0:T(8,128)(2,1)S(1)}, bf16[96,1536]{1,0:T(8,128)(2,1)S(1)}, u32[]{:S(2)}, u32[]{:S(2)}) %collective-permute-start.8) | collective-permute-done | bytes 294944 | tf_op jit(solution)/shard_map/ppermute | solution.py:33
  92.1 5.2 %collective-permute-start.9 = (bf16[96,1536]{1,0:T(8,128)(2,1)S(1)}, bf16[96,1536]{1,0:T(8,128)(2,1)S(1)}, u32[]{:S(2)}, u32[]{:S(2)}) collective-permute-start(bf16[96,1536]{1,0:T(8,128)(2,1)S(1)} %add_convert_fusion.3), channel_id=1, source_target_pairs={{0,32},{32,64},{64,96},{96,128},{128,160},{160,192},{192,224},{224... | collective-permute-start | bytes 884744 | tf_op jit(solution)/shard_map/ppermute | solution.py:33
  97.5 1.9 collective-permute-start.13
  99.4 3.2 %collective-permute-done.9 = bf16[96,1536]{1,0:T(8,128)(2,1)S(1)} collective-permute-done((bf16[96,1536]{1,0:T(8,128)(2,1)S(1)}, bf16[96,1536]{1,0:T(8,128)(2,1)S(1)}, u32[]{:S(2)}, u32[]{:S(2)}) %collective-permute-start.9) | collective-permute-done | bytes 294944 | tf_op jit(solution)/shard_map/ppermute | solution.py:33
  102.6 5.1 %collective-permute-done.13 = bf16[96,1536]{1,0:T(8,128)(2,1)S(1)} collective-permute-done((bf16[96,1536]{1,0:T(8,128)(2,1)S(1)}, bf16[96,1536]{1,0:T(8,128)(2,1)S(1)}, u32[]{:S(2)}, u32[]{:S(2)}) %collective-permute-start.13) | collective-permute-done | bytes 294944 | tf_op jit(solution)/shard_map/ppermute | solution.py:33
  107.8 8.2 %collective-permute-start.14 = (bf16[96,1536]{1,0:T(8,128)(2,1)S(1)}, bf16[96,1536]{1,0:T(8,128)(2,1)S(1)}, u32[]{:S(2)}, u32[]{:S(2)}) collective-permute-start(bf16[96,1536]{1,0:T(8,128)(2,1)S(1)} %add_convert_fusion), channel_id=1, source_target_pairs={{0,16},{16,0},{1,17},{17,1},{2,18},{18,2},{3,19},{19,3},{4,20},{20... | collective-permute-start | bytes 884744 | tf_op jit(solution)/shard_map/ppermute | solution.py:27
  116.1 4.2 %collective-permute-done.14 = bf16[96,1536]{1,0:T(8,128)(2,1)S(1)} collective-permute-done((bf16[96,1536]{1,0:T(8,128)(2,1)S(1)}, bf16[96,1536]{1,0:T(8,128)(2,1)S(1)}, u32[]{:S(2)}, u32[]{:S(2)}) %collective-permute-start.14) | collective-permute-done | bytes 294944 | tf_op jit(solution)/shard_map/ppermute | solution.py:27
  122.1 1.9 collective-permute-start.15
  124.0 3.4 %collective-permute-start.16 = (bf16[96,1664]{1,0:T(8,128)(2,1)S(1)}, bf16[96,1664]{1,0:T(8,128)(2,1)}, u32[]{:S(2)}, u32[]{:S(2)}) collective-permute-start(bf16[96,1664]{1,0:T(8,128)(2,1)S(1)} %pad_maximum_fusion.3), channel_id=1, source_target_pairs={{0,224},{32,0},{64,32},{96,64},{128,96},{160,128},{192,160},{224,1... | collective-permute-start | bytes 958472 | tf_op jit(solution)/shard_map/ppermute | solution.py:33
  127.5 2.4 %collective-permute-done.15 = bf16[96,1664]{1,0:T(8,128)(2,1)} collective-permute-done((bf16[96,1664]{1,0:T(8,128)(2,1)S(1)}, bf16[96,1664]{1,0:T(8,128)(2,1)}, u32[]{:S(2)}, u32[]{:S(2)}) %collective-permute-start.15) | collective-permute-done | bytes 319520 | tf_op jit(solution)/shard_map/ppermute | solution.py:33
  129.9 3.3 %collective-permute-start.17 = (bf16[96,1664]{1,0:T(8,128)(2,1)}, bf16[96,1664]{1,0:T(8,128)(2,1)S(1)}, u32[]{:S(2)}, u32[]{:S(2)}) collective-permute-start(bf16[96,1664]{1,0:T(8,128)(2,1)} %collective-permute-done.15), channel_id=1, source_target_pairs={{0,32},{32,64},{64,96},{96,128},{128,160},{160,192},{192,224},{224... | collective-permute-start | bytes 958472 | tf_op jit(solution)/shard_map/ppermute | solution.py:33
  133.3 2.0 collective-permute-start.18
  138.8 4.5 %collective-permute-start.19 = (bf16[96,1664]{1,0:T(8,128)(2,1)S(1)}, bf16[96,1664]{1,0:T(8,128)(2,1)S(1)}, u32[]{:S(2)}, u32[]{:S(2)}) collective-permute-start(bf16[96,1664]{1,0:T(8,128)(2,1)S(1)} %collective-permute-done.17), channel_id=1, source_target_pairs={{0,32},{32,64},{64,96},{96,128},{128,160},{160,192},{192,224},{224... | collective-permute-start | bytes 958472 | tf_op jit(solution)/shard_map/ppermute | solution.py:33
  143.3 2.2 %collective-permute-done.18 = bf16[96,1664]{1,0:T(8,128)(2,1)S(1)} collective-permute-done((bf16[96,1664]{1,0:T(8,128)(2,1)}, bf16[96,1664]{1,0:T(8,128)(2,1)S(1)}, u32[]{:S(2)}, u32[]{:S(2)}) %collective-permute-start.18) | collective-permute-done | bytes 319520 | tf_op jit(solution)/shard_map/ppermute | solution.py:33
  145.5 1.9 collective-permute-start.20
  147.6 4.7 %collective-permute-start.21 = (bf16[48,1664]{1,0:T(8,128)(2,1)S(1)}, bf16[48,1664]{1,0:T(8,128)(2,1)S(1)}, u32[]{:S(2)}, u32[]{:S(2)}) collective-permute-start(bf16[48,1664]{1,0:T(8,128)(2,1)S(1)} %slice.260), channel_id=1, source_target_pairs={{0,32},{32,64},{64,96},{96,128},{128,160},{160,192},{192,224},{224... | collective-permute-start | bytes 479240 | tf_op jit(solution)/shard_map/ppermute | solution.py:33
  152.3 4.8 %collective-permute-done.20 = bf16[96,1664]{1,0:T(8,128)(2,1)S(1)} collective-permute-done((bf16[96,1664]{1,0:T(8,128)(2,1)S(1)}, bf16[96,1664]{1,0:T(8,128)(2,1)S(1)}, u32[]{:S(2)}, u32[]{:S(2)}) %collective-permute-start.20) | collective-permute-done | bytes 319520 | tf_op jit(solution)/shard_map/ppermute | solution.py:33
  157.1 1.9 collective-permute-start.22
  159.2 5.2 %collective-permute-done.22 = bf16[48,1664]{1,0:T(8,128)(2,1)S(1)} collective-permute-done((bf16[48,1664]{1,0:T(8,128)(2,1)S(1)}, bf16[48,1664]{1,0:T(8,128)(2,1)S(1)}, u32[]{:S(2)}, u32[]{:S(2)}) %collective-permute-start.22) | collective-permute-done | bytes 159776 | tf_op jit(solution)/shard_map/ppermute | solution.py:33
  167.6 3.5 %all-to-all-start.1 = ((bf16[4,200,896]{2,1,0:T(8,128)(2,1)}), bf16[4,200,896]{2,1,0:T(8,128)(2,1)S(1)}, u32[]{:S(2)}, u32[]{:S(2)}) async-start(bf16[4,200,896]{2,1,0:T(8,128)(2,1)} %pad_maximum_fusion), calls=%async_computation.1 | async-start | bytes 2867200 | tf_op jit(solution)/shard_map/all_to_all | solution.py:115
  171.2 3.0 %convolution_convert_fusion.2 = bf16[768,384]{1,0:T(8,128)(2,1)} fusion(bf16[768,768]{1,0:T(8,128)(2,1)} %copy-done.4, bf16[768,384]{1,0:T(8,128)(2,1)S(1)} %maximum_dynamic-update-slice_fusion.1), kind=kOutput, calls=%fused_computation.5 | convolution fusion | flops 453279744 | bytes 2359296 | tf_op jit(solution)/shard_map/dot_general | solution.py:15
  174.2 16.1 %collective-permute-start.24 = (bf16[768,384]{1,0:T(8,128)(2,1)}, bf16[768,384]{1,0:T(8,128)(2,1)}, u32[]{:S(2)}, u32[]{:S(2)}) collective-permute-start(bf16[768,384]{1,0:T(8,128)(2,1)} %convolution_convert_fusion.2), channel_id=1, source_target_pairs={{0,256},{256,0},{1,257},{257,1},{2,258},{258,2},{3,259},{259,3},{4... | collective-permute-start | bytes 1769480 | tf_op jit(solution)/shard_map/ppermute | solution.py:27
  190.3 1.5 convolution_convert_fusion.3
  191.8 1.9 collective-permute-start.23
  194.8 3.5 %all-to-all-start.2 = ((bf16[4,56,896]{2,1,0:T(8,128)(2,1)}), bf16[4,56,896]{2,1,0:T(8,128)(2,1)S(1)}, u32[]{:S(2)}, u32[]{:S(2)}) async-start(bf16[4,56,896]{2,1,0:T(8,128)(2,1)} %pad_maximum_fusion.2), calls=%async_computation.2 | async-start | bytes 802816 | tf_op jit(solution)/shard_map/all_to_all | solution.py:115
  198.3 2.4 %convert_add_fusion = f32[768,384]{1,0:T(8,128)} fusion(bf16[768,384]{1,0:T(8,128)(2,1)} %collective-permute-done.24, bf16[768,384]{1,0:T(8,128)(2,1)} %convolution_convert_fusion.2), kind=kLoop, calls=%fused_computation.8 | loop fusion | flops 884736 | bytes 2359296 | tf_op jit(solution)/shard_map/add | solution.py:48
  200.7 2.2 %convert_add_fusion.1 = f32[384,768]{1,0:T(8,128)} fusion(bf16[384,768]{1,0:T(8,128)(2,1)S(1)} %collective-permute-done.23, bf16[384,768]{1,0:T(8,128)(2,1)} %convolution_convert_fusion.3), kind=kLoop, calls=%fused_computation.9 | loop fusion | flops 884736 | bytes 2359296 | tf_op jit(solution)/shard_map/add | solution.py:48
  202.9 3.2 %all-to-all-done.2 = bf16[4,56,896]{2,1,0:T(8,128)(2,1)S(1)} async-done(((bf16[4,56,896]{2,1,0:T(8,128)(2,1)}), bf16[4,56,896]{2,1,0:T(8,128)(2,1)S(1)}, u32[]{:S(2)}, u32[]{:S(2)}) %all-to-all-start.2) | async-done | bytes 401440 | tf_op jit(solution)/shard_map/all_to_all | solution.py:115
  206.2 7.5 %collective-permute-start.25 = (f32[384]{0:T(512)S(1)}, f32[384]{0:T(512)S(1)}, u32[]{:S(2)}, u32[]{:S(2)}) collective-permute-start(f32[384]{0:T(512)S(1)} %slice_add_fusion), channel_id=1, source_target_pairs={{0,256},{256,0},{1,257},{257,1},{2,258},{258,2},{3,259},{259,3},{4... | collective-permute-start | bytes 4616 | tf_op jit(solution)/shard_map/ppermute | solution.py:27
  (125 shorter events, 18.3 us)
Async XLA Ops:
  0.6 60.3 %copy-start = (bf16[768,384]{1,0:T(8,128)(2,1)S(1)}, bf16[768,384]{1,0:T(8,128)(2,1)}, u32[]{:S(2)}) copy-start(bf16[768,384]{1,0:T(8,128)(2,1)} %param.8) | copy-start | bytes 1769476
  17.1 27.2 %copy-start.7 = (f32[384]{0:T(512)S(1)}, f32[384]{0:T(512)}, u32[]{:S(2)}) copy-start(f32[384]{0:T(512)} %param.6) | copy-start | bytes 4612
  19.3 24.8 %all-to-all-start = ((f32[16,1,1152]{2,1,0:T(1,128)}), f32[16,1,1152]{2,1,0:T(1,128)S(1)}, u32[]{:S(2)}, u32[]{:S(2)}) async-start(f32[16,1,1152]{2,1,0:T(1,128)} %broadcast_in_dim.53), calls=%async_computation | async-start | bytes 147456 | tf_op jit(solution)/shard_map/all_to_all | solution.py:55
  32.3 12.1 %collective-permute-start = (bf16[192,384]{1,0:T(8,128)(2,1)S(1)}, bf16[192,384]{1,0:T(8,128)(2,1)S(1)}, u32[]{:S(2)}, u32[]{:S(2)}) collective-permute-start(bf16[192,384]{1,0:T(8,128)(2,1)S(1)} %get-tuple-element.54), channel_id=1, source_target_pairs={{0,4},{4,8},{8,12},{12,0},{256,268},{260,256},{264,260},{268,264},... | collective-permute-start | bytes 442376 | tf_op jit(solution)/shard_map/ppermute | solution.py:33
  36.7 7.7 %collective-permute-start.1 = (bf16[192,384]{1,0:T(8,128)(2,1)S(1)}, bf16[192,384]{1,0:T(8,128)(2,1)S(1)}, u32[]{:S(2)}, u32[]{:S(2)}) collective-permute-start(bf16[192,384]{1,0:T(8,128)(2,1)S(1)} %get-tuple-element.54), channel_id=1, source_target_pairs={{0,12},{4,0},{8,4},{12,8},{256,260},{260,264},{264,268},{268,256},... | collective-permute-start | bytes 442376 | tf_op jit(solution)/shard_map/ppermute | solution.py:33
  44.5 7.3 %collective-permute-start.2 = (bf16[288,384]{1,0:T(8,128)(2,1)S(1)}, bf16[288,384]{1,0:T(8,128)(2,1)S(1)}, u32[]{:S(2)}, u32[]{:S(2)}) collective-permute-start(bf16[288,384]{1,0:T(8,128)(2,1)S(1)} %get-tuple-element.64), channel_id=1, source_target_pairs={{0,4},{4,8},{8,12},{12,0},{256,268},{260,256},{264,260},{268,264},... | collective-permute-start | bytes 663560 | tf_op jit(solution)/shard_map/ppermute | solution.py:33
  48.9 10.0 %collective-permute-start.3 = (bf16[288,384]{1,0:T(8,128)(2,1)S(1)}, bf16[288,384]{1,0:T(8,128)(2,1)S(1)}, u32[]{:S(2)}, u32[]{:S(2)}) collective-permute-start(bf16[288,384]{1,0:T(8,128)(2,1)S(1)} %get-tuple-element.65), channel_id=1, source_target_pairs={{0,12},{4,0},{8,4},{12,8},{256,260},{260,264},{264,268},{268,256},... | collective-permute-start | bytes 663560 | tf_op jit(solution)/shard_map/ppermute | solution.py:33
  51.8 10.2 %collective-permute-start.4 = (bf16[96,384]{1,0:T(8,128)(2,1)S(1)}, bf16[96,384]{1,0:T(8,128)(2,1)S(1)}, u32[]{:S(2)}, u32[]{:S(2)}) collective-permute-start(bf16[96,384]{1,0:T(8,128)(2,1)S(1)} %get-tuple-element.56), channel_id=1, source_target_pairs={{0,4},{4,8},{8,12},{12,0},{256,268},{260,256},{264,260},{268,264},... | collective-permute-start | bytes 221192 | tf_op jit(solution)/shard_map/ppermute | solution.py:33
  59.0 6.3 %collective-permute-start.5 = (bf16[96,384]{1,0:T(8,128)(2,1)S(1)}, bf16[96,384]{1,0:T(8,128)(2,1)S(1)}, u32[]{:S(2)}, u32[]{:S(2)}) collective-permute-start(bf16[96,384]{1,0:T(8,128)(2,1)S(1)} %get-tuple-element.58), channel_id=1, source_target_pairs={{0,12},{4,0},{8,4},{12,8},{256,260},{260,264},{264,268},{268,256},... | collective-permute-start | bytes 221192 | tf_op jit(solution)/shard_map/ppermute | solution.py:33
  61.8 3.5 %copy-start.1 = (bf16[384,768]{1,0:T(8,128)(2,1)S(1)}, bf16[384,768]{1,0:T(8,128)(2,1)}, u32[]{:S(2)}) copy-start(bf16[384,768]{1,0:T(8,128)(2,1)} %param.7) | copy-start | bytes 1769476
  66.2 5.9 %collective-permute-start.6 = (bf16[48,1536]{1,0:T(8,128)(2,1)S(1)}, bf16[48,1536]{1,0:T(8,128)(2,1)S(1)}, u32[]{:S(2)}, u32[]{:S(2)}) collective-permute-start(bf16[48,1536]{1,0:T(8,128)(2,1)S(1)} %get-tuple-element.52), channel_id=1, source_target_pairs={{0,32},{32,64},{64,96},{96,128},{128,160},{160,192},{192,224},{224... | collective-permute-start | bytes 442376 | tf_op jit(solution)/shard_map/ppermute | solution.py:33
  68.3 7.2 %collective-permute-start.10 = (bf16[48,1536]{1,0:T(8,128)(2,1)S(1)}, bf16[48,1536]{1,0:T(8,128)(2,1)S(1)}, u32[]{:S(2)}, u32[]{:S(2)}) collective-permute-start(bf16[48,1536]{1,0:T(8,128)(2,1)S(1)} %get-tuple-element.53), channel_id=1, source_target_pairs={{0,224},{32,0},{64,32},{96,64},{128,96},{160,128},{192,160},{224,1... | collective-permute-start | bytes 442376 | tf_op jit(solution)/shard_map/ppermute | solution.py:33
  72.2 9.0 %collective-permute-start.7 = (bf16[96,1536]{1,0:T(8,128)(2,1)S(1)}, bf16[96,1536]{1,0:T(8,128)(2,1)S(1)}, u32[]{:S(2)}, u32[]{:S(2)}) collective-permute-start(bf16[96,1536]{1,0:T(8,128)(2,1)S(1)} %fusion.14), channel_id=1, source_target_pairs={{0,32},{32,64},{64,96},{96,128},{128,160},{160,192},{192,224},{224... | collective-permute-start | bytes 884744 | tf_op jit(solution)/shard_map/ppermute | solution.py:33
  75.6 10.2 %collective-permute-start.11 = (bf16[96,1536]{1,0:T(8,128)(2,1)S(1)}, bf16[96,1536]{1,0:T(8,128)(2,1)S(1)}, u32[]{:S(2)}, u32[]{:S(2)}) collective-permute-start(bf16[96,1536]{1,0:T(8,128)(2,1)S(1)} %pad_maximum_fusion.4), channel_id=1, source_target_pairs={{0,224},{32,0},{64,32},{96,64},{128,96},{160,128},{192,160},{224,1... | collective-permute-start | bytes 884744 | tf_op jit(solution)/shard_map/ppermute | solution.py:33
  81.3 10.7 %collective-permute-start.8 = (bf16[96,1536]{1,0:T(8,128)(2,1)S(1)}, bf16[96,1536]{1,0:T(8,128)(2,1)S(1)}, u32[]{:S(2)}, u32[]{:S(2)}) collective-permute-start(bf16[96,1536]{1,0:T(8,128)(2,1)S(1)} %add_convert_fusion.4), channel_id=1, source_target_pairs={{0,32},{32,64},{64,96},{96,128},{128,160},{160,192},{192,224},{224... | collective-permute-start | bytes 884744 | tf_op jit(solution)/shard_map/ppermute | solution.py:33
  85.9 11.5 %collective-permute-start.12 = (bf16[96,1536]{1,0:T(8,128)(2,1)S(1)}, bf16[96,1536]{1,0:T(8,128)(2,1)S(1)}, u32[]{:S(2)}, u32[]{:S(2)}) collective-permute-start(bf16[96,1536]{1,0:T(8,128)(2,1)S(1)} %add_convert_fusion.2), channel_id=1, source_target_pairs={{0,224},{32,0},{64,32},{96,64},{128,96},{160,128},{192,160},{224,1... | collective-permute-start | bytes 884744 | tf_op jit(solution)/shard_map/ppermute | solution.py:33
  92.1 10.5 %collective-permute-start.9 = (bf16[96,1536]{1,0:T(8,128)(2,1)S(1)}, bf16[96,1536]{1,0:T(8,128)(2,1)S(1)}, u32[]{:S(2)}, u32[]{:S(2)}) collective-permute-start(bf16[96,1536]{1,0:T(8,128)(2,1)S(1)} %add_convert_fusion.3), channel_id=1, source_target_pairs={{0,32},{32,64},{64,96},{96,128},{128,160},{160,192},{192,224},{224... | collective-permute-start | bytes 884744 | tf_op jit(solution)/shard_map/ppermute | solution.py:33
  97.5 10.3 %collective-permute-start.13 = (bf16[96,1536]{1,0:T(8,128)(2,1)S(1)}, bf16[96,1536]{1,0:T(8,128)(2,1)S(1)}, u32[]{:S(2)}, u32[]{:S(2)}) collective-permute-start(bf16[96,1536]{1,0:T(8,128)(2,1)S(1)} %add_convert_fusion.1), channel_id=1, source_target_pairs={{0,224},{32,0},{64,32},{96,64},{128,96},{160,128},{192,160},{224,1... | collective-permute-start | bytes 884744 | tf_op jit(solution)/shard_map/ppermute | solution.py:33
  107.8 12.4 %collective-permute-start.14 = (bf16[96,1536]{1,0:T(8,128)(2,1)S(1)}, bf16[96,1536]{1,0:T(8,128)(2,1)S(1)}, u32[]{:S(2)}, u32[]{:S(2)}) collective-permute-start(bf16[96,1536]{1,0:T(8,128)(2,1)S(1)} %add_convert_fusion), channel_id=1, source_target_pairs={{0,16},{16,0},{1,17},{17,1},{2,18},{18,2},{3,19},{19,3},{4,20},{20... | collective-permute-start | bytes 884744 | tf_op jit(solution)/shard_map/ppermute | solution.py:27
  120.9 1.0 copy-start.2
  122.1 7.8 %collective-permute-start.15 = (bf16[96,1664]{1,0:T(8,128)(2,1)S(1)}, bf16[96,1664]{1,0:T(8,128)(2,1)}, u32[]{:S(2)}, u32[]{:S(2)}) collective-permute-start(bf16[96,1664]{1,0:T(8,128)(2,1)S(1)} %pad_maximum_fusion.3), channel_id=1, source_target_pairs={{0,32},{32,64},{64,96},{96,128},{128,160},{160,192},{192,224},{224... | collective-permute-start | bytes 958472 | tf_op jit(solution)/shard_map/ppermute | solution.py:33
  124.0 9.2 %collective-permute-start.16 = (bf16[96,1664]{1,0:T(8,128)(2,1)S(1)}, bf16[96,1664]{1,0:T(8,128)(2,1)}, u32[]{:S(2)}, u32[]{:S(2)}) collective-permute-start(bf16[96,1664]{1,0:T(8,128)(2,1)S(1)} %pad_maximum_fusion.3), channel_id=1, source_target_pairs={{0,224},{32,0},{64,32},{96,64},{128,96},{160,128},{192,160},{224,1... | collective-permute-start | bytes 958472 | tf_op jit(solution)/shard_map/ppermute | solution.py:33
  127.4 7.8 %copy-start.3 = (bf16[768,768]{1,0:T(8,128)(2,1)S(1)}, bf16[768,768]{1,0:T(8,128)(2,1)}, u32[]{:S(2)}) copy-start(bf16[768,768]{1,0:T(8,128)(2,1)} %copy-done.2) | copy-start | bytes 3538948
  129.9 8.8 %collective-permute-start.17 = (bf16[96,1664]{1,0:T(8,128)(2,1)}, bf16[96,1664]{1,0:T(8,128)(2,1)S(1)}, u32[]{:S(2)}, u32[]{:S(2)}) collective-permute-start(bf16[96,1664]{1,0:T(8,128)(2,1)} %collective-permute-done.15), channel_id=1, source_target_pairs={{0,32},{32,64},{64,96},{96,128},{128,160},{160,192},{192,224},{224... | collective-permute-start | bytes 958472 | tf_op jit(solution)/shard_map/ppermute | solution.py:33
  133.3 12.3 %collective-permute-start.18 = (bf16[96,1664]{1,0:T(8,128)(2,1)}, bf16[96,1664]{1,0:T(8,128)(2,1)S(1)}, u32[]{:S(2)}, u32[]{:S(2)}) collective-permute-start(bf16[96,1664]{1,0:T(8,128)(2,1)} %collective-permute-done.16), channel_id=1, source_target_pairs={{0,224},{32,0},{64,32},{96,64},{128,96},{160,128},{192,160},{224,1... | collective-permute-start | bytes 958472 | tf_op jit(solution)/shard_map/ppermute | solution.py:33
  138.8 8.8 %collective-permute-start.19 = (bf16[96,1664]{1,0:T(8,128)(2,1)S(1)}, bf16[96,1664]{1,0:T(8,128)(2,1)S(1)}, u32[]{:S(2)}, u32[]{:S(2)}) collective-permute-start(bf16[96,1664]{1,0:T(8,128)(2,1)S(1)} %collective-permute-done.17), channel_id=1, source_target_pairs={{0,32},{32,64},{64,96},{96,128},{128,160},{160,192},{192,224},{224... | collective-permute-start | bytes 958472 | tf_op jit(solution)/shard_map/ppermute | solution.py:33
  145.5 11.6 %collective-permute-start.20 = (bf16[96,1664]{1,0:T(8,128)(2,1)S(1)}, bf16[96,1664]{1,0:T(8,128)(2,1)S(1)}, u32[]{:S(2)}, u32[]{:S(2)}) collective-permute-start(bf16[96,1664]{1,0:T(8,128)(2,1)S(1)} %collective-permute-done.18), channel_id=1, source_target_pairs={{0,224},{32,0},{64,32},{96,64},{128,96},{160,128},{192,160},{224,1... | collective-permute-start | bytes 958472 | tf_op jit(solution)/shard_map/ppermute | solution.py:33
  147.6 11.6 %collective-permute-start.21 = (bf16[48,1664]{1,0:T(8,128)(2,1)S(1)}, bf16[48,1664]{1,0:T(8,128)(2,1)S(1)}, u32[]{:S(2)}, u32[]{:S(2)}) collective-permute-start(bf16[48,1664]{1,0:T(8,128)(2,1)S(1)} %slice.260), channel_id=1, source_target_pairs={{0,32},{32,64},{64,96},{96,128},{128,160},{160,192},{192,224},{224... | collective-permute-start | bytes 479240 | tf_op jit(solution)/shard_map/ppermute | solution.py:33
  157.1 7.2 %collective-permute-start.22 = (bf16[48,1664]{1,0:T(8,128)(2,1)S(1)}, bf16[48,1664]{1,0:T(8,128)(2,1)S(1)}, u32[]{:S(2)}, u32[]{:S(2)}) collective-permute-start(bf16[48,1664]{1,0:T(8,128)(2,1)S(1)} %slice.262), channel_id=1, source_target_pairs={{0,224},{32,0},{64,32},{96,64},{128,96},{160,128},{192,160},{224,1... | collective-permute-start | bytes 479240 | tf_op jit(solution)/shard_map/ppermute | solution.py:33
  164.4 1.0 copy-start.5
  164.4 1.9 copy-start.4
  167.6 26.1 %all-to-all-start.1 = ((bf16[4,200,896]{2,1,0:T(8,128)(2,1)}), bf16[4,200,896]{2,1,0:T(8,128)(2,1)S(1)}, u32[]{:S(2)}, u32[]{:S(2)}) async-start(bf16[4,200,896]{2,1,0:T(8,128)(2,1)} %pad_maximum_fusion), calls=%async_computation.1 | async-start | bytes 2867200 | tf_op jit(solution)/shard_map/all_to_all | solution.py:115
  171.2 19.1 %copy-start.6 = (bf16[768,768]{1,0:T(8,128)(2,1)S(1)}, bf16[768,768]{1,0:T(8,128)(2,1)}, u32[]{:S(2)}) copy-start(bf16[768,768]{1,0:T(8,128)(2,1)} %copy-done.5) | copy-start | bytes 3538948
  174.2 24.1 %collective-permute-start.24 = (bf16[768,384]{1,0:T(8,128)(2,1)}, bf16[768,384]{1,0:T(8,128)(2,1)}, u32[]{:S(2)}, u32[]{:S(2)}) collective-permute-start(bf16[768,384]{1,0:T(8,128)(2,1)} %convolution_convert_fusion.2), channel_id=1, source_target_pairs={{0,256},{256,0},{1,257},{257,1},{2,258},{258,2},{3,259},{259,3},{4... | collective-permute-start | bytes 1769480 | tf_op jit(solution)/shard_map/ppermute | solution.py:27
  191.8 8.9 %collective-permute-start.23 = (bf16[384,768]{1,0:T(8,128)(2,1)}, bf16[384,768]{1,0:T(8,128)(2,1)S(1)}, u32[]{:S(2)}, u32[]{:S(2)}) collective-permute-start(bf16[384,768]{1,0:T(8,128)(2,1)} %convolution_convert_fusion.3), channel_id=1, source_target_pairs={{0,256},{256,0},{1,257},{257,1},{2,258},{258,2},{3,259},{259,3},{4... | collective-permute-start | bytes 1769480 | tf_op jit(solution)/shard_map/ppermute | solution.py:27
  194.8 11.4 %all-to-all-start.2 = ((bf16[4,56,896]{2,1,0:T(8,128)(2,1)}), bf16[4,56,896]{2,1,0:T(8,128)(2,1)S(1)}, u32[]{:S(2)}, u32[]{:S(2)}) async-start(bf16[4,56,896]{2,1,0:T(8,128)(2,1)} %pad_maximum_fusion.2), calls=%async_computation.2 | async-start | bytes 802816 | tf_op jit(solution)/shard_map/all_to_all | solution.py:115
  206.2 9.1 %collective-permute-start.25 = (f32[384]{0:T(512)S(1)}, f32[384]{0:T(512)S(1)}, u32[]{:S(2)}, u32[]{:S(2)}) collective-permute-start(f32[384]{0:T(512)S(1)} %slice_add_fusion), channel_id=1, source_target_pairs={{0,256},{256,0},{1,257},{257,1},{2,258},{258,2},{3,259},{259,3},{4... | collective-permute-start | bytes 4616 | tf_op jit(solution)/shard_map/ppermute | solution.py:27

commit v5 on v3

--- a/solution.py
+++ b/solution.py
@@ -55,16 +55,28 @@
     def at(by):
         return part((me + (by + Y)) & (Y - 1))
 
-    far = at(Y // 2)
+    far = at(4)
     half = far.shape[0] // 2
-    up, down = shift(far[:half], "y", Y, 1), shift(far[half:], "y", Y, -1)
-    above, below = at(Y // 2 - 1), at(1 - Y // 2)
-    up = jnp.concatenate([add(up, above[:half]).astype(BF16), above[half:]], axis=0)
-    down = jnp.concatenate([below[:half], add(down, below[half:]).astype(BF16)], axis=0)
-    for by in range(Y // 2 - 2, -1, -1):
-        up, down = shift(up, "y", Y, 1), shift(down, "y", Y, -1)
-        if by:
-            up, down = add(up, at(by)).astype(BF16), add(down, at(-by)).astype(BF16)
+    up, down = shift(at(3), "y", Y, 1), shift(at(-3), "y", Y, -1)
+    up_far, down_far = shift(far[:half], "y", Y, 2), shift(far[half:], "y", Y, -2)
+    above, below = at(2), at(-2)
+    up = jnp.concatenate(
+        [
+            add(up[:half], up_far, above[:half]).astype(BF16),
+            add(up[half:], above[half:]).astype(BF16),
+        ],
+        axis=0,
+    )
+    down = jnp.concatenate(
+        [
+            add(down[:half], below[:half]).astype(BF16),
+            add(down[half:], down_far, below[half:]).astype(BF16),
+        ],
+        axis=0,
+    )
+    up, down = shift(up, "y", Y, 1), shift(down, "y", Y, -1)
+    up, down = add(up, at(1)).astype(BF16), add(down, at(-1)).astype(BF16)
+    up, down = shift(up, "y", Y, 1), shift(down, "y", Y, -1)
     return add(at(0), up, down)
 
 
@@ -88,11 +100,14 @@
     block = jnp.concatenate(blocks, axis=1)
     panels = put(panels, block, 0)
     below = above = block
-    for by in range(1, size // 2):
+    for by in range(1, size // 2 - 1):
         below, above = shift(below, axis, size, 1), shift(above, axis, size, -1)
         panels = put(put(panels, below, -by), above, by)
-    panels = put(panels, shift(below[:half], axis, size, 1), size // 2)
-    return put(panels, shift(above[half:], axis, size, -1), size // 2, half)
+    by = size // 2
+    low = shift(below, axis, size, 1), shift(below[:half], axis, size, 2)
+    high = shift(above, axis, size, -1), shift(above[half:], axis, size, -2)
+    panels = put(put(panels, low[0], 1 - by), high[0], by - 1)
+    return put(put(panels, low[1], by), high[1], by, half)
 
 
 def scatter(sent, vector, axis, size):
@@ -149,11 +164,9 @@
 
     up = shift(jnp.concatenate([normed, below[:half]], axis=0), "x", X, 1)
     down = shift(jnp.concatenate([normed, above[half:]], axis=0), "x", X, -1)
+    normed_panel = panel(normed, up[:count], down[:count], shift(normed, "x", X, 2))
     far = jnp.concatenate([up[count:], down[count:]], axis=0)
     cotangent = panel(cotangent, below, above, far)
-    below, above = up[:count], down[:count]
-    far = shift(below[:half], "x", X, 1), shift(above[half:], "x", X, -1)
-    normed_panel = panel(normed, below, above, jnp.concatenate(far, axis=0))
     own = lax.axis_index("zl") * tokens
     centred, inverse = (
         lax.dynamic_slice(

time: 214 us -> 210 us (0.981)
  local copies, waits for them, and re-layouts: 7.85 us -> 5.57 us
    ppermute x26 -> x25, starting transfers between devices: 106 us -> 104 us  [shift(): lax.ppermute(values, axis, [(i, (i + by) % size) for i in range(size)])]
    ppermute x26 -> x25, waiting for transfers between devices: 30.6 us -> 29.8 us  [shift(): lax.ppermute(values, axis, [(i, (i + by) % size) for i in range(size)])]
  transfers between devices with their start and end apart: 29 -> 28, of which waited for: 16 -> 13; matrix products, arithmetic and copies ran while one was open for 8% -> 7% of each run, Pallas kernels for 0% -> 0%
where the time goes in v5:
time: 210 us; the launch traced here: 209 us
  starting transfers between devices  128 us (61%)
  waiting for transfers between devices  38.3 us (18%)
  blocking collectives  15.6 us (7%)
  other arithmetic  12.3 us (6%)
  matrix products  7.62 us (4%)
  local copies, waits for them, and re-layouts  5.57 us (3%)
    ppermute x25, starting transfers between devices, shift(): lax.ppermute(values, axis, [(i, (i + by) % size) for i in range(size)])  104 us
    ppermute x25, waiting for transfers between devices, shift(): lax.ppermute(values, axis, [(i, (i + by) % size) for i in range(size)])  29.8 us
    all_gather x1, blocking collectives, shards(): lax.all_gather(jnp.concatenate([patches, out_grad], axis=1), 'zl', axis=0...  15.6 us
    all_to_all x1, starting transfers between devices, to_all(): return lax.all_to_all(copies, axes, 0, 0, tiled=True)  12.9 us
    all_to_all x2, starting transfers between devices, scatter(): back = lax.all_to_all(parts, axis, 0, 0, tiled=True)  11 us
    all_to_all x1, waiting for transfers between devices, to_all(): return lax.all_to_all(copies, axes, 0, 0, tiled=True)  5.31 us
    add x3, other arithmetic, add(): total = total + term.astype(F32)  4.66 us
    dot_general x2, matrix products, contract_tokens(): lax.dot_general(left, right, (((0,), (0,)), ((), ())), preferred_element_...  4.48 us
  transfers between devices with their start and end apart: 28, of which 13 were waited for; matrix products, arithmetic and copies ran while one was open for 7% of the time, Pallas kernels for 0%

profile of v5, /device:TPU:1, one launch (start us, length us, event | category | flops | bytes accessed | tf_op | source)
XLA Modules:
  0.0 209.1 jit_solution(8739140104653817587)
XLA Ops:
  1.5 15.6 %all_gather.3 = bf16[192,768]{1,0:T(8,128)(2,1)S(1)} all-gather(bf16[48,768]{1,0:T(8,128)(2,1)S(1)} %pad_maximum_fusion.13), channel_id=1, replica_groups=mesh['dp'=2,'y'=8,'zh'=2,'x'=4,'zl'=4] {'zl'}, dimensions={0}, use_global_device_ids=true | all-gather | bytes 368640 | tf_op jit(solution)/shard_map/all_gather | solution.py:130
  17.3 1.3 multiply_reduce_fusion.1
  19.3 12.9 %all-to-all-start = ((f32[16,1,1152]{2,1,0:T(1,128)}), f32[16,1,1152]{2,1,0:T(1,128)S(1)}, u32[]{:S(2)}, u32[]{:S(2)}) async-start(f32[16,1,1152]{2,1,0:T(1,128)} %broadcast_in_dim.53), calls=%async_computation | async-start | bytes 147456 | tf_op jit(solution)/shard_map/all_to_all | solution.py:44
  32.3 3.1 %collective-permute-start = (bf16[192,384]{1,0:T(8,128)(2,1)S(1)}, bf16[192,384]{1,0:T(8,128)(2,1)S(1)}, u32[]{:S(2)}, u32[]{:S(2)}) collective-permute-start(bf16[192,384]{1,0:T(8,128)(2,1)S(1)} %get-tuple-element.58), channel_id=1, source_target_pairs={{0,4},{4,8},{8,12},{12,0},{1,5},{5,9},{9,13},{13,1},{2,6},{6,10},{... | collective-permute-start | bytes 442376 | tf_op jit(solution)/shard_map/ppermute | solution.py:27
  35.4 3.4 %collective-permute-start.1 = (bf16[192,384]{1,0:T(8,128)(2,1)S(1)}, bf16[192,384]{1,0:T(8,128)(2,1)S(1)}, u32[]{:S(2)}, u32[]{:S(2)}) collective-permute-start(bf16[192,384]{1,0:T(8,128)(2,1)S(1)} %get-tuple-element.58), channel_id=1, source_target_pairs={{0,12},{4,0},{8,4},{12,8},{1,13},{5,1},{9,5},{13,9},{2,14},{6,2},{... | collective-permute-start | bytes 442376 | tf_op jit(solution)/shard_map/ppermute | solution.py:27
  38.8 5.3 %all-to-all-done = f32[16,1,1152]{2,1,0:T(1,128)S(1)} async-done(((f32[16,1,1152]{2,1,0:T(1,128)}), f32[16,1,1152]{2,1,0:T(1,128)S(1)}, u32[]{:S(2)}, u32[]{:S(2)}) %all-to-all-start) | async-done | bytes 73760 | tf_op jit(solution)/shard_map/all_to_all | solution.py:44
  44.5 4.7 %collective-permute-start.4 = (bf16[192,384]{1,0:T(8,128)(2,1)S(1)}, bf16[192,384]{1,0:T(8,128)(2,1)S(1)}, u32[]{:S(2)}, u32[]{:S(2)}) collective-permute-start(bf16[192,384]{1,0:T(8,128)(2,1)S(1)} %get-tuple-element.8), channel_id=1, source_target_pairs={{0,8},{4,12},{8,0},{12,4},{1,9},{5,13},{9,1},{13,5},{2,10},{6,14},... | collective-permute-start | bytes 442376 | tf_op jit(solution)/shard_map/ppermute | solution.py:27
  49.2 2.2 %collective-permute-start.2 = (bf16[288,384]{1,0:T(8,128)(2,1)S(1)}, bf16[288,384]{1,0:T(8,128)(2,1)S(1)}, u32[]{:S(2)}, u32[]{:S(2)}) collective-permute-start(bf16[288,384]{1,0:T(8,128)(2,1)S(1)} %get-tuple-element.64), channel_id=1, source_target_pairs={{0,4},{4,8},{8,12},{12,0},{1,5},{5,9},{9,13},{13,1},{2,6},{6,10},{... | collective-permute-start | bytes 663560 | tf_op jit(solution)/shard_map/ppermute | solution.py:27
  51.4 4.3 %collective-permute-start.3 = (bf16[288,384]{1,0:T(8,128)(2,1)S(1)}, bf16[288,384]{1,0:T(8,128)(2,1)S(1)}, u32[]{:S(2)}, u32[]{:S(2)}) collective-permute-start(bf16[288,384]{1,0:T(8,128)(2,1)S(1)} %get-tuple-element.65), channel_id=1, source_target_pairs={{0,12},{4,0},{8,4},{12,8},{1,13},{5,1},{9,5},{13,9},{2,14},{6,2},{... | collective-permute-start | bytes 663560 | tf_op jit(solution)/shard_map/ppermute | solution.py:27
  55.9 2.6 %collective-permute-done.2 = bf16[288,384]{1,0:T(8,128)(2,1)S(1)} collective-permute-done((bf16[288,384]{1,0:T(8,128)(2,1)S(1)}, bf16[288,384]{1,0:T(8,128)(2,1)S(1)}, u32[]{:S(2)}, u32[]{:S(2)}) %collective-permute-start.2) | collective-permute-done | bytes 221216 | tf_op jit(solution)/shard_map/ppermute | solution.py:27
  60.6 2.0 collective-permute-start.5
  62.6 2.8 %collective-permute-start.6 = (bf16[48,1536]{1,0:T(8,128)(2,1)S(1)}, bf16[48,1536]{1,0:T(8,128)(2,1)S(1)}, u32[]{:S(2)}, u32[]{:S(2)}) collective-permute-start(bf16[48,1536]{1,0:T(8,128)(2,1)S(1)} %get-tuple-element.56), channel_id=1, source_target_pairs={{0,64},{32,96},{64,128},{96,160},{128,192},{160,224},{192,0},{224,... | collective-permute-start | bytes 442376 | tf_op jit(solution)/shard_map/ppermute | solution.py:27
  65.5 4.5 %collective-permute-start.10 = (bf16[48,1536]{1,0:T(8,128)(2,1)S(1)}, bf16[48,1536]{1,0:T(8,128)(2,1)S(1)}, u32[]{:S(2)}, u32[]{:S(2)}) collective-permute-start(bf16[48,1536]{1,0:T(8,128)(2,1)S(1)} %get-tuple-element.57), channel_id=1, source_target_pairs={{0,192},{32,224},{64,0},{96,32},{128,64},{160,96},{192,128},{224,1... | collective-permute-start | bytes 442376 | tf_op jit(solution)/shard_map/ppermute | solution.py:27
  70.1 3.3 %collective-permute-start.9 = (bf16[96,1536]{1,0:T(8,128)(2,1)S(1)}, bf16[96,1536]{1,0:T(8,128)(2,1)S(1)}, u32[]{:S(2)}, u32[]{:S(2)}) collective-permute-start(bf16[96,1536]{1,0:T(8,128)(2,1)S(1)} %pad_maximum_fusion.6), channel_id=1, source_target_pairs={{0,224},{32,0},{64,32},{96,64},{128,96},{160,128},{192,160},{224,1... | collective-permute-start | bytes 884744 | tf_op jit(solution)/shard_map/ppermute | solution.py:27
  73.5 2.9 %collective-permute-start.7 = (bf16[96,1536]{1,0:T(8,128)(2,1)S(1)}, bf16[96,1536]{1,0:T(8,128)(2,1)S(1)}, u32[]{:S(2)}, u32[]{:S(2)}) collective-permute-start(bf16[96,1536]{1,0:T(8,128)(2,1)S(1)} %pad_maximum_fusion.5), channel_id=1, source_target_pairs={{0,32},{32,64},{64,96},{96,128},{128,160},{160,192},{192,224},{224... | collective-permute-start | bytes 884744 | tf_op jit(solution)/shard_map/ppermute | solution.py:27
  76.3 2.8 %collective-permute-done.9 = bf16[96,1536]{1,0:T(8,128)(2,1)S(1)} collective-permute-done((bf16[96,1536]{1,0:T(8,128)(2,1)S(1)}, bf16[96,1536]{1,0:T(8,128)(2,1)S(1)}, u32[]{:S(2)}, u32[]{:S(2)}) %collective-permute-start.9) | collective-permute-done | bytes 294944 | tf_op jit(solution)/shard_map/ppermute | solution.py:27
  79.2 3.4 %collective-permute-start.11 = (bf16[96,1536]{1,0:T(8,128)(2,1)S(1)}, bf16[96,1536]{1,0:T(8,128)(2,1)S(1)}, u32[]{:S(2)}, u32[]{:S(2)}) collective-permute-start(bf16[96,1536]{1,0:T(8,128)(2,1)S(1)} %pad_maximum_fusion.7), channel_id=1, source_target_pairs={{0,224},{32,0},{64,32},{96,64},{128,96},{160,128},{192,160},{224,1... | collective-permute-start | bytes 884744 | tf_op jit(solution)/shard_map/ppermute | solution.py:27
  82.8 2.3 %collective-permute-start.8 = (bf16[96,1536]{1,0:T(8,128)(2,1)S(1)}, bf16[96,1536]{1,0:T(8,128)(2,1)S(1)}, u32[]{:S(2)}, u32[]{:S(2)}) collective-permute-start(bf16[96,1536]{1,0:T(8,128)(2,1)S(1)} %add_convert_fusion.2), channel_id=1, source_target_pairs={{0,32},{32,64},{64,96},{96,128},{128,160},{160,192},{192,224},{224... | collective-permute-start | bytes 884744 | tf_op jit(solution)/shard_map/ppermute | solution.py:27
  85.1 2.5 %collective-permute-done.11 = bf16[96,1536]{1,0:T(8,128)(2,1)S(1)} collective-permute-done((bf16[96,1536]{1,0:T(8,128)(2,1)S(1)}, bf16[96,1536]{1,0:T(8,128)(2,1)S(1)}, u32[]{:S(2)}, u32[]{:S(2)}) %collective-permute-start.11) | collective-permute-done | bytes 294944 | tf_op jit(solution)/shard_map/ppermute | solution.py:27
  87.7 4.0 %collective-permute-start.12 = (bf16[96,1536]{1,0:T(8,128)(2,1)S(1)}, bf16[96,1536]{1,0:T(8,128)(2,1)S(1)}, u32[]{:S(2)}, u32[]{:S(2)}) collective-permute-start(bf16[96,1536]{1,0:T(8,128)(2,1)S(1)} %add_convert_fusion.1), channel_id=1, source_target_pairs={{0,224},{32,0},{64,32},{96,64},{128,96},{160,128},{192,160},{224,1... | collective-permute-start | bytes 884744 | tf_op jit(solution)/shard_map/ppermute | solution.py:27
  92.0 4.9 %collective-permute-done.12 = bf16[96,1536]{1,0:T(8,128)(2,1)S(1)} collective-permute-done((bf16[96,1536]{1,0:T(8,128)(2,1)S(1)}, bf16[96,1536]{1,0:T(8,128)(2,1)S(1)}, u32[]{:S(2)}, u32[]{:S(2)}) %collective-permute-start.12) | collective-permute-done | bytes 294944 | tf_op jit(solution)/shard_map/ppermute | solution.py:27
  97.0 6.8 %collective-permute-start.13 = (bf16[96,1536]{1,0:T(8,128)(2,1)S(1)}, bf16[96,1536]{1,0:T(8,128)(2,1)S(1)}, u32[]{:S(2)}, u32[]{:S(2)}) collective-permute-start(bf16[96,1536]{1,0:T(8,128)(2,1)S(1)} %add_convert_fusion), channel_id=1, source_target_pairs={{0,16},{16,0},{1,17},{17,1},{2,18},{18,2},{3,19},{19,3},{4,20},{20... | collective-permute-start | bytes 884744 | tf_op jit(solution)/shard_map/ppermute | solution.py:27
  103.8 6.8 %collective-permute-done.13 = bf16[96,1536]{1,0:T(8,128)(2,1)S(1)} collective-permute-done((bf16[96,1536]{1,0:T(8,128)(2,1)S(1)}, bf16[96,1536]{1,0:T(8,128)(2,1)S(1)}, u32[]{:S(2)}, u32[]{:S(2)}) %collective-permute-start.13) | collective-permute-done | bytes 294944 | tf_op jit(solution)/shard_map/ppermute | solution.py:27
  111.2 1.0 copy-done.2
  112.4 1.9 collective-permute-start.14
  114.3 5.6 %collective-permute-start.15 = (bf16[96,1664]{1,0:T(8,128)(2,1)S(1)}, bf16[96,1664]{1,0:T(8,128)(2,1)S(1)}, u32[]{:S(2)}, u32[]{:S(2)}) collective-permute-start(bf16[96,1664]{1,0:T(8,128)(2,1)S(1)} %pad_maximum_fusion.3), channel_id=1, source_target_pairs={{0,224},{32,0},{64,32},{96,64},{128,96},{160,128},{192,160},{224,1... | collective-permute-start | bytes 958472 | tf_op jit(solution)/shard_map/ppermute | solution.py:27
  120.0 2.3 %collective-permute-done.14 = bf16[96,1664]{1,0:T(8,128)(2,1)} collective-permute-done((bf16[96,1664]{1,0:T(8,128)(2,1)S(1)}, bf16[96,1664]{1,0:T(8,128)(2,1)}, u32[]{:S(2)}, u32[]{:S(2)}) %collective-permute-start.14) | collective-permute-done | bytes 319520 | tf_op jit(solution)/shard_map/ppermute | solution.py:27
  122.3 1.9 collective-permute-start.16
  125.0 4.6 %collective-permute-start.17 = (bf16[96,1664]{1,0:T(8,128)(2,1)S(1)}, bf16[96,1664]{1,0:T(8,128)(2,1)S(1)}, u32[]{:S(2)}, u32[]{:S(2)}) collective-permute-start(bf16[96,1664]{1,0:T(8,128)(2,1)S(1)} %collective-permute-done.15), channel_id=1, source_target_pairs={{0,224},{32,0},{64,32},{96,64},{128,96},{160,128},{192,160},{224,1... | collective-permute-start | bytes 958472 | tf_op jit(solution)/shard_map/ppermute | solution.py:27
  129.5 1.0 slice_dynamic-update-slice_fusion.11
  130.6 3.5 %collective-permute-done.16 = bf16[96,1664]{1,0:T(8,128)(2,1)S(1)} collective-permute-done((bf16[96,1664]{1,0:T(8,128)(2,1)}, bf16[96,1664]{1,0:T(8,128)(2,1)S(1)}, u32[]{:S(2)}, u32[]{:S(2)}) %collective-permute-start.16) | collective-permute-done | bytes 319520 | tf_op jit(solution)/shard_map/ppermute | solution.py:27
  134.1 1.9 collective-permute-start.20
  136.1 5.5 %collective-permute-start.21 = (bf16[48,1664]{1,0:T(8,128)(2,1)S(1)}, bf16[48,1664]{1,0:T(8,128)(2,1)S(1)}, u32[]{:S(2)}, u32[]{:S(2)}) collective-permute-start(bf16[48,1664]{1,0:T(8,128)(2,1)S(1)} %slice.270), channel_id=1, source_target_pairs={{0,192},{32,224},{64,0},{96,32},{128,64},{160,96},{192,128},{224,1... | collective-permute-start | bytes 479240 | tf_op jit(solution)/shard_map/ppermute | solution.py:27
  141.6 2.7 %collective-permute-start.18 = (bf16[96,1664]{1,0:T(8,128)(2,1)S(1)}, bf16[96,1664]{1,0:T(8,128)(2,1)S(1)}, u32[]{:S(2)}, u32[]{:S(2)}) collective-permute-start(bf16[96,1664]{1,0:T(8,128)(2,1)S(1)} %collective-permute-done.16), channel_id=1, source_target_pairs={{0,32},{32,64},{64,96},{96,128},{128,160},{160,192},{192,224},{224... | collective-permute-start | bytes 958472 | tf_op jit(solution)/shard_map/ppermute | solution.py:27
  144.3 3.8 %collective-permute-start.19 = (bf16[96,1664]{1,0:T(8,128)(2,1)S(1)}, bf16[96,1664]{1,0:T(8,128)(2,1)S(1)}, u32[]{:S(2)}, u32[]{:S(2)}) collective-permute-start(bf16[96,1664]{1,0:T(8,128)(2,1)S(1)} %collective-permute-done.17), channel_id=1, source_target_pairs={{0,224},{32,0},{64,32},{96,64},{128,96},{160,128},{192,160},{224,1... | collective-permute-start | bytes 958472 | tf_op jit(solution)/shard_map/ppermute | solution.py:27
  148.2 2.3 %collective-permute-done.18 = bf16[96,1664]{1,0:T(8,128)(2,1)S(1)} collective-permute-done((bf16[96,1664]{1,0:T(8,128)(2,1)S(1)}, bf16[96,1664]{1,0:T(8,128)(2,1)S(1)}, u32[]{:S(2)}, u32[]{:S(2)}) %collective-permute-start.18) | collective-permute-done | bytes 319520 | tf_op jit(solution)/shard_map/ppermute | solution.py:27
  150.5 1.8 collective-permute-done.19
  154.5 1.2 pad_maximum_fusion
  155.7 6.2 %all-to-all-start.1 = ((bf16[4,200,896]{2,1,0:T(8,128)(2,1)}), bf16[4,200,896]{2,1,0:T(8,128)(2,1)S(1)}, u32[]{:S(2)}, u32[]{:S(2)}) async-start(bf16[4,200,896]{2,1,0:T(8,128)(2,1)} %pad_maximum_fusion), calls=%async_computation.1 | async-start | bytes 2867200 | tf_op jit(solution)/shard_map/all_to_all | solution.py:119
  161.9 3.0 %convolution_convert_fusion.2 = bf16[768,384]{1,0:T(8,128)(2,1)} fusion(bf16[768,768]{1,0:T(8,128)(2,1)} %copy-done.4, bf16[768,384]{1,0:T(8,128)(2,1)S(1)} %maximum_dynamic-update-slice_fusion), kind=kOutput, calls=%fused_computation.5 | convolution fusion | flops 453279744 | bytes 2359296 | tf_op jit(solution)/shard_map/dot_general | solution.py:15
  164.9 16.9 %collective-permute-start.23 = (bf16[768,384]{1,0:T(8,128)(2,1)}, bf16[768,384]{1,0:T(8,128)(2,1)}, u32[]{:S(2)}, u32[]{:S(2)}) collective-permute-start(bf16[768,384]{1,0:T(8,128)(2,1)} %convolution_convert_fusion.2), channel_id=1, source_target_pairs={{0,256},{256,0},{1,257},{257,1},{2,258},{258,2},{3,259},{259,3},{4... | collective-permute-start | bytes 1769480 | tf_op jit(solution)/shard_map/ppermute | solution.py:27
  181.8 1.5 convolution_convert_fusion.3
  183.3 1.9 collective-permute-start.22
  186.3 4.8 %all-to-all-start.2 = ((bf16[4,56,896]{2,1,0:T(8,128)(2,1)}), bf16[4,56,896]{2,1,0:T(8,128)(2,1)S(1)}, u32[]{:S(2)}, u32[]{:S(2)}) async-start(bf16[4,56,896]{2,1,0:T(8,128)(2,1)} %pad_maximum_fusion.2), calls=%async_computation.2 | async-start | bytes 802816 | tf_op jit(solution)/shard_map/all_to_all | solution.py:119
  191.2 2.4 %convert_add_fusion = f32[768,384]{1,0:T(8,128)} fusion(bf16[768,384]{1,0:T(8,128)(2,1)} %collective-permute-done.23, bf16[768,384]{1,0:T(8,128)(2,1)} %convolution_convert_fusion.2), kind=kLoop, calls=%fused_computation.8 | loop fusion | flops 884736 | bytes 2359296 | tf_op jit(solution)/shard_map/add | solution.py:37
  193.6 2.2 %convert_add_fusion.1 = f32[384,768]{1,0:T(8,128)} fusion(bf16[384,768]{1,0:T(8,128)(2,1)S(1)} %collective-permute-done.22, bf16[384,768]{1,0:T(8,128)(2,1)} %convolution_convert_fusion.3), kind=kLoop, calls=%fused_computation.9 | loop fusion | flops 884736 | bytes 2359296 | tf_op jit(solution)/shard_map/add | solution.py:37
  195.8 3.1 %all-to-all-done.2 = bf16[4,56,896]{2,1,0:T(8,128)(2,1)S(1)} async-done(((bf16[4,56,896]{2,1,0:T(8,128)(2,1)}), bf16[4,56,896]{2,1,0:T(8,128)(2,1)S(1)}, u32[]{:S(2)}, u32[]{:S(2)}) %all-to-all-start.2) | async-done | bytes 401440 | tf_op jit(solution)/shard_map/all_to_all | solution.py:119
  199.0 8.0 %collective-permute-start.24 = (f32[384]{0:T(512)S(1)}, f32[384]{0:T(512)S(1)}, u32[]{:S(2)}, u32[]{:S(2)}) collective-permute-start(f32[384]{0:T(512)S(1)} %slice_add_fusion), channel_id=1, source_target_pairs={{0,256},{256,0},{1,257},{257,1},{2,258},{258,2},{3,259},{259,3},{4... | collective-permute-start | bytes 4616 | tf_op jit(solution)/shard_map/ppermute | solution.py:27
  (122 shorter events, 12.4 us)
Async XLA Ops:
  0.6 58.9 %copy-start = (bf16[768,384]{1,0:T(8,128)(2,1)S(1)}, bf16[768,384]{1,0:T(8,128)(2,1)}, u32[]{:S(2)}) copy-start(bf16[768,384]{1,0:T(8,128)(2,1)} %param.8) | copy-start | bytes 1769476
  17.1 27.2 %copy-start.7 = (f32[384]{0:T(512)S(1)}, f32[384]{0:T(512)}, u32[]{:S(2)}) copy-start(f32[384]{0:T(512)} %param.6) | copy-start | bytes 4612
  19.3 24.8 %all-to-all-start = ((f32[16,1,1152]{2,1,0:T(1,128)}), f32[16,1,1152]{2,1,0:T(1,128)S(1)}, u32[]{:S(2)}, u32[]{:S(2)}) async-start(f32[16,1,1152]{2,1,0:T(1,128)} %broadcast_in_dim.53), calls=%async_computation | async-start | bytes 147456 | tf_op jit(solution)/shard_map/all_to_all | solution.py:44
  32.3 12.1 %collective-permute-start = (bf16[192,384]{1,0:T(8,128)(2,1)S(1)}, bf16[192,384]{1,0:T(8,128)(2,1)S(1)}, u32[]{:S(2)}, u32[]{:S(2)}) collective-permute-start(bf16[192,384]{1,0:T(8,128)(2,1)S(1)} %get-tuple-element.58), channel_id=1, source_target_pairs={{0,4},{4,8},{8,12},{12,0},{1,5},{5,9},{9,13},{13,1},{2,6},{6,10},{... | collective-permute-start | bytes 442376 | tf_op jit(solution)/shard_map/ppermute | solution.py:27
  35.4 9.0 %collective-permute-start.1 = (bf16[192,384]{1,0:T(8,128)(2,1)S(1)}, bf16[192,384]{1,0:T(8,128)(2,1)S(1)}, u32[]{:S(2)}, u32[]{:S(2)}) collective-permute-start(bf16[192,384]{1,0:T(8,128)(2,1)S(1)} %get-tuple-element.58), channel_id=1, source_target_pairs={{0,12},{4,0},{8,4},{12,8},{1,13},{5,1},{9,5},{13,9},{2,14},{6,2},{... | collective-permute-start | bytes 442376 | tf_op jit(solution)/shard_map/ppermute | solution.py:27
  44.5 14.1 %collective-permute-start.4 = (bf16[192,384]{1,0:T(8,128)(2,1)S(1)}, bf16[192,384]{1,0:T(8,128)(2,1)S(1)}, u32[]{:S(2)}, u32[]{:S(2)}) collective-permute-start(bf16[192,384]{1,0:T(8,128)(2,1)S(1)} %get-tuple-element.8), channel_id=1, source_target_pairs={{0,8},{4,12},{8,0},{12,4},{1,9},{5,13},{9,1},{13,5},{2,10},{6,14},... | collective-permute-start | bytes 442376 | tf_op jit(solution)/shard_map/ppermute | solution.py:27
  49.2 9.3 %collective-permute-start.2 = (bf16[288,384]{1,0:T(8,128)(2,1)S(1)}, bf16[288,384]{1,0:T(8,128)(2,1)S(1)}, u32[]{:S(2)}, u32[]{:S(2)}) collective-permute-start(bf16[288,384]{1,0:T(8,128)(2,1)S(1)} %get-tuple-element.64), channel_id=1, source_target_pairs={{0,4},{4,8},{8,12},{12,0},{1,5},{5,9},{9,13},{13,1},{2,6},{6,10},{... | collective-permute-start | bytes 663560 | tf_op jit(solution)/shard_map/ppermute | solution.py:27
  51.4 7.1 %collective-permute-start.3 = (bf16[288,384]{1,0:T(8,128)(2,1)S(1)}, bf16[288,384]{1,0:T(8,128)(2,1)S(1)}, u32[]{:S(2)}, u32[]{:S(2)}) collective-permute-start(bf16[288,384]{1,0:T(8,128)(2,1)S(1)} %get-tuple-element.65), channel_id=1, source_target_pairs={{0,12},{4,0},{8,4},{12,8},{1,13},{5,1},{9,5},{13,9},{2,14},{6,2},{... | collective-permute-start | bytes 663560 | tf_op jit(solution)/shard_map/ppermute | solution.py:27
  55.7 2.9 %copy-start.1 = (bf16[384,768]{1,0:T(8,128)(2,1)S(1)}, bf16[384,768]{1,0:T(8,128)(2,1)}, u32[]{:S(2)}) copy-start(bf16[384,768]{1,0:T(8,128)(2,1)} %param.7) | copy-start | bytes 1769476
  60.6 12.8 %collective-permute-start.5 = (bf16[96,1536]{1,0:T(8,128)(2,1)S(1)}, bf16[96,1536]{1,0:T(8,128)(2,1)S(1)}, u32[]{:S(2)}, u32[]{:S(2)}) collective-permute-start(bf16[96,1536]{1,0:T(8,128)(2,1)S(1)} %pad_maximum_fusion.4), channel_id=1, source_target_pairs={{0,32},{32,64},{64,96},{96,128},{128,160},{160,192},{192,224},{224... | collective-permute-start | bytes 884744 | tf_op jit(solution)/shard_map/ppermute | solution.py:27
  62.6 10.7 %collective-permute-start.6 = (bf16[48,1536]{1,0:T(8,128)(2,1)S(1)}, bf16[48,1536]{1,0:T(8,128)(2,1)S(1)}, u32[]{:S(2)}, u32[]{:S(2)}) collective-permute-start(bf16[48,1536]{1,0:T(8,128)(2,1)S(1)} %get-tuple-element.56), channel_id=1, source_target_pairs={{0,64},{32,96},{64,128},{96,160},{128,192},{160,224},{192,0},{224,... | collective-permute-start | bytes 442376 | tf_op jit(solution)/shard_map/ppermute | solution.py:27
  65.5 10.9 %collective-permute-start.10 = (bf16[48,1536]{1,0:T(8,128)(2,1)S(1)}, bf16[48,1536]{1,0:T(8,128)(2,1)S(1)}, u32[]{:S(2)}, u32[]{:S(2)}) collective-permute-start(bf16[48,1536]{1,0:T(8,128)(2,1)S(1)} %get-tuple-element.57), channel_id=1, source_target_pairs={{0,192},{32,224},{64,0},{96,32},{128,64},{160,96},{192,128},{224,1... | collective-permute-start | bytes 442376 | tf_op jit(solution)/shard_map/ppermute | solution.py:27
  70.1 9.1 %collective-permute-start.9 = (bf16[96,1536]{1,0:T(8,128)(2,1)S(1)}, bf16[96,1536]{1,0:T(8,128)(2,1)S(1)}, u32[]{:S(2)}, u32[]{:S(2)}) collective-permute-start(bf16[96,1536]{1,0:T(8,128)(2,1)S(1)} %pad_maximum_fusion.6), channel_id=1, source_target_pairs={{0,224},{32,0},{64,32},{96,64},{128,96},{160,128},{192,160},{224,1... | collective-permute-start | bytes 884744 | tf_op jit(solution)/shard_map/ppermute | solution.py:27
  73.5 9.2 %collective-permute-start.7 = (bf16[96,1536]{1,0:T(8,128)(2,1)S(1)}, bf16[96,1536]{1,0:T(8,128)(2,1)S(1)}, u32[]{:S(2)}, u32[]{:S(2)}) collective-permute-start(bf16[96,1536]{1,0:T(8,128)(2,1)S(1)} %pad_maximum_fusion.5), channel_id=1, source_target_pairs={{0,32},{32,64},{64,96},{96,128},{128,160},{160,192},{192,224},{224... | collective-permute-start | bytes 884744 | tf_op jit(solution)/shard_map/ppermute | solution.py:27
  79.2 8.3 %collective-permute-start.11 = (bf16[96,1536]{1,0:T(8,128)(2,1)S(1)}, bf16[96,1536]{1,0:T(8,128)(2,1)S(1)}, u32[]{:S(2)}, u32[]{:S(2)}) collective-permute-start(bf16[96,1536]{1,0:T(8,128)(2,1)S(1)} %pad_maximum_fusion.7), channel_id=1, source_target_pairs={{0,224},{32,0},{64,32},{96,64},{128,96},{160,128},{192,160},{224,1... | collective-permute-start | bytes 884744 | tf_op jit(solution)/shard_map/ppermute | solution.py:27
  82.8 9.2 %collective-permute-start.8 = (bf16[96,1536]{1,0:T(8,128)(2,1)S(1)}, bf16[96,1536]{1,0:T(8,128)(2,1)S(1)}, u32[]{:S(2)}, u32[]{:S(2)}) collective-permute-start(bf16[96,1536]{1,0:T(8,128)(2,1)S(1)} %add_convert_fusion.2), channel_id=1, source_target_pairs={{0,32},{32,64},{64,96},{96,128},{128,160},{160,192},{192,224},{224... | collective-permute-start | bytes 884744 | tf_op jit(solution)/shard_map/ppermute | solution.py:27
  87.7 9.2 %collective-permute-start.12 = (bf16[96,1536]{1,0:T(8,128)(2,1)S(1)}, bf16[96,1536]{1,0:T(8,128)(2,1)S(1)}, u32[]{:S(2)}, u32[]{:S(2)}) collective-permute-start(bf16[96,1536]{1,0:T(8,128)(2,1)S(1)} %add_convert_fusion.1), channel_id=1, source_target_pairs={{0,224},{32,0},{64,32},{96,64},{128,96},{160,128},{192,160},{224,1... | collective-permute-start | bytes 884744 | tf_op jit(solution)/shard_map/ppermute | solution.py:27
  97.0 13.6 %collective-permute-start.13 = (bf16[96,1536]{1,0:T(8,128)(2,1)S(1)}, bf16[96,1536]{1,0:T(8,128)(2,1)S(1)}, u32[]{:S(2)}, u32[]{:S(2)}) collective-permute-start(bf16[96,1536]{1,0:T(8,128)(2,1)S(1)} %add_convert_fusion), channel_id=1, source_target_pairs={{0,16},{16,0},{1,17},{17,1},{2,18},{18,2},{3,19},{19,3},{4,20},{20... | collective-permute-start | bytes 884744 | tf_op jit(solution)/shard_map/ppermute | solution.py:27
  111.1 1.0 copy-start.2
  112.4 9.9 %collective-permute-start.14 = (bf16[96,1664]{1,0:T(8,128)(2,1)S(1)}, bf16[96,1664]{1,0:T(8,128)(2,1)}, u32[]{:S(2)}, u32[]{:S(2)}) collective-permute-start(bf16[96,1664]{1,0:T(8,128)(2,1)S(1)} %pad_maximum_fusion.3), channel_id=1, source_target_pairs={{0,32},{32,64},{64,96},{96,128},{128,160},{160,192},{192,224},{224... | collective-permute-start | bytes 958472 | tf_op jit(solution)/shard_map/ppermute | solution.py:27
  114.3 15.2 %copy-start.3 = (bf16[768,768]{1,0:T(8,128)(2,1)S(1)}, bf16[768,768]{1,0:T(8,128)(2,1)}, u32[]{:S(2)}) copy-start(bf16[768,768]{1,0:T(8,128)(2,1)} %copy-done.2) | copy-start | bytes 3538948
  114.3 10.7 %collective-permute-start.15 = (bf16[96,1664]{1,0:T(8,128)(2,1)S(1)}, bf16[96,1664]{1,0:T(8,128)(2,1)S(1)}, u32[]{:S(2)}, u32[]{:S(2)}) collective-permute-start(bf16[96,1664]{1,0:T(8,128)(2,1)S(1)} %pad_maximum_fusion.3), channel_id=1, source_target_pairs={{0,224},{32,0},{64,32},{96,64},{128,96},{160,128},{192,160},{224,1... | collective-permute-start | bytes 958472 | tf_op jit(solution)/shard_map/ppermute | solution.py:27
  122.3 11.8 %collective-permute-start.16 = (bf16[96,1664]{1,0:T(8,128)(2,1)}, bf16[96,1664]{1,0:T(8,128)(2,1)S(1)}, u32[]{:S(2)}, u32[]{:S(2)}) collective-permute-start(bf16[96,1664]{1,0:T(8,128)(2,1)} %collective-permute-done.14), channel_id=1, source_target_pairs={{0,32},{32,64},{64,96},{96,128},{128,160},{160,192},{192,224},{224... | collective-permute-start | bytes 958472 | tf_op jit(solution)/shard_map/ppermute | solution.py:27
  125.0 11.1 %collective-permute-start.17 = (bf16[96,1664]{1,0:T(8,128)(2,1)S(1)}, bf16[96,1664]{1,0:T(8,128)(2,1)S(1)}, u32[]{:S(2)}, u32[]{:S(2)}) collective-permute-start(bf16[96,1664]{1,0:T(8,128)(2,1)S(1)} %collective-permute-done.15), channel_id=1, source_target_pairs={{0,224},{32,0},{64,32},{96,64},{128,96},{160,128},{192,160},{224,1... | collective-permute-start | bytes 958472 | tf_op jit(solution)/shard_map/ppermute | solution.py:27
  134.1 18.2 %collective-permute-start.20 = (bf16[48,1664]{1,0:T(8,128)(2,1)S(1)}, bf16[48,1664]{1,0:T(8,128)(2,1)S(1)}, u32[]{:S(2)}, u32[]{:S(2)}) collective-permute-start(bf16[48,1664]{1,0:T(8,128)(2,1)S(1)} %slice.268), channel_id=1, source_target_pairs={{0,64},{32,96},{64,128},{96,160},{128,192},{160,224},{192,0},{224,... | collective-permute-start | bytes 479240 | tf_op jit(solution)/shard_map/ppermute | solution.py:27
  136.1 16.3 %collective-permute-start.21 = (bf16[48,1664]{1,0:T(8,128)(2,1)S(1)}, bf16[48,1664]{1,0:T(8,128)(2,1)S(1)}, u32[]{:S(2)}, u32[]{:S(2)}) collective-permute-start(bf16[48,1664]{1,0:T(8,128)(2,1)S(1)} %slice.270), channel_id=1, source_target_pairs={{0,192},{32,224},{64,0},{96,32},{128,64},{160,96},{192,128},{224,1... | collective-permute-start | bytes 479240 | tf_op jit(solution)/shard_map/ppermute | solution.py:27
  141.6 8.9 %collective-permute-start.18 = (bf16[96,1664]{1,0:T(8,128)(2,1)S(1)}, bf16[96,1664]{1,0:T(8,128)(2,1)S(1)}, u32[]{:S(2)}, u32[]{:S(2)}) collective-permute-start(bf16[96,1664]{1,0:T(8,128)(2,1)S(1)} %collective-permute-done.16), channel_id=1, source_target_pairs={{0,32},{32,64},{64,96},{96,128},{128,160},{160,192},{192,224},{224... | collective-permute-start | bytes 958472 | tf_op jit(solution)/shard_map/ppermute | solution.py:27
  144.3 8.0 %collective-permute-start.19 = (bf16[96,1664]{1,0:T(8,128)(2,1)S(1)}, bf16[96,1664]{1,0:T(8,128)(2,1)S(1)}, u32[]{:S(2)}, u32[]{:S(2)}) collective-permute-start(bf16[96,1664]{1,0:T(8,128)(2,1)S(1)} %collective-permute-done.17), channel_id=1, source_target_pairs={{0,224},{32,0},{64,32},{96,64},{128,96},{160,128},{192,160},{224,1... | collective-permute-start | bytes 958472 | tf_op jit(solution)/shard_map/ppermute | solution.py:27
  152.4 1.0 copy-start.5
  152.4 1.9 copy-start.4
  155.7 29.5 %all-to-all-start.1 = ((bf16[4,200,896]{2,1,0:T(8,128)(2,1)}), bf16[4,200,896]{2,1,0:T(8,128)(2,1)S(1)}, u32[]{:S(2)}, u32[]{:S(2)}) async-start(bf16[4,200,896]{2,1,0:T(8,128)(2,1)} %pad_maximum_fusion), calls=%async_computation.1 | async-start | bytes 2867200 | tf_op jit(solution)/shard_map/all_to_all | solution.py:119
  161.9 19.9 %copy-start.6 = (bf16[768,768]{1,0:T(8,128)(2,1)S(1)}, bf16[768,768]{1,0:T(8,128)(2,1)}, u32[]{:S(2)}) copy-start(bf16[768,768]{1,0:T(8,128)(2,1)} %copy-done.5) | copy-start | bytes 3538948
  164.9 26.3 %collective-permute-start.23 = (bf16[768,384]{1,0:T(8,128)(2,1)}, bf16[768,384]{1,0:T(8,128)(2,1)}, u32[]{:S(2)}, u32[]{:S(2)}) collective-permute-start(bf16[768,384]{1,0:T(8,128)(2,1)} %convolution_convert_fusion.2), channel_id=1, source_target_pairs={{0,256},{256,0},{1,257},{257,1},{2,258},{258,2},{3,259},{259,3},{4... | collective-permute-start | bytes 1769480 | tf_op jit(solution)/shard_map/ppermute | solution.py:27
  183.3 10.3 %collective-permute-start.22 = (bf16[384,768]{1,0:T(8,128)(2,1)}, bf16[384,768]{1,0:T(8,128)(2,1)S(1)}, u32[]{:S(2)}, u32[]{:S(2)}) collective-permute-start(bf16[384,768]{1,0:T(8,128)(2,1)} %convolution_convert_fusion.3), channel_id=1, source_target_pairs={{0,256},{256,0},{1,257},{257,1},{2,258},{258,2},{3,259},{259,3},{4... | collective-permute-start | bytes 1769480 | tf_op jit(solution)/shard_map/ppermute | solution.py:27
  186.3 12.7 %all-to-all-start.2 = ((bf16[4,56,896]{2,1,0:T(8,128)(2,1)}), bf16[4,56,896]{2,1,0:T(8,128)(2,1)S(1)}, u32[]{:S(2)}, u32[]{:S(2)}) async-start(bf16[4,56,896]{2,1,0:T(8,128)(2,1)} %pad_maximum_fusion.2), calls=%async_computation.2 | async-start | bytes 802816 | tf_op jit(solution)/shard_map/all_to_all | solution.py:119
  199.0 9.5 %collective-permute-start.24 = (f32[384]{0:T(512)S(1)}, f32[384]{0:T(512)S(1)}, u32[]{:S(2)}, u32[]{:S(2)}) collective-permute-start(f32[384]{0:T(512)S(1)} %slice_add_fusion), channel_id=1, source_target_pairs={{0,256},{256,0},{1,257},{257,1},{2,258},{258,2},{3,259},{259,3},{4... | collective-permute-start | bytes 4616 | tf_op jit(solution)/shard_map/ppermute | solution.py:27

commit v6 on v5

--- a/solution.py
+++ b/solution.py
@@ -100,27 +100,24 @@
     block = jnp.concatenate(blocks, axis=1)
     panels = put(panels, block, 0)
     below = above = block
-    for by in range(1, size // 2 - 1):
+    for by in range(1, size // 2):
         below, above = shift(below, axis, size, 1), shift(above, axis, size, -1)
         panels = put(put(panels, below, -by), above, by)
-    by = size // 2
-    low = shift(below, axis, size, 1), shift(below[:half], axis, size, 2)
-    high = shift(above, axis, size, -1), shift(above[half:], axis, size, -2)
-    panels = put(put(panels, low[0], 1 - by), high[0], by - 1)
-    return put(put(panels, low[1], by), high[1], by, half)
+    panels = put(panels, shift(below[:half], axis, size, 1), size // 2)
+    return put(panels, shift(above[half:], axis, size, -1), size // 2, half)
 
 
 def scatter(sent, vector, axis, size):
     width, long = sent.shape[1], vector.shape[0]
-    row = jnp.pad(jnp.concatenate(split_high_low(vector)), (0, width - 2 * long))
+    rows = [jnp.pad(term, (0, width - long))[None] for term in split_high_low(vector)]
+    rows = jnp.concatenate(rows + [jnp.zeros((6, width), BF16)], axis=0)
     parts = jnp.concatenate(
-        [sent.reshape(size, -1, width), jnp.broadcast_to(row, (size, 8, width))], axis=1
+        [sent.reshape(size, -1, width), jnp.broadcast_to(rows, (size, 8, width))], axis=1
     )
     back = lax.all_to_all(parts, axis, 0, 0, tiled=True)
     rows = back.shape[1] - 8
-    row = jnp.sum(back[:, rows].astype(F32), axis=0)
-    total = jnp.sum(back[:, :rows].astype(F32), axis=0)
-    return total, row[:long] + row[long : 2 * long]
+    high, low = jnp.sum(back[:, rows : rows + 2, :long].astype(F32), axis=0)
+    return jnp.sum(back[:, :rows].astype(F32), axis=0), high + low
 
 
 def shards(patches, norm_gain, w_in, w_out, out_grad):
@@ -200,17 +197,17 @@
     shares = jnp.zeros((rows, LANES), BF16)
     for place, term in enumerate(split_high_low(first) + split_high_low(second)):
         shares = jnp.where(lane == place, term, shares)
-    hidden_panel, pre_grad_panel, shares = gather_ring(
-        [activation.astype(BF16), pre_grad, shares], "y", Y
-    )
+    hidden_panel = lax.all_gather(activation.astype(BF16), "y", axis=0, tiled=True)
+    pre_grad_panel, shares = gather_ring([pre_grad, shares], "y", Y)
     branch_part = jnp.dot(hidden_panel, w_out, preferred_element_type=F32).astype(BF16)
     normed_grad_part = contract_last(pre_grad_panel, w_in)
     gain_part = jnp.sum(normed_grad_part * normed_panel.astype(F32), axis=0)
-    sent = row_major(
-        jnp.concatenate([branch_part, normed_grad_part.astype(BF16), shares], axis=1)
-    )
+    sent = row_major(jnp.concatenate([normed_grad_part.astype(BF16), shares], axis=1))
     back, gain_sum = scatter(sent, gain_part, "x", X)
-    back, gain_sum = scatter(back.astype(BF16), gain_sum, "zl", ZL)
+    branch = lax.all_to_all(branch_part.reshape(X, -1, width), "x", 0, 0, tiled=True)
+    branch = jnp.sum(branch.astype(F32), axis=0)
+    back = jnp.concatenate([branch, back], axis=1).astype(BF16)
+    back, gain_sum = scatter(back, gain_sum, "zl", ZL)
     branch = back[:, :width].astype(BF16)
     normed_grad = back[:, width : 2 * width]
     rest = back[:, 2 * width :]

time: 210 us -> 229 us (1.090)
  between operations: 1.55 us -> 14.9 us
  starting transfers between devices: 128 us -> 138 us
  waiting for transfers between devices: 38.3 us -> 32.1 us
  local copies, waits for them, and re-layouts: 5.57 us -> 2.78 us
  matrix products: 7.62 us -> 10 us
    ppermute x25, waiting for transfers between devices: 29.8 us -> 23.6 us  [shift(): lax.ppermute(values, axis, [(i, (i + by) % size) for i in range(size)])]
    all_to_all x0 -> x1, starting transfers between devices: none -> 4.52 us  [shards(): lax.all_to_all(branch_part.reshape(X, -1, width), 'x', 0, 0, tiled=True)]
    all_to_all x2, starting transfers between devices: 11 us -> 14.3 us  [scatter(): back = lax.all_to_all(parts, axis, 0, 0, tiled=True)]
    ppermute x25, starting transfers between devices: 104 us -> 107 us  [shift(): lax.ppermute(values, axis, [(i, (i + by) % size) for i in range(size)])]
  transfers between devices with their start and end apart: 28 -> 30, of which waited for: 13 -> 13; matrix products, arithmetic and copies ran while one was open for 7% -> 8% of each run, Pallas kernels for 0% -> 0%
where the time goes in v6:
time: 229 us; the launch traced here: 227 us
  starting transfers between devices  138 us (60%)
  waiting for transfers between devices  32.1 us (14%)
  blocking collectives  15.6 us (7%)
  between operations  14.9 us (7%)
  other arithmetic  13.4 us (6%)
  matrix products  10 us (4%)
  local copies, waits for them, and re-layouts  2.78 us (1%)
    ppermute x25, starting transfers between devices, shift(): lax.ppermute(values, axis, [(i, (i + by) % size) for i in range(size)])  107 us
    ppermute x25, waiting for transfers between devices, shift(): lax.ppermute(values, axis, [(i, (i + by) % size) for i in range(size)])  23.6 us
    all_gather x1, blocking collectives, shards(): lax.all_gather(jnp.concatenate([patches, out_grad], axis=1), 'zl', axis=0...  15.6 us
    all_to_all x2, starting transfers between devices, scatter(): back = lax.all_to_all(parts, axis, 0, 0, tiled=True)  14.3 us
    all_to_all x1, starting transfers between devices, to_all(): return lax.all_to_all(copies, axes, 0, 0, tiled=True)  12.9 us
    all_to_all x1, waiting for transfers between devices, to_all(): return lax.all_to_all(copies, axes, 0, 0, tiled=True)  5.26 us
    dot_general x2, matrix products, contract_tokens(): lax.dot_general(left, right, (((0,), (0,)), ((), ())), preferred_element_...  4.82 us
    add x3, other arithmetic, add(): total = total + term.astype(F32)  4.63 us
  transfers between devices with their start and end apart: 30, of which 13 were waited for; matrix products, arithmetic and copies ran while one was open for 8% of the time, Pallas kernels for 0%

profile of v6, /device:TPU:1, one launch (start us, length us, event | category | flops | bytes accessed | tf_op | source)
XLA Modules:
  0.0 227.3 jit_solution(16171754619078416044)
XLA Ops:
  7.2 0.9 pad_maximum_fusion.13
  8.0 15.6 %all_gather.6 = bf16[192,768]{1,0:T(8,128)(2,1)S(1)} all-gather(bf16[48,768]{1,0:T(8,128)(2,1)S(1)} %pad_maximum_fusion.13), channel_id=1, replica_groups=mesh['dp'=2,'y'=8,'zh'=2,'x'=4,'zl'=4] {'zl'}, dimensions={0}, use_global_device_ids=true | all-gather | bytes 368640 | tf_op jit(solution)/shard_map/all_gather | solution.py:127
  23.8 1.3 multiply_reduce_fusion.1
  25.8 12.9 %all-to-all-start = ((f32[16,1,1152]{2,1,0:T(1,128)}), f32[16,1,1152]{2,1,0:T(1,128)S(1)}, u32[]{:S(2)}, u32[]{:S(2)}) async-start(f32[16,1,1152]{2,1,0:T(1,128)} %broadcast_in_dim.74), calls=%async_computation | async-start | bytes 147456 | tf_op jit(solution)/shard_map/all_to_all | solution.py:44
  38.9 3.1 %collective-permute-start = (bf16[192,384]{1,0:T(8,128)(2,1)S(1)}, bf16[192,384]{1,0:T(8,128)(2,1)S(1)}, u32[]{:S(2)}, u32[]{:S(2)}) collective-permute-start(bf16[192,384]{1,0:T(8,128)(2,1)S(1)} %get-tuple-element.45), channel_id=1, source_target_pairs={{0,4},{4,8},{8,12},{12,0},{1,5},{5,9},{9,13},{13,1},{2,6},{6,10},{... | collective-permute-start | bytes 442376 | tf_op jit(solution)/shard_map/ppermute | solution.py:27
  42.0 3.4 %collective-permute-start.1 = (bf16[192,384]{1,0:T(8,128)(2,1)S(1)}, bf16[192,384]{1,0:T(8,128)(2,1)S(1)}, u32[]{:S(2)}, u32[]{:S(2)}) collective-permute-start(bf16[192,384]{1,0:T(8,128)(2,1)S(1)} %get-tuple-element.45), channel_id=1, source_target_pairs={{0,12},{4,0},{8,4},{12,8},{1,13},{5,1},{9,5},{13,9},{2,14},{6,2},{... | collective-permute-start | bytes 442376 | tf_op jit(solution)/shard_map/ppermute | solution.py:27
  45.4 5.3 %all-to-all-done = f32[16,1,1152]{2,1,0:T(1,128)S(1)} async-done(((f32[16,1,1152]{2,1,0:T(1,128)}), f32[16,1,1152]{2,1,0:T(1,128)S(1)}, u32[]{:S(2)}, u32[]{:S(2)}) %all-to-all-start) | async-done | bytes 73760 | tf_op jit(solution)/shard_map/all_to_all | solution.py:44
  51.0 4.7 %collective-permute-start.4 = (bf16[192,384]{1,0:T(8,128)(2,1)S(1)}, bf16[192,384]{1,0:T(8,128)(2,1)S(1)}, u32[]{:S(2)}, u32[]{:S(2)}) collective-permute-start(bf16[192,384]{1,0:T(8,128)(2,1)S(1)} %get-tuple-element.8), channel_id=1, source_target_pairs={{0,8},{4,12},{8,0},{12,4},{1,9},{5,13},{9,1},{13,5},{2,10},{6,14},... | collective-permute-start | bytes 442376 | tf_op jit(solution)/shard_map/ppermute | solution.py:27
  55.7 2.2 collective-permute-start.2
  57.9 4.3 %collective-permute-start.3 = (bf16[288,384]{1,0:T(8,128)(2,1)S(1)}, bf16[288,384]{1,0:T(8,128)(2,1)S(1)}, u32[]{:S(2)}, u32[]{:S(2)}) collective-permute-start(bf16[288,384]{1,0:T(8,128)(2,1)S(1)} %get-tuple-element.48), channel_id=1, source_target_pairs={{0,12},{4,0},{8,4},{12,8},{1,13},{5,1},{9,5},{13,9},{2,14},{6,2},{... | collective-permute-start | bytes 663560 | tf_op jit(solution)/shard_map/ppermute | solution.py:27
  62.4 2.6 %collective-permute-done.2 = bf16[288,384]{1,0:T(8,128)(2,1)S(1)} collective-permute-done((bf16[288,384]{1,0:T(8,128)(2,1)S(1)}, bf16[288,384]{1,0:T(8,128)(2,1)S(1)}, u32[]{:S(2)}, u32[]{:S(2)}) %collective-permute-start.2) | collective-permute-done | bytes 221216 | tf_op jit(solution)/shard_map/ppermute | solution.py:27
  67.1 2.0 collective-permute-start.5
  69.2 2.9 %collective-permute-start.6 = (bf16[48,1536]{1,0:T(8,128)(2,1)S(1)}, bf16[48,1536]{1,0:T(8,128)(2,1)S(1)}, u32[]{:S(2)}, u32[]{:S(2)}) collective-permute-start(bf16[48,1536]{1,0:T(8,128)(2,1)S(1)} %get-tuple-element.43), channel_id=1, source_target_pairs={{0,64},{32,96},{64,128},{96,160},{128,192},{160,224},{192,0},{224,... | collective-permute-start | bytes 442376 | tf_op jit(solution)/shard_map/ppermute | solution.py:27
  72.1 4.5 %collective-permute-start.10 = (bf16[48,1536]{1,0:T(8,128)(2,1)S(1)}, bf16[48,1536]{1,0:T(8,128)(2,1)S(1)}, u32[]{:S(2)}, u32[]{:S(2)}) collective-permute-start(bf16[48,1536]{1,0:T(8,128)(2,1)S(1)} %get-tuple-element.44), channel_id=1, source_target_pairs={{0,192},{32,224},{64,0},{96,32},{128,64},{160,96},{192,128},{224,1... | collective-permute-start | bytes 442376 | tf_op jit(solution)/shard_map/ppermute | solution.py:27
  76.6 3.3 %collective-permute-start.9 = (bf16[96,1536]{1,0:T(8,128)(2,1)S(1)}, bf16[96,1536]{1,0:T(8,128)(2,1)S(1)}, u32[]{:S(2)}, u32[]{:S(2)}) collective-permute-start(bf16[96,1536]{1,0:T(8,128)(2,1)S(1)} %pad_maximum_fusion.5), channel_id=1, source_target_pairs={{0,224},{32,0},{64,32},{96,64},{128,96},{160,128},{192,160},{224,1... | collective-permute-start | bytes 884744 | tf_op jit(solution)/shard_map/ppermute | solution.py:27
  80.0 2.9 %collective-permute-start.7 = (bf16[96,1536]{1,0:T(8,128)(2,1)S(1)}, bf16[96,1536]{1,0:T(8,128)(2,1)S(1)}, u32[]{:S(2)}, u32[]{:S(2)}) collective-permute-start(bf16[96,1536]{1,0:T(8,128)(2,1)S(1)} %pad_maximum_fusion.4), channel_id=1, source_target_pairs={{0,32},{32,64},{64,96},{96,128},{128,160},{160,192},{192,224},{224... | collective-permute-start | bytes 884744 | tf_op jit(solution)/shard_map/ppermute | solution.py:27
  82.9 2.7 %collective-permute-done.9 = bf16[96,1536]{1,0:T(8,128)(2,1)S(1)} collective-permute-done((bf16[96,1536]{1,0:T(8,128)(2,1)S(1)}, bf16[96,1536]{1,0:T(8,128)(2,1)S(1)}, u32[]{:S(2)}, u32[]{:S(2)}) %collective-permute-start.9) | collective-permute-done | bytes 294944 | tf_op jit(solution)/shard_map/ppermute | solution.py:27
  85.7 3.5 %collective-permute-start.11 = (bf16[96,1536]{1,0:T(8,128)(2,1)S(1)}, bf16[96,1536]{1,0:T(8,128)(2,1)S(1)}, u32[]{:S(2)}, u32[]{:S(2)}) collective-permute-start(bf16[96,1536]{1,0:T(8,128)(2,1)S(1)} %pad_maximum_fusion.6), channel_id=1, source_target_pairs={{0,224},{32,0},{64,32},{96,64},{128,96},{160,128},{192,160},{224,1... | collective-permute-start | bytes 884744 | tf_op jit(solution)/shard_map/ppermute | solution.py:27
  89.3 2.4 %collective-permute-start.8 = (bf16[96,1536]{1,0:T(8,128)(2,1)S(1)}, bf16[96,1536]{1,0:T(8,128)(2,1)S(1)}, u32[]{:S(2)}, u32[]{:S(2)}) collective-permute-start(bf16[96,1536]{1,0:T(8,128)(2,1)S(1)} %add_convert_fusion.2), channel_id=1, source_target_pairs={{0,32},{32,64},{64,96},{96,128},{128,160},{160,192},{192,224},{224... | collective-permute-start | bytes 884744 | tf_op jit(solution)/shard_map/ppermute | solution.py:27
  91.7 2.4 %collective-permute-done.11 = bf16[96,1536]{1,0:T(8,128)(2,1)S(1)} collective-permute-done((bf16[96,1536]{1,0:T(8,128)(2,1)S(1)}, bf16[96,1536]{1,0:T(8,128)(2,1)S(1)}, u32[]{:S(2)}, u32[]{:S(2)}) %collective-permute-start.11) | collective-permute-done | bytes 294944 | tf_op jit(solution)/shard_map/ppermute | solution.py:27
  94.2 4.0 %collective-permute-start.12 = (bf16[96,1536]{1,0:T(8,128)(2,1)S(1)}, bf16[96,1536]{1,0:T(8,128)(2,1)S(1)}, u32[]{:S(2)}, u32[]{:S(2)}) collective-permute-start(bf16[96,1536]{1,0:T(8,128)(2,1)S(1)} %add_convert_fusion.1), channel_id=1, source_target_pairs={{0,224},{32,0},{64,32},{96,64},{128,96},{160,128},{192,160},{224,1... | collective-permute-start | bytes 884744 | tf_op jit(solution)/shard_map/ppermute | solution.py:27
  98.5 5.0 %collective-permute-done.12 = bf16[96,1536]{1,0:T(8,128)(2,1)S(1)} collective-permute-done((bf16[96,1536]{1,0:T(8,128)(2,1)S(1)}, bf16[96,1536]{1,0:T(8,128)(2,1)S(1)}, u32[]{:S(2)}, u32[]{:S(2)}) %collective-permute-start.12) | collective-permute-done | bytes 294944 | tf_op jit(solution)/shard_map/ppermute | solution.py:27
  103.6 6.7 %collective-permute-start.13 = (bf16[96,1536]{1,0:T(8,128)(2,1)S(1)}, bf16[96,1536]{1,0:T(8,128)(2,1)S(1)}, u32[]{:S(2)}, u32[]{:S(2)}) collective-permute-start(bf16[96,1536]{1,0:T(8,128)(2,1)S(1)} %add_convert_fusion), channel_id=1, source_target_pairs={{0,16},{16,0},{1,17},{17,1},{2,18},{18,2},{3,19},{19,3},{4,20},{20... | collective-permute-start | bytes 884744 | tf_op jit(solution)/shard_map/ppermute | solution.py:27
  110.4 6.8 %collective-permute-done.13 = bf16[96,1536]{1,0:T(8,128)(2,1)S(1)} collective-permute-done((bf16[96,1536]{1,0:T(8,128)(2,1)S(1)}, bf16[96,1536]{1,0:T(8,128)(2,1)S(1)}, u32[]{:S(2)}, u32[]{:S(2)}) %collective-permute-start.13) | collective-permute-done | bytes 294944 | tf_op jit(solution)/shard_map/ppermute | solution.py:27
  117.3 1.0 fusion
  119.2 1.9 collective-permute-start.14
  121.2 5.3 %collective-permute-start.15 = (bf16[96,896]{1,0:T(8,128)(2,1)}, bf16[96,896]{1,0:T(8,128)(2,1)S(1)}, u32[]{:S(2)}, u32[]{:S(2)}) collective-permute-start(bf16[96,896]{1,0:T(8,128)(2,1)} %pad_maximum_fusion.9), channel_id=1, source_target_pairs={{0,224},{32,0},{64,32},{96,64},{128,96},{160,128},{192,160},{224,1... | collective-permute-start | bytes 516104 | tf_op jit(solution)/shard_map/ppermute | solution.py:27
  126.6 0.9 collective-permute-done.14
  127.4 1.9 collective-permute-start.16
  129.4 4.6 %collective-permute-start.17 = (bf16[96,896]{1,0:T(8,128)(2,1)S(1)}, bf16[96,896]{1,0:T(8,128)(2,1)S(1)}, u32[]{:S(2)}, u32[]{:S(2)}) collective-permute-start(bf16[96,896]{1,0:T(8,128)(2,1)S(1)} %collective-permute-done.15), channel_id=1, source_target_pairs={{0,224},{32,0},{64,32},{96,64},{128,96},{160,128},{192,160},{224,1... | collective-permute-start | bytes 516104 | tf_op jit(solution)/shard_map/ppermute | solution.py:27
  134.8 1.9 collective-permute-start.18
  136.7 4.6 %collective-permute-start.19 = (bf16[96,896]{1,0:T(8,128)(2,1)S(1)}, bf16[96,896]{1,0:T(8,128)(2,1)S(1)}, u32[]{:S(2)}, u32[]{:S(2)}) collective-permute-start(bf16[96,896]{1,0:T(8,128)(2,1)S(1)} %collective-permute-done.17), channel_id=1, source_target_pairs={{0,224},{32,0},{64,32},{96,64},{128,96},{160,128},{192,160},{224,1... | collective-permute-start | bytes 516104 | tf_op jit(solution)/shard_map/ppermute | solution.py:27
  142.1 1.9 collective-permute-start.20
  144.1 4.6 %collective-permute-start.21 = (bf16[48,896]{1,0:T(8,128)(2,1)S(1)}, bf16[48,896]{1,0:T(8,128)(2,1)S(1)}, u32[]{:S(2)}, u32[]{:S(2)}) collective-permute-start(bf16[48,896]{1,0:T(8,128)(2,1)S(1)} %slice.222), channel_id=1, source_target_pairs={{0,224},{32,0},{64,32},{96,64},{128,96},{160,128},{192,160},{224,1... | collective-permute-start | bytes 258056 | tf_op jit(solution)/shard_map/ppermute | solution.py:27
  148.8 1.4 collective-permute-done.21
  151.5 1.0 pad_maximum_fusion
  152.4 8.2 %all-to-all-start.2 = ((bf16[4,200,512]{2,1,0:T(8,128)(2,1)}), bf16[4,200,512]{2,1,0:T(8,128)(2,1)S(1)}, u32[]{:S(2)}, u32[]{:S(2)}) async-start(bf16[4,200,512]{2,1,0:T(8,128)(2,1)} %pad_maximum_fusion), calls=%async_computation.2 | async-start | bytes 1638400 | tf_op jit(solution)/shard_map/all_to_all | solution.py:117
  160.6 1.9 convolution_convert_fusion.3
  162.5 16.7 %collective-permute-start.22 = (bf16[384,768]{1,0:T(8,128)(2,1)S(1)}, bf16[384,768]{1,0:T(8,128)(2,1)}, u32[]{:S(2)}, u32[]{:S(2)}) collective-permute-start(bf16[384,768]{1,0:T(8,128)(2,1)S(1)} %convolution_convert_fusion.3), channel_id=1, source_target_pairs={{0,256},{256,0},{1,257},{257,1},{2,258},{258,2},{3,259},{259,3},{4... | collective-permute-start | bytes 1769480 | tf_op jit(solution)/shard_map/ppermute | solution.py:27
  179.4 2.9 %convolution_convert_fusion.4 = bf16[768,384]{1,0:T(8,128)(2,1)} fusion(bf16[768,768]{1,0:T(8,128)(2,1)} %all-gather.2.cloned.1.call-done, bf16[768,384]{1,0:T(8,128)(2,1)S(1)} %copy-done), kind=kOutput, calls=%fused_computation.4 | convolution fusion | flops 453279744 | bytes 2359296 | tf_op jit(solution)/shard_map/dot_general | solution.py:202
  182.3 4.5 %all-to-all-start.1 = ((bf16[4,192,384]{2,1,0:T(8,128)(2,1)}), bf16[4,192,384]{2,1,0:T(8,128)(2,1)S(1)}, u32[]{:S(2)}, u32[]{:S(2)}) async-start(bf16[4,192,384]{2,1,0:T(8,128)(2,1)} %bitcast), calls=%async_computation.1 | async-start | bytes 1179648 | tf_op jit(solution)/shard_map/all_to_all | solution.py:207
  186.8 2.9 %convolution_convert_fusion.2 = bf16[768,384]{1,0:T(8,128)(2,1)} fusion(bf16[768,768]{1,0:T(8,128)(2,1)} %all-gather.2.cloned.1.call-done, bf16[768,384]{1,0:T(8,128)(2,1)S(1)} %maximum_dynamic-update-slice_fusion), kind=kOutput, calls=%fused_computation.2 | convolution fusion | flops 453279744 | bytes 2359296 | tf_op jit(solution)/shard_map/dot_general | solution.py:15
  189.7 6.7 %collective-permute-start.23 = (bf16[768,384]{1,0:T(8,128)(2,1)}, bf16[768,384]{1,0:T(8,128)(2,1)}, u32[]{:S(2)}, u32[]{:S(2)}) collective-permute-start(bf16[768,384]{1,0:T(8,128)(2,1)} %convolution_convert_fusion.2), channel_id=1, source_target_pairs={{0,256},{256,0},{1,257},{257,1},{2,258},{258,2},{3,259},{259,3},{4... | collective-permute-start | bytes 1769480 | tf_op jit(solution)/shard_map/ppermute | solution.py:27
  197.4 6.2 %all-to-all-start.3 = ((bf16[4,56,896]{2,1,0:T(8,128)(2,1)}), bf16[4,56,896]{2,1,0:T(8,128)(2,1)S(1)}, u32[]{:S(2)}, u32[]{:S(2)}) async-start(bf16[4,56,896]{2,1,0:T(8,128)(2,1)} %pad_maximum_fusion.2), calls=%async_computation.3 | async-start | bytes 802816 | tf_op jit(solution)/shard_map/all_to_all | solution.py:117
  203.6 2.2 convert_add_fusion.1
  205.8 2.4 %convert_add_fusion = f32[768,384]{1,0:T(8,128)} fusion(bf16[768,384]{1,0:T(8,128)(2,1)} %collective-permute-done.23, bf16[768,384]{1,0:T(8,128)(2,1)} %convolution_convert_fusion.2), kind=kLoop, calls=%fused_computation.5 | loop fusion | flops 884736 | bytes 2359296 | tf_op jit(solution)/shard_map/add | solution.py:37
  208.2 3.3 %all-to-all-done.3 = bf16[4,56,896]{2,1,0:T(8,128)(2,1)S(1)} async-done(((bf16[4,56,896]{2,1,0:T(8,128)(2,1)}), bf16[4,56,896]{2,1,0:T(8,128)(2,1)S(1)}, u32[]{:S(2)}, u32[]{:S(2)}) %all-to-all-start.3) | async-done | bytes 401440 | tf_op jit(solution)/shard_map/all_to_all | solution.py:117
  211.5 6.8 %collective-permute-start.24 = (f32[384]{0:T(512)S(1)}, f32[384]{0:T(512)S(1)}, u32[]{:S(2)}, u32[]{:S(2)}) collective-permute-start(f32[384]{0:T(512)S(1)} %fusion.20), channel_id=1, source_target_pairs={{0,256},{256,0},{1,257},{257,1},{2,258},{258,2},{3,259},{259,3},{4... | collective-permute-start | bytes 4616 | tf_op jit(solution)/shard_map/ppermute | solution.py:27
  (129 shorter events, 11.8 us)
Async XLA Ops:
  7.2 58.9 %copy-start = (bf16[768,384]{1,0:T(8,128)(2,1)S(1)}, bf16[768,384]{1,0:T(8,128)(2,1)}, u32[]{:S(2)}) copy-start(bf16[768,384]{1,0:T(8,128)(2,1)} %param.8) | copy-start | bytes 1769476
  23.7 27.2 %copy-start.3 = (f32[384]{0:T(512)S(1)}, f32[384]{0:T(512)}, u32[]{:S(2)}) copy-start(f32[384]{0:T(512)} %param.6) | copy-start | bytes 4612
  25.8 24.8 %all-to-all-start = ((f32[16,1,1152]{2,1,0:T(1,128)}), f32[16,1,1152]{2,1,0:T(1,128)S(1)}, u32[]{:S(2)}, u32[]{:S(2)}) async-start(f32[16,1,1152]{2,1,0:T(1,128)} %broadcast_in_dim.74), calls=%async_computation | async-start | bytes 147456 | tf_op jit(solution)/shard_map/all_to_all | solution.py:44
  38.7 140.7 %all-gather.2.cloned.1.call-start = ((), (), s32[]{:S(2)}) async-start(), calls=%async_computation.4 | async-start | bytes 1327104 | tf_op jit(solution)/shard_map/all_gather | solution.py:200
  38.9 12.1 %collective-permute-start = (bf16[192,384]{1,0:T(8,128)(2,1)S(1)}, bf16[192,384]{1,0:T(8,128)(2,1)S(1)}, u32[]{:S(2)}, u32[]{:S(2)}) collective-permute-start(bf16[192,384]{1,0:T(8,128)(2,1)S(1)} %get-tuple-element.45), channel_id=1, source_target_pairs={{0,4},{4,8},{8,12},{12,0},{1,5},{5,9},{9,13},{13,1},{2,6},{6,10},{... | collective-permute-start | bytes 442376 | tf_op jit(solution)/shard_map/ppermute | solution.py:27
  42.0 9.0 %collective-permute-start.1 = (bf16[192,384]{1,0:T(8,128)(2,1)S(1)}, bf16[192,384]{1,0:T(8,128)(2,1)S(1)}, u32[]{:S(2)}, u32[]{:S(2)}) collective-permute-start(bf16[192,384]{1,0:T(8,128)(2,1)S(1)} %get-tuple-element.45), channel_id=1, source_target_pairs={{0,12},{4,0},{8,4},{12,8},{1,13},{5,1},{9,5},{13,9},{2,14},{6,2},{... | collective-permute-start | bytes 442376 | tf_op jit(solution)/shard_map/ppermute | solution.py:27
  51.0 14.1 %collective-permute-start.4 = (bf16[192,384]{1,0:T(8,128)(2,1)S(1)}, bf16[192,384]{1,0:T(8,128)(2,1)S(1)}, u32[]{:S(2)}, u32[]{:S(2)}) collective-permute-start(bf16[192,384]{1,0:T(8,128)(2,1)S(1)} %get-tuple-element.8), channel_id=1, source_target_pairs={{0,8},{4,12},{8,0},{12,4},{1,9},{5,13},{9,1},{13,5},{2,10},{6,14},... | collective-permute-start | bytes 442376 | tf_op jit(solution)/shard_map/ppermute | solution.py:27
  55.7 9.3 %collective-permute-start.2 = (bf16[288,384]{1,0:T(8,128)(2,1)S(1)}, bf16[288,384]{1,0:T(8,128)(2,1)S(1)}, u32[]{:S(2)}, u32[]{:S(2)}) collective-permute-start(bf16[288,384]{1,0:T(8,128)(2,1)S(1)} %get-tuple-element.47), channel_id=1, source_target_pairs={{0,4},{4,8},{8,12},{12,0},{1,5},{5,9},{9,13},{13,1},{2,6},{6,10},{... | collective-permute-start | bytes 663560 | tf_op jit(solution)/shard_map/ppermute | solution.py:27
  57.9 7.1 %collective-permute-start.3 = (bf16[288,384]{1,0:T(8,128)(2,1)S(1)}, bf16[288,384]{1,0:T(8,128)(2,1)S(1)}, u32[]{:S(2)}, u32[]{:S(2)}) collective-permute-start(bf16[288,384]{1,0:T(8,128)(2,1)S(1)} %get-tuple-element.48), channel_id=1, source_target_pairs={{0,12},{4,0},{8,4},{12,8},{1,13},{5,1},{9,5},{13,9},{2,14},{6,2},{... | collective-permute-start | bytes 663560 | tf_op jit(solution)/shard_map/ppermute | solution.py:27
  62.2 2.9 %copy-start.1 = (bf16[384,768]{1,0:T(8,128)(2,1)S(1)}, bf16[384,768]{1,0:T(8,128)(2,1)}, u32[]{:S(2)}) copy-start(bf16[384,768]{1,0:T(8,128)(2,1)} %param.7) | copy-start | bytes 1769476
  67.1 12.8 %collective-permute-start.5 = (bf16[96,1536]{1,0:T(8,128)(2,1)S(1)}, bf16[96,1536]{1,0:T(8,128)(2,1)S(1)}, u32[]{:S(2)}, u32[]{:S(2)}) collective-permute-start(bf16[96,1536]{1,0:T(8,128)(2,1)S(1)} %pad_maximum_fusion.3), channel_id=1, source_target_pairs={{0,32},{32,64},{64,96},{96,128},{128,160},{160,192},{192,224},{224... | collective-permute-start | bytes 884744 | tf_op jit(solution)/shard_map/ppermute | solution.py:27
  69.2 10.7 %collective-permute-start.6 = (bf16[48,1536]{1,0:T(8,128)(2,1)S(1)}, bf16[48,1536]{1,0:T(8,128)(2,1)S(1)}, u32[]{:S(2)}, u32[]{:S(2)}) collective-permute-start(bf16[48,1536]{1,0:T(8,128)(2,1)S(1)} %get-tuple-element.43), channel_id=1, source_target_pairs={{0,64},{32,96},{64,128},{96,160},{128,192},{160,224},{192,0},{224,... | collective-permute-start | bytes 442376 | tf_op jit(solution)/shard_map/ppermute | solution.py:27
  72.1 10.8 %collective-permute-start.10 = (bf16[48,1536]{1,0:T(8,128)(2,1)S(1)}, bf16[48,1536]{1,0:T(8,128)(2,1)S(1)}, u32[]{:S(2)}, u32[]{:S(2)}) collective-permute-start(bf16[48,1536]{1,0:T(8,128)(2,1)S(1)} %get-tuple-element.44), channel_id=1, source_target_pairs={{0,192},{32,224},{64,0},{96,32},{128,64},{160,96},{192,128},{224,1... | collective-permute-start | bytes 442376 | tf_op jit(solution)/shard_map/ppermute | solution.py:27
  76.6 8.9 %collective-permute-start.9 = (bf16[96,1536]{1,0:T(8,128)(2,1)S(1)}, bf16[96,1536]{1,0:T(8,128)(2,1)S(1)}, u32[]{:S(2)}, u32[]{:S(2)}) collective-permute-start(bf16[96,1536]{1,0:T(8,128)(2,1)S(1)} %pad_maximum_fusion.5), channel_id=1, source_target_pairs={{0,224},{32,0},{64,32},{96,64},{128,96},{160,128},{192,160},{224,1... | collective-permute-start | bytes 884744 | tf_op jit(solution)/shard_map/ppermute | solution.py:27
  80.0 9.2 %collective-permute-start.7 = (bf16[96,1536]{1,0:T(8,128)(2,1)S(1)}, bf16[96,1536]{1,0:T(8,128)(2,1)S(1)}, u32[]{:S(2)}, u32[]{:S(2)}) collective-permute-start(bf16[96,1536]{1,0:T(8,128)(2,1)S(1)} %pad_maximum_fusion.4), channel_id=1, source_target_pairs={{0,32},{32,64},{64,96},{96,128},{128,160},{160,192},{192,224},{224... | collective-permute-start | bytes 884744 | tf_op jit(solution)/shard_map/ppermute | solution.py:27
  85.7 8.4 %collective-permute-start.11 = (bf16[96,1536]{1,0:T(8,128)(2,1)S(1)}, bf16[96,1536]{1,0:T(8,128)(2,1)S(1)}, u32[]{:S(2)}, u32[]{:S(2)}) collective-permute-start(bf16[96,1536]{1,0:T(8,128)(2,1)S(1)} %pad_maximum_fusion.6), channel_id=1, source_target_pairs={{0,224},{32,0},{64,32},{96,64},{128,96},{160,128},{192,160},{224,1... | collective-permute-start | bytes 884744 | tf_op jit(solution)/shard_map/ppermute | solution.py:27
  89.3 9.2 %collective-permute-start.8 = (bf16[96,1536]{1,0:T(8,128)(2,1)S(1)}, bf16[96,1536]{1,0:T(8,128)(2,1)S(1)}, u32[]{:S(2)}, u32[]{:S(2)}) collective-permute-start(bf16[96,1536]{1,0:T(8,128)(2,1)S(1)} %add_convert_fusion.2), channel_id=1, source_target_pairs={{0,32},{32,64},{64,96},{96,128},{128,160},{160,192},{192,224},{224... | collective-permute-start | bytes 884744 | tf_op jit(solution)/shard_map/ppermute | solution.py:27
  94.2 9.3 %collective-permute-start.12 = (bf16[96,1536]{1,0:T(8,128)(2,1)S(1)}, bf16[96,1536]{1,0:T(8,128)(2,1)S(1)}, u32[]{:S(2)}, u32[]{:S(2)}) collective-permute-start(bf16[96,1536]{1,0:T(8,128)(2,1)S(1)} %add_convert_fusion.1), channel_id=1, source_target_pairs={{0,224},{32,0},{64,32},{96,64},{128,96},{160,128},{192,160},{224,1... | collective-permute-start | bytes 884744 | tf_op jit(solution)/shard_map/ppermute | solution.py:27
  103.6 13.6 %collective-permute-start.13 = (bf16[96,1536]{1,0:T(8,128)(2,1)S(1)}, bf16[96,1536]{1,0:T(8,128)(2,1)S(1)}, u32[]{:S(2)}, u32[]{:S(2)}) collective-permute-start(bf16[96,1536]{1,0:T(8,128)(2,1)S(1)} %add_convert_fusion), channel_id=1, source_target_pairs={{0,16},{16,0},{1,17},{17,1},{2,18},{18,2},{3,19},{19,3},{4,20},{20... | collective-permute-start | bytes 884744 | tf_op jit(solution)/shard_map/ppermute | solution.py:27
  119.2 8.3 %collective-permute-start.14 = (bf16[96,896]{1,0:T(8,128)(2,1)}, bf16[96,896]{1,0:T(8,128)(2,1)S(1)}, u32[]{:S(2)}, u32[]{:S(2)}) collective-permute-start(bf16[96,896]{1,0:T(8,128)(2,1)} %pad_maximum_fusion.9), channel_id=1, source_target_pairs={{0,32},{32,64},{64,96},{96,128},{128,160},{160,192},{192,224},{224... | collective-permute-start | bytes 516104 | tf_op jit(solution)/shard_map/ppermute | solution.py:27
  121.2 8.2 %collective-permute-start.15 = (bf16[96,896]{1,0:T(8,128)(2,1)}, bf16[96,896]{1,0:T(8,128)(2,1)S(1)}, u32[]{:S(2)}, u32[]{:S(2)}) collective-permute-start(bf16[96,896]{1,0:T(8,128)(2,1)} %pad_maximum_fusion.9), channel_id=1, source_target_pairs={{0,224},{32,0},{64,32},{96,64},{128,96},{160,128},{192,160},{224,1... | collective-permute-start | bytes 516104 | tf_op jit(solution)/shard_map/ppermute | solution.py:27
  127.4 7.3 %collective-permute-start.16 = (bf16[96,896]{1,0:T(8,128)(2,1)S(1)}, bf16[96,896]{1,0:T(8,128)(2,1)S(1)}, u32[]{:S(2)}, u32[]{:S(2)}) collective-permute-start(bf16[96,896]{1,0:T(8,128)(2,1)S(1)} %collective-permute-done.14), channel_id=1, source_target_pairs={{0,32},{32,64},{64,96},{96,128},{128,160},{160,192},{192,224},{224... | collective-permute-start | bytes 516104 | tf_op jit(solution)/shard_map/ppermute | solution.py:27
  129.4 7.3 %collective-permute-start.17 = (bf16[96,896]{1,0:T(8,128)(2,1)S(1)}, bf16[96,896]{1,0:T(8,128)(2,1)S(1)}, u32[]{:S(2)}, u32[]{:S(2)}) collective-permute-start(bf16[96,896]{1,0:T(8,128)(2,1)S(1)} %collective-permute-done.15), channel_id=1, source_target_pairs={{0,224},{32,0},{64,32},{96,64},{128,96},{160,128},{192,160},{224,1... | collective-permute-start | bytes 516104 | tf_op jit(solution)/shard_map/ppermute | solution.py:27
  134.8 7.3 %collective-permute-start.18 = (bf16[96,896]{1,0:T(8,128)(2,1)S(1)}, bf16[96,896]{1,0:T(8,128)(2,1)S(1)}, u32[]{:S(2)}, u32[]{:S(2)}) collective-permute-start(bf16[96,896]{1,0:T(8,128)(2,1)S(1)} %collective-permute-done.16), channel_id=1, source_target_pairs={{0,32},{32,64},{64,96},{96,128},{128,160},{160,192},{192,224},{224... | collective-permute-start | bytes 516104 | tf_op jit(solution)/shard_map/ppermute | solution.py:27
  136.7 7.3 %collective-permute-start.19 = (bf16[96,896]{1,0:T(8,128)(2,1)S(1)}, bf16[96,896]{1,0:T(8,128)(2,1)S(1)}, u32[]{:S(2)}, u32[]{:S(2)}) collective-permute-start(bf16[96,896]{1,0:T(8,128)(2,1)S(1)} %collective-permute-done.17), channel_id=1, source_target_pairs={{0,224},{32,0},{64,32},{96,64},{128,96},{160,128},{192,160},{224,1... | collective-permute-start | bytes 516104 | tf_op jit(solution)/shard_map/ppermute | solution.py:27
  142.1 6.7 %collective-permute-start.20 = (bf16[48,896]{1,0:T(8,128)(2,1)S(1)}, bf16[48,896]{1,0:T(8,128)(2,1)S(1)}, u32[]{:S(2)}, u32[]{:S(2)}) collective-permute-start(bf16[48,896]{1,0:T(8,128)(2,1)S(1)} %slice.220), channel_id=1, source_target_pairs={{0,32},{32,64},{64,96},{96,128},{128,160},{160,192},{192,224},{224... | collective-permute-start | bytes 258056 | tf_op jit(solution)/shard_map/ppermute | solution.py:27
  144.1 6.1 %collective-permute-start.21 = (bf16[48,896]{1,0:T(8,128)(2,1)S(1)}, bf16[48,896]{1,0:T(8,128)(2,1)S(1)}, u32[]{:S(2)}, u32[]{:S(2)}) collective-permute-start(bf16[48,896]{1,0:T(8,128)(2,1)S(1)} %slice.222), channel_id=1, source_target_pairs={{0,224},{32,0},{64,32},{96,64},{128,96},{160,128},{192,160},{224,1... | collective-permute-start | bytes 258056 | tf_op jit(solution)/shard_map/ppermute | solution.py:27
  150.2 1.0 copy-start.2
  152.4 26.8 %all-to-all-start.2 = ((bf16[4,200,512]{2,1,0:T(8,128)(2,1)}), bf16[4,200,512]{2,1,0:T(8,128)(2,1)S(1)}, u32[]{:S(2)}, u32[]{:S(2)}) async-start(bf16[4,200,512]{2,1,0:T(8,128)(2,1)} %pad_maximum_fusion), calls=%async_computation.2 | async-start | bytes 1638400 | tf_op jit(solution)/shard_map/all_to_all | solution.py:117
  162.5 41.1 %collective-permute-start.22 = (bf16[384,768]{1,0:T(8,128)(2,1)S(1)}, bf16[384,768]{1,0:T(8,128)(2,1)}, u32[]{:S(2)}, u32[]{:S(2)}) collective-permute-start(bf16[384,768]{1,0:T(8,128)(2,1)S(1)} %convolution_convert_fusion.3), channel_id=1, source_target_pairs={{0,256},{256,0},{1,257},{257,1},{2,258},{258,2},{3,259},{259,3},{4... | collective-permute-start | bytes 1769480 | tf_op jit(solution)/shard_map/ppermute | solution.py:27
  182.3 14.2 %all-to-all-start.1 = ((bf16[4,192,384]{2,1,0:T(8,128)(2,1)}), bf16[4,192,384]{2,1,0:T(8,128)(2,1)S(1)}, u32[]{:S(2)}, u32[]{:S(2)}) async-start(bf16[4,192,384]{2,1,0:T(8,128)(2,1)} %bitcast), calls=%async_computation.1 | async-start | bytes 1179648 | tf_op jit(solution)/shard_map/all_to_all | solution.py:207
  189.7 16.1 %collective-permute-start.23 = (bf16[768,384]{1,0:T(8,128)(2,1)}, bf16[768,384]{1,0:T(8,128)(2,1)}, u32[]{:S(2)}, u32[]{:S(2)}) collective-permute-start(bf16[768,384]{1,0:T(8,128)(2,1)} %convolution_convert_fusion.2), channel_id=1, source_target_pairs={{0,256},{256,0},{1,257},{257,1},{2,258},{258,2},{3,259},{259,3},{4... | collective-permute-start | bytes 1769480 | tf_op jit(solution)/shard_map/ppermute | solution.py:27
  197.4 14.1 %all-to-all-start.3 = ((bf16[4,56,896]{2,1,0:T(8,128)(2,1)}), bf16[4,56,896]{2,1,0:T(8,128)(2,1)S(1)}, u32[]{:S(2)}, u32[]{:S(2)}) async-start(bf16[4,56,896]{2,1,0:T(8,128)(2,1)} %pad_maximum_fusion.2), calls=%async_computation.3 | async-start | bytes 802816 | tf_op jit(solution)/shard_map/all_to_all | solution.py:117
  211.5 8.3 %collective-permute-start.24 = (f32[384]{0:T(512)S(1)}, f32[384]{0:T(512)S(1)}, u32[]{:S(2)}, u32[]{:S(2)}) collective-permute-start(f32[384]{0:T(512)S(1)} %fusion.20), channel_id=1, source_target_pairs={{0,256},{256,0},{1,257},{257,1},{2,258},{258,2},{3,259},{259,3},{4... | collective-permute-start | bytes 4616 | tf_op jit(solution)/shard_map/ppermute | solution.py:27
Sparse Core Ops, SparseCore 0:
  126.6 50.3 all-gather.1

commit v7 on v5

--- a/solution.py
+++ b/solution.py
@@ -100,14 +100,11 @@
     block = jnp.concatenate(blocks, axis=1)
     panels = put(panels, block, 0)
     below = above = block
-    for by in range(1, size // 2 - 1):
+    for by in range(1, size // 2):
         below, above = shift(below, axis, size, 1), shift(above, axis, size, -1)
         panels = put(put(panels, below, -by), above, by)
-    by = size // 2
-    low = shift(below, axis, size, 1), shift(below[:half], axis, size, 2)
-    high = shift(above, axis, size, -1), shift(above[half:], axis, size, -2)
-    panels = put(put(panels, low[0], 1 - by), high[0], by - 1)
-    return put(put(panels, low[1], by), high[1], by, half)
+    panels = put(panels, shift(below[:half], axis, size, 1), size // 2)
+    return put(panels, shift(above[half:], axis, size, -1), size // 2, half)
 
 
 def scatter(sent, vector, axis, size):

time: 210 us -> 210 us (level)
  transfers between devices with their start and end apart: 28 -> 28, of which waited for: 13 -> 14; matrix products, arithmetic and copies ran while one was open for 7% -> 8% of each run, Pallas kernels for 0% -> 0%
where the time goes in v7:
time: 210 us; the launch traced here: 208 us
  starting transfers between devices  126 us (60%)
  waiting for transfers between devices  38.4 us (18%)
  blocking collectives  15.6 us (7%)
  other arithmetic  12.3 us (6%)
  matrix products  7.62 us (4%)
  local copies, waits for them, and re-layouts  7.27 us (3%)
    ppermute x25, starting transfers between devices, shift(): lax.ppermute(values, axis, [(i, (i + by) % size) for i in range(size)])  103 us
    ppermute x25, waiting for transfers between devices, shift(): lax.ppermute(values, axis, [(i, (i + by) % size) for i in range(size)])  30 us
    all_gather x1, blocking collectives, shards(): lax.all_gather(jnp.concatenate([patches, out_grad], axis=1), 'zl', axis=0...  15.6 us
    all_to_all x1, starting transfers between devices, to_all(): return lax.all_to_all(copies, axes, 0, 0, tiled=True)  12.9 us
    all_to_all x2, starting transfers between devices, scatter(): back = lax.all_to_all(parts, axis, 0, 0, tiled=True)  10.2 us
    all_to_all x1, waiting for transfers between devices, to_all(): return lax.all_to_all(copies, axes, 0, 0, tiled=True)  5.31 us
    add x3, other arithmetic, add(): total = total + term.astype(F32)  4.66 us
    dot_general x2, matrix products, contract_tokens(): lax.dot_general(left, right, (((0,), (0,)), ((), ())), preferred_element_...  4.48 us
  transfers between devices with their start and end apart: 28, of which 14 were waited for; matrix products, arithmetic and copies ran while one was open for 8% of the time, Pallas kernels for 0%

profile of v7, /device:TPU:1, one launch (start us, length us, event | category | flops | bytes accessed | tf_op | source)
XLA Modules:
  0.0 208.4 jit_solution(17888844750479949158)
XLA Ops:
  1.5 15.6 %all_gather.3 = bf16[192,768]{1,0:T(8,128)(2,1)S(1)} all-gather(bf16[48,768]{1,0:T(8,128)(2,1)S(1)} %pad_maximum_fusion.13), channel_id=1, replica_groups=mesh['dp'=2,'y'=8,'zh'=2,'x'=4,'zl'=4] {'zl'}, dimensions={0}, use_global_device_ids=true | all-gather | bytes 368640 | tf_op jit(solution)/shard_map/all_gather | solution.py:127
  17.3 1.3 multiply_reduce_fusion.1
  19.3 12.9 %all-to-all-start = ((f32[16,1,1152]{2,1,0:T(1,128)}), f32[16,1,1152]{2,1,0:T(1,128)S(1)}, u32[]{:S(2)}, u32[]{:S(2)}) async-start(f32[16,1,1152]{2,1,0:T(1,128)} %broadcast_in_dim.53), calls=%async_computation | async-start | bytes 147456 | tf_op jit(solution)/shard_map/all_to_all | solution.py:44
  32.3 3.1 %collective-permute-start = (bf16[192,384]{1,0:T(8,128)(2,1)S(1)}, bf16[192,384]{1,0:T(8,128)(2,1)S(1)}, u32[]{:S(2)}, u32[]{:S(2)}) collective-permute-start(bf16[192,384]{1,0:T(8,128)(2,1)S(1)} %get-tuple-element.58), channel_id=1, source_target_pairs={{0,4},{4,8},{8,12},{12,0},{1,5},{5,9},{9,13},{13,1},{2,6},{6,10},{... | collective-permute-start | bytes 442376 | tf_op jit(solution)/shard_map/ppermute | solution.py:27
  35.4 3.4 %collective-permute-start.1 = (bf16[192,384]{1,0:T(8,128)(2,1)S(1)}, bf16[192,384]{1,0:T(8,128)(2,1)S(1)}, u32[]{:S(2)}, u32[]{:S(2)}) collective-permute-start(bf16[192,384]{1,0:T(8,128)(2,1)S(1)} %get-tuple-element.58), channel_id=1, source_target_pairs={{0,12},{4,0},{8,4},{12,8},{1,13},{5,1},{9,5},{13,9},{2,14},{6,2},{... | collective-permute-start | bytes 442376 | tf_op jit(solution)/shard_map/ppermute | solution.py:27
  38.8 5.3 %all-to-all-done = f32[16,1,1152]{2,1,0:T(1,128)S(1)} async-done(((f32[16,1,1152]{2,1,0:T(1,128)}), f32[16,1,1152]{2,1,0:T(1,128)S(1)}, u32[]{:S(2)}, u32[]{:S(2)}) %all-to-all-start) | async-done | bytes 73760 | tf_op jit(solution)/shard_map/all_to_all | solution.py:44
  44.5 4.7 %collective-permute-start.4 = (bf16[192,384]{1,0:T(8,128)(2,1)S(1)}, bf16[192,384]{1,0:T(8,128)(2,1)S(1)}, u32[]{:S(2)}, u32[]{:S(2)}) collective-permute-start(bf16[192,384]{1,0:T(8,128)(2,1)S(1)} %get-tuple-element.8), channel_id=1, source_target_pairs={{0,8},{4,12},{8,0},{12,4},{1,9},{5,13},{9,1},{13,5},{2,10},{6,14},... | collective-permute-start | bytes 442376 | tf_op jit(solution)/shard_map/ppermute | solution.py:27
  49.2 2.2 %collective-permute-start.2 = (bf16[288,384]{1,0:T(8,128)(2,1)S(1)}, bf16[288,384]{1,0:T(8,128)(2,1)S(1)}, u32[]{:S(2)}, u32[]{:S(2)}) collective-permute-start(bf16[288,384]{1,0:T(8,128)(2,1)S(1)} %get-tuple-element.64), channel_id=1, source_target_pairs={{0,4},{4,8},{8,12},{12,0},{1,5},{5,9},{9,13},{13,1},{2,6},{6,10},{... | collective-permute-start | bytes 663560 | tf_op jit(solution)/shard_map/ppermute | solution.py:27
  51.4 4.3 %collective-permute-start.3 = (bf16[288,384]{1,0:T(8,128)(2,1)S(1)}, bf16[288,384]{1,0:T(8,128)(2,1)S(1)}, u32[]{:S(2)}, u32[]{:S(2)}) collective-permute-start(bf16[288,384]{1,0:T(8,128)(2,1)S(1)} %get-tuple-element.65), channel_id=1, source_target_pairs={{0,12},{4,0},{8,4},{12,8},{1,13},{5,1},{9,5},{13,9},{2,14},{6,2},{... | collective-permute-start | bytes 663560 | tf_op jit(solution)/shard_map/ppermute | solution.py:27
  55.9 2.6 %collective-permute-done.2 = bf16[288,384]{1,0:T(8,128)(2,1)S(1)} collective-permute-done((bf16[288,384]{1,0:T(8,128)(2,1)S(1)}, bf16[288,384]{1,0:T(8,128)(2,1)S(1)}, u32[]{:S(2)}, u32[]{:S(2)}) %collective-permute-start.2) | collective-permute-done | bytes 221216 | tf_op jit(solution)/shard_map/ppermute | solution.py:27
  60.6 2.0 collective-permute-start.5
  62.6 2.8 %collective-permute-start.6 = (bf16[48,1536]{1,0:T(8,128)(2,1)S(1)}, bf16[48,1536]{1,0:T(8,128)(2,1)S(1)}, u32[]{:S(2)}, u32[]{:S(2)}) collective-permute-start(bf16[48,1536]{1,0:T(8,128)(2,1)S(1)} %get-tuple-element.56), channel_id=1, source_target_pairs={{0,64},{32,96},{64,128},{96,160},{128,192},{160,224},{192,0},{224,... | collective-permute-start | bytes 442376 | tf_op jit(solution)/shard_map/ppermute | solution.py:27
  65.5 4.5 %collective-permute-start.10 = (bf16[48,1536]{1,0:T(8,128)(2,1)S(1)}, bf16[48,1536]{1,0:T(8,128)(2,1)S(1)}, u32[]{:S(2)}, u32[]{:S(2)}) collective-permute-start(bf16[48,1536]{1,0:T(8,128)(2,1)S(1)} %get-tuple-element.57), channel_id=1, source_target_pairs={{0,192},{32,224},{64,0},{96,32},{128,64},{160,96},{192,128},{224,1... | collective-permute-start | bytes 442376 | tf_op jit(solution)/shard_map/ppermute | solution.py:27
  70.1 3.3 %collective-permute-start.9 = (bf16[96,1536]{1,0:T(8,128)(2,1)S(1)}, bf16[96,1536]{1,0:T(8,128)(2,1)S(1)}, u32[]{:S(2)}, u32[]{:S(2)}) collective-permute-start(bf16[96,1536]{1,0:T(8,128)(2,1)S(1)} %pad_maximum_fusion.6), channel_id=1, source_target_pairs={{0,224},{32,0},{64,32},{96,64},{128,96},{160,128},{192,160},{224,1... | collective-permute-start | bytes 884744 | tf_op jit(solution)/shard_map/ppermute | solution.py:27
  73.5 2.9 %collective-permute-start.7 = (bf16[96,1536]{1,0:T(8,128)(2,1)S(1)}, bf16[96,1536]{1,0:T(8,128)(2,1)S(1)}, u32[]{:S(2)}, u32[]{:S(2)}) collective-permute-start(bf16[96,1536]{1,0:T(8,128)(2,1)S(1)} %pad_maximum_fusion.5), channel_id=1, source_target_pairs={{0,32},{32,64},{64,96},{96,128},{128,160},{160,192},{192,224},{224... | collective-permute-start | bytes 884744 | tf_op jit(solution)/shard_map/ppermute | solution.py:27
  76.3 2.8 %collective-permute-done.9 = bf16[96,1536]{1,0:T(8,128)(2,1)S(1)} collective-permute-done((bf16[96,1536]{1,0:T(8,128)(2,1)S(1)}, bf16[96,1536]{1,0:T(8,128)(2,1)S(1)}, u32[]{:S(2)}, u32[]{:S(2)}) %collective-permute-start.9) | collective-permute-done | bytes 294944 | tf_op jit(solution)/shard_map/ppermute | solution.py:27
  79.2 3.4 %collective-permute-start.11 = (bf16[96,1536]{1,0:T(8,128)(2,1)S(1)}, bf16[96,1536]{1,0:T(8,128)(2,1)S(1)}, u32[]{:S(2)}, u32[]{:S(2)}) collective-permute-start(bf16[96,1536]{1,0:T(8,128)(2,1)S(1)} %pad_maximum_fusion.7), channel_id=1, source_target_pairs={{0,224},{32,0},{64,32},{96,64},{128,96},{160,128},{192,160},{224,1... | collective-permute-start | bytes 884744 | tf_op jit(solution)/shard_map/ppermute | solution.py:27
  82.8 2.3 %collective-permute-start.8 = (bf16[96,1536]{1,0:T(8,128)(2,1)S(1)}, bf16[96,1536]{1,0:T(8,128)(2,1)S(1)}, u32[]{:S(2)}, u32[]{:S(2)}) collective-permute-start(bf16[96,1536]{1,0:T(8,128)(2,1)S(1)} %add_convert_fusion.2), channel_id=1, source_target_pairs={{0,32},{32,64},{64,96},{96,128},{128,160},{160,192},{192,224},{224... | collective-permute-start | bytes 884744 | tf_op jit(solution)/shard_map/ppermute | solution.py:27
  85.1 2.5 %collective-permute-done.11 = bf16[96,1536]{1,0:T(8,128)(2,1)S(1)} collective-permute-done((bf16[96,1536]{1,0:T(8,128)(2,1)S(1)}, bf16[96,1536]{1,0:T(8,128)(2,1)S(1)}, u32[]{:S(2)}, u32[]{:S(2)}) %collective-permute-start.11) | collective-permute-done | bytes 294944 | tf_op jit(solution)/shard_map/ppermute | solution.py:27
  87.7 4.0 %collective-permute-start.12 = (bf16[96,1536]{1,0:T(8,128)(2,1)S(1)}, bf16[96,1536]{1,0:T(8,128)(2,1)S(1)}, u32[]{:S(2)}, u32[]{:S(2)}) collective-permute-start(bf16[96,1536]{1,0:T(8,128)(2,1)S(1)} %add_convert_fusion.1), channel_id=1, source_target_pairs={{0,224},{32,0},{64,32},{96,64},{128,96},{160,128},{192,160},{224,1... | collective-permute-start | bytes 884744 | tf_op jit(solution)/shard_map/ppermute | solution.py:27
  92.0 4.9 %collective-permute-done.12 = bf16[96,1536]{1,0:T(8,128)(2,1)S(1)} collective-permute-done((bf16[96,1536]{1,0:T(8,128)(2,1)S(1)}, bf16[96,1536]{1,0:T(8,128)(2,1)S(1)}, u32[]{:S(2)}, u32[]{:S(2)}) %collective-permute-start.12) | collective-permute-done | bytes 294944 | tf_op jit(solution)/shard_map/ppermute | solution.py:27
  97.0 6.8 %collective-permute-start.13 = (bf16[96,1536]{1,0:T(8,128)(2,1)S(1)}, bf16[96,1536]{1,0:T(8,128)(2,1)S(1)}, u32[]{:S(2)}, u32[]{:S(2)}) collective-permute-start(bf16[96,1536]{1,0:T(8,128)(2,1)S(1)} %add_convert_fusion), channel_id=1, source_target_pairs={{0,16},{16,0},{1,17},{17,1},{2,18},{18,2},{3,19},{19,3},{4,20},{20... | collective-permute-start | bytes 884744 | tf_op jit(solution)/shard_map/ppermute | solution.py:27
  103.8 6.8 %collective-permute-done.13 = bf16[96,1536]{1,0:T(8,128)(2,1)S(1)} collective-permute-done((bf16[96,1536]{1,0:T(8,128)(2,1)S(1)}, bf16[96,1536]{1,0:T(8,128)(2,1)S(1)}, u32[]{:S(2)}, u32[]{:S(2)}) %collective-permute-start.13) | collective-permute-done | bytes 294944 | tf_op jit(solution)/shard_map/ppermute | solution.py:27
  112.4 1.9 collective-permute-start.14
  114.3 5.4 %collective-permute-start.15 = (bf16[96,1664]{1,0:T(8,128)(2,1)S(1)}, bf16[96,1664]{1,0:T(8,128)(2,1)}, u32[]{:S(2)}, u32[]{:S(2)}) collective-permute-start(bf16[96,1664]{1,0:T(8,128)(2,1)S(1)} %pad_maximum_fusion.3), channel_id=1, source_target_pairs={{0,224},{32,0},{64,32},{96,64},{128,96},{160,128},{192,160},{224,1... | collective-permute-start | bytes 958472 | tf_op jit(solution)/shard_map/ppermute | solution.py:27
  119.9 2.4 %collective-permute-done.14 = bf16[96,1664]{1,0:T(8,128)(2,1)} collective-permute-done((bf16[96,1664]{1,0:T(8,128)(2,1)S(1)}, bf16[96,1664]{1,0:T(8,128)(2,1)}, u32[]{:S(2)}, u32[]{:S(2)}) %collective-permute-start.14) | collective-permute-done | bytes 319520 | tf_op jit(solution)/shard_map/ppermute | solution.py:27
  122.3 1.9 collective-permute-start.16
  124.2 4.6 %collective-permute-start.17 = (bf16[96,1664]{1,0:T(8,128)(2,1)}, bf16[96,1664]{1,0:T(8,128)(2,1)S(1)}, u32[]{:S(2)}, u32[]{:S(2)}) collective-permute-start(bf16[96,1664]{1,0:T(8,128)(2,1)} %collective-permute-done.15), channel_id=1, source_target_pairs={{0,224},{32,0},{64,32},{96,64},{128,96},{160,128},{192,160},{224,1... | collective-permute-start | bytes 958472 | tf_op jit(solution)/shard_map/ppermute | solution.py:27
  128.8 1.0 slice_dynamic-update-slice_fusion.11
  129.8 1.0 slice_dynamic-update-slice_fusion.10
  132.3 1.8 collective-permute-done.16
  134.1 1.9 collective-permute-start.18
  136.1 4.6 %collective-permute-start.19 = (bf16[96,1664]{1,0:T(8,128)(2,1)S(1)}, bf16[96,1664]{1,0:T(8,128)(2,1)S(1)}, u32[]{:S(2)}, u32[]{:S(2)}) collective-permute-start(bf16[96,1664]{1,0:T(8,128)(2,1)S(1)} %collective-permute-done.17), channel_id=1, source_target_pairs={{0,224},{32,0},{64,32},{96,64},{128,96},{160,128},{192,160},{224,1... | collective-permute-start | bytes 958472 | tf_op jit(solution)/shard_map/ppermute | solution.py:27
  140.7 3.8 %collective-permute-done.18 = bf16[96,1664]{1,0:T(8,128)(2,1)S(1)} collective-permute-done((bf16[96,1664]{1,0:T(8,128)(2,1)S(1)}, bf16[96,1664]{1,0:T(8,128)(2,1)S(1)}, u32[]{:S(2)}, u32[]{:S(2)}) %collective-permute-start.18) | collective-permute-done | bytes 319520 | tf_op jit(solution)/shard_map/ppermute | solution.py:27
  144.5 1.9 collective-permute-start.20
  146.5 4.6 %collective-permute-start.21 = (bf16[48,1664]{1,0:T(8,128)(2,1)S(1)}, bf16[48,1664]{1,0:T(8,128)(2,1)S(1)}, u32[]{:S(2)}, u32[]{:S(2)}) collective-permute-start(bf16[48,1664]{1,0:T(8,128)(2,1)S(1)} %slice.270), channel_id=1, source_target_pairs={{0,224},{32,0},{64,32},{96,64},{128,96},{160,128},{192,160},{224,1... | collective-permute-start | bytes 479240 | tf_op jit(solution)/shard_map/ppermute | solution.py:27
  151.8 1.5 collective-permute-done.21
  155.3 1.2 pad_maximum_fusion
  156.5 5.1 %all-to-all-start.1 = ((bf16[4,200,896]{2,1,0:T(8,128)(2,1)}), bf16[4,200,896]{2,1,0:T(8,128)(2,1)S(1)}, u32[]{:S(2)}, u32[]{:S(2)}) async-start(bf16[4,200,896]{2,1,0:T(8,128)(2,1)} %pad_maximum_fusion), calls=%async_computation.1 | async-start | bytes 2867200 | tf_op jit(solution)/shard_map/all_to_all | solution.py:116
  161.7 3.0 %convolution_convert_fusion.2 = bf16[768,384]{1,0:T(8,128)(2,1)} fusion(bf16[768,768]{1,0:T(8,128)(2,1)} %copy-done.4, bf16[768,384]{1,0:T(8,128)(2,1)S(1)} %maximum_dynamic-update-slice_fusion), kind=kOutput, calls=%fused_computation.5 | convolution fusion | flops 453279744 | bytes 2359296 | tf_op jit(solution)/shard_map/dot_general | solution.py:15
  164.7 16.2 %collective-permute-start.23 = (bf16[768,384]{1,0:T(8,128)(2,1)}, bf16[768,384]{1,0:T(8,128)(2,1)}, u32[]{:S(2)}, u32[]{:S(2)}) collective-permute-start(bf16[768,384]{1,0:T(8,128)(2,1)} %convolution_convert_fusion.2), channel_id=1, source_target_pairs={{0,256},{256,0},{1,257},{257,1},{2,258},{258,2},{3,259},{259,3},{4... | collective-permute-start | bytes 1769480 | tf_op jit(solution)/shard_map/ppermute | solution.py:27
  180.9 1.5 convolution_convert_fusion.3
  182.4 1.9 collective-permute-start.22
  185.4 5.0 %all-to-all-start.2 = ((bf16[4,56,896]{2,1,0:T(8,128)(2,1)}), bf16[4,56,896]{2,1,0:T(8,128)(2,1)S(1)}, u32[]{:S(2)}, u32[]{:S(2)}) async-start(bf16[4,56,896]{2,1,0:T(8,128)(2,1)} %pad_maximum_fusion.2), calls=%async_computation.2 | async-start | bytes 802816 | tf_op jit(solution)/shard_map/all_to_all | solution.py:116
  190.5 2.4 %convert_add_fusion = f32[768,384]{1,0:T(8,128)} fusion(bf16[768,384]{1,0:T(8,128)(2,1)} %collective-permute-done.23, bf16[768,384]{1,0:T(8,128)(2,1)} %convolution_convert_fusion.2), kind=kLoop, calls=%fused_computation.8 | loop fusion | flops 884736 | bytes 2359296 | tf_op jit(solution)/shard_map/add | solution.py:37
  192.9 2.2 %convert_add_fusion.1 = f32[384,768]{1,0:T(8,128)} fusion(bf16[384,768]{1,0:T(8,128)(2,1)S(1)} %collective-permute-done.22, bf16[384,768]{1,0:T(8,128)(2,1)} %convolution_convert_fusion.3), kind=kLoop, calls=%fused_computation.9 | loop fusion | flops 884736 | bytes 2359296 | tf_op jit(solution)/shard_map/add | solution.py:37
  195.1 3.1 %all-to-all-done.2 = bf16[4,56,896]{2,1,0:T(8,128)(2,1)S(1)} async-done(((bf16[4,56,896]{2,1,0:T(8,128)(2,1)}), bf16[4,56,896]{2,1,0:T(8,128)(2,1)S(1)}, u32[]{:S(2)}, u32[]{:S(2)}) %all-to-all-start.2) | async-done | bytes 401440 | tf_op jit(solution)/shard_map/all_to_all | solution.py:116
  198.3 8.0 %collective-permute-start.24 = (f32[384]{0:T(512)S(1)}, f32[384]{0:T(512)S(1)}, u32[]{:S(2)}, u32[]{:S(2)}) collective-permute-start(f32[384]{0:T(512)S(1)} %slice_add_fusion), channel_id=1, source_target_pairs={{0,256},{256,0},{1,257},{257,1},{2,258},{258,2},{3,259},{259,3},{4... | collective-permute-start | bytes 4616 | tf_op jit(solution)/shard_map/ppermute | solution.py:27
  (122 shorter events, 14.6 us)
Async XLA Ops:
  0.6 58.9 %copy-start = (bf16[768,384]{1,0:T(8,128)(2,1)S(1)}, bf16[768,384]{1,0:T(8,128)(2,1)}, u32[]{:S(2)}) copy-start(bf16[768,384]{1,0:T(8,128)(2,1)} %param.8) | copy-start | bytes 1769476
  17.1 27.2 %copy-start.7 = (f32[384]{0:T(512)S(1)}, f32[384]{0:T(512)}, u32[]{:S(2)}) copy-start(f32[384]{0:T(512)} %param.6) | copy-start | bytes 4612
  19.3 24.8 %all-to-all-start = ((f32[16,1,1152]{2,1,0:T(1,128)}), f32[16,1,1152]{2,1,0:T(1,128)S(1)}, u32[]{:S(2)}, u32[]{:S(2)}) async-start(f32[16,1,1152]{2,1,0:T(1,128)} %broadcast_in_dim.53), calls=%async_computation | async-start | bytes 147456 | tf_op jit(solution)/shard_map/all_to_all | solution.py:44
  32.3 12.1 %collective-permute-start = (bf16[192,384]{1,0:T(8,128)(2,1)S(1)}, bf16[192,384]{1,0:T(8,128)(2,1)S(1)}, u32[]{:S(2)}, u32[]{:S(2)}) collective-permute-start(bf16[192,384]{1,0:T(8,128)(2,1)S(1)} %get-tuple-element.58), channel_id=1, source_target_pairs={{0,4},{4,8},{8,12},{12,0},{1,5},{5,9},{9,13},{13,1},{2,6},{6,10},{... | collective-permute-start | bytes 442376 | tf_op jit(solution)/shard_map/ppermute | solution.py:27
  35.4 9.0 %collective-permute-start.1 = (bf16[192,384]{1,0:T(8,128)(2,1)S(1)}, bf16[192,384]{1,0:T(8,128)(2,1)S(1)}, u32[]{:S(2)}, u32[]{:S(2)}) collective-permute-start(bf16[192,384]{1,0:T(8,128)(2,1)S(1)} %get-tuple-element.58), channel_id=1, source_target_pairs={{0,12},{4,0},{8,4},{12,8},{1,13},{5,1},{9,5},{13,9},{2,14},{6,2},{... | collective-permute-start | bytes 442376 | tf_op jit(solution)/shard_map/ppermute | solution.py:27
  44.5 14.1 %collective-permute-start.4 = (bf16[192,384]{1,0:T(8,128)(2,1)S(1)}, bf16[192,384]{1,0:T(8,128)(2,1)S(1)}, u32[]{:S(2)}, u32[]{:S(2)}) collective-permute-start(bf16[192,384]{1,0:T(8,128)(2,1)S(1)} %get-tuple-element.8), channel_id=1, source_target_pairs={{0,8},{4,12},{8,0},{12,4},{1,9},{5,13},{9,1},{13,5},{2,10},{6,14},... | collective-permute-start | bytes 442376 | tf_op jit(solution)/shard_map/ppermute | solution.py:27
  49.2 9.3 %collective-permute-start.2 = (bf16[288,384]{1,0:T(8,128)(2,1)S(1)}, bf16[288,384]{1,0:T(8,128)(2,1)S(1)}, u32[]{:S(2)}, u32[]{:S(2)}) collective-permute-start(bf16[288,384]{1,0:T(8,128)(2,1)S(1)} %get-tuple-element.64), channel_id=1, source_target_pairs={{0,4},{4,8},{8,12},{12,0},{1,5},{5,9},{9,13},{13,1},{2,6},{6,10},{... | collective-permute-start | bytes 663560 | tf_op jit(solution)/shard_map/ppermute | solution.py:27
  51.4 7.1 %collective-permute-start.3 = (bf16[288,384]{1,0:T(8,128)(2,1)S(1)}, bf16[288,384]{1,0:T(8,128)(2,1)S(1)}, u32[]{:S(2)}, u32[]{:S(2)}) collective-permute-start(bf16[288,384]{1,0:T(8,128)(2,1)S(1)} %get-tuple-element.65), channel_id=1, source_target_pairs={{0,12},{4,0},{8,4},{12,8},{1,13},{5,1},{9,5},{13,9},{2,14},{6,2},{... | collective-permute-start | bytes 663560 | tf_op jit(solution)/shard_map/ppermute | solution.py:27
  55.7 2.9 %copy-start.1 = (bf16[384,768]{1,0:T(8,128)(2,1)S(1)}, bf16[384,768]{1,0:T(8,128)(2,1)}, u32[]{:S(2)}) copy-start(bf16[384,768]{1,0:T(8,128)(2,1)} %param.7) | copy-start | bytes 1769476
  60.6 12.8 %collective-permute-start.5 = (bf16[96,1536]{1,0:T(8,128)(2,1)S(1)}, bf16[96,1536]{1,0:T(8,128)(2,1)S(1)}, u32[]{:S(2)}, u32[]{:S(2)}) collective-permute-start(bf16[96,1536]{1,0:T(8,128)(2,1)S(1)} %pad_maximum_fusion.4), channel_id=1, source_target_pairs={{0,32},{32,64},{64,96},{96,128},{128,160},{160,192},{192,224},{224... | collective-permute-start | bytes 884744 | tf_op jit(solution)/shard_map/ppermute | solution.py:27
  62.6 10.7 %collective-permute-start.6 = (bf16[48,1536]{1,0:T(8,128)(2,1)S(1)}, bf16[48,1536]{1,0:T(8,128)(2,1)S(1)}, u32[]{:S(2)}, u32[]{:S(2)}) collective-permute-start(bf16[48,1536]{1,0:T(8,128)(2,1)S(1)} %get-tuple-element.56), channel_id=1, source_target_pairs={{0,64},{32,96},{64,128},{96,160},{128,192},{160,224},{192,0},{224,... | collective-permute-start | bytes 442376 | tf_op jit(solution)/shard_map/ppermute | solution.py:27
  65.5 10.9 %collective-permute-start.10 = (bf16[48,1536]{1,0:T(8,128)(2,1)S(1)}, bf16[48,1536]{1,0:T(8,128)(2,1)S(1)}, u32[]{:S(2)}, u32[]{:S(2)}) collective-permute-start(bf16[48,1536]{1,0:T(8,128)(2,1)S(1)} %get-tuple-element.57), channel_id=1, source_target_pairs={{0,192},{32,224},{64,0},{96,32},{128,64},{160,96},{192,128},{224,1... | collective-permute-start | bytes 442376 | tf_op jit(solution)/shard_map/ppermute | solution.py:27
  70.1 9.1 %collective-permute-start.9 = (bf16[96,1536]{1,0:T(8,128)(2,1)S(1)}, bf16[96,1536]{1,0:T(8,128)(2,1)S(1)}, u32[]{:S(2)}, u32[]{:S(2)}) collective-permute-start(bf16[96,1536]{1,0:T(8,128)(2,1)S(1)} %pad_maximum_fusion.6), channel_id=1, source_target_pairs={{0,224},{32,0},{64,32},{96,64},{128,96},{160,128},{192,160},{224,1... | collective-permute-start | bytes 884744 | tf_op jit(solution)/shard_map/ppermute | solution.py:27
  73.5 9.2 %collective-permute-start.7 = (bf16[96,1536]{1,0:T(8,128)(2,1)S(1)}, bf16[96,1536]{1,0:T(8,128)(2,1)S(1)}, u32[]{:S(2)}, u32[]{:S(2)}) collective-permute-start(bf16[96,1536]{1,0:T(8,128)(2,1)S(1)} %pad_maximum_fusion.5), channel_id=1, source_target_pairs={{0,32},{32,64},{64,96},{96,128},{128,160},{160,192},{192,224},{224... | collective-permute-start | bytes 884744 | tf_op jit(solution)/shard_map/ppermute | solution.py:27
  79.2 8.3 %collective-permute-start.11 = (bf16[96,1536]{1,0:T(8,128)(2,1)S(1)}, bf16[96,1536]{1,0:T(8,128)(2,1)S(1)}, u32[]{:S(2)}, u32[]{:S(2)}) collective-permute-start(bf16[96,1536]{1,0:T(8,128)(2,1)S(1)} %pad_maximum_fusion.7), channel_id=1, source_target_pairs={{0,224},{32,0},{64,32},{96,64},{128,96},{160,128},{192,160},{224,1... | collective-permute-start | bytes 884744 | tf_op jit(solution)/shard_map/ppermute | solution.py:27
  82.8 9.2 %collective-permute-start.8 = (bf16[96,1536]{1,0:T(8,128)(2,1)S(1)}, bf16[96,1536]{1,0:T(8,128)(2,1)S(1)}, u32[]{:S(2)}, u32[]{:S(2)}) collective-permute-start(bf16[96,1536]{1,0:T(8,128)(2,1)S(1)} %add_convert_fusion.2), channel_id=1, source_target_pairs={{0,32},{32,64},{64,96},{96,128},{128,160},{160,192},{192,224},{224... | collective-permute-start | bytes 884744 | tf_op jit(solution)/shard_map/ppermute | solution.py:27
  87.7 9.2 %collective-permute-start.12 = (bf16[96,1536]{1,0:T(8,128)(2,1)S(1)}, bf16[96,1536]{1,0:T(8,128)(2,1)S(1)}, u32[]{:S(2)}, u32[]{:S(2)}) collective-permute-start(bf16[96,1536]{1,0:T(8,128)(2,1)S(1)} %add_convert_fusion.1), channel_id=1, source_target_pairs={{0,224},{32,0},{64,32},{96,64},{128,96},{160,128},{192,160},{224,1... | collective-permute-start | bytes 884744 | tf_op jit(solution)/shard_map/ppermute | solution.py:27
  97.0 13.6 %collective-permute-start.13 = (bf16[96,1536]{1,0:T(8,128)(2,1)S(1)}, bf16[96,1536]{1,0:T(8,128)(2,1)S(1)}, u32[]{:S(2)}, u32[]{:S(2)}) collective-permute-start(bf16[96,1536]{1,0:T(8,128)(2,1)S(1)} %add_convert_fusion), channel_id=1, source_target_pairs={{0,16},{16,0},{1,17},{17,1},{2,18},{18,2},{3,19},{19,3},{4,20},{20... | collective-permute-start | bytes 884744 | tf_op jit(solution)/shard_map/ppermute | solution.py:27
  111.1 1.0 copy-start.2
  112.4 9.9 %collective-permute-start.14 = (bf16[96,1664]{1,0:T(8,128)(2,1)S(1)}, bf16[96,1664]{1,0:T(8,128)(2,1)}, u32[]{:S(2)}, u32[]{:S(2)}) collective-permute-start(bf16[96,1664]{1,0:T(8,128)(2,1)S(1)} %pad_maximum_fusion.3), channel_id=1, source_target_pairs={{0,32},{32,64},{64,96},{96,128},{128,160},{160,192},{192,224},{224... | collective-permute-start | bytes 958472 | tf_op jit(solution)/shard_map/ppermute | solution.py:27
  114.3 9.9 %collective-permute-start.15 = (bf16[96,1664]{1,0:T(8,128)(2,1)S(1)}, bf16[96,1664]{1,0:T(8,128)(2,1)}, u32[]{:S(2)}, u32[]{:S(2)}) collective-permute-start(bf16[96,1664]{1,0:T(8,128)(2,1)S(1)} %pad_maximum_fusion.3), channel_id=1, source_target_pairs={{0,224},{32,0},{64,32},{96,64},{128,96},{160,128},{192,160},{224,1... | collective-permute-start | bytes 958472 | tf_op jit(solution)/shard_map/ppermute | solution.py:27
  119.7 9.0 %copy-start.3 = (bf16[768,768]{1,0:T(8,128)(2,1)S(1)}, bf16[768,768]{1,0:T(8,128)(2,1)}, u32[]{:S(2)}) copy-start(bf16[768,768]{1,0:T(8,128)(2,1)} %copy-done.2) | copy-start | bytes 3538948
  122.3 11.8 %collective-permute-start.16 = (bf16[96,1664]{1,0:T(8,128)(2,1)}, bf16[96,1664]{1,0:T(8,128)(2,1)S(1)}, u32[]{:S(2)}, u32[]{:S(2)}) collective-permute-start(bf16[96,1664]{1,0:T(8,128)(2,1)} %collective-permute-done.14), channel_id=1, source_target_pairs={{0,32},{32,64},{64,96},{96,128},{128,160},{160,192},{192,224},{224... | collective-permute-start | bytes 958472 | tf_op jit(solution)/shard_map/ppermute | solution.py:27
  124.2 11.9 %collective-permute-start.17 = (bf16[96,1664]{1,0:T(8,128)(2,1)}, bf16[96,1664]{1,0:T(8,128)(2,1)S(1)}, u32[]{:S(2)}, u32[]{:S(2)}) collective-permute-start(bf16[96,1664]{1,0:T(8,128)(2,1)} %collective-permute-done.15), channel_id=1, source_target_pairs={{0,224},{32,0},{64,32},{96,64},{128,96},{160,128},{192,160},{224,1... | collective-permute-start | bytes 958472 | tf_op jit(solution)/shard_map/ppermute | solution.py:27
  134.1 10.4 %collective-permute-start.18 = (bf16[96,1664]{1,0:T(8,128)(2,1)S(1)}, bf16[96,1664]{1,0:T(8,128)(2,1)S(1)}, u32[]{:S(2)}, u32[]{:S(2)}) collective-permute-start(bf16[96,1664]{1,0:T(8,128)(2,1)S(1)} %collective-permute-done.16), channel_id=1, source_target_pairs={{0,32},{32,64},{64,96},{96,128},{128,160},{160,192},{192,224},{224... | collective-permute-start | bytes 958472 | tf_op jit(solution)/shard_map/ppermute | solution.py:27
  136.1 10.4 %collective-permute-start.19 = (bf16[96,1664]{1,0:T(8,128)(2,1)S(1)}, bf16[96,1664]{1,0:T(8,128)(2,1)S(1)}, u32[]{:S(2)}, u32[]{:S(2)}) collective-permute-start(bf16[96,1664]{1,0:T(8,128)(2,1)S(1)} %collective-permute-done.17), channel_id=1, source_target_pairs={{0,224},{32,0},{64,32},{96,64},{128,96},{160,128},{192,160},{224,1... | collective-permute-start | bytes 958472 | tf_op jit(solution)/shard_map/ppermute | solution.py:27
  144.5 7.2 %collective-permute-start.20 = (bf16[48,1664]{1,0:T(8,128)(2,1)S(1)}, bf16[48,1664]{1,0:T(8,128)(2,1)S(1)}, u32[]{:S(2)}, u32[]{:S(2)}) collective-permute-start(bf16[48,1664]{1,0:T(8,128)(2,1)S(1)} %slice.268), channel_id=1, source_target_pairs={{0,32},{32,64},{64,96},{96,128},{128,160},{160,192},{192,224},{224... | collective-permute-start | bytes 479240 | tf_op jit(solution)/shard_map/ppermute | solution.py:27
  146.5 6.8 %collective-permute-start.21 = (bf16[48,1664]{1,0:T(8,128)(2,1)S(1)}, bf16[48,1664]{1,0:T(8,128)(2,1)S(1)}, u32[]{:S(2)}, u32[]{:S(2)}) collective-permute-start(bf16[48,1664]{1,0:T(8,128)(2,1)S(1)} %slice.270), channel_id=1, source_target_pairs={{0,224},{32,0},{64,32},{96,64},{128,96},{160,128},{192,160},{224,1... | collective-permute-start | bytes 479240 | tf_op jit(solution)/shard_map/ppermute | solution.py:27
  153.3 1.0 copy-start.5
  153.3 1.9 copy-start.4
  156.5 27.8 %all-to-all-start.1 = ((bf16[4,200,896]{2,1,0:T(8,128)(2,1)}), bf16[4,200,896]{2,1,0:T(8,128)(2,1)S(1)}, u32[]{:S(2)}, u32[]{:S(2)}) async-start(bf16[4,200,896]{2,1,0:T(8,128)(2,1)} %pad_maximum_fusion), calls=%async_computation.1 | async-start | bytes 2867200 | tf_op jit(solution)/shard_map/all_to_all | solution.py:116
  161.7 19.2 %copy-start.6 = (bf16[768,768]{1,0:T(8,128)(2,1)S(1)}, bf16[768,768]{1,0:T(8,128)(2,1)}, u32[]{:S(2)}) copy-start(bf16[768,768]{1,0:T(8,128)(2,1)} %copy-done.5) | copy-start | bytes 3538948
  164.7 25.8 %collective-permute-start.23 = (bf16[768,384]{1,0:T(8,128)(2,1)}, bf16[768,384]{1,0:T(8,128)(2,1)}, u32[]{:S(2)}, u32[]{:S(2)}) collective-permute-start(bf16[768,384]{1,0:T(8,128)(2,1)} %convolution_convert_fusion.2), channel_id=1, source_target_pairs={{0,256},{256,0},{1,257},{257,1},{2,258},{258,2},{3,259},{259,3},{4... | collective-permute-start | bytes 1769480 | tf_op jit(solution)/shard_map/ppermute | solution.py:27
  182.4 10.5 %collective-permute-start.22 = (bf16[384,768]{1,0:T(8,128)(2,1)}, bf16[384,768]{1,0:T(8,128)(2,1)S(1)}, u32[]{:S(2)}, u32[]{:S(2)}) collective-permute-start(bf16[384,768]{1,0:T(8,128)(2,1)} %convolution_convert_fusion.3), channel_id=1, source_target_pairs={{0,256},{256,0},{1,257},{257,1},{2,258},{258,2},{3,259},{259,3},{4... | collective-permute-start | bytes 1769480 | tf_op jit(solution)/shard_map/ppermute | solution.py:27
  185.4 12.9 %all-to-all-start.2 = ((bf16[4,56,896]{2,1,0:T(8,128)(2,1)}), bf16[4,56,896]{2,1,0:T(8,128)(2,1)S(1)}, u32[]{:S(2)}, u32[]{:S(2)}) async-start(bf16[4,56,896]{2,1,0:T(8,128)(2,1)} %pad_maximum_fusion.2), calls=%async_computation.2 | async-start | bytes 802816 | tf_op jit(solution)/shard_map/all_to_all | solution.py:116
  198.3 9.5 %collective-permute-start.24 = (f32[384]{0:T(512)S(1)}, f32[384]{0:T(512)S(1)}, u32[]{:S(2)}, u32[]{:S(2)}) collective-permute-start(f32[384]{0:T(512)S(1)} %slice_add_fusion), channel_id=1, source_target_pairs={{0,256},{256,0},{1,257},{257,1},{2,258},{258,2},{3,259},{259,3},{4... | collective-permute-start | bytes 4616 | tf_op jit(solution)/shard_map/ppermute | solution.py:27

commit v8 on v7

--- a/solution.py
+++ b/solution.py
@@ -74,10 +74,9 @@
         ],
         axis=0,
     )
-    up, down = shift(up, "y", Y, 1), shift(down, "y", Y, -1)
-    up, down = add(up, at(1)).astype(BF16), add(down, at(-1)).astype(BF16)
-    up, down = shift(up, "y", Y, 1), shift(down, "y", Y, -1)
-    return add(at(0), up, down)
+    near = shift(at(1), "y", Y, 1), shift(at(-1), "y", Y, -1)
+    up, down = shift(up, "y", Y, 2), shift(down, "y", Y, -2)
+    return add(at(0), up, down, *near)
 
 
 def gather_ring(blocks, axis, size):

time: 210 us -> 208 us (level)
  starting transfers between devices: 126 us -> 115 us
  waiting for transfers between devices: 38.4 us -> 46.4 us
    ppermute x25, waiting for transfers between devices: 30 us -> 38 us  [shift(): lax.ppermute(values, axis, [(i, (i + by) % size) for i in range(size)])]
    ppermute x25, starting transfers between devices: 103 us -> 95.3 us  [shift(): lax.ppermute(values, axis, [(i, (i + by) % size) for i in range(size)])]
    all_to_all x2, starting transfers between devices: 10.2 us -> 7.01 us  [scatter(): back = lax.all_to_all(parts, axis, 0, 0, tiled=True)]
  transfers between devices with their start and end apart: 28 -> 28, of which waited for: 14 -> 11; matrix products, arithmetic and copies ran while one was open for 8% -> 8% of each run, Pallas kernels for 0% -> 0%
where the time goes in v8:
time: 208 us; the launch traced here: 206 us
  starting transfers between devices  115 us (55%)
  waiting for transfers between devices  46.4 us (22%)
  blocking collectives  15.6 us (8%)
  other arithmetic  12.3 us (6%)
  matrix products  7.62 us (4%)
  local copies, waits for them, and re-layouts  7.28 us (4%)
    ppermute x25, starting transfers between devices, shift(): lax.ppermute(values, axis, [(i, (i + by) % size) for i in range(size)])  95.3 us
    ppermute x25, waiting for transfers between devices, shift(): lax.ppermute(values, axis, [(i, (i + by) % size) for i in range(size)])  38 us
    all_gather x1, blocking collectives, shards(): lax.all_gather(jnp.concatenate([patches, out_grad], axis=1), 'zl', axis=0...  15.6 us
    all_to_all x1, starting transfers between devices, to_all(): return lax.all_to_all(copies, axes, 0, 0, tiled=True)  12.9 us
    all_to_all x2, starting transfers between devices, scatter(): back = lax.all_to_all(parts, axis, 0, 0, tiled=True)  7.01 us
    all_to_all x1, waiting for transfers between devices, to_all(): return lax.all_to_all(copies, axes, 0, 0, tiled=True)  5.31 us
    add x3, other arithmetic, add(): total = total + term.astype(F32)  4.66 us
    dot_general x2, matrix products, contract_tokens(): lax.dot_general(left, right, (((0,), (0,)), ((), ())), preferred_element_...  4.48 us
  transfers between devices with their start and end apart: 28, of which 11 were waited for; matrix products, arithmetic and copies ran while one was open for 8% of the time, Pallas kernels for 0%

profile of v8, /device:TPU:1, one launch (start us, length us, event | category | flops | bytes accessed | tf_op | source)
XLA Modules:
  0.0 205.9 jit_solution(3967497354519158155)
XLA Ops:
  0.6 0.9 pad_maximum_fusion.15
  1.5 15.6 %all_gather.3 = bf16[192,768]{1,0:T(8,128)(2,1)S(1)} all-gather(bf16[48,768]{1,0:T(8,128)(2,1)S(1)} %pad_maximum_fusion.15), channel_id=1, replica_groups=mesh['dp'=2,'y'=8,'zh'=2,'x'=4,'zl'=4] {'zl'}, dimensions={0}, use_global_device_ids=true | all-gather | bytes 368640 | tf_op jit(solution)/shard_map/all_gather | solution.py:126
  17.3 1.3 multiply_reduce_fusion.1
  19.3 12.9 %all-to-all-start = ((f32[16,1,1152]{2,1,0:T(1,128)}), f32[16,1,1152]{2,1,0:T(1,128)S(1)}, u32[]{:S(2)}, u32[]{:S(2)}) async-start(f32[16,1,1152]{2,1,0:T(1,128)} %broadcast_in_dim.53), calls=%async_computation | async-start | bytes 147456 | tf_op jit(solution)/shard_map/all_to_all | solution.py:44
  32.3 3.1 %collective-permute-start = (bf16[192,384]{1,0:T(8,128)(2,1)S(1)}, bf16[192,384]{1,0:T(8,128)(2,1)S(1)}, u32[]{:S(2)}, u32[]{:S(2)}) collective-permute-start(bf16[192,384]{1,0:T(8,128)(2,1)S(1)} %get-tuple-element.58), channel_id=1, source_target_pairs={{0,4},{4,8},{8,12},{12,0},{1,5},{5,9},{9,13},{13,1},{2,6},{6,10},{... | collective-permute-start | bytes 442376 | tf_op jit(solution)/shard_map/ppermute | solution.py:27
  35.4 3.4 %collective-permute-start.1 = (bf16[192,384]{1,0:T(8,128)(2,1)S(1)}, bf16[192,384]{1,0:T(8,128)(2,1)S(1)}, u32[]{:S(2)}, u32[]{:S(2)}) collective-permute-start(bf16[192,384]{1,0:T(8,128)(2,1)S(1)} %get-tuple-element.58), channel_id=1, source_target_pairs={{0,12},{4,0},{8,4},{12,8},{1,13},{5,1},{9,5},{13,9},{2,14},{6,2},{... | collective-permute-start | bytes 442376 | tf_op jit(solution)/shard_map/ppermute | solution.py:27
  38.8 5.3 %all-to-all-done = f32[16,1,1152]{2,1,0:T(1,128)S(1)} async-done(((f32[16,1,1152]{2,1,0:T(1,128)}), f32[16,1,1152]{2,1,0:T(1,128)S(1)}, u32[]{:S(2)}, u32[]{:S(2)}) %all-to-all-start) | async-done | bytes 73760 | tf_op jit(solution)/shard_map/all_to_all | solution.py:44
  44.5 4.7 %collective-permute-start.4 = (bf16[192,384]{1,0:T(8,128)(2,1)S(1)}, bf16[192,384]{1,0:T(8,128)(2,1)S(1)}, u32[]{:S(2)}, u32[]{:S(2)}) collective-permute-start(bf16[192,384]{1,0:T(8,128)(2,1)S(1)} %get-tuple-element.8), channel_id=1, source_target_pairs={{0,8},{4,12},{8,0},{12,4},{1,9},{5,13},{9,1},{13,5},{2,10},{6,14},... | collective-permute-start | bytes 442376 | tf_op jit(solution)/shard_map/ppermute | solution.py:27
  49.2 2.2 %collective-permute-start.2 = (bf16[288,384]{1,0:T(8,128)(2,1)S(1)}, bf16[288,384]{1,0:T(8,128)(2,1)S(1)}, u32[]{:S(2)}, u32[]{:S(2)}) collective-permute-start(bf16[288,384]{1,0:T(8,128)(2,1)S(1)} %get-tuple-element.64), channel_id=1, source_target_pairs={{0,4},{4,8},{8,12},{12,0},{1,5},{5,9},{9,13},{13,1},{2,6},{6,10},{... | collective-permute-start | bytes 663560 | tf_op jit(solution)/shard_map/ppermute | solution.py:27
  51.4 4.3 %collective-permute-start.3 = (bf16[288,384]{1,0:T(8,128)(2,1)S(1)}, bf16[288,384]{1,0:T(8,128)(2,1)S(1)}, u32[]{:S(2)}, u32[]{:S(2)}) collective-permute-start(bf16[288,384]{1,0:T(8,128)(2,1)S(1)} %get-tuple-element.65), channel_id=1, source_target_pairs={{0,12},{4,0},{8,4},{12,8},{1,13},{5,1},{9,5},{13,9},{2,14},{6,2},{... | collective-permute-start | bytes 663560 | tf_op jit(solution)/shard_map/ppermute | solution.py:27
  55.9 2.6 %collective-permute-done.2 = bf16[288,384]{1,0:T(8,128)(2,1)S(1)} collective-permute-done((bf16[288,384]{1,0:T(8,128)(2,1)S(1)}, bf16[288,384]{1,0:T(8,128)(2,1)S(1)}, u32[]{:S(2)}, u32[]{:S(2)}) %collective-permute-start.2) | collective-permute-done | bytes 221216 | tf_op jit(solution)/shard_map/ppermute | solution.py:27
  60.6 2.0 collective-permute-start.5
  62.6 2.8 %collective-permute-start.6 = (bf16[48,1536]{1,0:T(8,128)(2,1)S(1)}, bf16[48,1536]{1,0:T(8,128)(2,1)S(1)}, u32[]{:S(2)}, u32[]{:S(2)}) collective-permute-start(bf16[48,1536]{1,0:T(8,128)(2,1)S(1)} %get-tuple-element.56), channel_id=1, source_target_pairs={{0,64},{32,96},{64,128},{96,160},{128,192},{160,224},{192,0},{224,... | collective-permute-start | bytes 442376 | tf_op jit(solution)/shard_map/ppermute | solution.py:27
  65.5 4.5 %collective-permute-start.9 = (bf16[48,1536]{1,0:T(8,128)(2,1)S(1)}, bf16[48,1536]{1,0:T(8,128)(2,1)S(1)}, u32[]{:S(2)}, u32[]{:S(2)}) collective-permute-start(bf16[48,1536]{1,0:T(8,128)(2,1)S(1)} %get-tuple-element.57), channel_id=1, source_target_pairs={{0,192},{32,224},{64,0},{96,32},{128,64},{160,96},{192,128},{224,1... | collective-permute-start | bytes 442376 | tf_op jit(solution)/shard_map/ppermute | solution.py:27
  70.1 3.3 %collective-permute-start.8 = (bf16[96,1536]{1,0:T(8,128)(2,1)S(1)}, bf16[96,1536]{1,0:T(8,128)(2,1)S(1)}, u32[]{:S(2)}, u32[]{:S(2)}) collective-permute-start(bf16[96,1536]{1,0:T(8,128)(2,1)S(1)} %pad_maximum_fusion.6), channel_id=1, source_target_pairs={{0,224},{32,0},{64,32},{96,64},{128,96},{160,128},{192,160},{224,1... | collective-permute-start | bytes 884744 | tf_op jit(solution)/shard_map/ppermute | solution.py:27
  73.4 2.0 collective-permute-start.11
  75.4 4.5 %collective-permute-start.12 = (bf16[96,1536]{1,0:T(8,128)(2,1)S(1)}, bf16[96,1536]{1,0:T(8,128)(2,1)S(1)}, u32[]{:S(2)}, u32[]{:S(2)}) collective-permute-start(bf16[96,1536]{1,0:T(8,128)(2,1)S(1)} %pad_maximum_fusion.9), channel_id=1, source_target_pairs={{0,224},{32,0},{64,32},{96,64},{128,96},{160,128},{192,160},{224,1... | collective-permute-start | bytes 884744 | tf_op jit(solution)/shard_map/ppermute | solution.py:27
  80.0 1.9 collective-permute-start.7
  82.1 5.5 %collective-permute-start.10 = (bf16[96,1536]{1,0:T(8,128)(2,1)S(1)}, bf16[96,1536]{1,0:T(8,128)(2,1)S(1)}, u32[]{:S(2)}, u32[]{:S(2)}) collective-permute-start(bf16[96,1536]{1,0:T(8,128)(2,1)S(1)} %pad_maximum_fusion.7), channel_id=1, source_target_pairs={{0,192},{32,224},{64,0},{96,32},{128,64},{160,96},{192,128},{224,1... | collective-permute-start | bytes 884744 | tf_op jit(solution)/shard_map/ppermute | solution.py:27
  87.6 5.4 %collective-permute-done.7 = bf16[96,1536]{1,0:T(8,128)(2,1)S(1)} collective-permute-done((bf16[96,1536]{1,0:T(8,128)(2,1)S(1)}, bf16[96,1536]{1,0:T(8,128)(2,1)S(1)}, u32[]{:S(2)}, u32[]{:S(2)}) %collective-permute-start.7) | collective-permute-done | bytes 294944 | tf_op jit(solution)/shard_map/ppermute | solution.py:27
  93.0 8.1 %collective-permute-done.10 = bf16[96,1536]{1,0:T(8,128)(2,1)S(1)} collective-permute-done((bf16[96,1536]{1,0:T(8,128)(2,1)S(1)}, bf16[96,1536]{1,0:T(8,128)(2,1)S(1)}, u32[]{:S(2)}, u32[]{:S(2)}) %collective-permute-start.10) | collective-permute-done | bytes 294944 | tf_op jit(solution)/shard_map/ppermute | solution.py:27
  101.3 3.8 %collective-permute-start.13 = (bf16[96,1536]{1,0:T(8,128)(2,1)S(1)}, bf16[96,1536]{1,0:T(8,128)(2,1)S(1)}, u32[]{:S(2)}, u32[]{:S(2)}) collective-permute-start(bf16[96,1536]{1,0:T(8,128)(2,1)S(1)} %add_convert_fusion), channel_id=1, source_target_pairs={{0,16},{16,0},{1,17},{17,1},{2,18},{18,2},{3,19},{19,3},{4,20},{20... | collective-permute-start | bytes 884744 | tf_op jit(solution)/shard_map/ppermute | solution.py:27
  105.2 14.7 %collective-permute-done.13 = bf16[96,1536]{1,0:T(8,128)(2,1)S(1)} collective-permute-done((bf16[96,1536]{1,0:T(8,128)(2,1)S(1)}, bf16[96,1536]{1,0:T(8,128)(2,1)S(1)}, u32[]{:S(2)}, u32[]{:S(2)}) %collective-permute-start.13) | collective-permute-done | bytes 294944 | tf_op jit(solution)/shard_map/ppermute | solution.py:27
  120.5 1.0 copy-done.2
  121.7 1.9 collective-permute-start.14
  123.6 4.6 %collective-permute-start.15 = (bf16[96,1664]{1,0:T(8,128)(2,1)S(1)}, bf16[96,1664]{1,0:T(8,128)(2,1)}, u32[]{:S(2)}, u32[]{:S(2)}) collective-permute-start(bf16[96,1664]{1,0:T(8,128)(2,1)S(1)} %pad_maximum_fusion.3), channel_id=1, source_target_pairs={{0,224},{32,0},{64,32},{96,64},{128,96},{160,128},{192,160},{224,1... | collective-permute-start | bytes 958472 | tf_op jit(solution)/shard_map/ppermute | solution.py:27
  128.3 2.7 %collective-permute-done.14 = bf16[96,1664]{1,0:T(8,128)(2,1)} collective-permute-done((bf16[96,1664]{1,0:T(8,128)(2,1)S(1)}, bf16[96,1664]{1,0:T(8,128)(2,1)}, u32[]{:S(2)}, u32[]{:S(2)}) %collective-permute-start.14) | collective-permute-done | bytes 319520 | tf_op jit(solution)/shard_map/ppermute | solution.py:27
  131.0 1.9 collective-permute-start.16
  133.0 4.6 %collective-permute-start.17 = (bf16[96,1664]{1,0:T(8,128)(2,1)}, bf16[96,1664]{1,0:T(8,128)(2,1)S(1)}, u32[]{:S(2)}, u32[]{:S(2)}) collective-permute-start(bf16[96,1664]{1,0:T(8,128)(2,1)} %collective-permute-done.15), channel_id=1, source_target_pairs={{0,224},{32,0},{64,32},{96,64},{128,96},{160,128},{192,160},{224,1... | collective-permute-start | bytes 958472 | tf_op jit(solution)/shard_map/ppermute | solution.py:27
  137.6 1.0 slice_dynamic-update-slice_fusion.11
  138.6 1.0 slice_dynamic-update-slice_fusion.10
  141.1 1.9 collective-permute-start.18
  143.0 4.6 %collective-permute-start.19 = (bf16[96,1664]{1,0:T(8,128)(2,1)S(1)}, bf16[96,1664]{1,0:T(8,128)(2,1)S(1)}, u32[]{:S(2)}, u32[]{:S(2)}) collective-permute-start(bf16[96,1664]{1,0:T(8,128)(2,1)S(1)} %collective-permute-done.17), channel_id=1, source_target_pairs={{0,224},{32,0},{64,32},{96,64},{128,96},{160,128},{192,160},{224,1... | collective-permute-start | bytes 958472 | tf_op jit(solution)/shard_map/ppermute | solution.py:27
  147.7 2.3 %collective-permute-done.18 = bf16[96,1664]{1,0:T(8,128)(2,1)S(1)} collective-permute-done((bf16[96,1664]{1,0:T(8,128)(2,1)S(1)}, bf16[96,1664]{1,0:T(8,128)(2,1)S(1)}, u32[]{:S(2)}, u32[]{:S(2)}) %collective-permute-start.18) | collective-permute-done | bytes 319520 | tf_op jit(solution)/shard_map/ppermute | solution.py:27
  150.0 1.9 collective-permute-start.20
  152.0 4.6 %collective-permute-start.21 = (bf16[48,1664]{1,0:T(8,128)(2,1)S(1)}, bf16[48,1664]{1,0:T(8,128)(2,1)S(1)}, u32[]{:S(2)}, u32[]{:S(2)}) collective-permute-start(bf16[48,1664]{1,0:T(8,128)(2,1)S(1)} %slice.270), channel_id=1, source_target_pairs={{0,224},{32,0},{64,32},{96,64},{128,96},{160,128},{192,160},{224,1... | collective-permute-start | bytes 479240 | tf_op jit(solution)/shard_map/ppermute | solution.py:27
  157.3 1.5 collective-permute-done.21
  160.8 1.2 pad_maximum_fusion
  162.1 3.5 %all-to-all-start.1 = ((bf16[4,200,896]{2,1,0:T(8,128)(2,1)}), bf16[4,200,896]{2,1,0:T(8,128)(2,1)S(1)}, u32[]{:S(2)}, u32[]{:S(2)}) async-start(bf16[4,200,896]{2,1,0:T(8,128)(2,1)} %pad_maximum_fusion), calls=%async_computation.1 | async-start | bytes 2867200 | tf_op jit(solution)/shard_map/all_to_all | solution.py:115
  165.6 3.0 %convolution_convert_fusion.2 = bf16[768,384]{1,0:T(8,128)(2,1)} fusion(bf16[768,768]{1,0:T(8,128)(2,1)} %copy-done.4, bf16[768,384]{1,0:T(8,128)(2,1)S(1)} %maximum_dynamic-update-slice_fusion), kind=kOutput, calls=%fused_computation.5 | convolution fusion | flops 453279744 | bytes 2359296 | tf_op jit(solution)/shard_map/dot_general | solution.py:15
  168.6 11.7 %collective-permute-start.23 = (bf16[768,384]{1,0:T(8,128)(2,1)}, bf16[768,384]{1,0:T(8,128)(2,1)}, u32[]{:S(2)}, u32[]{:S(2)}) collective-permute-start(bf16[768,384]{1,0:T(8,128)(2,1)} %convolution_convert_fusion.2), channel_id=1, source_target_pairs={{0,256},{256,0},{1,257},{257,1},{2,258},{258,2},{3,259},{259,3},{4... | collective-permute-start | bytes 1769480 | tf_op jit(solution)/shard_map/ppermute | solution.py:27
  180.4 1.5 convolution_convert_fusion.3
  181.8 1.9 collective-permute-start.22
  184.8 3.5 %all-to-all-start.2 = ((bf16[4,56,896]{2,1,0:T(8,128)(2,1)}), bf16[4,56,896]{2,1,0:T(8,128)(2,1)S(1)}, u32[]{:S(2)}, u32[]{:S(2)}) async-start(bf16[4,56,896]{2,1,0:T(8,128)(2,1)} %pad_maximum_fusion.2), calls=%async_computation.2 | async-start | bytes 802816 | tf_op jit(solution)/shard_map/all_to_all | solution.py:115
  188.4 2.4 %convert_add_fusion = f32[768,384]{1,0:T(8,128)} fusion(bf16[768,384]{1,0:T(8,128)(2,1)} %collective-permute-done.23, bf16[768,384]{1,0:T(8,128)(2,1)} %convolution_convert_fusion.2), kind=kLoop, calls=%fused_computation.8 | loop fusion | flops 884736 | bytes 2359296 | tf_op jit(solution)/shard_map/add | solution.py:37
  190.8 2.2 %convert_add_fusion.1 = f32[384,768]{1,0:T(8,128)} fusion(bf16[384,768]{1,0:T(8,128)(2,1)S(1)} %collective-permute-done.22, bf16[384,768]{1,0:T(8,128)(2,1)} %convolution_convert_fusion.3), kind=kLoop, calls=%fused_computation.9 | loop fusion | flops 884736 | bytes 2359296 | tf_op jit(solution)/shard_map/add | solution.py:37
  193.0 3.1 %all-to-all-done.2 = bf16[4,56,896]{2,1,0:T(8,128)(2,1)S(1)} async-done(((bf16[4,56,896]{2,1,0:T(8,128)(2,1)}), bf16[4,56,896]{2,1,0:T(8,128)(2,1)S(1)}, u32[]{:S(2)}, u32[]{:S(2)}) %all-to-all-start.2) | async-done | bytes 401440 | tf_op jit(solution)/shard_map/all_to_all | solution.py:115
  196.1 7.7 %collective-permute-start.24 = (f32[384]{0:T(512)S(1)}, f32[384]{0:T(512)S(1)}, u32[]{:S(2)}, u32[]{:S(2)}) collective-permute-start(f32[384]{0:T(512)S(1)} %slice_add_fusion), channel_id=1, source_target_pairs={{0,256},{256,0},{1,257},{257,1},{2,258},{258,2},{3,259},{259,3},{4... | collective-permute-start | bytes 4616 | tf_op jit(solution)/shard_map/ppermute | solution.py:27
  (122 shorter events, 12.4 us)
Async XLA Ops:
  0.6 58.9 %copy-start = (bf16[768,384]{1,0:T(8,128)(2,1)S(1)}, bf16[768,384]{1,0:T(8,128)(2,1)}, u32[]{:S(2)}) copy-start(bf16[768,384]{1,0:T(8,128)(2,1)} %param.8) | copy-start | bytes 1769476
  17.1 27.2 %copy-start.7 = (f32[384]{0:T(512)S(1)}, f32[384]{0:T(512)}, u32[]{:S(2)}) copy-start(f32[384]{0:T(512)} %param.6) | copy-start | bytes 4612
  19.3 24.8 %all-to-all-start = ((f32[16,1,1152]{2,1,0:T(1,128)}), f32[16,1,1152]{2,1,0:T(1,128)S(1)}, u32[]{:S(2)}, u32[]{:S(2)}) async-start(f32[16,1,1152]{2,1,0:T(1,128)} %broadcast_in_dim.53), calls=%async_computation | async-start | bytes 147456 | tf_op jit(solution)/shard_map/all_to_all | solution.py:44
  32.3 12.1 %collective-permute-start = (bf16[192,384]{1,0:T(8,128)(2,1)S(1)}, bf16[192,384]{1,0:T(8,128)(2,1)S(1)}, u32[]{:S(2)}, u32[]{:S(2)}) collective-permute-start(bf16[192,384]{1,0:T(8,128)(2,1)S(1)} %get-tuple-element.58), channel_id=1, source_target_pairs={{0,4},{4,8},{8,12},{12,0},{1,5},{5,9},{9,13},{13,1},{2,6},{6,10},{... | collective-permute-start | bytes 442376 | tf_op jit(solution)/shard_map/ppermute | solution.py:27
  35.4 9.0 %collective-permute-start.1 = (bf16[192,384]{1,0:T(8,128)(2,1)S(1)}, bf16[192,384]{1,0:T(8,128)(2,1)S(1)}, u32[]{:S(2)}, u32[]{:S(2)}) collective-permute-start(bf16[192,384]{1,0:T(8,128)(2,1)S(1)} %get-tuple-element.58), channel_id=1, source_target_pairs={{0,12},{4,0},{8,4},{12,8},{1,13},{5,1},{9,5},{13,9},{2,14},{6,2},{... | collective-permute-start | bytes 442376 | tf_op jit(solution)/shard_map/ppermute | solution.py:27
  44.5 14.1 %collective-permute-start.4 = (bf16[192,384]{1,0:T(8,128)(2,1)S(1)}, bf16[192,384]{1,0:T(8,128)(2,1)S(1)}, u32[]{:S(2)}, u32[]{:S(2)}) collective-permute-start(bf16[192,384]{1,0:T(8,128)(2,1)S(1)} %get-tuple-element.8), channel_id=1, source_target_pairs={{0,8},{4,12},{8,0},{12,4},{1,9},{5,13},{9,1},{13,5},{2,10},{6,14},... | collective-permute-start | bytes 442376 | tf_op jit(solution)/shard_map/ppermute | solution.py:27
  49.2 9.3 %collective-permute-start.2 = (bf16[288,384]{1,0:T(8,128)(2,1)S(1)}, bf16[288,384]{1,0:T(8,128)(2,1)S(1)}, u32[]{:S(2)}, u32[]{:S(2)}) collective-permute-start(bf16[288,384]{1,0:T(8,128)(2,1)S(1)} %get-tuple-element.64), channel_id=1, source_target_pairs={{0,4},{4,8},{8,12},{12,0},{1,5},{5,9},{9,13},{13,1},{2,6},{6,10},{... | collective-permute-start | bytes 663560 | tf_op jit(solution)/shard_map/ppermute | solution.py:27
  51.4 7.1 %collective-permute-start.3 = (bf16[288,384]{1,0:T(8,128)(2,1)S(1)}, bf16[288,384]{1,0:T(8,128)(2,1)S(1)}, u32[]{:S(2)}, u32[]{:S(2)}) collective-permute-start(bf16[288,384]{1,0:T(8,128)(2,1)S(1)} %get-tuple-element.65), channel_id=1, source_target_pairs={{0,12},{4,0},{8,4},{12,8},{1,13},{5,1},{9,5},{13,9},{2,14},{6,2},{... | collective-permute-start | bytes 663560 | tf_op jit(solution)/shard_map/ppermute | solution.py:27
  55.7 2.9 %copy-start.1 = (bf16[384,768]{1,0:T(8,128)(2,1)S(1)}, bf16[384,768]{1,0:T(8,128)(2,1)}, u32[]{:S(2)}) copy-start(bf16[384,768]{1,0:T(8,128)(2,1)} %param.7) | copy-start | bytes 1769476
  60.6 19.3 %collective-permute-start.5 = (bf16[96,1536]{1,0:T(8,128)(2,1)S(1)}, bf16[96,1536]{1,0:T(8,128)(2,1)S(1)}, u32[]{:S(2)}, u32[]{:S(2)}) collective-permute-start(bf16[96,1536]{1,0:T(8,128)(2,1)S(1)} %pad_maximum_fusion.4), channel_id=1, source_target_pairs={{0,32},{32,64},{64,96},{96,128},{128,160},{160,192},{192,224},{224... | collective-permute-start | bytes 884744 | tf_op jit(solution)/shard_map/ppermute | solution.py:27
  62.6 12.8 %collective-permute-start.6 = (bf16[48,1536]{1,0:T(8,128)(2,1)S(1)}, bf16[48,1536]{1,0:T(8,128)(2,1)S(1)}, u32[]{:S(2)}, u32[]{:S(2)}) collective-permute-start(bf16[48,1536]{1,0:T(8,128)(2,1)S(1)} %get-tuple-element.56), channel_id=1, source_target_pairs={{0,64},{32,96},{64,128},{96,160},{128,192},{160,224},{192,0},{224,... | collective-permute-start | bytes 442376 | tf_op jit(solution)/shard_map/ppermute | solution.py:27
  65.5 16.5 %collective-permute-start.9 = (bf16[48,1536]{1,0:T(8,128)(2,1)S(1)}, bf16[48,1536]{1,0:T(8,128)(2,1)S(1)}, u32[]{:S(2)}, u32[]{:S(2)}) collective-permute-start(bf16[48,1536]{1,0:T(8,128)(2,1)S(1)} %get-tuple-element.57), channel_id=1, source_target_pairs={{0,192},{32,224},{64,0},{96,32},{128,64},{160,96},{192,128},{224,1... | collective-permute-start | bytes 442376 | tf_op jit(solution)/shard_map/ppermute | solution.py:27
  70.1 11.9 %collective-permute-start.8 = (bf16[96,1536]{1,0:T(8,128)(2,1)S(1)}, bf16[96,1536]{1,0:T(8,128)(2,1)S(1)}, u32[]{:S(2)}, u32[]{:S(2)}) collective-permute-start(bf16[96,1536]{1,0:T(8,128)(2,1)S(1)} %pad_maximum_fusion.6), channel_id=1, source_target_pairs={{0,224},{32,0},{64,32},{96,64},{128,96},{160,128},{192,160},{224,1... | collective-permute-start | bytes 884744 | tf_op jit(solution)/shard_map/ppermute | solution.py:27
  73.4 14.3 %collective-permute-start.11 = (bf16[96,1536]{1,0:T(8,128)(2,1)S(1)}, bf16[96,1536]{1,0:T(8,128)(2,1)S(1)}, u32[]{:S(2)}, u32[]{:S(2)}) collective-permute-start(bf16[96,1536]{1,0:T(8,128)(2,1)S(1)} %pad_maximum_fusion.8), channel_id=1, source_target_pairs={{0,32},{32,64},{64,96},{96,128},{128,160},{160,192},{192,224},{224... | collective-permute-start | bytes 884744 | tf_op jit(solution)/shard_map/ppermute | solution.py:27
  75.4 12.2 %collective-permute-start.12 = (bf16[96,1536]{1,0:T(8,128)(2,1)S(1)}, bf16[96,1536]{1,0:T(8,128)(2,1)S(1)}, u32[]{:S(2)}, u32[]{:S(2)}) collective-permute-start(bf16[96,1536]{1,0:T(8,128)(2,1)S(1)} %pad_maximum_fusion.9), channel_id=1, source_target_pairs={{0,224},{32,0},{64,32},{96,64},{128,96},{160,128},{192,160},{224,1... | collective-permute-start | bytes 884744 | tf_op jit(solution)/shard_map/ppermute | solution.py:27
  80.0 13.0 %collective-permute-start.7 = (bf16[96,1536]{1,0:T(8,128)(2,1)S(1)}, bf16[96,1536]{1,0:T(8,128)(2,1)S(1)}, u32[]{:S(2)}, u32[]{:S(2)}) collective-permute-start(bf16[96,1536]{1,0:T(8,128)(2,1)S(1)} %pad_maximum_fusion.5), channel_id=1, source_target_pairs={{0,64},{32,96},{64,128},{96,160},{128,192},{160,224},{192,0},{224,... | collective-permute-start | bytes 884744 | tf_op jit(solution)/shard_map/ppermute | solution.py:27
  82.1 19.0 %collective-permute-start.10 = (bf16[96,1536]{1,0:T(8,128)(2,1)S(1)}, bf16[96,1536]{1,0:T(8,128)(2,1)S(1)}, u32[]{:S(2)}, u32[]{:S(2)}) collective-permute-start(bf16[96,1536]{1,0:T(8,128)(2,1)S(1)} %pad_maximum_fusion.7), channel_id=1, source_target_pairs={{0,192},{32,224},{64,0},{96,32},{128,64},{160,96},{192,128},{224,1... | collective-permute-start | bytes 884744 | tf_op jit(solution)/shard_map/ppermute | solution.py:27
  101.3 18.5 %collective-permute-start.13 = (bf16[96,1536]{1,0:T(8,128)(2,1)S(1)}, bf16[96,1536]{1,0:T(8,128)(2,1)S(1)}, u32[]{:S(2)}, u32[]{:S(2)}) collective-permute-start(bf16[96,1536]{1,0:T(8,128)(2,1)S(1)} %add_convert_fusion), channel_id=1, source_target_pairs={{0,16},{16,0},{1,17},{17,1},{2,18},{18,2},{3,19},{19,3},{4,20},{20... | collective-permute-start | bytes 884744 | tf_op jit(solution)/shard_map/ppermute | solution.py:27
  120.5 1.0 copy-start.2
  121.7 9.4 %collective-permute-start.14 = (bf16[96,1664]{1,0:T(8,128)(2,1)S(1)}, bf16[96,1664]{1,0:T(8,128)(2,1)}, u32[]{:S(2)}, u32[]{:S(2)}) collective-permute-start(bf16[96,1664]{1,0:T(8,128)(2,1)S(1)} %pad_maximum_fusion.3), channel_id=1, source_target_pairs={{0,32},{32,64},{64,96},{96,128},{128,160},{160,192},{192,224},{224... | collective-permute-start | bytes 958472 | tf_op jit(solution)/shard_map/ppermute | solution.py:27
  123.6 9.3 %collective-permute-start.15 = (bf16[96,1664]{1,0:T(8,128)(2,1)S(1)}, bf16[96,1664]{1,0:T(8,128)(2,1)}, u32[]{:S(2)}, u32[]{:S(2)}) collective-permute-start(bf16[96,1664]{1,0:T(8,128)(2,1)S(1)} %pad_maximum_fusion.3), channel_id=1, source_target_pairs={{0,224},{32,0},{64,32},{96,64},{128,96},{160,128},{192,160},{224,1... | collective-permute-start | bytes 958472 | tf_op jit(solution)/shard_map/ppermute | solution.py:27
  128.2 9.4 %copy-start.3 = (bf16[768,768]{1,0:T(8,128)(2,1)S(1)}, bf16[768,768]{1,0:T(8,128)(2,1)}, u32[]{:S(2)}) copy-start(bf16[768,768]{1,0:T(8,128)(2,1)} %copy-done.2) | copy-start | bytes 3538948
  131.0 10.0 %collective-permute-start.16 = (bf16[96,1664]{1,0:T(8,128)(2,1)}, bf16[96,1664]{1,0:T(8,128)(2,1)S(1)}, u32[]{:S(2)}, u32[]{:S(2)}) collective-permute-start(bf16[96,1664]{1,0:T(8,128)(2,1)} %collective-permute-done.14), channel_id=1, source_target_pairs={{0,32},{32,64},{64,96},{96,128},{128,160},{160,192},{192,224},{224... | collective-permute-start | bytes 958472 | tf_op jit(solution)/shard_map/ppermute | solution.py:27
  133.0 10.1 %collective-permute-start.17 = (bf16[96,1664]{1,0:T(8,128)(2,1)}, bf16[96,1664]{1,0:T(8,128)(2,1)S(1)}, u32[]{:S(2)}, u32[]{:S(2)}) collective-permute-start(bf16[96,1664]{1,0:T(8,128)(2,1)} %collective-permute-done.15), channel_id=1, source_target_pairs={{0,224},{32,0},{64,32},{96,64},{128,96},{160,128},{192,160},{224,1... | collective-permute-start | bytes 958472 | tf_op jit(solution)/shard_map/ppermute | solution.py:27
  141.1 8.9 %collective-permute-start.18 = (bf16[96,1664]{1,0:T(8,128)(2,1)S(1)}, bf16[96,1664]{1,0:T(8,128)(2,1)S(1)}, u32[]{:S(2)}, u32[]{:S(2)}) collective-permute-start(bf16[96,1664]{1,0:T(8,128)(2,1)S(1)} %collective-permute-done.16), channel_id=1, source_target_pairs={{0,32},{32,64},{64,96},{96,128},{128,160},{160,192},{192,224},{224... | collective-permute-start | bytes 958472 | tf_op jit(solution)/shard_map/ppermute | solution.py:27
  143.0 8.9 %collective-permute-start.19 = (bf16[96,1664]{1,0:T(8,128)(2,1)S(1)}, bf16[96,1664]{1,0:T(8,128)(2,1)S(1)}, u32[]{:S(2)}, u32[]{:S(2)}) collective-permute-start(bf16[96,1664]{1,0:T(8,128)(2,1)S(1)} %collective-permute-done.17), channel_id=1, source_target_pairs={{0,224},{32,0},{64,32},{96,64},{128,96},{160,128},{192,160},{224,1... | collective-permute-start | bytes 958472 | tf_op jit(solution)/shard_map/ppermute | solution.py:27
  150.0 7.2 %collective-permute-start.20 = (bf16[48,1664]{1,0:T(8,128)(2,1)S(1)}, bf16[48,1664]{1,0:T(8,128)(2,1)S(1)}, u32[]{:S(2)}, u32[]{:S(2)}) collective-permute-start(bf16[48,1664]{1,0:T(8,128)(2,1)S(1)} %slice.268), channel_id=1, source_target_pairs={{0,32},{32,64},{64,96},{96,128},{128,160},{160,192},{192,224},{224... | collective-permute-start | bytes 479240 | tf_op jit(solution)/shard_map/ppermute | solution.py:27
  152.0 6.8 %collective-permute-start.21 = (bf16[48,1664]{1,0:T(8,128)(2,1)S(1)}, bf16[48,1664]{1,0:T(8,128)(2,1)S(1)}, u32[]{:S(2)}, u32[]{:S(2)}) collective-permute-start(bf16[48,1664]{1,0:T(8,128)(2,1)S(1)} %slice.270), channel_id=1, source_target_pairs={{0,224},{32,0},{64,32},{96,64},{128,96},{160,128},{192,160},{224,1... | collective-permute-start | bytes 479240 | tf_op jit(solution)/shard_map/ppermute | solution.py:27
  158.8 1.0 copy-start.5
  158.8 1.9 copy-start.4
  162.1 21.7 %all-to-all-start.1 = ((bf16[4,200,896]{2,1,0:T(8,128)(2,1)}), bf16[4,200,896]{2,1,0:T(8,128)(2,1)S(1)}, u32[]{:S(2)}, u32[]{:S(2)}) async-start(bf16[4,200,896]{2,1,0:T(8,128)(2,1)} %pad_maximum_fusion), calls=%async_computation.1 | async-start | bytes 2867200 | tf_op jit(solution)/shard_map/all_to_all | solution.py:115
  165.6 14.7 %copy-start.6 = (bf16[768,768]{1,0:T(8,128)(2,1)S(1)}, bf16[768,768]{1,0:T(8,128)(2,1)}, u32[]{:S(2)}) copy-start(bf16[768,768]{1,0:T(8,128)(2,1)} %copy-done.5) | copy-start | bytes 3538948
  168.6 19.8 %collective-permute-start.23 = (bf16[768,384]{1,0:T(8,128)(2,1)}, bf16[768,384]{1,0:T(8,128)(2,1)}, u32[]{:S(2)}, u32[]{:S(2)}) collective-permute-start(bf16[768,384]{1,0:T(8,128)(2,1)} %convolution_convert_fusion.2), channel_id=1, source_target_pairs={{0,256},{256,0},{1,257},{257,1},{2,258},{258,2},{3,259},{259,3},{4... | collective-permute-start | bytes 1769480 | tf_op jit(solution)/shard_map/ppermute | solution.py:27
  181.8 8.9 %collective-permute-start.22 = (bf16[384,768]{1,0:T(8,128)(2,1)}, bf16[384,768]{1,0:T(8,128)(2,1)S(1)}, u32[]{:S(2)}, u32[]{:S(2)}) collective-permute-start(bf16[384,768]{1,0:T(8,128)(2,1)} %convolution_convert_fusion.3), channel_id=1, source_target_pairs={{0,256},{256,0},{1,257},{257,1},{2,258},{258,2},{3,259},{259,3},{4... | collective-permute-start | bytes 1769480 | tf_op jit(solution)/shard_map/ppermute | solution.py:27
  184.8 11.3 %all-to-all-start.2 = ((bf16[4,56,896]{2,1,0:T(8,128)(2,1)}), bf16[4,56,896]{2,1,0:T(8,128)(2,1)S(1)}, u32[]{:S(2)}, u32[]{:S(2)}) async-start(bf16[4,56,896]{2,1,0:T(8,128)(2,1)} %pad_maximum_fusion.2), calls=%async_computation.2 | async-start | bytes 802816 | tf_op jit(solution)/shard_map/all_to_all | solution.py:115
  196.1 9.2 %collective-permute-start.24 = (f32[384]{0:T(512)S(1)}, f32[384]{0:T(512)S(1)}, u32[]{:S(2)}, u32[]{:S(2)}) collective-permute-start(f32[384]{0:T(512)S(1)} %slice_add_fusion), channel_id=1, source_target_pairs={{0,256},{256,0},{1,257},{257,1},{2,258},{258,2},{3,259},{259,3},{4... | collective-permute-start | bytes 4616 | tf_op jit(solution)/shard_map/ppermute | solution.py:27

commit v9 on v8

--- a/solution.py
+++ b/solution.py
@@ -74,7 +74,8 @@
         ],
         axis=0,
     )
-    near = shift(at(1), "y", Y, 1), shift(at(-1), "y", Y, -1)
+    up, down, *near = lax.optimization_barrier((up, down, at(1), at(-1)))
+    near = shift(near[0], "y", Y, 1), shift(near[1], "y", Y, -1)
     up, down = shift(up, "y", Y, 2), shift(down, "y", Y, -2)
     return add(at(0), up, down, *near)
 

time: 208 us -> 214 us (1.029)
  starting transfers between devices: 115 us -> 128 us
  waiting for transfers between devices: 46.4 us -> 41.2 us
    ppermute x25, starting transfers between devices: 95.3 us -> 102 us  [shift(): lax.ppermute(values, axis, [(i, (i + by) % size) for i in range(size)])]
    all_to_all x2, starting transfers between devices: 7.01 us -> 13 us  [scatter(): back = lax.all_to_all(parts, axis, 0, 0, tiled=True)]
    ppermute x25, waiting for transfers between devices: 38 us -> 32.7 us  [shift(): lax.ppermute(values, axis, [(i, (i + by) % size) for i in range(size)])]
  transfers between devices with their start and end apart: 28 -> 28, of which waited for: 11 -> 12; matrix products, arithmetic and copies ran while one was open for 8% -> 8% of each run, Pallas kernels for 0% -> 0%
where the time goes in v9:
time: 214 us; the launch traced here: 213 us
  starting transfers between devices  128 us (60%)
  waiting for transfers between devices  41.2 us (19%)
  blocking collectives  15.6 us (7%)
  other arithmetic  12.3 us (6%)
  matrix products  7.61 us (4%)
  local copies, waits for them, and re-layouts  7.28 us (3%)
    ppermute x25, starting transfers between devices, shift(): lax.ppermute(values, axis, [(i, (i + by) % size) for i in range(size)])  102 us
    ppermute x25, waiting for transfers between devices, shift(): lax.ppermute(values, axis, [(i, (i + by) % size) for i in range(size)])  32.7 us
    all_gather x1, blocking collectives, shards(): lax.all_gather(jnp.concatenate([patches, out_grad], axis=1), 'zl', axis=0...  15.6 us
    all_to_all x2, starting transfers between devices, scatter(): back = lax.all_to_all(parts, axis, 0, 0, tiled=True)  13 us
    all_to_all x1, starting transfers between devices, to_all(): return lax.all_to_all(copies, axes, 0, 0, tiled=True)  12.9 us
    all_to_all x1, waiting for transfers between devices, to_all(): return lax.all_to_all(copies, axes, 0, 0, tiled=True)  5.31 us
    add x3, other arithmetic, add(): total = total + term.astype(F32)  4.66 us
    dot_general x2, matrix products, contract_tokens(): lax.dot_general(left, right, (((0,), (0,)), ((), ())), preferred_element_...  4.48 us
  transfers between devices with their start and end apart: 28, of which 12 were waited for; matrix products, arithmetic and copies ran while one was open for 8% of the time, Pallas kernels for 0%

profile of v9, /device:TPU:1, one launch (start us, length us, event | category | flops | bytes accessed | tf_op | source)
XLA Modules:
  0.0 213.1 jit_solution(6218410312624884057)
XLA Ops:
  1.5 15.6 %all_gather.3 = bf16[192,768]{1,0:T(8,128)(2,1)S(1)} all-gather(bf16[48,768]{1,0:T(8,128)(2,1)S(1)} %pad_maximum_fusion.15), channel_id=1, replica_groups=mesh['dp'=2,'y'=8,'zh'=2,'x'=4,'zl'=4] {'zl'}, dimensions={0}, use_global_device_ids=true | all-gather | bytes 368640 | tf_op jit(solution)/shard_map/all_gather | solution.py:127
  17.3 1.3 multiply_reduce_fusion.1
  19.3 12.9 %all-to-all-start = ((f32[16,1,1152]{2,1,0:T(1,128)}), f32[16,1,1152]{2,1,0:T(1,128)S(1)}, u32[]{:S(2)}, u32[]{:S(2)}) async-start(f32[16,1,1152]{2,1,0:T(1,128)} %broadcast_in_dim.53), calls=%async_computation | async-start | bytes 147456 | tf_op jit(solution)/shard_map/all_to_all | solution.py:44
  32.3 3.1 %collective-permute-start = (bf16[192,384]{1,0:T(8,128)(2,1)S(1)}, bf16[192,384]{1,0:T(8,128)(2,1)S(1)}, u32[]{:S(2)}, u32[]{:S(2)}) collective-permute-start(bf16[192,384]{1,0:T(8,128)(2,1)S(1)} %get-tuple-element.66), channel_id=1, source_target_pairs={{0,4},{4,8},{8,12},{12,0},{1,5},{5,9},{9,13},{13,1},{2,6},{6,10},{... | collective-permute-start | bytes 442376 | tf_op jit(solution)/shard_map/ppermute | solution.py:27
  35.4 3.4 %collective-permute-start.1 = (bf16[192,384]{1,0:T(8,128)(2,1)S(1)}, bf16[192,384]{1,0:T(8,128)(2,1)S(1)}, u32[]{:S(2)}, u32[]{:S(2)}) collective-permute-start(bf16[192,384]{1,0:T(8,128)(2,1)S(1)} %get-tuple-element.66), channel_id=1, source_target_pairs={{0,12},{4,0},{8,4},{12,8},{1,13},{5,1},{9,5},{13,9},{2,14},{6,2},{... | collective-permute-start | bytes 442376 | tf_op jit(solution)/shard_map/ppermute | solution.py:27
  38.8 5.3 %all-to-all-done = f32[16,1,1152]{2,1,0:T(1,128)S(1)} async-done(((f32[16,1,1152]{2,1,0:T(1,128)}), f32[16,1,1152]{2,1,0:T(1,128)S(1)}, u32[]{:S(2)}, u32[]{:S(2)}) %all-to-all-start) | async-done | bytes 73760 | tf_op jit(solution)/shard_map/all_to_all | solution.py:44
  44.5 4.7 %collective-permute-start.4 = (bf16[192,384]{1,0:T(8,128)(2,1)S(1)}, bf16[192,384]{1,0:T(8,128)(2,1)S(1)}, u32[]{:S(2)}, u32[]{:S(2)}) collective-permute-start(bf16[192,384]{1,0:T(8,128)(2,1)S(1)} %get-tuple-element.12), channel_id=1, source_target_pairs={{0,8},{4,12},{8,0},{12,4},{1,9},{5,13},{9,1},{13,5},{2,10},{6,14},... | collective-permute-start | bytes 442376 | tf_op jit(solution)/shard_map/ppermute | solution.py:27
  49.2 2.2 %collective-permute-start.2 = (bf16[288,384]{1,0:T(8,128)(2,1)S(1)}, bf16[288,384]{1,0:T(8,128)(2,1)S(1)}, u32[]{:S(2)}, u32[]{:S(2)}) collective-permute-start(bf16[288,384]{1,0:T(8,128)(2,1)S(1)} %get-tuple-element.72), channel_id=1, source_target_pairs={{0,4},{4,8},{8,12},{12,0},{1,5},{5,9},{9,13},{13,1},{2,6},{6,10},{... | collective-permute-start | bytes 663560 | tf_op jit(solution)/shard_map/ppermute | solution.py:27
  51.4 4.3 %collective-permute-start.3 = (bf16[288,384]{1,0:T(8,128)(2,1)S(1)}, bf16[288,384]{1,0:T(8,128)(2,1)S(1)}, u32[]{:S(2)}, u32[]{:S(2)}) collective-permute-start(bf16[288,384]{1,0:T(8,128)(2,1)S(1)} %get-tuple-element.73), channel_id=1, source_target_pairs={{0,12},{4,0},{8,4},{12,8},{1,13},{5,1},{9,5},{13,9},{2,14},{6,2},{... | collective-permute-start | bytes 663560 | tf_op jit(solution)/shard_map/ppermute | solution.py:27
  55.9 2.6 %collective-permute-done.2 = bf16[288,384]{1,0:T(8,128)(2,1)S(1)} collective-permute-done((bf16[288,384]{1,0:T(8,128)(2,1)S(1)}, bf16[288,384]{1,0:T(8,128)(2,1)S(1)}, u32[]{:S(2)}, u32[]{:S(2)}) %collective-permute-start.2) | collective-permute-done | bytes 221216 | tf_op jit(solution)/shard_map/ppermute | solution.py:27
  60.6 2.1 collective-permute-start.7
  62.7 4.0 %collective-permute-start.8 = (bf16[48,1536]{1,0:T(8,128)(2,1)S(1)}, bf16[48,1536]{1,0:T(8,128)(2,1)S(1)}, u32[]{:S(2)}, u32[]{:S(2)}) collective-permute-start(bf16[48,1536]{1,0:T(8,128)(2,1)S(1)} %get-tuple-element.64), channel_id=1, source_target_pairs={{0,192},{32,224},{64,0},{96,32},{128,64},{160,96},{192,128},{224,1... | collective-permute-start | bytes 442376 | tf_op jit(solution)/shard_map/ppermute | solution.py:27
  66.7 2.2 %collective-permute-start.5 = (bf16[96,1536]{1,0:T(8,128)(2,1)S(1)}, bf16[96,1536]{1,0:T(8,128)(2,1)S(1)}, u32[]{:S(2)}, u32[]{:S(2)}) collective-permute-start(bf16[96,1536]{1,0:T(8,128)(2,1)S(1)} %pad_maximum_fusion.4), channel_id=1, source_target_pairs={{0,32},{32,64},{64,96},{96,128},{128,160},{160,192},{192,224},{224... | collective-permute-start | bytes 884744 | tf_op jit(solution)/shard_map/ppermute | solution.py:27
  68.9 3.2 %collective-permute-start.6 = (bf16[48,1536]{1,0:T(8,128)(2,1)S(1)}, bf16[48,1536]{1,0:T(8,128)(2,1)S(1)}, u32[]{:S(2)}, u32[]{:S(2)}) collective-permute-start(bf16[48,1536]{1,0:T(8,128)(2,1)S(1)} %get-tuple-element.65), channel_id=1, source_target_pairs={{0,64},{32,96},{64,128},{96,160},{128,192},{160,224},{192,0},{224,... | collective-permute-start | bytes 442376 | tf_op jit(solution)/shard_map/ppermute | solution.py:27
  72.3 4.7 %collective-permute-done.6 = bf16[48,1536]{1,0:T(8,128)(2,1)S(1)} collective-permute-done((bf16[48,1536]{1,0:T(8,128)(2,1)S(1)}, bf16[48,1536]{1,0:T(8,128)(2,1)S(1)}, u32[]{:S(2)}, u32[]{:S(2)}) %collective-permute-start.6) | collective-permute-done | bytes 147488 | tf_op jit(solution)/shard_map/ppermute | solution.py:27
  77.2 3.0 %collective-permute-start.10 = (bf16[96,1536]{1,0:T(8,128)(2,1)S(1)}, bf16[96,1536]{1,0:T(8,128)(2,1)S(1)}, u32[]{:S(2)}, u32[]{:S(2)}) collective-permute-start(bf16[96,1536]{1,0:T(8,128)(2,1)S(1)} %pad_maximum_fusion.7), channel_id=1, source_target_pairs={{0,192},{32,224},{64,0},{96,32},{128,64},{160,96},{192,128},{224,1... | collective-permute-start | bytes 884744 | tf_op jit(solution)/shard_map/ppermute | solution.py:27
  80.1 5.4 %collective-permute-start.11 = (bf16[96,1536]{1,0:T(8,128)(2,1)S(1)}, bf16[96,1536]{1,0:T(8,128)(2,1)S(1)}, u32[]{:S(2)}, u32[]{:S(2)}) collective-permute-start(bf16[96,1536]{1,0:T(8,128)(2,1)S(1)} %pad_maximum_fusion.8), channel_id=1, source_target_pairs={{0,32},{32,64},{64,96},{96,128},{128,160},{160,192},{192,224},{224... | collective-permute-start | bytes 884744 | tf_op jit(solution)/shard_map/ppermute | solution.py:27
  85.6 1.9 collective-permute-start.12
  87.5 3.1 %collective-permute-start.9 = (bf16[96,1536]{1,0:T(8,128)(2,1)S(1)}, bf16[96,1536]{1,0:T(8,128)(2,1)S(1)}, u32[]{:S(2)}, u32[]{:S(2)}) collective-permute-start(bf16[96,1536]{1,0:T(8,128)(2,1)S(1)} %pad_maximum_fusion.5), channel_id=1, source_target_pairs={{0,64},{32,96},{64,128},{96,160},{128,192},{160,224},{192,0},{224,... | collective-permute-start | bytes 884744 | tf_op jit(solution)/shard_map/ppermute | solution.py:27
  90.6 6.4 %collective-permute-done.12 = bf16[96,1536]{1,0:T(8,128)(2,1)S(1)} collective-permute-done((bf16[96,1536]{1,0:T(8,128)(2,1)S(1)}, bf16[96,1536]{1,0:T(8,128)(2,1)S(1)}, u32[]{:S(2)}, u32[]{:S(2)}) %collective-permute-start.12) | collective-permute-done | bytes 294944 | tf_op jit(solution)/shard_map/ppermute | solution.py:27
  97.0 6.0 %collective-permute-done.9 = bf16[96,1536]{1,0:T(8,128)(2,1)S(1)} collective-permute-done((bf16[96,1536]{1,0:T(8,128)(2,1)S(1)}, bf16[96,1536]{1,0:T(8,128)(2,1)S(1)}, u32[]{:S(2)}, u32[]{:S(2)}) %collective-permute-start.9) | collective-permute-done | bytes 294944 | tf_op jit(solution)/shard_map/ppermute | solution.py:27
  103.2 8.1 %collective-permute-start.13 = (bf16[96,1536]{1,0:T(8,128)(2,1)S(1)}, bf16[96,1536]{1,0:T(8,128)(2,1)S(1)}, u32[]{:S(2)}, u32[]{:S(2)}) collective-permute-start(bf16[96,1536]{1,0:T(8,128)(2,1)S(1)} %add_convert_fusion), channel_id=1, source_target_pairs={{0,16},{16,0},{1,17},{17,1},{2,18},{18,2},{3,19},{19,3},{4,20},{20... | collective-permute-start | bytes 884744 | tf_op jit(solution)/shard_map/ppermute | solution.py:27
  111.3 4.2 %collective-permute-done.13 = bf16[96,1536]{1,0:T(8,128)(2,1)S(1)} collective-permute-done((bf16[96,1536]{1,0:T(8,128)(2,1)S(1)}, bf16[96,1536]{1,0:T(8,128)(2,1)S(1)}, u32[]{:S(2)}, u32[]{:S(2)}) %collective-permute-start.13) | collective-permute-done | bytes 294944 | tf_op jit(solution)/shard_map/ppermute | solution.py:27
  116.1 1.0 copy-done.2
  117.3 2.1 collective-permute-start.14
  119.4 4.4 %collective-permute-start.15 = (bf16[96,1664]{1,0:T(8,128)(2,1)S(1)}, bf16[96,1664]{1,0:T(8,128)(2,1)}, u32[]{:S(2)}, u32[]{:S(2)}) collective-permute-start(bf16[96,1664]{1,0:T(8,128)(2,1)S(1)} %pad_maximum_fusion.3), channel_id=1, source_target_pairs={{0,224},{32,0},{64,32},{96,64},{128,96},{160,128},{192,160},{224,1... | collective-permute-start | bytes 958472 | tf_op jit(solution)/shard_map/ppermute | solution.py:27
  124.0 2.6 %collective-permute-done.14 = bf16[96,1664]{1,0:T(8,128)(2,1)} collective-permute-done((bf16[96,1664]{1,0:T(8,128)(2,1)S(1)}, bf16[96,1664]{1,0:T(8,128)(2,1)}, u32[]{:S(2)}, u32[]{:S(2)}) %collective-permute-start.14) | collective-permute-done | bytes 319520 | tf_op jit(solution)/shard_map/ppermute | solution.py:27
  126.6 1.9 collective-permute-start.16
  128.5 4.6 %collective-permute-start.17 = (bf16[96,1664]{1,0:T(8,128)(2,1)}, bf16[96,1664]{1,0:T(8,128)(2,1)S(1)}, u32[]{:S(2)}, u32[]{:S(2)}) collective-permute-start(bf16[96,1664]{1,0:T(8,128)(2,1)} %collective-permute-done.15), channel_id=1, source_target_pairs={{0,224},{32,0},{64,32},{96,64},{128,96},{160,128},{192,160},{224,1... | collective-permute-start | bytes 958472 | tf_op jit(solution)/shard_map/ppermute | solution.py:27
  133.1 1.0 slice_dynamic-update-slice_fusion.11
  134.1 1.0 slice_dynamic-update-slice_fusion.10
  136.6 1.9 collective-permute-start.18
  138.6 4.6 %collective-permute-start.19 = (bf16[96,1664]{1,0:T(8,128)(2,1)S(1)}, bf16[96,1664]{1,0:T(8,128)(2,1)S(1)}, u32[]{:S(2)}, u32[]{:S(2)}) collective-permute-start(bf16[96,1664]{1,0:T(8,128)(2,1)S(1)} %collective-permute-done.17), channel_id=1, source_target_pairs={{0,224},{32,0},{64,32},{96,64},{128,96},{160,128},{192,160},{224,1... | collective-permute-start | bytes 958472 | tf_op jit(solution)/shard_map/ppermute | solution.py:27
  143.2 2.3 %collective-permute-done.18 = bf16[96,1664]{1,0:T(8,128)(2,1)S(1)} collective-permute-done((bf16[96,1664]{1,0:T(8,128)(2,1)S(1)}, bf16[96,1664]{1,0:T(8,128)(2,1)S(1)}, u32[]{:S(2)}, u32[]{:S(2)}) %collective-permute-start.18) | collective-permute-done | bytes 319520 | tf_op jit(solution)/shard_map/ppermute | solution.py:27
  145.6 1.9 collective-permute-start.20
  147.5 5.4 %collective-permute-start.21 = (bf16[48,1664]{1,0:T(8,128)(2,1)S(1)}, bf16[48,1664]{1,0:T(8,128)(2,1)S(1)}, u32[]{:S(2)}, u32[]{:S(2)}) collective-permute-start(bf16[48,1664]{1,0:T(8,128)(2,1)S(1)} %slice.270), channel_id=1, source_target_pairs={{0,224},{32,0},{64,32},{96,64},{128,96},{160,128},{192,160},{224,1... | collective-permute-start | bytes 479240 | tf_op jit(solution)/shard_map/ppermute | solution.py:27
  153.6 3.2 %collective-permute-done.21 = bf16[48,1664]{1,0:T(8,128)(2,1)S(1)} collective-permute-done((bf16[48,1664]{1,0:T(8,128)(2,1)S(1)}, bf16[48,1664]{1,0:T(8,128)(2,1)S(1)}, u32[]{:S(2)}, u32[]{:S(2)}) %collective-permute-start.21) | collective-permute-done | bytes 159776 | tf_op jit(solution)/shard_map/ppermute | solution.py:27
  158.9 1.2 pad_maximum_fusion
  160.2 9.5 %all-to-all-start.1 = ((bf16[4,200,896]{2,1,0:T(8,128)(2,1)}), bf16[4,200,896]{2,1,0:T(8,128)(2,1)S(1)}, u32[]{:S(2)}, u32[]{:S(2)}) async-start(bf16[4,200,896]{2,1,0:T(8,128)(2,1)} %pad_maximum_fusion), calls=%async_computation.1 | async-start | bytes 2867200 | tf_op jit(solution)/shard_map/all_to_all | solution.py:116
  169.7 3.0 %convolution_convert_fusion.2 = bf16[768,384]{1,0:T(8,128)(2,1)} fusion(bf16[768,768]{1,0:T(8,128)(2,1)} %copy-done.4, bf16[768,384]{1,0:T(8,128)(2,1)S(1)} %maximum_dynamic-update-slice_fusion), kind=kOutput, calls=%fused_computation.5 | convolution fusion | flops 453279744 | bytes 2359296 | tf_op jit(solution)/shard_map/dot_general | solution.py:15
  172.7 14.9 %collective-permute-start.23 = (bf16[768,384]{1,0:T(8,128)(2,1)}, bf16[768,384]{1,0:T(8,128)(2,1)}, u32[]{:S(2)}, u32[]{:S(2)}) collective-permute-start(bf16[768,384]{1,0:T(8,128)(2,1)} %convolution_convert_fusion.2), channel_id=1, source_target_pairs={{0,256},{256,0},{1,257},{257,1},{2,258},{258,2},{3,259},{259,3},{4... | collective-permute-start | bytes 1769480 | tf_op jit(solution)/shard_map/ppermute | solution.py:27
  187.5 1.5 convolution_convert_fusion.3
  189.0 1.9 collective-permute-start.22
  192.0 3.5 %all-to-all-start.2 = ((bf16[4,56,896]{2,1,0:T(8,128)(2,1)}), bf16[4,56,896]{2,1,0:T(8,128)(2,1)S(1)}, u32[]{:S(2)}, u32[]{:S(2)}) async-start(bf16[4,56,896]{2,1,0:T(8,128)(2,1)} %pad_maximum_fusion.2), calls=%async_computation.2 | async-start | bytes 802816 | tf_op jit(solution)/shard_map/all_to_all | solution.py:116
  195.6 2.4 %convert_add_fusion = f32[768,384]{1,0:T(8,128)} fusion(bf16[768,384]{1,0:T(8,128)(2,1)} %collective-permute-done.23, bf16[768,384]{1,0:T(8,128)(2,1)} %convolution_convert_fusion.2), kind=kLoop, calls=%fused_computation.8 | loop fusion | flops 884736 | bytes 2359296 | tf_op jit(solution)/shard_map/add | solution.py:37
  197.9 2.2 %convert_add_fusion.1 = f32[384,768]{1,0:T(8,128)} fusion(bf16[384,768]{1,0:T(8,128)(2,1)S(1)} %collective-permute-done.22, bf16[384,768]{1,0:T(8,128)(2,1)} %convolution_convert_fusion.3), kind=kLoop, calls=%fused_computation.9 | loop fusion | flops 884736 | bytes 2359296 | tf_op jit(solution)/shard_map/add | solution.py:37
  200.2 3.2 %all-to-all-done.2 = bf16[4,56,896]{2,1,0:T(8,128)(2,1)S(1)} async-done(((bf16[4,56,896]{2,1,0:T(8,128)(2,1)}), bf16[4,56,896]{2,1,0:T(8,128)(2,1)S(1)}, u32[]{:S(2)}, u32[]{:S(2)}) %all-to-all-start.2) | async-done | bytes 401440 | tf_op jit(solution)/shard_map/all_to_all | solution.py:116
  203.4 7.6 %collective-permute-start.24 = (f32[384]{0:T(512)S(1)}, f32[384]{0:T(512)S(1)}, u32[]{:S(2)}, u32[]{:S(2)}) collective-permute-start(f32[384]{0:T(512)S(1)} %slice_add_fusion), channel_id=1, source_target_pairs={{0,256},{256,0},{1,257},{257,1},{2,258},{258,2},{3,259},{259,3},{4... | collective-permute-start | bytes 4616 | tf_op jit(solution)/shard_map/ppermute | solution.py:27
  (122 shorter events, 13.3 us)
Async XLA Ops:
  0.6 58.9 %copy-start = (bf16[768,384]{1,0:T(8,128)(2,1)S(1)}, bf16[768,384]{1,0:T(8,128)(2,1)}, u32[]{:S(2)}) copy-start(bf16[768,384]{1,0:T(8,128)(2,1)} %param.8) | copy-start | bytes 1769476
  17.1 27.2 %copy-start.7 = (f32[384]{0:T(512)S(1)}, f32[384]{0:T(512)}, u32[]{:S(2)}) copy-start(f32[384]{0:T(512)} %param.6) | copy-start | bytes 4612
  19.3 24.8 %all-to-all-start = ((f32[16,1,1152]{2,1,0:T(1,128)}), f32[16,1,1152]{2,1,0:T(1,128)S(1)}, u32[]{:S(2)}, u32[]{:S(2)}) async-start(f32[16,1,1152]{2,1,0:T(1,128)} %broadcast_in_dim.53), calls=%async_computation | async-start | bytes 147456 | tf_op jit(solution)/shard_map/all_to_all | solution.py:44
  32.3 12.1 %collective-permute-start = (bf16[192,384]{1,0:T(8,128)(2,1)S(1)}, bf16[192,384]{1,0:T(8,128)(2,1)S(1)}, u32[]{:S(2)}, u32[]{:S(2)}) collective-permute-start(bf16[192,384]{1,0:T(8,128)(2,1)S(1)} %get-tuple-element.66), channel_id=1, source_target_pairs={{0,4},{4,8},{8,12},{12,0},{1,5},{5,9},{9,13},{13,1},{2,6},{6,10},{... | collective-permute-start | bytes 442376 | tf_op jit(solution)/shard_map/ppermute | solution.py:27
  35.4 9.0 %collective-permute-start.1 = (bf16[192,384]{1,0:T(8,128)(2,1)S(1)}, bf16[192,384]{1,0:T(8,128)(2,1)S(1)}, u32[]{:S(2)}, u32[]{:S(2)}) collective-permute-start(bf16[192,384]{1,0:T(8,128)(2,1)S(1)} %get-tuple-element.66), channel_id=1, source_target_pairs={{0,12},{4,0},{8,4},{12,8},{1,13},{5,1},{9,5},{13,9},{2,14},{6,2},{... | collective-permute-start | bytes 442376 | tf_op jit(solution)/shard_map/ppermute | solution.py:27
  44.5 14.1 %collective-permute-start.4 = (bf16[192,384]{1,0:T(8,128)(2,1)S(1)}, bf16[192,384]{1,0:T(8,128)(2,1)S(1)}, u32[]{:S(2)}, u32[]{:S(2)}) collective-permute-start(bf16[192,384]{1,0:T(8,128)(2,1)S(1)} %get-tuple-element.12), channel_id=1, source_target_pairs={{0,8},{4,12},{8,0},{12,4},{1,9},{5,13},{9,1},{13,5},{2,10},{6,14},... | collective-permute-start | bytes 442376 | tf_op jit(solution)/shard_map/ppermute | solution.py:27
  49.2 9.3 %collective-permute-start.2 = (bf16[288,384]{1,0:T(8,128)(2,1)S(1)}, bf16[288,384]{1,0:T(8,128)(2,1)S(1)}, u32[]{:S(2)}, u32[]{:S(2)}) collective-permute-start(bf16[288,384]{1,0:T(8,128)(2,1)S(1)} %get-tuple-element.72), channel_id=1, source_target_pairs={{0,4},{4,8},{8,12},{12,0},{1,5},{5,9},{9,13},{13,1},{2,6},{6,10},{... | collective-permute-start | bytes 663560 | tf_op jit(solution)/shard_map/ppermute | solution.py:27
  51.4 7.1 %collective-permute-start.3 = (bf16[288,384]{1,0:T(8,128)(2,1)S(1)}, bf16[288,384]{1,0:T(8,128)(2,1)S(1)}, u32[]{:S(2)}, u32[]{:S(2)}) collective-permute-start(bf16[288,384]{1,0:T(8,128)(2,1)S(1)} %get-tuple-element.73), channel_id=1, source_target_pairs={{0,12},{4,0},{8,4},{12,8},{1,13},{5,1},{9,5},{13,9},{2,14},{6,2},{... | collective-permute-start | bytes 663560 | tf_op jit(solution)/shard_map/ppermute | solution.py:27
  55.7 2.9 %copy-start.1 = (bf16[384,768]{1,0:T(8,128)(2,1)S(1)}, bf16[384,768]{1,0:T(8,128)(2,1)}, u32[]{:S(2)}) copy-start(bf16[384,768]{1,0:T(8,128)(2,1)} %param.7) | copy-start | bytes 1769476
  60.6 11.6 %collective-permute-start.7 = (bf16[96,1536]{1,0:T(8,128)(2,1)S(1)}, bf16[96,1536]{1,0:T(8,128)(2,1)S(1)}, u32[]{:S(2)}, u32[]{:S(2)}) collective-permute-start(bf16[96,1536]{1,0:T(8,128)(2,1)S(1)} %pad_maximum_fusion.6), channel_id=1, source_target_pairs={{0,224},{32,0},{64,32},{96,64},{128,96},{160,128},{192,160},{224,1... | collective-permute-start | bytes 884744 | tf_op jit(solution)/shard_map/ppermute | solution.py:27
  62.7 9.5 %collective-permute-start.8 = (bf16[48,1536]{1,0:T(8,128)(2,1)S(1)}, bf16[48,1536]{1,0:T(8,128)(2,1)S(1)}, u32[]{:S(2)}, u32[]{:S(2)}) collective-permute-start(bf16[48,1536]{1,0:T(8,128)(2,1)S(1)} %get-tuple-element.64), channel_id=1, source_target_pairs={{0,192},{32,224},{64,0},{96,32},{128,64},{160,96},{192,128},{224,1... | collective-permute-start | bytes 442376 | tf_op jit(solution)/shard_map/ppermute | solution.py:27
  66.7 10.3 %collective-permute-start.5 = (bf16[96,1536]{1,0:T(8,128)(2,1)S(1)}, bf16[96,1536]{1,0:T(8,128)(2,1)S(1)}, u32[]{:S(2)}, u32[]{:S(2)}) collective-permute-start(bf16[96,1536]{1,0:T(8,128)(2,1)S(1)} %pad_maximum_fusion.4), channel_id=1, source_target_pairs={{0,32},{32,64},{64,96},{96,128},{128,160},{160,192},{192,224},{224... | collective-permute-start | bytes 884744 | tf_op jit(solution)/shard_map/ppermute | solution.py:27
  68.9 8.1 %collective-permute-start.6 = (bf16[48,1536]{1,0:T(8,128)(2,1)S(1)}, bf16[48,1536]{1,0:T(8,128)(2,1)S(1)}, u32[]{:S(2)}, u32[]{:S(2)}) collective-permute-start(bf16[48,1536]{1,0:T(8,128)(2,1)S(1)} %get-tuple-element.65), channel_id=1, source_target_pairs={{0,64},{32,96},{64,128},{96,160},{128,192},{160,224},{192,0},{224,... | collective-permute-start | bytes 442376 | tf_op jit(solution)/shard_map/ppermute | solution.py:27
  77.2 13.4 %collective-permute-start.10 = (bf16[96,1536]{1,0:T(8,128)(2,1)S(1)}, bf16[96,1536]{1,0:T(8,128)(2,1)S(1)}, u32[]{:S(2)}, u32[]{:S(2)}) collective-permute-start(bf16[96,1536]{1,0:T(8,128)(2,1)S(1)} %pad_maximum_fusion.7), channel_id=1, source_target_pairs={{0,192},{32,224},{64,0},{96,32},{128,64},{160,96},{192,128},{224,1... | collective-permute-start | bytes 884744 | tf_op jit(solution)/shard_map/ppermute | solution.py:27
  80.1 10.5 %collective-permute-start.11 = (bf16[96,1536]{1,0:T(8,128)(2,1)S(1)}, bf16[96,1536]{1,0:T(8,128)(2,1)S(1)}, u32[]{:S(2)}, u32[]{:S(2)}) collective-permute-start(bf16[96,1536]{1,0:T(8,128)(2,1)S(1)} %pad_maximum_fusion.8), channel_id=1, source_target_pairs={{0,32},{32,64},{64,96},{96,128},{128,160},{160,192},{192,224},{224... | collective-permute-start | bytes 884744 | tf_op jit(solution)/shard_map/ppermute | solution.py:27
  85.6 11.5 %collective-permute-start.12 = (bf16[96,1536]{1,0:T(8,128)(2,1)S(1)}, bf16[96,1536]{1,0:T(8,128)(2,1)S(1)}, u32[]{:S(2)}, u32[]{:S(2)}) collective-permute-start(bf16[96,1536]{1,0:T(8,128)(2,1)S(1)} %pad_maximum_fusion.9), channel_id=1, source_target_pairs={{0,224},{32,0},{64,32},{96,64},{128,96},{160,128},{192,160},{224,1... | collective-permute-start | bytes 884744 | tf_op jit(solution)/shard_map/ppermute | solution.py:27
  87.5 15.5 %collective-permute-start.9 = (bf16[96,1536]{1,0:T(8,128)(2,1)S(1)}, bf16[96,1536]{1,0:T(8,128)(2,1)S(1)}, u32[]{:S(2)}, u32[]{:S(2)}) collective-permute-start(bf16[96,1536]{1,0:T(8,128)(2,1)S(1)} %pad_maximum_fusion.5), channel_id=1, source_target_pairs={{0,64},{32,96},{64,128},{96,160},{128,192},{160,224},{192,0},{224,... | collective-permute-start | bytes 884744 | tf_op jit(solution)/shard_map/ppermute | solution.py:27
  103.2 12.3 %collective-permute-start.13 = (bf16[96,1536]{1,0:T(8,128)(2,1)S(1)}, bf16[96,1536]{1,0:T(8,128)(2,1)S(1)}, u32[]{:S(2)}, u32[]{:S(2)}) collective-permute-start(bf16[96,1536]{1,0:T(8,128)(2,1)S(1)} %add_convert_fusion), channel_id=1, source_target_pairs={{0,16},{16,0},{1,17},{17,1},{2,18},{18,2},{3,19},{19,3},{4,20},{20... | collective-permute-start | bytes 884744 | tf_op jit(solution)/shard_map/ppermute | solution.py:27
  116.1 1.0 copy-start.2
  117.3 9.2 %collective-permute-start.14 = (bf16[96,1664]{1,0:T(8,128)(2,1)S(1)}, bf16[96,1664]{1,0:T(8,128)(2,1)}, u32[]{:S(2)}, u32[]{:S(2)}) collective-permute-start(bf16[96,1664]{1,0:T(8,128)(2,1)S(1)} %pad_maximum_fusion.3), channel_id=1, source_target_pairs={{0,32},{32,64},{64,96},{96,128},{128,160},{160,192},{192,224},{224... | collective-permute-start | bytes 958472 | tf_op jit(solution)/shard_map/ppermute | solution.py:27
  119.4 9.1 %collective-permute-start.15 = (bf16[96,1664]{1,0:T(8,128)(2,1)S(1)}, bf16[96,1664]{1,0:T(8,128)(2,1)}, u32[]{:S(2)}, u32[]{:S(2)}) collective-permute-start(bf16[96,1664]{1,0:T(8,128)(2,1)S(1)} %pad_maximum_fusion.3), channel_id=1, source_target_pairs={{0,224},{32,0},{64,32},{96,64},{128,96},{160,128},{192,160},{224,1... | collective-permute-start | bytes 958472 | tf_op jit(solution)/shard_map/ppermute | solution.py:27
  123.9 9.2 %copy-start.3 = (bf16[768,768]{1,0:T(8,128)(2,1)S(1)}, bf16[768,768]{1,0:T(8,128)(2,1)}, u32[]{:S(2)}) copy-start(bf16[768,768]{1,0:T(8,128)(2,1)} %copy-done.2) | copy-start | bytes 3538948
  126.6 10.0 %collective-permute-start.16 = (bf16[96,1664]{1,0:T(8,128)(2,1)}, bf16[96,1664]{1,0:T(8,128)(2,1)S(1)}, u32[]{:S(2)}, u32[]{:S(2)}) collective-permute-start(bf16[96,1664]{1,0:T(8,128)(2,1)} %collective-permute-done.14), channel_id=1, source_target_pairs={{0,32},{32,64},{64,96},{96,128},{128,160},{160,192},{192,224},{224... | collective-permute-start | bytes 958472 | tf_op jit(solution)/shard_map/ppermute | solution.py:27
  128.5 10.1 %collective-permute-start.17 = (bf16[96,1664]{1,0:T(8,128)(2,1)}, bf16[96,1664]{1,0:T(8,128)(2,1)S(1)}, u32[]{:S(2)}, u32[]{:S(2)}) collective-permute-start(bf16[96,1664]{1,0:T(8,128)(2,1)} %collective-permute-done.15), channel_id=1, source_target_pairs={{0,224},{32,0},{64,32},{96,64},{128,96},{160,128},{192,160},{224,1... | collective-permute-start | bytes 958472 | tf_op jit(solution)/shard_map/ppermute | solution.py:27
  136.6 8.9 %collective-permute-start.18 = (bf16[96,1664]{1,0:T(8,128)(2,1)S(1)}, bf16[96,1664]{1,0:T(8,128)(2,1)S(1)}, u32[]{:S(2)}, u32[]{:S(2)}) collective-permute-start(bf16[96,1664]{1,0:T(8,128)(2,1)S(1)} %collective-permute-done.16), channel_id=1, source_target_pairs={{0,32},{32,64},{64,96},{96,128},{128,160},{160,192},{192,224},{224... | collective-permute-start | bytes 958472 | tf_op jit(solution)/shard_map/ppermute | solution.py:27
  138.6 8.9 %collective-permute-start.19 = (bf16[96,1664]{1,0:T(8,128)(2,1)S(1)}, bf16[96,1664]{1,0:T(8,128)(2,1)S(1)}, u32[]{:S(2)}, u32[]{:S(2)}) collective-permute-start(bf16[96,1664]{1,0:T(8,128)(2,1)S(1)} %collective-permute-done.17), channel_id=1, source_target_pairs={{0,224},{32,0},{64,32},{96,64},{128,96},{160,128},{192,160},{224,1... | collective-permute-start | bytes 958472 | tf_op jit(solution)/shard_map/ppermute | solution.py:27
  145.6 8.1 %collective-permute-start.20 = (bf16[48,1664]{1,0:T(8,128)(2,1)S(1)}, bf16[48,1664]{1,0:T(8,128)(2,1)S(1)}, u32[]{:S(2)}, u32[]{:S(2)}) collective-permute-start(bf16[48,1664]{1,0:T(8,128)(2,1)S(1)} %slice.268), channel_id=1, source_target_pairs={{0,32},{32,64},{64,96},{96,128},{128,160},{160,192},{192,224},{224... | collective-permute-start | bytes 479240 | tf_op jit(solution)/shard_map/ppermute | solution.py:27
  147.5 9.4 %collective-permute-start.21 = (bf16[48,1664]{1,0:T(8,128)(2,1)S(1)}, bf16[48,1664]{1,0:T(8,128)(2,1)S(1)}, u32[]{:S(2)}, u32[]{:S(2)}) collective-permute-start(bf16[48,1664]{1,0:T(8,128)(2,1)S(1)} %slice.270), channel_id=1, source_target_pairs={{0,224},{32,0},{64,32},{96,64},{128,96},{160,128},{192,160},{224,1... | collective-permute-start | bytes 479240 | tf_op jit(solution)/shard_map/ppermute | solution.py:27
  156.9 1.0 copy-start.5
  156.9 1.9 copy-start.4
  160.2 30.8 %all-to-all-start.1 = ((bf16[4,200,896]{2,1,0:T(8,128)(2,1)}), bf16[4,200,896]{2,1,0:T(8,128)(2,1)S(1)}, u32[]{:S(2)}, u32[]{:S(2)}) async-start(bf16[4,200,896]{2,1,0:T(8,128)(2,1)} %pad_maximum_fusion), calls=%async_computation.1 | async-start | bytes 2867200 | tf_op jit(solution)/shard_map/all_to_all | solution.py:116
  169.7 17.9 %copy-start.6 = (bf16[768,768]{1,0:T(8,128)(2,1)S(1)}, bf16[768,768]{1,0:T(8,128)(2,1)}, u32[]{:S(2)}) copy-start(bf16[768,768]{1,0:T(8,128)(2,1)} %copy-done.5) | copy-start | bytes 3538948
  172.7 22.9 %collective-permute-start.23 = (bf16[768,384]{1,0:T(8,128)(2,1)}, bf16[768,384]{1,0:T(8,128)(2,1)}, u32[]{:S(2)}, u32[]{:S(2)}) collective-permute-start(bf16[768,384]{1,0:T(8,128)(2,1)} %convolution_convert_fusion.2), channel_id=1, source_target_pairs={{0,256},{256,0},{1,257},{257,1},{2,258},{258,2},{3,259},{259,3},{4... | collective-permute-start | bytes 1769480 | tf_op jit(solution)/shard_map/ppermute | solution.py:27
  189.0 8.9 %collective-permute-start.22 = (bf16[384,768]{1,0:T(8,128)(2,1)}, bf16[384,768]{1,0:T(8,128)(2,1)S(1)}, u32[]{:S(2)}, u32[]{:S(2)}) collective-permute-start(bf16[384,768]{1,0:T(8,128)(2,1)} %convolution_convert_fusion.3), channel_id=1, source_target_pairs={{0,256},{256,0},{1,257},{257,1},{2,258},{258,2},{3,259},{259,3},{4... | collective-permute-start | bytes 1769480 | tf_op jit(solution)/shard_map/ppermute | solution.py:27
  192.0 11.4 %all-to-all-start.2 = ((bf16[4,56,896]{2,1,0:T(8,128)(2,1)}), bf16[4,56,896]{2,1,0:T(8,128)(2,1)S(1)}, u32[]{:S(2)}, u32[]{:S(2)}) async-start(bf16[4,56,896]{2,1,0:T(8,128)(2,1)} %pad_maximum_fusion.2), calls=%async_computation.2 | async-start | bytes 802816 | tf_op jit(solution)/shard_map/all_to_all | solution.py:116
  203.4 9.1 %collective-permute-start.24 = (f32[384]{0:T(512)S(1)}, f32[384]{0:T(512)S(1)}, u32[]{:S(2)}, u32[]{:S(2)}) collective-permute-start(f32[384]{0:T(512)S(1)} %slice_add_fusion), channel_id=1, source_target_pairs={{0,256},{256,0},{1,257},{257,1},{2,258},{258,2},{3,259},{259,3},{4... | collective-permute-start | bytes 4616 | tf_op jit(solution)/shard_map/ppermute | solution.py:27
